TPU v7x, 512 devices: a whole 4x4x16 slice. The times are simulated.
512 devices in a mesh: seq: 32 (over z, core), expert: 8 (over y, x_hi), tensor: 2 (over x_lo).
Axes of the slice: x: 4 (x_hi: 2, x_lo: 2; x = x_hi * 2 + x_lo), y: 4, z: 16, core: 2. Of those that a mesh axis runs over, the one named last changes fastest.
Arguments:
- tokens: bfloat16 [2048, 4096], P('seq', 'expert'), may hold values from -60 to 60
- routes: int32 [2048, 2], P('seq'), may hold values from 0 to 7, as said below
- chosen_expert_weight: float32 [2048, 2], P('seq'), may hold values from 0.1 to 1
- expert_gate_weight: bfloat16 [8, 4096, 8192], P('expert', None, ('seq', 'tensor')), may hold values from -0.09375 to 0.09375
- expert_up_weight: bfloat16 [8, 4096, 8192], P('expert', None, ('seq', 'tensor')), may hold values from -0.09375 to 0.09375
- expert_down_weight: bfloat16 [8, 8192, 4096], P('expert', None, 'seq'), may hold values from -0.0625 to 0.0625
- adapter_down_weight: bfloat16 [32, 4096], P(None, 'expert'), may hold values from -0.09375 to 0.09375
- adapter_up_weight: bfloat16 [32, 4096], P(None, 'expert'), may hold values from -1.5 to 1.5
- document_task_index: int32 [1], replicated, may hold values from 0 to 1
- counts: int32 [1], replicated, may hold values from 1024 to 2048
- final_norm_scale: float32 [4096], P('expert'), may hold values from 0.25 to 1.75
Outputs:
- embedding: float32 [1, 4096], replicated
Inputs may be any that keep to these rules, and one draw needn't show every extreme that they name: `routes`: within each aligned block of 64 rows the two ids of a token differ and no id is named more than 20 times; one id, the same in every block, is named exactly 20 times in every block.
All inputs are finite; a program needn't handle non-finite values.
Results may differ from a plain program's by a relative error of at most 0.0025.
Values may be sent and summed in bfloat16 or wider, within the bound.
No kernel may reach another device: no remote copies, remote signals or barrier semaphores. Data moves between devices by JAX's collectives and lax.ppermute only.
A program may use at most 64 MiB of HBM per device.

v0:
```python
import jax
import jax.numpy as jnp
from jax import lax
from jax.sharding import PartitionSpec as P

TASK_COUNT = 2


adapter_scale = 0.5


def expert_hidden(block_in, expert_gate_weight, expert_up_weight):
    gate_act = jnp.einsum(
        "...jcd,jdf->...jcf", block_in, expert_gate_weight, preferred_element_type=jnp.float32
    )
    up_act = jnp.einsum(
        "...jcd,jdf->...jcf", block_in, expert_up_weight, preferred_element_type=jnp.float32
    )
    return (jax.nn.silu(gate_act) * up_act).astype(jnp.bfloat16)


def local(
    tokens,
    routes,
    chosen_expert_weight,
    expert_gate_weight,
    expert_up_weight,
    expert_down_weight,
    adapter_down_weight,
    adapter_up_weight,
    document_task_index,
    counts,
    final_norm_scale,
):
    tok_rows, feat_cols = tokens.shape
    local_experts = expert_gate_weight.shape[0]
    seq_count = lax.axis_size("seq")
    group_count = lax.axis_size("expert")
    total_experts = local_experts * group_count
    capacity = tok_rows * 5 // 16
    slot_count = total_experts * capacity
    full_width = feat_cols * group_count
    pair_ids = routes.reshape(-1)
    expert_iota = jnp.arange(total_experts, dtype=jnp.int32)
    one_hot = (pair_ids[:, None] == expert_iota[None, :]).astype(jnp.int32)
    slot_index = jnp.sum(jnp.cumsum(one_hot, axis=0) * one_hot, axis=1) - 1
    target = pair_ids * capacity + slot_index
    placed = (target[:, None] == jnp.arange(slot_count, dtype=jnp.int32)[None, :]).reshape(
        tok_rows, 2, slot_count
    )
    chooser = jnp.any(placed, axis=1).astype(jnp.bfloat16)
    combiner = jnp.sum(placed.astype(jnp.float32) * chosen_expert_weight[:, :, None], axis=1)
    outgoing = lax.dot_general(
        chooser, tokens, (((0,), (0,)), ((), ())), preferred_element_type=jnp.float32
    )
    outgoing = outgoing.astype(jnp.bfloat16).reshape(
        group_count, local_experts, capacity, feat_cols
    )
    received = lax.all_to_all(outgoing, "expert", split_axis=0, concat_axis=3, tiled=True)
    hidden = expert_hidden(
        lax.all_gather(received, "seq", axis=0, tiled=True), expert_gate_weight, expert_up_weight
    )
    summed = jnp.einsum(
        "sjcf,jfe->sjce",
        lax.all_gather(hidden, ("seq", "tensor"), axis=3, tiled=True),
        expert_down_weight,
        preferred_element_type=jnp.float32,
    )
    expert_out = summed.astype(jnp.bfloat16)
    returned = lax.all_to_all(
        lax.all_to_all(expert_out, "seq", split_axis=0, concat_axis=3, tiled=True),
        "expert",
        split_axis=3,
        concat_axis=1,
        tiled=True,
    )
    returned = returned.reshape(slot_count, feat_cols).astype(jnp.float32)
    expert_mixture_layer = jnp.dot(combiner, returned, precision=lax.Precision.HIGHEST)
    doc_total = document_task_index.shape[0]
    doc_length = tok_rows * seq_count // doc_total
    position = lax.axis_index("seq") * tok_rows + jnp.arange(tok_rows, dtype=jnp.int32)
    doc_of = position // doc_length
    doc_iota = jnp.arange(doc_total, dtype=jnp.int32)
    member = doc_of[:, None] == doc_iota[None, :]
    token_task_index = jnp.sum(jnp.where(member, document_task_index[None, :], 0), axis=1)
    allowed = jnp.sum(jnp.where(member, counts[None, :], 0), axis=1)
    low_part = lax.dot_general(
        tokens, adapter_down_weight, (((1,), (1,)), ((), ())), preferred_element_type=jnp.float32
    )
    narrow_all_tasks = lax.psum(low_part, "expert")
    adapter_depth = adapter_down_weight.shape[0] // TASK_COUNT
    task_mask = (
        jnp.arange(adapter_down_weight.shape[0], dtype=jnp.int32)[None, :] // adapter_depth
        == token_task_index[:, None]
    )
    narrow_projection = jnp.where(task_mask, narrow_all_tasks, 0.0).astype(jnp.bfloat16)
    adapted_rows = jnp.dot(narrow_projection, adapter_up_weight, preferred_element_type=jnp.float32)
    mixture_rows = tokens.astype(jnp.float32) + expert_mixture_layer + adapter_scale * adapted_rows
    squares = lax.psum(jnp.sum(mixture_rows * mixture_rows, axis=1), "expert")
    normed = mixture_rows * lax.rsqrt(squares[:, None] / full_width + 1e-05) * final_norm_scale
    in_count = position - doc_of * doc_length < allowed
    pooling = (member & in_count[:, None]).astype(jnp.float32)
    partial_value = lax.dot_general(
        pooling, normed, (((0,), (0,)), ((), ())), precision=lax.Precision.HIGHEST
    )
    own_group = (jnp.arange(group_count, dtype=jnp.int32) == lax.axis_index("expert")).astype(
        jnp.float32
    )
    spread_out = (own_group[None, :, None] * partial_value[:, None, :]).reshape(
        doc_total, full_width
    )
    pooled = lax.psum(spread_out, ("seq", "expert"))
    return pooled * lax.rsqrt(jnp.mean(pooled * pooled, axis=1, keepdims=True) + 1e-06)


def solution(mesh):
    return jax.shard_map(
        local,
        mesh=mesh,
        in_specs=(
            P("seq", "expert"),
            P("seq", None),
            P("seq", None),
            P("expert", None, ("seq", "tensor")),
            P("expert", None, ("seq", "tensor")),
            P("expert", None, "seq"),
            P(None, "expert"),
            P(None, "expert"),
            P(),
            P(),
            P("expert"),
        ),
        out_specs=P(),
        check_vma=False,
    )
```

profile of v0, /device:TPU:1, one launch (start us, length us, event | category | flops | bytes accessed | tf_op | source)
XLA Modules:
  0.0 1719.8 jit_solution(15725330755377553947)
XLA Ops:
  6.5 0.0 copy-start
  6.5 0.0 all-gather.3.cloned.1.call-start
  6.5 0.9 copy.64
  7.5 0.1 eq.71
  7.6 0.1 fusion.40
  7.7 0.2 reduce_window_sum.11
  7.9 0.2 select_reduce_fusion.1
  8.1 0.1 sub.26
  8.2 0.1 copy.65
  8.3 0.7 multiply_add_fusion
  9.0 0.1 fusion.37
  9.1 1.1 convolution_convert_fusion
  10.2 14.8 all_to_all.51
  25.0 0.1 copy.67
  25.1 0.8 all_to_all.40
  25.9 0.0 all-gather.3.cloned.1.call-update
  25.9 0.0 copy-start.7
  25.9 0.0 all-gather.5.cloned.1.call-start
  25.9 78.9 %all-gather.3.cloned.1.call-done = bf16[32,1,20,4096]{3,2,1,0:T(8,128)(2,1)} async-done(((bf16[1,1,20,4096]{3,2,1,0:T(8,128)(2,1)}), bf16[32,1,20,4096]{3,2,1,0:T(8,128)(2,1)}) %all-gather.3.cloned.1.call-update) | async-done | bytes 5242896 | tf_op jit(solution)/shard_map/all_gather | solution.py:61
  104.8 0.0 copy-start.6
  104.8 6.7 fusion.9
  111.5 0.0 copy-done.7
  111.5 0.0 copy-done.6
  111.5 4.3 fusion.18
  115.8 0.0 all-gather.5.cloned.1.call-update
  115.8 0.0 copy-start.1
  115.8 0.0 copy-start.2
  115.8 0.0 copy-start.3
  115.8 183.2 %all-gather.5.cloned.1.call-done = bf16[32,1,20,8192]{3,0,2,1:T(8,128)(2,1)} async-done(((bf16[32,1,20,128]{3,0,2,1:T(8,128)(2,1)}), bf16[32,1,20,8192]{3,0,2,1:T(8,128)(2,1)}) %all-gather.5.cloned.1.call-update) | async-done | bytes 10485776 | tf_op jit(solution)/shard_map/all_gather | solution.py:65
  299.1 0.0 copy-done
  299.1 5.6 fusion.26
  304.7 0.0 copy-start.5
  304.7 0.7 copy.69
  305.4 10.8 all-to-all-start.1
  316.2 0.0 copy-done.1
  316.2 0.0 copy-done.2
  316.2 0.1 fusion.62
  317.0 35.2 %psum.21 = bf16[64,32]{0,1:T(8,128)(2,1)S(1)} all-reduce(f32[64,32]{0,1:T(8,128)S(1)} %fusion.62), channel_id=1, replica_groups=mesh['seq'=32,'expert'=8,'tensor'=2] {'expert'}, use_global_device_ids=true, to_apply=%region_4.5 | all-reduce | flops 2048 | bytes 12288 | tf_op jit(solution)/shard_map/psum | solution.py:90
  352.2 0.0 copy-done.3
  352.2 0.3 convolution_multiply_fusion
  352.5 0.0 all-to-all-done.1
  352.5 0.1 all_to_all.44
  352.6 3.9 copy.71
  356.5 0.5 broadcast.248
  357.0 0.0 copy-start.4
  357.0 23.5 %reduce.1 = bf16[4096,20]{1,0:T(8,128)(2,1)S(1)} reduce(bf16[4096,1,1,20]{3,2,1,0:T(2,128)(2,1)} %bitcast.104, bf16[]{:T(256)} %broadcast.248), dimensions={1,2}, to_apply=%bitcast.93.reduce_sub_computation | reduce | bytes 327682
  380.5 2.9 reshape.195
  383.4 3.4 all-to-all-start.2
  386.8 0.1 broadcast_bitcast_fusion.1
  387.5 0.0 copy-done.5
  387.5 0.1 select_reduce_fusion
  387.6 6.2 all-to-all-done.2
  393.9 4.6 reshape.196
  398.5 4.6 copy.72
  403.1 0.1 copy.75
  403.2 0.1 copy.73
  403.3 0.3 multiply_reduce_fusion
  403.6 16.7 psum.22
  420.3 0.0 copy-done.4
  420.3 0.2 fusion.34
  420.6 1290.5 %psum.23 = f32[1,4096]{1,0:T(1,128)S(1)} all-reduce(f32[1,4096]{1,0:T(1,128)S(1)} %mul.119), channel_id=1, replica_groups=mesh['seq'=32,'expert'=8,'tensor'=2] {'seq','expert'}, use_global_device_ids=true, to_apply=%region_7.8 | all-reduce | flops 4096 | bytes 32768 | tf_op jit(solution)/shard_map/psum | solution.py:112
  1711.1 0.6 multiply_reduce_fusion.1
  1712.4 0.6 broadcast_multiply_fusion
  (13 shorter events, 0.2 us)
Async XLA Ops:
  6.5 292.5 %copy-start = (bf16[1,8192,128]{2,1,0:T(8,128)(2,1)S(1)}, bf16[1,8192,128]{2,1,0:T(8,128)(2,1)}, u32[]{:S(2)}) copy-start(bf16[1,8192,128]{2,1,0:T(8,128)(2,1)} %param.16) | copy-start | bytes 6291460
  6.5 98.3 %all-gather.3.cloned.1.call-start = ((), (), s32[]{:S(2)}) async-start(), calls=%async_computation.3 | async-start | bytes 6488064 | tf_op jit(solution)/shard_map/all_gather | solution.py:61
  25.9 85.6 %copy-start.7 = (bf16[1,4096,128]{2,1,0:T(8,128)(2,1)S(1)}, bf16[1,4096,128]{2,1,0:T(8,128)(2,1)}, u32[]{:S(2)}) copy-start(bf16[1,4096,128]{2,1,0:T(8,128)(2,1)} %param.15) | copy-start | bytes 3145732
  25.9 273.2 %all-gather.5.cloned.1.call-start = ((), (), s32[]{:S(2)}) async-start(), calls=%async_computation.4 | async-start | bytes 10649600 | tf_op jit(solution)/shard_map/all_gather | solution.py:65
  104.8 6.7 copy-start.6
  115.8 200.4 %copy-start.1 = (bf16[64,512]{1,0:T(8,128)(2,1)S(1)}, bf16[64,512]{1,0:T(8,128)(2,1)}, u32[]{:S(2)}) copy-start(bf16[64,512]{1,0:T(8,128)(2,1)} %param.11) | copy-start | bytes 196612
  115.8 200.4 %copy-start.2 = (bf16[32,512]{1,0:T(8,128)(2,1)S(1)}, bf16[32,512]{1,0:T(8,128)(2,1)}, u32[]{:S(2)}) copy-start(bf16[32,512]{1,0:T(8,128)(2,1)} %param.17) | copy-start | bytes 98308
  115.8 236.4 %copy-start.3 = (bf16[32,512]{1,0:T(8,128)(2,1)S(1)}, bf16[32,512]{1,0:T(8,128)(2,1)}, u32[]{:S(2)}) copy-start(bf16[32,512]{1,0:T(8,128)(2,1)} %param.18) | copy-start | bytes 98308
  304.7 82.8 %copy-start.5 = (f32[64,2]{0,1:T(2,128)S(1)}, f32[64,2]{0,1:T(2,128)}, u32[]{:S(2)}) copy-start(f32[64,2]{0,1:T(2,128)} %param.13) | copy-start | bytes 1540
  305.4 47.1 %all-to-all-start.1 = ((bf16[32,1,20,128]{3,2,1,0:T(8,128)(2,1)}), bf16[32,1,20,128]{3,2,1,0:T(8,128)(2,1)S(1)}, u32[]{:S(2)}, u32[]{:S(2)}) async-start(bf16[32,1,20,128]{3,2,1,0:T(8,128)(2,1)} %copy.69), calls=%async_computation.1 | async-start | bytes 393216 | tf_op jit(solution)/shard_map/all_to_all | solution.py:71
  357.0 63.3 %copy-start.4 = (f32[512]{0:T(512)S(1)}, f32[512]{0:T(512)}, u32[]{:S(2)}) copy-start(f32[512]{0:T(512)} %param.21) | copy-start | bytes 6148
  383.4 10.5 all-to-all-start.2
Sparse Core Ops, SparseCore 0:
  26.0 78.7 all-gather.2
  115.9 183.0 all-gather.4
where the time goes:
time: 1730 us; the launch traced here: 1720 us
  blocking collectives  1360 us (79%)
  waiting for transfers between devices  268 us (15%)
  other arithmetic  26.1 us (2%)
  local copies, waits for them, and re-layouts  19.8 us (1%)
  matrix products  18.6 us (1%)
    psum x1, blocking collectives, local(): pooled = lax.psum(spread_out, ('seq', 'expert'))  1290 us
    all_gather x1, waiting for transfers between devices, local(): lax.all_gather(hidden, ('seq', 'tensor'), axis=3, tiled=True)  183 us
    all_gather x1, waiting for transfers between devices, local(): lax.all_gather(received, 'seq', axis=0, tiled=True)  78.9 us
    psum x1, blocking collectives, local(): narrow_all_tasks = lax.psum(low_part, 'expert')  35.2 us
  transfers between devices with their start and end apart: 4, of which 3 were waited for; matrix products, arithmetic and copies ran while one was open for 0% of the time, Pallas kernels for 0%

commit v1 on v0

v1 whole, which is shorter than its diff:
```python
import jax
import jax.numpy as jnp
from jax import lax
from jax.sharding import Mesh
from jax.sharding import PartitionSpec as P

TASK_COUNT = 2
ADAPTER_SCALE = 0.5

SEQ = ("z", "c")
EXPERT = ("y", "h")
GROUP = ("y", "h", "t")

BF16 = jnp.bfloat16
F16 = jnp.float16
F32 = jnp.float32
HIGH = lax.Precision.HIGHEST
LANES = 128
LEAST_EXPONENT = -40.0


def swap(x, axes):
    return lax.all_to_all(x, axes, split_axis=0, concat_axis=0, tiled=True)


def spread(x, axes):
    return swap(jnp.broadcast_to(x[None], (lax.axis_size(axes),) + x.shape), axes)


def three_parts(x):
    first = x.astype(BF16)
    rest = x - first.astype(F32)
    second = rest.astype(BF16)
    third = (rest - second.astype(F32)).astype(BF16)
    return first, second, third


def slots_of(ids, experts):
    pairs = ids.shape[1]
    one_hot = (ids[:, None, :] == jnp.arange(experts, dtype=jnp.int32)[None, :, None]).astype(BF16)
    before = (
        jnp.arange(pairs, dtype=jnp.int32)[:, None] < jnp.arange(pairs, dtype=jnp.int32)[None, :]
    ).astype(BF16)
    earlier = lax.dot_general(
        one_hot, before, (((2,), (0,)), ((), ())), preferred_element_type=F32
    )
    return jnp.sum(earlier * one_hot.astype(F32), axis=1).astype(jnp.int32)


def local(
    tokens,
    routes,
    chosen_expert_weight,
    expert_gate_weight,
    expert_up_weight,
    expert_down_weight,
    adapter_down_weight,
    adapter_up_weight,
    document_task_index,
    counts,
    final_norm_scale,
):
    rows, feats = tokens.shape
    seq = lax.axis_size(SEQ)
    experts = lax.axis_size(EXPERT)
    cores = lax.axis_size("c")
    groups = lax.axis_size(GROUP)
    tensors = lax.axis_size("t")
    chips = seq // cores
    capacity = rows * 5 // 16
    width = feats * experts
    half = feats // cores
    slice_width = width // seq
    slots = seq * capacity
    pairs = 2 * rows
    s = lax.axis_index(SEQ)
    e = lax.axis_index(EXPERT)
    t = lax.axis_index("t")
    g = lax.axis_index(GROUP)

    pair_ids = routes.reshape(1, pairs)
    target = pair_ids[0] * capacity + slots_of(pair_ids, experts)[0]
    chooser = jnp.any(
        (target[:, None] == jnp.arange(experts * capacity, dtype=jnp.int32)[None, :]).reshape(
            rows, 2, experts * capacity
        ),
        axis=1,
    ).astype(BF16)
    outgoing = lax.dot_general(
        chooser, tokens, (((0,), (0,)), ((), ())), preferred_element_type=F32
    ).astype(BF16)
    outgoing = outgoing.reshape(experts, capacity, cores, half).transpose(0, 2, 1, 3)
    received = swap(outgoing.reshape(experts * cores, capacity, half), EXPERT + ("c",))
    shard = received.reshape(experts, cores, capacity, half).transpose(1, 2, 0, 3)
    shard = shard.reshape(cores * capacity, experts * half).astype(F32)

    table = jnp.stack(
        [routes.reshape(pairs).astype(F32), chosen_expert_weight.reshape(pairs)]
    )
    tables = spread(table, SEQ)
    task_rows = adapter_down_weight.shape[0]
    params = spread(
        jnp.concatenate(
            [adapter_down_weight, adapter_up_weight]
            + [part[None] for part in three_parts(final_norm_scale)]
        ),
        EXPERT,
    )

    largest = jnp.max(jnp.abs(shard), axis=1, keepdims=True)
    exponent = jnp.maximum(
        jnp.floor(jnp.log2(jnp.maximum(largest, 1e-30)) + 1.01), LEAST_EXPONENT
    )
    scaled = (shard * jnp.exp2(15.0 - exponent)).astype(F16)
    sent = jnp.concatenate(
        [scaled, jnp.broadcast_to(exponent, (cores * capacity, LANES)).astype(F16)], axis=1
    )
    gathered = lax.all_gather(sent, SEQ, axis=0, tiled=False)
    gathered = gathered.reshape(chips, cores, cores * capacity, -1).transpose(1, 0, 2, 3)
    exponents = gathered[..., experts * half : experts * half + 1].astype(F32)
    dispatched = (
        gathered[..., : experts * half].astype(F32) * jnp.exp2(exponents - 15.0)
    ).astype(BF16)
    dispatched = dispatched.reshape(cores, slots, experts * half)
    row_exponent = jnp.max(exponents, axis=0).reshape(slots, 1)

    def reorder(weight):
        columns = weight.shape[-1]
        return (
            weight.reshape(experts, cores, half, columns)
            .transpose(1, 0, 2, 3)
            .reshape(cores, experts * half, columns)
        )

    both = ((0, 2), (0, 1)), ((), ())
    gate_act = lax.dot_general(
        dispatched, reorder(expert_gate_weight[0]), both, preferred_element_type=F32
    )
    up_act = lax.dot_general(
        dispatched, reorder(expert_up_weight[0]), both, preferred_element_type=F32
    )
    hidden = (jax.nn.silu(gate_act) * up_act).astype(BF16).astype(F32)
    hidden = (hidden * jnp.exp2(-2.0 * row_exponent - 2.0)).astype(F16)
    hidden = lax.all_gather(hidden, SEQ, axis=0, tiled=False)
    hidden_units = hidden.shape[-1]
    down = lax.dynamic_index_in_dim(
        expert_down_weight[0].reshape(seq, tensors, hidden_units, slice_width),
        t,
        axis=1,
        keepdims=False,
    )
    part = lax.dot_general(hidden.astype(BF16), down, both, preferred_element_type=F32)

    adapter_down = (
        params[:, :task_rows]
        .reshape(experts, task_rows, cores, half)
        .transpose(2, 1, 0, 3)
        .reshape(cores, task_rows, experts * half)
    )
    low_rank = lax.dot_general(
        dispatched, adapter_down, (((0, 2), (0, 2)), ((), ())), preferred_element_type=F32
    )
    task_of_row = jnp.arange(task_rows, dtype=jnp.int32) // (task_rows // TASK_COUNT)
    low_rank = jnp.where(
        task_of_row[None, :] == document_task_index[0], low_rank, 0.0
    ).astype(BF16)
    per_feature_group = feats // slice_width
    per_half = half // slice_width
    adapter_up = lax.dynamic_slice(
        params,
        (s // per_feature_group, task_rows, (s % per_feature_group) * slice_width),
        (1, task_rows, slice_width),
    )[0]
    adapted = jnp.dot(low_rank, adapter_up, preferred_element_type=F32)
    own = lax.dynamic_slice(
        dispatched,
        (
            (s // per_half) % cores,
            0,
            (s // per_feature_group) * half + (s % per_half) * slice_width,
        ),
        (1, slots, slice_width),
    )[0]
    base = own.astype(F32) + ADAPTER_SCALE * adapted

    ids = tables[:, 0].astype(jnp.int32)
    weights = tables[:, 1]
    slot_of = slots_of(ids, experts)
    is_mine = jnp.where(ids == e, slot_of, -1)
    slot_weight = jnp.sum(
        jnp.where(
            is_mine[:, None, :] == jnp.arange(capacity, dtype=jnp.int32)[None, :, None],
            weights[:, None, :],
            0.0,
        ),
        axis=2,
    ).reshape(slots, 1)
    payload = slot_weight * jnp.exp2(2.0 * row_exponent + 2.0) * part + base / (2 * tensors)
    blocks = seq // groups
    returned = swap(payload.reshape(groups, blocks * capacity, slice_width), GROUP)
    returned = jnp.sum(
        returned.reshape(experts, tensors, blocks * capacity, slice_width), axis=1
    ).reshape(experts * blocks * capacity, slice_width)

    group_ids = lax.dynamic_slice_in_dim(ids, g * blocks, blocks, axis=0)
    group_slots = lax.dynamic_slice_in_dim(slot_of, g * blocks, blocks, axis=0)
    place = (
        group_ids * (blocks * capacity)
        + jnp.arange(blocks, dtype=jnp.int32)[:, None] * capacity
        + group_slots
    )
    group_rows = blocks * rows
    combiner = jnp.any(
        place.reshape(group_rows, 2)[:, :, None]
        == jnp.arange(experts * blocks * capacity, dtype=jnp.int32)[None, None, :],
        axis=1,
    ).astype(F32)
    mixed = jnp.dot(combiner, returned, precision=HIGH)
    squares = jnp.sum(spread(jnp.sum(mixed * mixed, axis=1)[None], SEQ), axis=0)
    position = g * group_rows + jnp.arange(group_rows, dtype=jnp.int32)[None, :]
    factor = jnp.where(position < counts[0], lax.rsqrt(squares / width + 1e-05), 0.0)
    pooled = jnp.dot(factor, mixed, precision=HIGH)
    pooled = jnp.sum(spread(pooled, GROUP), axis=0)
    pooled = spread(pooled, SEQ).reshape(1, width)
    scale = jnp.sum(params[:, 2 * task_rows :].astype(F32), axis=1).reshape(1, width)
    pooled = pooled * scale
    return pooled * lax.rsqrt(jnp.mean(pooled * pooled, axis=1, keepdims=True) + 1e-06)


def solution(mesh):
    seq, experts, tensors = mesh.devices.shape
    parts = Mesh(
        mesh.devices.reshape(seq // 2, 2, experts // 2, 2, tensors), ("z", "c", "y", "h", "t")
    )
    return jax.shard_map(
        local,
        mesh=parts,
        in_specs=(
            P(SEQ, EXPERT),
            P(SEQ, None),
            P(SEQ, None),
            P(EXPERT, None, SEQ + ("t",)),
            P(EXPERT, None, SEQ + ("t",)),
            P(EXPERT, None, SEQ),
            P(None, EXPERT),
            P(None, EXPERT),
            P(),
            P(),
            P(EXPERT),
        ),
        out_specs=P(),
        check_vma=False,
    )
```

time: 1730 us -> 292 us (0.17)
  blocking collectives: 1360 us -> 104 us
  waiting for transfers between devices: 268 us -> 43 us
  starting transfers between devices: 14.2 us -> 51.1 us
  local copies, waits for them, and re-layouts: 19.8 us -> 49.7 us
    psum x3 -> x0, blocking collectives: 1340 us -> none  [the longest x1 1290 us: local(): pooled = lax.psum(spread_out, ('seq', 'expert'))]
    all_gather x2 -> x0, waiting for transfers between devices: 262 us -> none  [the longest x1 183 us: local(): lax.all_gather(hidden, ('seq', 'tensor'), axis=3, tiled=True)]
    all_gather x0 -> x2, blocking collectives: none -> 94.7 us  [the longest x1 49.1 us: local(): gathered = lax.all_gather(sent, SEQ, axis=0, tiled=False)]
    all_to_all x2 -> x6, starting transfers between devices: 14.1 us -> 51.1 us  [swap(): return lax.all_to_all(x, axes, split_axis=0, concat_axis=0, tiled=True)]
    all_to_all x2 -> x6, waiting for transfers between devices: 6.24 us -> 43 us  [swap(): return lax.all_to_all(x, axes, split_axis=0, concat_axis=0, tiled=True)]
    unnamed x1 -> x0, other arithmetic: 23.5 us -> none
    reshape x2 -> x7, local copies, waits for them, and re-layouts: 0.08 us -> 20.9 us  [the longest x1 19.9 us: local(): gathered.reshape(chips, cores, cores * capacity, -1).transpose(1, 0, 2, 3)]
    convert_element_type x2 -> x6, other arithmetic: 0.09 us -> 18.5 us  [the longest x1 14.7 us: local(): dispatched = (gathered[..., :experts * half].astype(F32) * jnp.exp2(expon...]
  transfers between devices with their start and end apart: 4 -> 6, of which waited for: 3 -> 5; matrix products, arithmetic and copies ran while one was open for 0% -> 26% of each run, Pallas kernels for 0% -> 0%
where the time goes in v1:
time: 292 us; the launch traced here: 290 us
  blocking collectives  104 us (36%)
  starting transfers between devices  51.1 us (18%)
  local copies, waits for them, and re-layouts  49.7 us (17%)
  waiting for transfers between devices  43 us (15%)
  other arithmetic  22 us (8%)
  matrix products  17.9 us (6%)
    all_to_all x6, starting transfers between devices, swap(): return lax.all_to_all(x, axes, split_axis=0, concat_axis=0, tiled=True)  51.1 us
    all_gather x1, blocking collectives, local(): gathered = lax.all_gather(sent, SEQ, axis=0, tiled=False)  49.1 us
    all_gather x1, blocking collectives, local(): hidden = lax.all_gather(hidden, SEQ, axis=0, tiled=False)  45.6 us
    all_to_all x6, waiting for transfers between devices, swap(): return lax.all_to_all(x, axes, split_axis=0, concat_axis=0, tiled=True)  43 us
    reshape x1, local copies, waits for them, and re-layouts, local(): gathered.reshape(chips, cores, cores * capacity, -1).transpose(1, 0, 2, 3)  19.9 us
    convert_element_type x1, local copies, waits for them, and re-layouts, local(): dispatched = (gathered[..., :experts * half].astype(F32) * jnp.exp2(expon...  17.7 us
    convert_element_type x1, other arithmetic, local(): dispatched = (gathered[..., :experts * half].astype(F32) * jnp.exp2(expon...  14.7 us
    all_to_all x1, blocking collectives, swap(): return lax.all_to_all(x, axes, split_axis=0, concat_axis=0, tiled=True)  8.99 us
  transfers between devices with their start and end apart: 6, of which 5 were waited for; matrix products, arithmetic and copies ran while one was open for 26% of the time, Pallas kernels for 0%

profile of v1, /device:TPU:1, one launch (start us, length us, event | category | flops | bytes accessed | tf_op | source)
XLA Modules:
  0.0 289.8 jit_solution(14728130272018749459)
XLA Ops:
  0.0 0.9 copy.154
  0.9 0.1 eq.113
  1.1 0.1 fusion.12
  1.2 0.1 convert_element_type.148
  1.4 0.1 copy.155
  1.4 0.8 multiply_add_fusion
  2.2 0.1 copy.149
  2.3 0.1 convert_element_type.139
  2.5 0.8 copy.150
  3.2 0.1 stack_reshape.3
  3.4 0.6 broadcast_in_dim.51
  4.0 16.7 %all-to-all-start = ((f32[32,2,128]{2,1,0:T(2,128)}), f32[32,2,128]{2,1,0:T(2,128)S(1)}, u32[]{:S(2)}, u32[]{:S(2)}) async-start(f32[32,2,128]{2,1,0:T(2,128)} %broadcast_in_dim.51), calls=%async_computation | async-start | bytes 65536 | tf_op jit(solution)/shard_map/all_to_all | solution.py:23
  20.7 0.1 fusion.17
  20.8 0.8 subtract_convert_fusion
  21.6 1.1 convolution_convert_fusion
  22.8 0.7 copy.169
  23.5 2.3 copy.163
  25.8 2.3 copy.164
  28.9 4.0 %all-to-all-done = f32[32,2,128]{2,1,0:T(2,128)S(1)} async-done(((f32[32,2,128]{2,1,0:T(2,128)}), f32[32,2,128]{2,1,0:T(2,128)S(1)}, u32[]{:S(2)}, u32[]{:S(2)}) %all-to-all-start) | async-done | bytes 32800 | tf_op jit(solution)/shard_map/all_to_all | solution.py:23
  32.9 8.1 %all-to-all-start.1 = ((bf16[16,20,256]{2,1,0:T(8,128)(2,1)}), bf16[16,20,256]{2,1,0:T(8,128)(2,1)S(1)}, u32[]{:S(2)}, u32[]{:S(2)}) async-start(bf16[16,20,256]{2,1,0:T(8,128)(2,1)} %bitcast.9), calls=%async_computation.1 | async-start | bytes 393216 | tf_op jit(solution)/shard_map/all_to_all | solution.py:23
  41.0 0.2 fusion.10
  41.2 0.2 select_reduce_fusion
  41.4 0.1 copy.153
  41.4 0.1 reshape.298
  41.5 7.6 %all-to-all-done.1 = bf16[16,20,256]{2,1,0:T(8,128)(2,1)S(1)} async-done(((bf16[16,20,256]{2,1,0:T(8,128)(2,1)}), bf16[16,20,256]{2,1,0:T(8,128)(2,1)S(1)}, u32[]{:S(2)}, u32[]{:S(2)}) %all-to-all-start.1) | async-done | bytes 163872 | tf_op jit(solution)/shard_map/all_to_all | solution.py:23
  49.1 0.9 broadcast_in_dim.104
  50.0 3.5 %all-to-all-start.2 = ((bf16[8,67,512]{2,1,0:T(8,128)(2,1)}), bf16[8,67,512]{2,1,0:T(8,128)(2,1)S(1)}, u32[]{:S(2)}, u32[]{:S(2)}) async-start(bf16[8,67,512]{2,1,0:T(8,128)(2,1)} %broadcast_in_dim.104), calls=%async_computation.2 | async-start | bytes 1179648 | tf_op jit(solution)/shard_map/all_to_all | solution.py:23
  53.5 0.1 abs_reduce_fusion
  53.7 0.1 reshape.326
  53.8 0.1 copy.173
  54.0 0.1 reshape.320
  54.0 0.1 multiply_convert_fusion.1
  54.1 0.1 broadcast_in_dim.57
  54.3 49.1 %all-gather.4 = f16[1280,2176]{1,0:T(8,128)(2,1)} all-gather(f16[40,2176]{1,0:T(8,128)(2,1)S(1)} %pad_maximum_fusion), channel_id=2, replica_groups=mesh['z'=16,'c'=2,'y'=4,'h'=2,'t'=2] {'z','c'}, dimensions={0}, use_global_device_ids=true | all-gather | bytes 5744640 | tf_op jit(solution)/shard_map/all_gather | solution.py:118
  103.4 19.9 %copy.161 = f16[16,2,40,2176]{2,0,3,1:T(8,128)(2,1)} copy(f16[16,2,40,2176]{3,2,1,0:T(8,128)(2,1)} %bitcast.114) | data formatting | bytes 11141120 | tf_op jit(solution)/shard_map/reshape | solution.py:119
  123.3 0.7 convert_reduce_fusion.1
  124.0 14.7 %multiply_convert_fusion = bf16[2,16,40,2048]{2,1,3,0:T(8,128)(2,1)} fusion(f16[2,16,40,2176]{2,1,3,0:T(8,128)(2,1)} %bitcast.113, f32[2,16,40]{2,1,0:T(8,128)S(1)} %get-tuple-element.6), kind=kLoop, calls=%fused_computation | loop fusion | flops 7864320 | bytes 10490880 | tf_op jit(solution)/shard_map/convert_element_type | solution.py:123
  138.7 17.7 %copy.162 = bf16[2,16,40,2048]{3,2,1,0:T(8,128)(2,1)} copy(bf16[2,16,40,2048]{2,1,3,0:T(8,128)(2,1)} %multiply_convert_fusion) | data formatting | bytes 10485760 | tf_op jit(solution)/shard_map/convert_element_type | solution.py:123
  156.4 0.1 exp2.79
  156.6 4.4 %convolution_bitcast_fusion.2 = f32[640,128]{1,0:T(8,128)S(1)} fusion(bf16[2,640,2048]{2,1,0:T(8,128)(2,1)} %bitcast.115, bf16[2,2048,128]{2,1,0:T(8,128)(2,1)} %bitcast.125), kind=kOutput, calls=%fused_computation.9 | convolution fusion | flops 671088640 | bytes 6619136 | tf_op jit(solution)/shard_map/dot_general | solution.py:136
  161.0 0.2 copy-done.2
  161.2 1.5 fusion.8
  162.7 45.6 %all-gather.5 = f16[20480,128]{1,0:T(8,128)(2,1)S(1)} all-gather(f16[640,128]{1,0:T(8,128)(2,1)S(1)} %fusion.8), channel_id=3, replica_groups=mesh['z'=16,'c'=2,'y'=4,'h'=2,'t'=2] {'z','c'}, dimensions={0}, use_global_device_ids=true | all-gather | bytes 5406720 | tf_op jit(solution)/shard_map/all_gather | solution.py:144
  208.3 2.9 %convert_element_type.178 = bf16[20480,128]{1,0:T(8,128)(2,1)} convert(f16[20480,128]{1,0:T(8,128)(2,1)S(1)} %all-gather.5) | non-fusion elementwise | flops 2621440 | bytes 10485760 | tf_op jit(solution)/shard_map/convert_element_type | solution.py:152
  211.2 0.1 exp2.73
  211.3 4.7 %fusion.3 = f32[640,128]{1,0:T(8,128)} fusion(bf16[32,640,128]{2,1,0:T(8,128)(2,1)} %bitcast.118, bf16[32,2,128,128]{3,2,1,0:T(8,128)(2,1)S(1)} %bitcast.111, s32[]{:T(128)S(6)} %select_n.75, f32[640]{0:T(1024)S(1)} %mul.194), kind=kOutput, calls=%fused_computation.6 | convolution fusion | flops 671170560 | bytes 6623236 | tf_op jit(solution)/shard_map/dot_general | solution.py:152
  216.2 0.2 copy.166
  216.3 0.1 reshape.306
  216.4 5.2 %fusion.2 = f32[640,128]{1,0:T(8,128)} fusion(f32[640,128]{1,0:T(8,128)} %fusion.3, bf16[2,640,2048]{2,1,0:T(8,128)(2,1)} %bitcast.116, bf16[2,32,2048]{2,1,0:T(8,128)(2,1)S(1)} %reshape.306, s32[]{:T(128)S(6)} %select_n.78, s32[]{:T(128)S(6)} %select_n.81, pred[32]{0:T(512)(128)(4,1)S(1)} %fusion.34, bf16[8,67,512]{2,1,0:T(8,128)(2,1)S(1)} %all-to-all-done.2, ...), kind=kOutput, calls=%fused_computation.4 | convolution fusion | flops 173465600 | bytes 6332944 | tf_op jit(solution)/shard_map/dot_general | solution.py:174
  221.7 7.3 %all-to-all-start.3 = ((f32[16,40,128]{2,1,0:T(8,128)}), f32[16,40,128]{2,1,0:T(8,128)S(1)}, u32[]{:S(2)}, u32[]{:S(2)}) async-start(f32[16,40,128]{2,1,0:T(8,128)} %bitcast.34), calls=%async_computation.3 | async-start | bytes 655360 | tf_op jit(solution)/shard_map/all_to_all | solution.py:23
  229.0 0.1 fusion.32
  229.1 0.1 eq.103
  229.3 8.7 %all-to-all-done.3 = f32[16,40,128]{2,1,0:T(8,128)S(1)} async-done(((f32[16,40,128]{2,1,0:T(8,128)}), f32[16,40,128]{2,1,0:T(8,128)S(1)}, u32[]{:S(2)}, u32[]{:S(2)}) %all-to-all-start.3) | async-done | bytes 327712 | tf_op jit(solution)/shard_map/all_to_all | solution.py:23
  238.1 0.4 multiply_reduce_fusion
  238.4 0.6 broadcast_in_dim.106
  239.1 9.6 %all-to-all-start.4 = ((f32[32,1,128]{2,1,0:T(1,128)}), f32[32,1,128]{2,1,0:T(1,128)S(1)}, u32[]{:S(2)}, u32[]{:S(2)}) async-start(f32[32,1,128]{2,1,0:T(1,128)} %broadcast_in_dim.106), calls=%async_computation.4 | async-start | bytes 32768 | tf_op jit(solution)/shard_map/all_to_all | solution.py:23
  249.3 11.1 %all-to-all-done.4 = f32[32,1,128]{2,1,0:T(1,128)S(1)} async-done(((f32[32,1,128]{2,1,0:T(1,128)}), f32[32,1,128]{2,1,0:T(1,128)S(1)}, u32[]{:S(2)}, u32[]{:S(2)}) %all-to-all-start.4) | async-done | bytes 16416 | tf_op jit(solution)/shard_map/all_to_all | solution.py:23
  260.4 0.2 convolution_bitcast_fusion.4
  260.6 9.0 %all_to_all.35 = f32[16,1,128]{2,1,0:T(1,128)S(1)} all-to-all(f32[16,1,128]{2,1,0:T(1,128)S(1)} %broadcast_in_dim.108), channel_id=1, replica_groups=mesh['z'=16,'c'=2,'y'=4,'h'=2,'t'=2] {'y','h','t'}, dimensions={0} | all-to-all | bytes 16384 | tf_op jit(solution)/shard_map/all_to_all | solution.py:23
  269.6 0.6 broadcast_in_dim.109
  270.2 5.8 %all-to-all-start.6 = ((f32[32,1,128]{2,1,0:T(1,128)}), f32[32,1,128]{2,1,0:T(1,128)S(1)}, u32[]{:S(2)}, u32[]{:S(2)}) async-start(f32[32,1,128]{2,1,0:T(1,128)} %broadcast_in_dim.109), calls=%async_computation.6 | async-start | bytes 32768 | tf_op jit(solution)/shard_map/all_to_all | solution.py:23
  276.2 11.7 %all-to-all-done.6 = f32[32,1,128]{2,1,0:T(1,128)S(1)} async-done(((f32[32,1,128]{2,1,0:T(1,128)}), f32[32,1,128]{2,1,0:T(1,128)S(1)}, u32[]{:S(2)}, u32[]{:S(2)}) %all-to-all-start.6) | async-done | bytes 16416 | tf_op jit(solution)/shard_map/all_to_all | solution.py:23
  287.9 0.6 multiply_reduce_fusion.1
  289.2 0.6 fusion.26
  (39 shorter events, 0.7 us)
Async XLA Ops:
  0.0 211.3 %copy-start = (bf16[1,8192,128]{2,1,0:T(8,128)(2,1)S(1)}, bf16[1,8192,128]{2,1,0:T(8,128)(2,1)}, u32[]{:S(2)}) copy-start(bf16[1,8192,128]{2,1,0:T(8,128)(2,1)} %param.16) | copy-start | bytes 6291460
  0.0 28.8 %copy-start.3 = (bf16[32,512]{1,0:T(8,128)(2,1)S(1)}, bf16[32,512]{1,0:T(8,128)(2,1)}, u32[]{:S(2)}) copy-start(bf16[32,512]{1,0:T(8,128)(2,1)} %param.17) | copy-start | bytes 98308
  0.0 28.8 %copy-start.4 = (bf16[32,512]{1,0:T(8,128)(2,1)S(1)}, bf16[32,512]{1,0:T(8,128)(2,1)}, u32[]{:S(2)}) copy-start(bf16[32,512]{1,0:T(8,128)(2,1)} %param.18) | copy-start | bytes 98308
  4.0 28.9 %all-to-all-start = ((f32[32,2,128]{2,1,0:T(2,128)}), f32[32,2,128]{2,1,0:T(2,128)S(1)}, u32[]{:S(2)}, u32[]{:S(2)}) async-start(f32[32,2,128]{2,1,0:T(2,128)} %broadcast_in_dim.51), calls=%async_computation | async-start | bytes 65536 | tf_op jit(solution)/shard_map/all_to_all | solution.py:23
  32.9 16.3 %all-to-all-start.1 = ((bf16[16,20,256]{2,1,0:T(8,128)(2,1)}), bf16[16,20,256]{2,1,0:T(8,128)(2,1)S(1)}, u32[]{:S(2)}, u32[]{:S(2)}) async-start(bf16[16,20,256]{2,1,0:T(8,128)(2,1)} %bitcast.9), calls=%async_computation.1 | async-start | bytes 393216 | tf_op jit(solution)/shard_map/all_to_all | solution.py:23
  50.0 166.1 %all-to-all-start.2 = ((bf16[8,67,512]{2,1,0:T(8,128)(2,1)}), bf16[8,67,512]{2,1,0:T(8,128)(2,1)S(1)}, u32[]{:S(2)}, u32[]{:S(2)}) async-start(bf16[8,67,512]{2,1,0:T(8,128)(2,1)} %broadcast_in_dim.104), calls=%async_computation.2 | async-start | bytes 1179648 | tf_op jit(solution)/shard_map/all_to_all | solution.py:23
  156.5 4.5 %copy-start.1 = (bf16[2,16,40,2048]{3,2,1,0:T(8,128)(2,1)S(1)}, bf16[2,16,40,2048]{3,2,1,0:T(8,128)(2,1)}, u32[]{:S(2)}) copy-start(bf16[2,16,40,2048]{3,2,1,0:T(8,128)(2,1)} %copy.162) | copy-start | bytes 15728644
  156.5 4.6 %copy-start.2 = (bf16[2,8,256,128]{3,2,1,0:T(8,128)(2,1)S(1)}, bf16[2,8,256,128]{3,2,1,0:T(8,128)(2,1)}, u32[]{:S(2)}) copy-start(bf16[2,8,256,128]{3,2,1,0:T(8,128)(2,1)} %copy.164) | copy-start | bytes 3145732
  221.7 16.4 %all-to-all-start.3 = ((f32[16,40,128]{2,1,0:T(8,128)}), f32[16,40,128]{2,1,0:T(8,128)S(1)}, u32[]{:S(2)}, u32[]{:S(2)}) async-start(f32[16,40,128]{2,1,0:T(8,128)} %bitcast.34), calls=%async_computation.3 | async-start | bytes 655360 | tf_op jit(solution)/shard_map/all_to_all | solution.py:23
  239.1 21.3 %all-to-all-start.4 = ((f32[32,1,128]{2,1,0:T(1,128)}), f32[32,1,128]{2,1,0:T(1,128)S(1)}, u32[]{:S(2)}, u32[]{:S(2)}) async-start(f32[32,1,128]{2,1,0:T(1,128)} %broadcast_in_dim.106), calls=%async_computation.4 | async-start | bytes 32768 | tf_op jit(solution)/shard_map/all_to_all | solution.py:23
  270.2 17.6 %all-to-all-start.6 = ((f32[32,1,128]{2,1,0:T(1,128)}), f32[32,1,128]{2,1,0:T(1,128)S(1)}, u32[]{:S(2)}, u32[]{:S(2)}) async-start(f32[32,1,128]{2,1,0:T(1,128)} %broadcast_in_dim.109), calls=%async_computation.6 | async-start | bytes 32768 | tf_op jit(solution)/shard_map/all_to_all | solution.py:23

commit v2 on v1

--- a/solution.py
+++ b/solution.py
@@ -27,12 +27,15 @@
     return swap(jnp.broadcast_to(x[None], (lax.axis_size(axes),) + x.shape), axes)
 
 
-def three_parts(x):
-    first = x.astype(BF16)
-    rest = x - first.astype(F32)
-    second = rest.astype(BF16)
-    third = (rest - second.astype(F32)).astype(BF16)
-    return first, second, third
+def rounded(x):
+    return lax.reduce_precision(x, 8, 7)
+
+
+def three_parts(x, step):
+    first = rounded(x)
+    rest = (x - first) * step
+    second = rounded(rest)
+    return first, second, (rest - second) * step
 
 
 def slots_of(ids, experts):
@@ -90,76 +93,82 @@
         chooser, tokens, (((0,), (0,)), ((), ())), preferred_element_type=F32
     ).astype(BF16)
     outgoing = outgoing.reshape(experts, capacity, cores, half).transpose(0, 2, 1, 3)
-    received = swap(outgoing.reshape(experts * cores, capacity, half), EXPERT + ("c",))
+    outgoing = outgoing.reshape(experts * cores, capacity, half)
+
+    task_rows = adapter_down_weight.shape[0]
+    own_params = jnp.concatenate(
+        [adapter_down_weight, adapter_up_weight]
+        + [part[None].astype(BF16) for part in three_parts(final_norm_scale, 1.0)]
+    )
+    outgoing, own_params = lax.optimization_barrier((outgoing, own_params))
+    received = swap(outgoing, EXPERT + ("c",))
+    params = spread(own_params, EXPERT)
+    shard_rows = cores * capacity
     shard = received.reshape(experts, cores, capacity, half).transpose(1, 2, 0, 3)
-    shard = shard.reshape(cores * capacity, experts * half).astype(F32)
-
-    table = jnp.stack(
-        [routes.reshape(pairs).astype(F32), chosen_expert_weight.reshape(pairs)]
-    )
-    tables = spread(table, SEQ)
-    task_rows = adapter_down_weight.shape[0]
-    params = spread(
-        jnp.concatenate(
-            [adapter_down_weight, adapter_up_weight]
-            + [part[None] for part in three_parts(final_norm_scale)]
-        ),
-        EXPERT,
-    )
+    shard = shard.reshape(shard_rows, experts * half).astype(F32)
 
     largest = jnp.max(jnp.abs(shard), axis=1, keepdims=True)
     exponent = jnp.maximum(
         jnp.floor(jnp.log2(jnp.maximum(largest, 1e-30)) + 1.01), LEAST_EXPONENT
     )
     scaled = (shard * jnp.exp2(15.0 - exponent)).astype(F16)
+    table = jnp.stack(
+        [routes.reshape(pairs).astype(F32)]
+        + list(three_parts(chosen_expert_weight.reshape(pairs), 256.0))
+    ).astype(F16)
     sent = jnp.concatenate(
-        [scaled, jnp.broadcast_to(exponent, (cores * capacity, LANES)).astype(F16)], axis=1
+        [
+            scaled,
+            jnp.broadcast_to(exponent, (shard_rows, LANES)).astype(F16),
+            jnp.pad(table, ((0, shard_rows - table.shape[0]), (0, 0))),
+        ],
+        axis=1,
     )
     gathered = lax.all_gather(sent, SEQ, axis=0, tiled=False)
-    gathered = gathered.reshape(chips, cores, cores * capacity, -1).transpose(1, 0, 2, 3)
-    exponents = gathered[..., experts * half : experts * half + 1].astype(F32)
-    dispatched = (
-        gathered[..., : experts * half].astype(F32) * jnp.exp2(exponents - 15.0)
-    ).astype(BF16)
-    dispatched = dispatched.reshape(cores, slots, experts * half)
-    row_exponent = jnp.max(exponents, axis=0).reshape(slots, 1)
-
-    def reorder(weight):
-        columns = weight.shape[-1]
-        return (
-            weight.reshape(experts, cores, half, columns)
-            .transpose(1, 0, 2, 3)
-            .reshape(cores, experts * half, columns)
-        )
-
-    both = ((0, 2), (0, 1)), ((), ())
-    gate_act = lax.dot_general(
-        dispatched, reorder(expert_gate_weight[0]), both, preferred_element_type=F32
-    )
-    up_act = lax.dot_general(
-        dispatched, reorder(expert_up_weight[0]), both, preferred_element_type=F32
-    )
-    hidden = (jax.nn.silu(gate_act) * up_act).astype(BF16).astype(F32)
+    gathered = lax.optimization_barrier(gathered.astype(BF16))
+    columns = experts * half
+    tables = gathered[:, :4, columns + LANES :].astype(F32)
+    gathered = gathered.reshape(chips, cores, shard_rows, -1).transpose(1, 0, 2, 3)
+    dispatched = gathered[..., :columns].reshape(cores, slots, columns)
+    exponents = gathered[..., columns : columns + LANES].reshape(cores, slots, LANES).astype(F32)
+    row_scale = jnp.exp2(exponents - 15.0)
+    row_exponent = jnp.max(exponents, axis=0)
+
+    weights_in = jnp.concatenate([expert_gate_weight[0], expert_up_weight[0]], axis=1)
+    hidden_units = expert_gate_weight.shape[2]
+    weights_in = (
+        weights_in.reshape(experts, cores, half, 2 * hidden_units)
+        .transpose(1, 0, 2, 3)
+        .reshape(cores, columns, 2 * hidden_units)
+    )
+    acts = lax.dot_general(
+        dispatched, weights_in, (((2,), (1,)), ((0,), (0,))), preferred_element_type=F32
+    )
+    gate_act = jnp.sum(acts[..., :hidden_units] * row_scale, axis=0)
+    up_act = jnp.sum(acts[..., hidden_units:] * row_scale, axis=0)
+    hidden = rounded(jax.nn.silu(gate_act) * up_act)
     hidden = (hidden * jnp.exp2(-2.0 * row_exponent - 2.0)).astype(F16)
     hidden = lax.all_gather(hidden, SEQ, axis=0, tiled=False)
-    hidden_units = hidden.shape[-1]
     down = lax.dynamic_index_in_dim(
         expert_down_weight[0].reshape(seq, tensors, hidden_units, slice_width),
         t,
         axis=1,
         keepdims=False,
     )
-    part = lax.dot_general(hidden.astype(BF16), down, both, preferred_element_type=F32)
+    part = lax.dot_general(
+        hidden.astype(BF16), down, (((0, 2), (0, 1)), ((), ())), preferred_element_type=F32
+    )
 
     adapter_down = (
         params[:, :task_rows]
         .reshape(experts, task_rows, cores, half)
         .transpose(2, 1, 0, 3)
-        .reshape(cores, task_rows, experts * half)
+        .reshape(cores, task_rows, columns)
     )
     low_rank = lax.dot_general(
-        dispatched, adapter_down, (((0, 2), (0, 2)), ((), ())), preferred_element_type=F32
-    )
+        dispatched, adapter_down, (((2,), (2,)), ((0,), (0,))), preferred_element_type=F32
+    )
+    low_rank = jnp.sum(low_rank * row_scale[..., :task_rows], axis=0)
     task_of_row = jnp.arange(task_rows, dtype=jnp.int32) // (task_rows // TASK_COUNT)
     low_rank = jnp.where(
         task_of_row[None, :] == document_task_index[0], low_rank, 0.0
@@ -172,19 +181,17 @@
         (1, task_rows, slice_width),
     )[0]
     adapted = jnp.dot(low_rank, adapter_up, preferred_element_type=F32)
+    own_half = (s // per_half) % cores
     own = lax.dynamic_slice(
         dispatched,
-        (
-            (s // per_half) % cores,
-            0,
-            (s // per_feature_group) * half + (s % per_half) * slice_width,
-        ),
+        (own_half, 0, (s // per_feature_group) * half + (s % per_half) * slice_width),
         (1, slots, slice_width),
     )[0]
-    base = own.astype(F32) + ADAPTER_SCALE * adapted
+    own_scale = lax.dynamic_index_in_dim(row_scale, own_half, axis=0, keepdims=False)
+    base = own.astype(F32) * own_scale + ADAPTER_SCALE * adapted
 
     ids = tables[:, 0].astype(jnp.int32)
-    weights = tables[:, 1]
+    weights = tables[:, 1] + (tables[:, 2] + tables[:, 3] / 256.0) / 256.0
     slot_of = slots_of(ids, experts)
     is_mine = jnp.where(ids == e, slot_of, -1)
     slot_weight = jnp.sum(

time: 292 us -> 225 us (0.77)
  local copies, waits for them, and re-layouts: 49.7 us -> 19.1 us
  starting transfers between devices: 51.1 us -> 38.7 us
  other arithmetic: 22 us -> 9.68 us
  waiting for transfers between devices: 43 us -> 30.7 us
  blocking collectives: 104 us -> 110 us
  matrix products: 17.9 us -> 14 us
    reshape x3, local copies, waits for them, and re-layouts: 20.7 us -> 0.59 us  [the longest x1 0.38 us: local(): gathered.reshape(chips, cores, shard_rows, -1).transpose(1, 0, 2, 3)]
    convert_element_type x3 -> x5, local copies, waits for them, and re-layouts: 17.9 us -> 0.16 us  [the longest x1 0.08 us: local(): jnp.broadcast_to(exponent, (shard_rows, LANES)).astype(F16)]
    convert_element_type x3 -> x4, other arithmetic: 18.4 us -> 2.04 us  [the longest x1 1.05 us: local(): gathered = lax.optimization_barrier(gathered.astype(BF16))]
    all_to_all x6 -> x5, starting transfers between devices: 51.1 us -> 38.7 us  [swap(): return lax.all_to_all(x, axes, split_axis=0, concat_axis=0, tiled=True)]
    all_to_all x6 -> x5, waiting for transfers between devices: 43 us -> 30.7 us  [swap(): return lax.all_to_all(x, axes, split_axis=0, concat_axis=0, tiled=True)]
    all_gather x1, blocking collectives: 49.1 us -> 55.6 us  [local(): gathered = lax.all_gather(sent, SEQ, axis=0, tiled=False)]
    concatenate x1 -> x2, local copies, waits for them, and re-layouts: 0.03 us -> 4.7 us  [the longest x1 3.15 us: local(): jnp.concatenate([expert_gate_weight[0], expert_up_weight[0]], axis=1)]
    transpose x2 -> x0, local copies, waits for them, and re-layouts: 4.63 us -> none  [reorder(): return weight.reshape(experts, cores, half, columns).transpose(1, 0, 2, 3...]
  transfers between devices with their start and end apart: 6 -> 5, of which waited for: 5 -> 3; matrix products, arithmetic and copies ran while one was open for 26% -> 10% of each run, Pallas kernels for 0% -> 0%
where the time goes in v2:
time: 225 us; the launch traced here: 224 us
  blocking collectives  110 us (49%)
  starting transfers between devices  38.7 us (17%)
  waiting for transfers between devices  30.7 us (14%)
  local copies, waits for them, and re-layouts  19.1 us (8%)
  matrix products  14 us (6%)
  other arithmetic  9.68 us (4%)
  between operations  2.31 us (1%)
    all_gather x1, blocking collectives, local(): gathered = lax.all_gather(sent, SEQ, axis=0, tiled=False)  55.6 us
    all_gather x1, blocking collectives, local(): hidden = lax.all_gather(hidden, SEQ, axis=0, tiled=False)  45.6 us
    all_to_all x5, starting transfers between devices, swap(): return lax.all_to_all(x, axes, split_axis=0, concat_axis=0, tiled=True)  38.7 us
    all_to_all x5, waiting for transfers between devices, swap(): return lax.all_to_all(x, axes, split_axis=0, concat_axis=0, tiled=True)  30.7 us
    all_to_all x1, blocking collectives, swap(): return lax.all_to_all(x, axes, split_axis=0, concat_axis=0, tiled=True)  8.99 us
    dot_general x1, matrix products, local(): lax.dot_general(dispatched, weights_in, (((2,), (1,)), ((0,), (0,))), pre...  4.68 us
  transfers between devices with their start and end apart: 5, of which 3 were waited for; matrix products, arithmetic and copies ran while one was open for 10% of the time, Pallas kernels for 0%

profile of v2, /device:TPU:1, one launch (start us, length us, event | category | flops | bytes accessed | tf_op | source)
XLA Modules:
  0.0 224.5 jit_solution(5028985790815505174)
XLA Ops:
  0.0 0.8 fusion.49
  0.9 0.8 copy.122
  1.6 0.1 eq.99
  1.8 0.1 fusion.13
  1.9 0.1 convert_element_type.147
  2.1 0.8 convert_convert_fusion
  2.9 0.1 fusion.33
  3.0 1.1 convolution_convert_fusion
  4.1 0.1 copy.151
  4.3 1.6 concatenate.14
  5.9 0.7 copy.125
  6.6 10.2 %all-to-all-start = ((bf16[16,20,256]{2,1,0:T(8,128)(2,1)}), bf16[16,20,256]{2,1,0:T(8,128)(2,1)S(1)}, u32[]{:S(2)}, u32[]{:S(2)}) async-start(bf16[16,20,256]{2,1,0:T(8,128)(2,1)} %copy.125), calls=%async_computation | async-start | bytes 393216 | tf_op jit(solution)/shard_map/all_to_all | solution.py:23
  17.5 0.8 copy.130
  18.3 0.1 reshape.381
  18.4 3.2 %pad_maximum_fusion = bf16[8,2,256,256]{3,2,1,0:T(8,128)(2,1)} fusion(bf16[8,2,256,128]{3,2,1,0:T(8,128)(2,1)} %bitcast.132, bf16[8,2,256,128]{3,2,1,0:T(8,128)(2,1)} %bitcast.133), kind=kLoop, calls=%fused_computation.3 | loop fusion | flops 4194304 | bytes 4194304 | tf_op jit(solution)/shard_map/concatenate | solution.py:137
  21.6 0.1 copy.129
  21.7 0.1 convert_element_type.163
  21.9 3.1 %copy.143 = bf16[8,2,256,256]{3,2,0,1:T(8,128)(2,1)} copy(bf16[8,2,256,256]{3,2,1,0:T(8,128)(2,1)} %pad_maximum_fusion) | data formatting | bytes 4194304 | tf_op jit(solution)/shard_map/concatenate | solution.py:137
  25.0 0.9 broadcast_in_dim.50
  25.9 6.6 %all-to-all-start.1 = ((bf16[8,67,512]{2,1,0:T(8,128)(2,1)}), bf16[8,67,512]{2,1,0:T(8,128)(2,1)}, u32[]{:S(2)}, u32[]{:S(2)}) async-start(bf16[8,67,512]{2,1,0:T(8,128)(2,1)} %broadcast_in_dim.50), calls=%async_computation.1 | async-start | bytes 1179648 | tf_op jit(solution)/shard_map/all_to_all | solution.py:23
  32.6 0.1 abs_reduce_fusion
  32.8 0.1 reshape.406
  32.8 0.1 reshape.401
  33.0 0.1 copy.146
  33.1 0.1 multiply_convert_fusion
  33.2 0.1 broadcast_in_dim.43
  33.3 55.6 %all-gather.3 = f16[1280,2304]{1,0:T(8,128)(2,1)S(1)} all-gather(f16[40,2304]{1,0:T(8,128)(2,1)S(1)} %pad_maximum_fusion.1), channel_id=2, replica_groups=mesh['z'=16,'c'=2,'y'=4,'h'=2,'t'=2] {'z','c'}, dimensions={0}, use_global_device_ids=true | all-gather | bytes 6082560 | tf_op jit(solution)/shard_map/all_gather | solution.py:127
  88.9 1.1 convert_element_type.181
  90.0 0.4 copy.150
  90.4 0.1 multiply_exponential_fusion
  90.5 3.0 %slice.54 = bf16[2,16,40,2048]{3,2,1,0:T(8,128)(2,1)} slice(bf16[2,16,40,2304]{3,2,1,0:T(8,128)(2,1)S(1)} %bitcast.120), slice={[0:2], [0:16], [0:40], [0:2048]} | slice | bytes 10485760 | tf_op jit(solution)/shard_map/slice | solution.py:132
  93.6 0.2 fusion.12
  93.9 0.2 select_reduce_fusion
  94.0 0.1 copy.133
  94.1 0.1 mul.234
  94.2 0.1 fusion.23
  94.4 4.7 %fusion.78 = f32[2,640,256]{2,1,0:T(8,128)S(1)} fusion(bf16[2,640,2048]{2,1,0:T(8,128)(2,1)} %bitcast.121, bf16[2,2048,256]{2,1,0:T(8,128)(2,1)} %bitcast.126), kind=kOutput, calls=%fused_computation.134 | convolution fusion | flops 1342177280 | bytes 8650752 | tf_op jit(solution)/shard_map/dot_general | solution.py:144
  99.0 0.2 fusion.17
  99.3 0.1 fusion.24
  99.4 45.6 %all-gather.4 = f16[32,640,128]{2,1,0:T(8,128)(2,1)S(1)} all-gather(f16[1,640,128]{2,1,0:T(8,128)(2,1)S(1)} %fusion.24), channel_id=1, replica_groups=mesh['z'=16,'c'=2,'y'=4,'h'=2,'t'=2] {'z','c'}, dimensions={0}, use_global_device_ids=true | all-gather | bytes 5406720 | tf_op jit(solution)/shard_map/all_gather | solution.py:151
  145.0 0.1 bitcast_multiply_fusion.3
  145.1 1.5 fusion.9
  146.7 1.7 slice.57
  148.4 1.0 reshape.385
  149.4 0.9 copy.138
  150.2 1.1 reshape.386
  151.3 4.0 %fusion.2 = bf16[640,32]{1,0:T(8,128)(2,1)S(1)} fusion(bf16[2,640,2048]{2,1,0:T(8,128)(2,1)} %bitcast.122, bf16[2,32,2048]{2,1,0:T(8,128)(2,1)S(1)} %reshape.386, f32[2,640,128]{2,1,0:T(8,128)S(1)} %bitcast.124), kind=kOutput, calls=%fused_computation.5 | convolution fusion | flops 167833600 | bytes 5709824 | tf_op jit(solution)/shard_map/dot_general | solution.py:168
  155.3 1.9 fusion.5
  157.2 6.5 %all-to-all-start.2 = ((f32[16,40,128]{2,1,0:T(8,128)}), f32[16,40,128]{2,1,0:T(8,128)S(1)}, u32[]{:S(2)}, u32[]{:S(2)}) async-start(f32[16,40,128]{2,1,0:T(8,128)} %bitcast.32), calls=%async_computation.2 | async-start | bytes 655360 | tf_op jit(solution)/shard_map/all_to_all | solution.py:23
  163.7 0.1 fusion.55
  163.8 0.1 eq.110
  164.1 8.7 %all-to-all-done.2 = f32[16,40,128]{2,1,0:T(8,128)S(1)} async-done(((f32[16,40,128]{2,1,0:T(8,128)}), f32[16,40,128]{2,1,0:T(8,128)S(1)}, u32[]{:S(2)}, u32[]{:S(2)}) %all-to-all-start.2) | async-done | bytes 327712 | tf_op jit(solution)/shard_map/all_to_all | solution.py:23
  172.8 0.4 multiply_reduce_fusion
  173.2 0.6 broadcast_in_dim.52
  173.8 9.5 %all-to-all-start.3 = ((f32[32,1,128]{2,1,0:T(1,128)}), f32[32,1,128]{2,1,0:T(1,128)S(1)}, u32[]{:S(2)}, u32[]{:S(2)}) async-start(f32[32,1,128]{2,1,0:T(1,128)} %broadcast_in_dim.52), calls=%async_computation.3 | async-start | bytes 32768 | tf_op jit(solution)/shard_map/all_to_all | solution.py:23
  183.9 11.1 %all-to-all-done.3 = f32[32,1,128]{2,1,0:T(1,128)S(1)} async-done(((f32[32,1,128]{2,1,0:T(1,128)}), f32[32,1,128]{2,1,0:T(1,128)S(1)}, u32[]{:S(2)}, u32[]{:S(2)}) %all-to-all-start.3) | async-done | bytes 16416 | tf_op jit(solution)/shard_map/all_to_all | solution.py:23
  195.0 0.2 convolution_bitcast_fusion
  195.3 9.0 %all_to_all.30 = f32[16,1,128]{2,1,0:T(1,128)S(1)} all-to-all(f32[16,1,128]{2,1,0:T(1,128)S(1)} %broadcast_in_dim.54), channel_id=1, replica_groups=mesh['z'=16,'c'=2,'y'=4,'h'=2,'t'=2] {'y','h','t'}, dimensions={0} | all-to-all | bytes 16384 | tf_op jit(solution)/shard_map/all_to_all | solution.py:23
  204.3 0.6 broadcast_in_dim.55
  204.9 5.8 %all-to-all-start.5 = ((f32[32,1,128]{2,1,0:T(1,128)}), f32[32,1,128]{2,1,0:T(1,128)S(1)}, u32[]{:S(2)}, u32[]{:S(2)}) async-start(f32[32,1,128]{2,1,0:T(1,128)} %broadcast_in_dim.55), calls=%async_computation.5 | async-start | bytes 32768 | tf_op jit(solution)/shard_map/all_to_all | solution.py:23
  210.7 0.9 convert_reduce_fusion
  211.7 10.9 %all-to-all-done.5 = f32[32,1,128]{2,1,0:T(1,128)S(1)} async-done(((f32[32,1,128]{2,1,0:T(1,128)}), f32[32,1,128]{2,1,0:T(1,128)S(1)}, u32[]{:S(2)}, u32[]{:S(2)}) %all-to-all-start.5) | async-done | bytes 16416 | tf_op jit(solution)/shard_map/all_to_all | solution.py:23
  222.5 0.6 multiply_reduce_fusion.1
  223.8 0.6 fusion.42
  (32 shorter events, 0.8 us)
Async XLA Ops:
  0.0 145.1 %copy-start = (bf16[1,8192,128]{2,1,0:T(8,128)(2,1)S(1)}, bf16[1,8192,128]{2,1,0:T(8,128)(2,1)}, u32[]{:S(2)}) copy-start(bf16[1,8192,128]{2,1,0:T(8,128)(2,1)} %param.16) | copy-start | bytes 6291460
  6.6 18.4 %all-to-all-start = ((bf16[16,20,256]{2,1,0:T(8,128)(2,1)}), bf16[16,20,256]{2,1,0:T(8,128)(2,1)S(1)}, u32[]{:S(2)}, u32[]{:S(2)}) async-start(bf16[16,20,256]{2,1,0:T(8,128)(2,1)} %copy.125), calls=%async_computation | async-start | bytes 393216 | tf_op jit(solution)/shard_map/all_to_all | solution.py:23
  25.9 120.7 %all-to-all-start.1 = ((bf16[8,67,512]{2,1,0:T(8,128)(2,1)}), bf16[8,67,512]{2,1,0:T(8,128)(2,1)}, u32[]{:S(2)}, u32[]{:S(2)}) async-start(bf16[8,67,512]{2,1,0:T(8,128)(2,1)} %broadcast_in_dim.50), calls=%async_computation.1 | async-start | bytes 1179648 | tf_op jit(solution)/shard_map/all_to_all | solution.py:23
  157.2 15.6 %all-to-all-start.2 = ((f32[16,40,128]{2,1,0:T(8,128)}), f32[16,40,128]{2,1,0:T(8,128)S(1)}, u32[]{:S(2)}, u32[]{:S(2)}) async-start(f32[16,40,128]{2,1,0:T(8,128)} %bitcast.32), calls=%async_computation.2 | async-start | bytes 655360 | tf_op jit(solution)/shard_map/all_to_all | solution.py:23
  173.8 21.2 %all-to-all-start.3 = ((f32[32,1,128]{2,1,0:T(1,128)}), f32[32,1,128]{2,1,0:T(1,128)S(1)}, u32[]{:S(2)}, u32[]{:S(2)}) async-start(f32[32,1,128]{2,1,0:T(1,128)} %broadcast_in_dim.52), calls=%async_computation.3 | async-start | bytes 32768 | tf_op jit(solution)/shard_map/all_to_all | solution.py:23
  204.9 17.6 %all-to-all-start.5 = ((f32[32,1,128]{2,1,0:T(1,128)}), f32[32,1,128]{2,1,0:T(1,128)S(1)}, u32[]{:S(2)}, u32[]{:S(2)}) async-start(f32[32,1,128]{2,1,0:T(1,128)} %broadcast_in_dim.55), calls=%async_computation.5 | async-start | bytes 32768 | tf_op jit(solution)/shard_map/all_to_all | solution.py:23

commit v3 on v2

--- a/solution.py
+++ b/solution.py
@@ -17,6 +17,7 @@
 HIGH = lax.Precision.HIGHEST
 LANES = 128
 LEAST_EXPONENT = -40.0
+LOW_STEP = 2.0**28
 
 
 def swap(x, axes):
@@ -96,13 +97,38 @@
     outgoing = outgoing.reshape(experts * cores, capacity, half)
 
     task_rows = adapter_down_weight.shape[0]
+    column = (s % (feats // slice_width)) * slice_width
+    low_part = lax.dot_general(
+        tokens, adapter_down_weight, (((1,), (1,)), ((), ())), preferred_element_type=F32
+    )
+    low_lines = rows * task_rows // LANES
     own_params = jnp.concatenate(
-        [adapter_down_weight, adapter_up_weight]
-        + [part[None].astype(BF16) for part in three_parts(final_norm_scale, 1.0)]
-    )
-    outgoing, own_params = lax.optimization_barrier((outgoing, own_params))
+        [
+            low_part.reshape(low_lines, LANES),
+            lax.dynamic_slice_in_dim(adapter_up_weight, column, slice_width, axis=1).astype(F32),
+            lax.dynamic_slice_in_dim(final_norm_scale, column, slice_width)[None],
+        ]
+    )
+    own_params, _ = lax.optimization_barrier((own_params, outgoing))
     received = swap(outgoing, EXPERT + ("c",))
     params = spread(own_params, EXPERT)
+    holder = lax.dynamic_index_in_dim(
+        params[:, low_lines:], s // (feats // slice_width), axis=0, keepdims=False
+    )
+    adapter_up = holder[:task_rows].astype(BF16)
+    norm_scale = holder[task_rows:]
+    task_of_lane = (
+        jnp.arange(LANES, dtype=jnp.int32) % task_rows // (task_rows // TASK_COUNT)
+    )
+    low_rank = rounded(
+        jnp.where(
+            task_of_lane[None, :] == document_task_index[0],
+            jnp.sum(params[:, :low_lines], axis=0),
+            0.0,
+        )
+    )
+    low_first = lax.reduce_precision(low_rank, 5, 10)
+    low_second = (low_rank - low_first) * LOW_STEP
     shard_rows = cores * capacity
     shard = received.reshape(experts, cores, capacity, half).transpose(1, 2, 0, 3)
     shard = shard.reshape(shard_rows, experts * half).astype(F32)
@@ -115,7 +141,8 @@
     table = jnp.stack(
         [routes.reshape(pairs).astype(F32)]
         + list(three_parts(chosen_expert_weight.reshape(pairs), 256.0))
-    ).astype(F16)
+    )
+    table = jnp.concatenate([table, low_first, low_second]).astype(F16)
     sent = jnp.concatenate(
         [
             scaled,
@@ -127,7 +154,7 @@
     gathered = lax.all_gather(sent, SEQ, axis=0, tiled=False)
     gathered = lax.optimization_barrier(gathered.astype(BF16))
     columns = experts * half
-    tables = gathered[:, :4, columns + LANES :].astype(F32)
+    tables = gathered[:, : 4 + 2 * low_lines, columns + LANES :].astype(F32)
     gathered = gathered.reshape(chips, cores, shard_rows, -1).transpose(1, 0, 2, 3)
     dispatched = gathered[..., :columns].reshape(cores, slots, columns)
     exponents = gathered[..., columns : columns + LANES].reshape(cores, slots, LANES).astype(F32)
@@ -159,36 +186,19 @@
         hidden.astype(BF16), down, (((0, 2), (0, 1)), ((), ())), preferred_element_type=F32
     )
 
-    adapter_down = (
-        params[:, :task_rows]
-        .reshape(experts, task_rows, cores, half)
-        .transpose(2, 1, 0, 3)
-        .reshape(cores, task_rows, columns)
-    )
-    low_rank = lax.dot_general(
-        dispatched, adapter_down, (((2,), (2,)), ((0,), (0,))), preferred_element_type=F32
-    )
-    low_rank = jnp.sum(low_rank * row_scale[..., :task_rows], axis=0)
-    task_of_row = jnp.arange(task_rows, dtype=jnp.int32) // (task_rows // TASK_COUNT)
-    low_rank = jnp.where(
-        task_of_row[None, :] == document_task_index[0], low_rank, 0.0
-    ).astype(BF16)
-    per_feature_group = feats // slice_width
     per_half = half // slice_width
-    adapter_up = lax.dynamic_slice(
-        params,
-        (s // per_feature_group, task_rows, (s % per_feature_group) * slice_width),
-        (1, task_rows, slice_width),
-    )[0]
-    adapted = jnp.dot(low_rank, adapter_up, preferred_element_type=F32)
     own_half = (s // per_half) % cores
     own = lax.dynamic_slice(
         dispatched,
-        (own_half, 0, (s // per_feature_group) * half + (s % per_half) * slice_width),
+        (
+            own_half,
+            0,
+            (s // (feats // slice_width)) * half + (s % per_half) * slice_width,
+        ),
         (1, slots, slice_width),
     )[0]
     own_scale = lax.dynamic_index_in_dim(row_scale, own_half, axis=0, keepdims=False)
-    base = own.astype(F32) * own_scale + ADAPTER_SCALE * adapted
+    base = own.astype(F32) * own_scale
 
     ids = tables[:, 0].astype(jnp.int32)
     weights = tables[:, 1] + (tables[:, 2] + tables[:, 3] / 256.0) / 256.0
@@ -222,15 +232,20 @@
         == jnp.arange(experts * blocks * capacity, dtype=jnp.int32)[None, None, :],
         axis=1,
     ).astype(F32)
-    mixed = jnp.dot(combiner, returned, precision=HIGH)
+    group_low = lax.dynamic_slice_in_dim(tables, g * blocks, blocks, axis=0)[:, 4:]
+    group_low = group_low[:, :low_lines] + group_low[:, low_lines:] / LOW_STEP
+    adapted = jnp.dot(
+        group_low.reshape(group_rows, task_rows).astype(BF16),
+        adapter_up,
+        preferred_element_type=F32,
+    )
+    mixed = jnp.dot(combiner, returned, precision=HIGH) + ADAPTER_SCALE * adapted
     squares = jnp.sum(spread(jnp.sum(mixed * mixed, axis=1)[None], SEQ), axis=0)
     position = g * group_rows + jnp.arange(group_rows, dtype=jnp.int32)[None, :]
     factor = jnp.where(position < counts[0], lax.rsqrt(squares / width + 1e-05), 0.0)
-    pooled = jnp.dot(factor, mixed, precision=HIGH)
+    pooled = jnp.dot(factor, mixed, precision=HIGH) * norm_scale
     pooled = jnp.sum(spread(pooled, GROUP), axis=0)
     pooled = spread(pooled, SEQ).reshape(1, width)
-    scale = jnp.sum(params[:, 2 * task_rows :].astype(F32), axis=1).reshape(1, width)
-    pooled = pooled * scale
     return pooled * lax.rsqrt(jnp.mean(pooled * pooled, axis=1, keepdims=True) + 1e-06)
 
 

time: 225 us -> 222 us (0.987)
  blocking collectives: 110 us -> 130 us
  starting transfers between devices: 38.7 us -> 28.6 us
  local copies, waits for them, and re-layouts: 19.1 us -> 13.4 us
  waiting for transfers between devices: 30.7 us -> 26.7 us
  matrix products: 14 us -> 11 us
    all_to_all x1 -> x2, blocking collectives: 8.99 us -> 25.8 us  [swap(): return lax.all_to_all(x, axes, split_axis=0, concat_axis=0, tiled=True)]
    all_to_all x5 -> x4, starting transfers between devices: 38.7 us -> 28.6 us  [swap(): return lax.all_to_all(x, axes, split_axis=0, concat_axis=0, tiled=True)]
    dot_general x4, matrix products: 6.39 us -> 1.74 us  [the longest x1 0.98 us: local(): lax.dot_general(tokens, adapter_down_weight, (((1,), (1,)), ((), ())), pr...]
    all_to_all x5 -> x4, waiting for transfers between devices: 30.7 us -> 26.7 us  [swap(): return lax.all_to_all(x, axes, split_axis=0, concat_axis=0, tiled=True)]
    all_gather x1, blocking collectives: 45.6 us -> 48.2 us  [local(): hidden = lax.all_gather(hidden, SEQ, axis=0, tiled=False)]
  transfers between devices with their start and end apart: 5 -> 4, of which waited for: 3 -> 3; matrix products, arithmetic and copies ran while one was open for 10% -> 5% of each run, Pallas kernels for 0% -> 0%
where the time goes in v3:
time: 222 us; the launch traced here: 221 us
  blocking collectives  130 us (59%)
  starting transfers between devices  28.6 us (13%)
  waiting for transfers between devices  26.7 us (12%)
  local copies, waits for them, and re-layouts  13.4 us (6%)
  matrix products  11 us (5%)
  other arithmetic  9.63 us (4%)
  between operations  2.36 us (1%)
    all_gather x1, blocking collectives, local(): gathered = lax.all_gather(sent, SEQ, axis=0, tiled=False)  55.5 us
    all_gather x1, blocking collectives, local(): hidden = lax.all_gather(hidden, SEQ, axis=0, tiled=False)  48.2 us
    all_to_all x4, starting transfers between devices, swap(): return lax.all_to_all(x, axes, split_axis=0, concat_axis=0, tiled=True)  28.6 us
    all_to_all x4, waiting for transfers between devices, swap(): return lax.all_to_all(x, axes, split_axis=0, concat_axis=0, tiled=True)  26.7 us
    all_to_all x2, blocking collectives, swap(): return lax.all_to_all(x, axes, split_axis=0, concat_axis=0, tiled=True)  25.8 us
    dot_general x1, matrix products, local(): lax.dot_general(dispatched, weights_in, (((2,), (1,)), ((0,), (0,))), pre...  4.68 us
  transfers between devices with their start and end apart: 4, of which 3 were waited for; matrix products, arithmetic and copies ran while one was open for 5% of the time, Pallas kernels for 0%

profile of v3, /device:TPU:1, one launch (start us, length us, event | category | flops | bytes accessed | tf_op | source)
XLA Modules:
  0.0 221.2 jit_solution(7298998398226645996)
XLA Ops:
  0.0 0.9 copy.105
  0.9 0.1 eq.101
  1.1 0.1 fusion.13
  1.2 0.1 convert_element_type.136
  1.4 0.1 copy.106
  1.4 0.8 multiply_add_fusion
  2.2 0.1 fusion.34
  2.3 1.1 convolution_convert_fusion
  3.4 0.1 copy.132
  3.6 0.1 reshape.376
  3.6 0.7 copy.108
  4.4 10.2 %all-to-all-start = ((bf16[16,20,256]{2,1,0:T(8,128)(2,1)}), bf16[16,20,256]{2,1,0:T(8,128)(2,1)S(1)}, u32[]{:S(2)}, u32[]{:S(2)}) async-start(bf16[16,20,256]{2,1,0:T(8,128)(2,1)} %copy.108), calls=%async_computation | async-start | bytes 393216 | tf_op jit(solution)/shard_map/all_to_all | solution.py:24
  14.6 0.8 dynamic-slice_bitcast_fusion
  15.3 0.7 dynamic-slice_convert_fusion.1
  16.0 0.8 copy.113
  16.8 0.1 reshape.377
  16.9 1.0 fusion.74
  17.9 0.1 reshape.378
  18.0 3.2 %pad_maximum_fusion = bf16[8,2,256,256]{3,2,1,0:T(8,128)(2,1)} fusion(bf16[8,2,256,128]{3,2,1,0:T(8,128)(2,1)} %bitcast.134, bf16[8,2,256,128]{3,2,1,0:T(8,128)(2,1)} %bitcast.135), kind=kLoop, calls=%fused_computation.3 | loop fusion | flops 4194304 | bytes 4194304 | tf_op jit(solution)/shard_map/concatenate | solution.py:164
  21.9 0.1 copy.112
  22.0 0.1 convert_element_type.146
  22.2 3.1 %copy.125 = bf16[8,2,256,256]{3,2,0,1:T(8,128)(2,1)} copy(bf16[8,2,256,256]{3,2,1,0:T(8,128)(2,1)} %pad_maximum_fusion) | data formatting | bytes 4194304 | tf_op jit(solution)/shard_map/concatenate | solution.py:164
  25.4 0.7 broadcast_in_dim.49
  26.0 6.6 %all-to-all-start.1 = ((f32[8,49,128]{2,1,0:T(8,128)}), f32[8,49,128]{2,1,0:T(8,128)S(1)}, u32[]{:S(2)}, u32[]{:S(2)}) async-start(f32[8,49,128]{2,1,0:T(8,128)} %broadcast_in_dim.49), calls=%async_computation.1 | async-start | bytes 458752 | tf_op jit(solution)/shard_map/all_to_all | solution.py:24
  32.7 0.1 abs_reduce_fusion
  32.9 0.1 reshape.398
  33.0 0.1 copy.128
  33.1 0.1 multiply_convert_fusion
  33.2 0.1 reshape.393
  33.3 7.0 %all-to-all-done.1 = f32[8,49,128]{2,1,0:T(8,128)S(1)} async-done(((f32[8,49,128]{2,1,0:T(8,128)}), f32[8,49,128]{2,1,0:T(8,128)S(1)}, u32[]{:S(2)}, u32[]{:S(2)}) %all-to-all-start.1) | async-done | bytes 200736 | tf_op jit(solution)/shard_map/all_to_all | solution.py:24
  40.3 0.3 concatenate.19
  40.6 0.1 broadcast_in_dim.45
  40.7 55.5 %all-gather.3 = f16[1280,2304]{1,0:T(8,128)(2,1)S(1)} all-gather(f16[40,2304]{1,0:T(8,128)(2,1)S(1)} %fusion.32), channel_id=2, replica_groups=mesh['z'=16,'c'=2,'y'=4,'h'=2,'t'=2] {'z','c'}, dimensions={0}, use_global_device_ids=true | all-gather | bytes 6082560 | tf_op jit(solution)/shard_map/all_gather | solution.py:154
  96.2 1.1 convert_element_type.166
  97.3 0.4 copy.131
  97.8 0.1 multiply_exponential_fusion
  97.9 3.0 %slice.76 = bf16[2,16,40,2048]{3,2,1,0:T(8,128)(2,1)} slice(bf16[2,16,40,2304]{3,2,1,0:T(8,128)(2,1)S(1)} %bitcast.125), slice={[0:2], [0:16], [0:40], [0:2048]} | slice | bytes 10485760 | tf_op jit(solution)/shard_map/slice | solution.py:159
  101.0 0.1 convert_element_type.160
  101.1 0.2 fusion.11
  101.3 0.9 compare_select_fusion
  102.2 0.2 select_reduce_fusion
  102.4 0.1 copy.117
  102.5 0.1 mul.232
  102.6 0.1 fusion.25
  102.7 4.7 %fusion.75 = f32[2,640,256]{2,1,0:T(8,128)S(1)} fusion(bf16[2,640,2048]{2,1,0:T(8,128)(2,1)} %bitcast.126, bf16[2,2048,256]{2,1,0:T(8,128)(2,1)} %bitcast.129), kind=kOutput, calls=%fused_computation.131 | convolution fusion | flops 1342177280 | bytes 8650752 | tf_op jit(solution)/shard_map/dot_general | solution.py:171
  107.4 0.2 fusion.18
  107.6 0.1 fusion.26
  107.8 48.2 %all-gather.4 = f16[32,640,128]{2,1,0:T(8,128)(2,1)S(1)} all-gather(f16[1,640,128]{2,1,0:T(8,128)(2,1)S(1)} %fusion.26), channel_id=1, replica_groups=mesh['z'=16,'c'=2,'y'=4,'h'=2,'t'=2] {'z','c'}, dimensions={0}, use_global_device_ids=true | all-gather | bytes 5406720 | tf_op jit(solution)/shard_map/all_gather | solution.py:178
  156.0 0.1 bitcast_multiply_fusion.3
  156.2 3.2 %fusion.8 = f32[640,128]{1,0:T(8,128)} fusion(f32[640,128]{1,0:T(8,128)S(1)} %bitcast_multiply_fusion.3, f16[32,640,128]{2,1,0:T(8,128)(2,1)S(1)} %all-gather.4, bf16[32,2,128,128]{3,2,1,0:T(8,128)(2,1)S(1)} %bitcast.120, s32[]{:T(128)S(6)} %select_n.95, f32[2,640,128]{2,1,0:T(8,128)S(1)} %bitcast.128, s32[]{:T(128)S(6)} %select_n.98, ...), kind=kOutput, calls=%fused_computation.6 | convolution fusion | flops 674119680 | bytes 7438348 | tf_op jit(solution)/shard_map/dot_general | solution.py:185
  159.3 3.5 %all-to-all-start.2 = ((f32[16,40,128]{2,1,0:T(8,128)}), f32[16,40,128]{2,1,0:T(8,128)S(1)}, u32[]{:S(2)}, u32[]{:S(2)}) async-start(f32[16,40,128]{2,1,0:T(8,128)} %bitcast.31), calls=%async_computation.2 | async-start | bytes 655360 | tf_op jit(solution)/shard_map/all_to_all | solution.py:24
  162.9 0.1 fusion.52
  163.0 0.1 eq.114
  163.3 8.7 %all-to-all-done.2 = f32[16,40,128]{2,1,0:T(8,128)S(1)} async-done(((f32[16,40,128]{2,1,0:T(8,128)}), f32[16,40,128]{2,1,0:T(8,128)S(1)}, u32[]{:S(2)}, u32[]{:S(2)}) %all-to-all-start.2) | async-done | bytes 327712 | tf_op jit(solution)/shard_map/all_to_all | solution.py:24
  172.0 0.4 fusion.76
  172.3 0.2 multiply_reduce_fusion
  172.6 0.6 broadcast_in_dim.55
  173.2 8.3 %all-to-all-start.3 = ((f32[32,1,128]{2,1,0:T(1,128)}), f32[32,1,128]{2,1,0:T(1,128)S(1)}, u32[]{:S(2)}, u32[]{:S(2)}) async-start(f32[32,1,128]{2,1,0:T(1,128)} %broadcast_in_dim.55), calls=%async_computation.3 | async-start | bytes 32768 | tf_op jit(solution)/shard_map/all_to_all | solution.py:24
  182.1 11.1 %all-to-all-done.3 = f32[32,1,128]{2,1,0:T(1,128)S(1)} async-done(((f32[32,1,128]{2,1,0:T(1,128)}), f32[32,1,128]{2,1,0:T(1,128)S(1)}, u32[]{:S(2)}, u32[]{:S(2)}) %all-to-all-start.3) | async-done | bytes 16416 | tf_op jit(solution)/shard_map/all_to_all | solution.py:24
  193.2 0.2 fusion.14
  193.4 9.0 %all_to_all.30 = f32[16,1,128]{2,1,0:T(1,128)S(1)} all-to-all(f32[16,1,128]{2,1,0:T(1,128)S(1)} %broadcast_in_dim.94), channel_id=1, replica_groups=mesh['z'=16,'c'=2,'y'=4,'h'=2,'t'=2] {'y','h','t'}, dimensions={0} | all-to-all | bytes 16384 | tf_op jit(solution)/shard_map/all_to_all | solution.py:24
  202.4 16.8 %all_to_all.31 = f32[32,1,128]{2,1,0:T(1,128)S(1)} all-to-all(f32[32,1,128]{2,1,0:T(1,128)S(1)} %broadcast_in_dim.95), channel_id=1, replica_groups=mesh['z'=16,'c'=2,'y'=4,'h'=2,'t'=2] {'z','c'}, dimensions={0} | all-to-all | bytes 32768 | tf_op jit(solution)/shard_map/all_to_all | solution.py:24
  219.3 0.6 multiply_reduce_fusion.1
  220.6 0.6 multiply_bitcast_fusion
  (30 shorter events, 0.7 us)
Async XLA Ops:
  0.0 156.1 %copy-start = (bf16[1,8192,128]{2,1,0:T(8,128)(2,1)S(1)}, bf16[1,8192,128]{2,1,0:T(8,128)(2,1)}, u32[]{:S(2)}) copy-start(bf16[1,8192,128]{2,1,0:T(8,128)(2,1)} %param.16) | copy-start | bytes 6291460
  4.4 21.0 %all-to-all-start = ((bf16[16,20,256]{2,1,0:T(8,128)(2,1)}), bf16[16,20,256]{2,1,0:T(8,128)(2,1)S(1)}, u32[]{:S(2)}, u32[]{:S(2)}) async-start(bf16[16,20,256]{2,1,0:T(8,128)(2,1)} %copy.108), calls=%async_computation | async-start | bytes 393216 | tf_op jit(solution)/shard_map/all_to_all | solution.py:24
  26.0 14.2 %all-to-all-start.1 = ((f32[8,49,128]{2,1,0:T(8,128)}), f32[8,49,128]{2,1,0:T(8,128)S(1)}, u32[]{:S(2)}, u32[]{:S(2)}) async-start(f32[8,49,128]{2,1,0:T(8,128)} %broadcast_in_dim.49), calls=%async_computation.1 | async-start | bytes 458752 | tf_op jit(solution)/shard_map/all_to_all | solution.py:24
  97.3 3.7 %copy-start.1 = (f32[32,36,128]{2,1,0:T(8,128)}, f32[32,36,128]{2,1,0:T(8,128)S(1)}, u32[]{:S(2)}) copy-start(f32[32,36,128]{2,1,0:T(8,128)S(1)} %slice_convert_fusion) | copy-start | bytes 1769476
  159.3 12.6 %all-to-all-start.2 = ((f32[16,40,128]{2,1,0:T(8,128)}), f32[16,40,128]{2,1,0:T(8,128)S(1)}, u32[]{:S(2)}, u32[]{:S(2)}) async-start(f32[16,40,128]{2,1,0:T(8,128)} %bitcast.31), calls=%async_computation.2 | async-start | bytes 655360 | tf_op jit(solution)/shard_map/all_to_all | solution.py:24
  173.2 20.0 %all-to-all-start.3 = ((f32[32,1,128]{2,1,0:T(1,128)}), f32[32,1,128]{2,1,0:T(1,128)S(1)}, u32[]{:S(2)}, u32[]{:S(2)}) async-start(f32[32,1,128]{2,1,0:T(1,128)} %broadcast_in_dim.55), calls=%async_computation.3 | async-start | bytes 32768 | tf_op jit(solution)/shard_map/all_to_all | solution.py:24

commit v4 on v3

--- a/solution.py
+++ b/solution.py
@@ -1,6 +1,10 @@
+import functools
+
 import jax
 import jax.numpy as jnp
 from jax import lax
+from jax.experimental import pallas as pl
+from jax.experimental.pallas import tpu as pltpu
 from jax.sharding import Mesh
 from jax.sharding import PartitionSpec as P
 
@@ -49,6 +53,80 @@
         one_hot, before, (((2,), (0,)), ((), ())), preferred_element_type=F32
     )
     return jnp.sum(earlier * one_hot.astype(F32), axis=1).astype(jnp.int32)
+
+
+def expert_kernel(
+    shard_rows, own_ref, x_ref, gate_ref, up_ref, hidden_ref, scale_ref, base_ref, weight_ref
+):
+    columns = weight_ref.shape[0]
+    units = gate_ref.shape[1]
+    halves = 2
+    half = 256
+    for block in range(columns // half):
+        for c in range(halves):
+            source = pl.ds((block * halves + c) * half, half)
+            target = pl.ds(block * half, half)
+            weight_ref[target, pl.ds(c * 2 * units, units)] = gate_ref[source, :]
+            weight_ref[target, pl.ds((c * 2 + 1) * units, units)] = up_ref[source, :]
+    chips = 4
+    step_rows = chips * halves * shard_rows
+    shape = (chips, halves, shard_rows, units)
+    own_half = own_ref[0]
+    own_column = pl.multiple_of(own_ref[1], LANES)
+
+    def step(i, carry):
+        rows = pl.ds(pl.multiple_of(i * step_rows, step_rows), step_rows)
+        out_rows = pl.ds(
+            pl.multiple_of(i * chips * shard_rows, chips * shard_rows), chips * shard_rows
+        )
+        acts = jnp.dot(
+            x_ref[rows, pl.ds(0, columns)], weight_ref[...], preferred_element_type=F32
+        )
+        acts = acts.reshape(chips, halves, shard_rows, 4 * units)
+        exponents = x_ref[rows, pl.ds(columns, LANES)].astype(F32).reshape(shape)
+        own = x_ref[rows, pl.ds(own_column, LANES)].astype(F32).reshape(shape)
+        first, second = exponents[:, 0], exponents[:, 1]
+        first_scale, second_scale = jnp.exp2(first - 15.0), jnp.exp2(second - 15.0)
+        gate_act = (
+            acts[:, 0, :, :units] * first_scale
+            + acts[:, 1, :, 2 * units : 3 * units] * second_scale
+        )
+        up_act = (
+            acts[:, 0, :, units : 2 * units] * first_scale
+            + acts[:, 1, :, 3 * units :] * second_scale
+        )
+        hidden = (gate_act / (1.0 + jnp.exp(-gate_act)) * up_act).astype(BF16).astype(F32)
+        row_exponent = jnp.maximum(first, second)
+        flat = (chips * shard_rows, units)
+        hidden_ref[out_rows, :] = (hidden * jnp.exp2(-2.0 * row_exponent - 2.0)).reshape(flat)
+        scale_ref[out_rows, :] = jnp.exp2(2.0 * row_exponent + 2.0).reshape(flat)
+        base_ref[out_rows, :] = jnp.where(
+            own_half == 0, own[:, 0] * first_scale, own[:, 1] * second_scale
+        ).reshape(flat)
+        return carry
+
+    lax.fori_loop(0, x_ref.shape[0] // step_rows, step, 0)
+
+
+def expert_layer(gathered, gate_weight, up_weight, own_half, own_column, shard_rows):
+    rows = gathered.shape[0]
+    columns = gathered.shape[1] - LANES
+    units = gate_weight.shape[1]
+    out = jax.ShapeDtypeStruct((rows // 2, units), F32)
+    vmem = pl.BlockSpec(memory_space=pltpu.VMEM)
+    return pl.pallas_call(
+        functools.partial(expert_kernel, shard_rows),
+        out_shape=(out, out, out),
+        in_specs=[pl.BlockSpec(memory_space=pltpu.SMEM), vmem, vmem, vmem],
+        out_specs=(vmem, vmem, vmem),
+        scratch_shapes=[pltpu.VMEM((columns, 4 * units), BF16)],
+        compiler_params=pltpu.CompilerParams(vmem_limit_bytes=32 * 2**20),
+        cost_estimate=pl.CostEstimate(
+            flops=8 * rows * columns * units,
+            bytes_accessed=2 * rows * columns + 8 * columns * units,
+            transcendentals=2 * rows * units,
+        ),
+    )(jnp.stack([own_half, own_column]), gathered, gate_weight, up_weight)
 
 
 def local(
@@ -70,7 +148,6 @@
     cores = lax.axis_size("c")
     groups = lax.axis_size(GROUP)
     tensors = lax.axis_size("t")
-    chips = seq // cores
     capacity = rows * 5 // 16
     width = feats * experts
     half = feats // cores
@@ -138,44 +215,38 @@
         jnp.floor(jnp.log2(jnp.maximum(largest, 1e-30)) + 1.01), LEAST_EXPONENT
     )
     scaled = (shard * jnp.exp2(15.0 - exponent)).astype(F16)
-    table = jnp.stack(
+    notes = jnp.stack(
         [routes.reshape(pairs).astype(F32)]
         + list(three_parts(chosen_expert_weight.reshape(pairs), 256.0))
     )
-    table = jnp.concatenate([table, low_first, low_second]).astype(F16)
+    notes = jnp.concatenate([notes, low_first, low_second])
+    notes = jnp.pad(notes, ((0, -notes.shape[0] % 8), (0, 0))).astype(F16)
     sent = jnp.concatenate(
         [
             scaled,
             jnp.broadcast_to(exponent, (shard_rows, LANES)).astype(F16),
-            jnp.pad(table, ((0, shard_rows - table.shape[0]), (0, 0))),
         ],
         axis=1,
     )
     gathered = lax.all_gather(sent, SEQ, axis=0, tiled=False)
-    gathered = lax.optimization_barrier(gathered.astype(BF16))
     columns = experts * half
-    tables = gathered[:, : 4 + 2 * low_lines, columns + LANES :].astype(F32)
-    gathered = gathered.reshape(chips, cores, shard_rows, -1).transpose(1, 0, 2, 3)
-    dispatched = gathered[..., :columns].reshape(cores, slots, columns)
-    exponents = gathered[..., columns : columns + LANES].reshape(cores, slots, LANES).astype(F32)
-    row_scale = jnp.exp2(exponents - 15.0)
-    row_exponent = jnp.max(exponents, axis=0)
-
-    weights_in = jnp.concatenate([expert_gate_weight[0], expert_up_weight[0]], axis=1)
-    hidden_units = expert_gate_weight.shape[2]
-    weights_in = (
-        weights_in.reshape(experts, cores, half, 2 * hidden_units)
-        .transpose(1, 0, 2, 3)
-        .reshape(cores, columns, 2 * hidden_units)
-    )
-    acts = lax.dot_general(
-        dispatched, weights_in, (((2,), (1,)), ((0,), (0,))), preferred_element_type=F32
-    )
-    gate_act = jnp.sum(acts[..., :hidden_units] * row_scale, axis=0)
-    up_act = jnp.sum(acts[..., hidden_units:] * row_scale, axis=0)
-    hidden = rounded(jax.nn.silu(gate_act) * up_act)
-    hidden = (hidden * jnp.exp2(-2.0 * row_exponent - 2.0)).astype(F16)
-    hidden = lax.all_gather(hidden, SEQ, axis=0, tiled=False)
+    gathered = gathered.astype(BF16).reshape(seq * shard_rows, columns + LANES)
+    per_half = half // slice_width
+    hidden, return_scale, base = expert_layer(
+        gathered,
+        expert_gate_weight[0],
+        expert_up_weight[0],
+        (s // per_half) % cores,
+        (s // (feats // slice_width)) * half + (s % per_half) * slice_width,
+        shard_rows,
+    )
+
+    hidden = lax.all_gather(
+        jnp.concatenate([hidden.astype(F16), notes]), SEQ, axis=0, tiled=False
+    )
+    tables = hidden[:, slots : slots + 4 + 2 * low_lines].astype(F32)
+    hidden = hidden[:, :slots]
+    hidden_units = hidden.shape[-1]
     down = lax.dynamic_index_in_dim(
         expert_down_weight[0].reshape(seq, tensors, hidden_units, slice_width),
         t,
@@ -185,20 +256,6 @@
     part = lax.dot_general(
         hidden.astype(BF16), down, (((0, 2), (0, 1)), ((), ())), preferred_element_type=F32
     )
-
-    per_half = half // slice_width
-    own_half = (s // per_half) % cores
-    own = lax.dynamic_slice(
-        dispatched,
-        (
-            own_half,
-            0,
-            (s // (feats // slice_width)) * half + (s % per_half) * slice_width,
-        ),
-        (1, slots, slice_width),
-    )[0]
-    own_scale = lax.dynamic_index_in_dim(row_scale, own_half, axis=0, keepdims=False)
-    base = own.astype(F32) * own_scale
 
     ids = tables[:, 0].astype(jnp.int32)
     weights = tables[:, 1] + (tables[:, 2] + tables[:, 3] / 256.0) / 256.0
@@ -212,7 +269,7 @@
         ),
         axis=2,
     ).reshape(slots, 1)
-    payload = slot_weight * jnp.exp2(2.0 * row_exponent + 2.0) * part + base / (2 * tensors)
+    payload = slot_weight * return_scale * part + base / (2 * tensors)
     blocks = seq // groups
     returned = swap(payload.reshape(groups, blocks * capacity, slice_width), GROUP)
     returned = jnp.sum(

time: 222 us -> 210 us (0.946)
  Pallas kernels: 0 us -> 4.39 us
  waiting for transfers between devices: 26.7 us -> 22.5 us
  other arithmetic: 9.63 us -> 5.65 us
  matrix products: 11 us -> 7.9 us
  blocking collectives: 130 us -> 127 us
  local copies, waits for them, and re-layouts: 13.4 us -> 10.5 us
    dot_general x1 -> x0, matrix products: 4.68 us -> none  [local(): lax.dot_general(dispatched, weights_in, (((2,), (1,)), ((0,), (0,))), pre...]
    pallas_call x0 -> x1, Pallas kernels: none -> 4.39 us  [expert_layer(): pl.pallas_call(functools.partial(expert_kernel, shard_rows), out_shape=(o...]
    all_to_all x4, waiting for transfers between devices: 26.7 us -> 22.5 us  [swap(): return lax.all_to_all(x, axes, split_axis=0, concat_axis=0, tiled=True)]
    unnamed x7 -> x13, local copies, waits for them, and re-layouts: 1.8 us -> 5.35 us
    concatenate x1, other arithmetic: 3.21 us -> 0.04 us  [local(): jnp.concatenate([hidden.astype(F16), notes])]
    concatenate x2 -> x1, local copies, waits for them, and re-layouts: 3.43 us -> 0.28 us  [local(): notes = jnp.concatenate([notes, low_first, low_second])]
    slice x1 -> x0, local copies, waits for them, and re-layouts: 3.05 us -> none  [local(): dispatched = gathered[..., :columns].reshape(cores, slots, columns)]
  transfers between devices with their start and end apart: 4 -> 4, of which waited for: 3 -> 3; matrix products, arithmetic and copies ran while one was open for 5% -> 3% of each run, Pallas kernels for 0% -> 2%
where the time goes in v4:
time: 210 us; the launch traced here: 209 us
  blocking collectives  127 us (60%)
  starting transfers between devices  29 us (14%)
  waiting for transfers between devices  22.5 us (11%)
  local copies, waits for them, and re-layouts  10.5 us (5%)
  matrix products  7.9 us (4%)
  other arithmetic  5.65 us (3%)
  Pallas kernels  4.39 us (2%)
  between operations  2.41 us (1%)
    all_gather x1, blocking collectives, local(): gathered = lax.all_gather(sent, SEQ, axis=0, tiled=False)  54.1 us
    all_gather x1, blocking collectives, local(): lax.all_gather(jnp.concatenate([hidden.astype(F16), notes]), SEQ, axis=0,...  47.1 us
    all_to_all x4, starting transfers between devices, swap(): return lax.all_to_all(x, axes, split_axis=0, concat_axis=0, tiled=True)  29 us
    all_to_all x2, blocking collectives, swap(): return lax.all_to_all(x, axes, split_axis=0, concat_axis=0, tiled=True)  25.8 us
    all_to_all x4, waiting for transfers between devices, swap(): return lax.all_to_all(x, axes, split_axis=0, concat_axis=0, tiled=True)  22.5 us
    unnamed x13, local copies, waits for them, and re-layouts  5.35 us
    dot_general x1, matrix products, local(): lax.dot_general(hidden.astype(BF16), down, (((0, 2), (0, 1)), ((), ())),...  4.75 us
    pallas_call x1, Pallas kernels, expert_layer(): pl.pallas_call(functools.partial(expert_kernel, shard_rows), out_shape=(o...  4.39 us
  transfers between devices with their start and end apart: 4, of which 3 were waited for; matrix products, arithmetic and copies ran while one was open for 3% of the time, Pallas kernels for 2%

profile of v4, /device:TPU:1, one launch (start us, length us, event | category | flops | bytes accessed | tf_op | source)
XLA Modules:
  0.0 209.4 jit_solution(9902172874513920050)
XLA Ops:
  0.0 0.9 copy.92
  0.9 0.1 eq.101
  1.1 0.1 fusion.6
  1.2 0.1 convert_element_type.121
  1.4 0.1 copy.93
  1.4 0.8 multiply_add_fusion
  2.2 0.1 fusion.14
  2.3 1.1 convolution_convert_fusion
  3.4 0.1 copy.115
  3.6 0.1 reshape.281
  3.6 0.7 copy.95
  4.4 10.2 %all-to-all-start = ((bf16[16,20,256]{2,1,0:T(8,128)(2,1)}), bf16[16,20,256]{2,1,0:T(8,128)(2,1)S(1)}, u32[]{:S(2)}, u32[]{:S(2)}) async-start(bf16[16,20,256]{2,1,0:T(8,128)(2,1)} %copy.95), calls=%async_computation | async-start | bytes 393216 | tf_op jit(solution)/shard_map/all_to_all | solution.py:28
  14.6 0.7 dynamic-slice_convert_fusion.1
  15.3 0.8 dynamic-slice_bitcast_fusion
  16.0 1.0 fusion.54
  17.0 0.1 reshape.284
  17.7 0.8 copy.100
  18.5 0.1 reshape.283
  18.8 0.1 copy.99
  18.9 0.1 convert_element_type.133
  19.0 0.1 pad_add_fusion.own_ref
  19.1 3.6 %all-to-all-done = bf16[16,20,256]{2,1,0:T(8,128)(2,1)S(1)} async-done(((bf16[16,20,256]{2,1,0:T(8,128)(2,1)}), bf16[16,20,256]{2,1,0:T(8,128)(2,1)S(1)}, u32[]{:S(2)}, u32[]{:S(2)}) %all-to-all-start) | async-done | bytes 163872 | tf_op jit(solution)/shard_map/all_to_all | solution.py:28
  22.8 0.7 broadcast_in_dim.49
  23.5 3.4 %all-to-all-start.1 = ((f32[8,49,128]{2,1,0:T(8,128)}), f32[8,49,128]{2,1,0:T(8,128)S(1)}, u32[]{:S(2)}, u32[]{:S(2)}) async-start(f32[8,49,128]{2,1,0:T(8,128)} %broadcast_in_dim.49), calls=%async_computation.1 | async-start | bytes 458752 | tf_op jit(solution)/shard_map/all_to_all | solution.py:28
  26.9 0.1 abs_reduce_fusion
  27.0 0.1 copy.98
  27.1 0.1 reshape.300
  27.3 0.2 reshape.295
  27.5 0.1 copy.110
  27.6 0.1 reshape.294
  27.7 0.1 multiply_convert_fusion
  27.8 0.1 broadcast_in_dim.45
  27.9 54.1 %all-gather.4 = f16[1280,2176]{1,0:T(8,128)(2,1)S(1)} all-gather(f16[40,2176]{1,0:T(8,128)(2,1)S(1)} %pad_maximum_fusion), channel_id=2, replica_groups=mesh['z'=16,'c'=2,'y'=4,'h'=2,'t'=2] {'z','c'}, dimensions={0}, use_global_device_ids=true | all-gather | bytes 5744640 | tf_op jit(solution)/shard_map/all_gather | solution.py:231
  82.0 1.0 convert_element_type.149.x_ref
  83.0 0.3 copy-done.1
  83.3 0.3 copy-done.2
  83.6 4.4 %shard_map.109 = (f32[640,128]{1,0:T(8,128)S(1)}, f32[640,128]{1,0:T(8,128)S(1)}, f32[640,128]{1,0:T(8,128)S(1)}) custom-call(s32[2]{0:T(128)S(1)} %pad_add_fusion.own_ref, bf16[1280,2176]{1,0:T(8,128)(2,1)S(1)} %convert_element_type.149.x_ref, bf16[4096,128]{1,0:T(8,128)(2,1)S(1)} %bitcast.82, bf16[4096,128]{1,0:T(8,128)(2,1)S(1)} %bitcast.83), custom_call_target="tpu_custom_call" | custom-call | flops 2684354560 | bytes 7340032 | tf_op jit(solution)/shard_map/pallas_call | solution.py:117
  88.1 0.3 concatenate.15
  88.4 47.1 %all-gather.5 = f16[21760,128]{1,0:T(8,128)(2,1)S(1)} all-gather(f16[680,128]{1,0:T(8,128)(2,1)S(1)} %fusion.12), channel_id=3, replica_groups=mesh['z'=16,'c'=2,'y'=4,'h'=2,'t'=2] {'z','c'}, dimensions={0}, use_global_device_ids=true | all-gather | bytes 5744640 | tf_op jit(solution)/shard_map/all_gather | solution.py:244
  135.5 2.4 %copy-done.3 = f16[21760,128]{1,0:T(8,128)(2,1)} copy-done((f16[21760,128]{1,0:T(8,128)(2,1)}, f16[21760,128]{1,0:T(8,128)(2,1)S(1)}, u32[]{:S(2)}) %copy-start.3) | copy-done | bytes 5570584
  137.9 0.1 slice_add_fusion
  138.0 0.2 fusion.4
  138.2 0.6 copy-done.4
  138.8 0.2 select_reduce_fusion
  139.0 0.1 copy.104
  139.0 0.1 mul.175
  139.2 4.8 %fusion.3 = f32[640,128]{1,0:T(8,128)} fusion(f16[32,680,128]{2,1,0:T(8,128)(2,1)} %bitcast.85, bf16[32,2,128,128]{3,2,1,0:T(8,128)(2,1)S(1)} %bitcast.81, s32[]{:T(128)S(6)} %select_n.91, f32[640,128]{1,0:T(8,128)S(1)} %get-tuple-element.12, f32[640,128]{1,0:T(8,128)S(1)} %get-tuple-element.11, f32[640]{0:T(1024)S(1)} %mul.175), kind=kOutput, calls=%fused_computation.4 | convolution fusion | flops 674037760 | bytes 7278596 | tf_op jit(solution)/shard_map/dot_general | solution.py:256
  143.9 6.4 %all-to-all-start.2 = ((f32[16,40,128]{2,1,0:T(8,128)}), f32[16,40,128]{2,1,0:T(8,128)S(1)}, u32[]{:S(2)}, u32[]{:S(2)}) async-start(f32[16,40,128]{2,1,0:T(8,128)} %bitcast.21), calls=%async_computation.2 | async-start | bytes 655360 | tf_op jit(solution)/shard_map/all_to_all | solution.py:28
  150.3 0.1 fusion.32
  150.4 0.1 eq.114
  150.5 0.1 copy.103
  150.6 0.8 fusion.19
  151.4 0.1 convert_element_type.143
  151.6 7.8 %all-to-all-done.2 = f32[16,40,128]{2,1,0:T(8,128)S(1)} async-done(((f32[16,40,128]{2,1,0:T(8,128)}), f32[16,40,128]{2,1,0:T(8,128)S(1)}, u32[]{:S(2)}, u32[]{:S(2)}) %all-to-all-start.2) | async-done | bytes 327712 | tf_op jit(solution)/shard_map/all_to_all | solution.py:28
  159.4 0.4 fusion.55
  159.7 0.2 multiply_reduce_fusion
  160.0 0.6 broadcast_in_dim.55
  160.6 9.1 %all-to-all-start.3 = ((f32[32,1,128]{2,1,0:T(1,128)}), f32[32,1,128]{2,1,0:T(1,128)S(1)}, u32[]{:S(2)}, u32[]{:S(2)}) async-start(f32[32,1,128]{2,1,0:T(1,128)} %broadcast_in_dim.55), calls=%async_computation.3 | async-start | bytes 32768 | tf_op jit(solution)/shard_map/all_to_all | solution.py:28
  170.3 11.1 %all-to-all-done.3 = f32[32,1,128]{2,1,0:T(1,128)S(1)} async-done(((f32[32,1,128]{2,1,0:T(1,128)}), f32[32,1,128]{2,1,0:T(1,128)S(1)}, u32[]{:S(2)}, u32[]{:S(2)}) %all-to-all-start.3) | async-done | bytes 16416 | tf_op jit(solution)/shard_map/all_to_all | solution.py:28
  181.4 0.2 fusion.7
  181.6 9.0 %all_to_all.30 = f32[16,1,128]{2,1,0:T(1,128)S(1)} all-to-all(f32[16,1,128]{2,1,0:T(1,128)S(1)} %broadcast_in_dim.94), channel_id=1, replica_groups=mesh['z'=16,'c'=2,'y'=4,'h'=2,'t'=2] {'y','h','t'}, dimensions={0} | all-to-all | bytes 16384 | tf_op jit(solution)/shard_map/all_to_all | solution.py:28
  190.7 16.8 %all_to_all.31 = f32[32,1,128]{2,1,0:T(1,128)S(1)} all-to-all(f32[32,1,128]{2,1,0:T(1,128)S(1)} %broadcast_in_dim.95), channel_id=1, replica_groups=mesh['z'=16,'c'=2,'y'=4,'h'=2,'t'=2] {'z','c'}, dimensions={0} | all-to-all | bytes 32768 | tf_op jit(solution)/shard_map/all_to_all | solution.py:28
  207.5 0.6 multiply_reduce_fusion.1
  208.8 0.6 multiply_bitcast_fusion
  (32 shorter events, 0.6 us)
Async XLA Ops:
  0.0 139.1 %copy-start = (bf16[1,8192,128]{2,1,0:T(8,128)(2,1)S(1)}, bf16[1,8192,128]{2,1,0:T(8,128)(2,1)}, u32[]{:S(2)}) copy-start(bf16[1,8192,128]{2,1,0:T(8,128)(2,1)} %param.16) | copy-start | bytes 6291460
  4.4 18.4 %all-to-all-start = ((bf16[16,20,256]{2,1,0:T(8,128)(2,1)}), bf16[16,20,256]{2,1,0:T(8,128)(2,1)S(1)}, u32[]{:S(2)}, u32[]{:S(2)}) async-start(bf16[16,20,256]{2,1,0:T(8,128)(2,1)} %copy.95), calls=%async_computation | async-start | bytes 393216 | tf_op jit(solution)/shard_map/all_to_all | solution.py:28
  23.5 64.6 %all-to-all-start.1 = ((f32[8,49,128]{2,1,0:T(8,128)}), f32[8,49,128]{2,1,0:T(8,128)S(1)}, u32[]{:S(2)}, u32[]{:S(2)}) async-start(f32[8,49,128]{2,1,0:T(8,128)} %broadcast_in_dim.49), calls=%async_computation.1 | async-start | bytes 458752 | tf_op jit(solution)/shard_map/all_to_all | solution.py:28
  82.0 1.2 copy-start.1
  82.0 1.5 copy-start.2
  135.5 2.4 %copy-start.3 = (f16[21760,128]{1,0:T(8,128)(2,1)}, f16[21760,128]{1,0:T(8,128)(2,1)S(1)}, u32[]{:S(2)}) copy-start(f16[21760,128]{1,0:T(8,128)(2,1)S(1)} %all-gather.5) | copy-start | bytes 16711684
  137.9 0.9 copy-start.4
  143.9 15.5 %all-to-all-start.2 = ((f32[16,40,128]{2,1,0:T(8,128)}), f32[16,40,128]{2,1,0:T(8,128)S(1)}, u32[]{:S(2)}, u32[]{:S(2)}) async-start(f32[16,40,128]{2,1,0:T(8,128)} %bitcast.21), calls=%async_computation.2 | async-start | bytes 655360 | tf_op jit(solution)/shard_map/all_to_all | solution.py:28
  160.6 20.8 %all-to-all-start.3 = ((f32[32,1,128]{2,1,0:T(1,128)}), f32[32,1,128]{2,1,0:T(1,128)S(1)}, u32[]{:S(2)}, u32[]{:S(2)}) async-start(f32[32,1,128]{2,1,0:T(1,128)} %broadcast_in_dim.55), calls=%async_computation.3 | async-start | bytes 32768 | tf_op jit(solution)/shard_map/all_to_all | solution.py:28

commit v5 on v4

v5 whole, which is shorter than its diff:
```python
import functools

import jax
import jax.numpy as jnp
from jax import lax
from jax.experimental import pallas as pl
from jax.experimental.pallas import tpu as pltpu
from jax.sharding import Mesh
from jax.sharding import PartitionSpec as P

TASK_COUNT = 2
ADAPTER_SCALE = 0.5

SEQ = ("z", "c")
EXPERT = ("y", "h")
GROUP = ("y", "h", "t")
HALVES = 2

BF16 = jnp.bfloat16
F16 = jnp.float16
F32 = jnp.float32
HIGH = lax.Precision.HIGHEST
LANES = 128
LEAST_EXPONENT = -40.0
NOTE_ROWS = 16
PART_STEP = 256.0
PARAM_ROWS = 128


def swap(x, axes):
    return lax.all_to_all(x, axes, split_axis=0, concat_axis=0, tiled=True)


def spread(x, axes):
    return swap(jnp.broadcast_to(x[None], (lax.axis_size(axes),) + x.shape), axes)


def three_parts(x, step):
    first = lax.reduce_precision(x, 8, 7)
    rest = (x - first) * step
    second = lax.reduce_precision(rest, 8, 7)
    return first, second, (rest - second) * step


def earlier_in_block(lanes, block):
    i = lax.broadcasted_iota(jnp.int32, (lanes, lanes), 0)
    j = lax.broadcasted_iota(jnp.int32, (lanes, lanes), 1)
    return ((i < j) & (i // block == j // block)).astype(F32).astype(BF16)


def positions(named, block, capacity):
    lanes = named.shape[1]
    before = jnp.dot(
        named.astype(F32).astype(BF16),
        earlier_in_block(lanes, block),
        preferred_element_type=F32,
    )
    first = (lax.broadcasted_iota(jnp.int32, named.shape, 1) // block * capacity).astype(F32)
    return jnp.where(named, before + first, -1.0)


def expert_kernel(
    shard_rows,
    own_ref,
    x_ref,
    gate_ref,
    up_ref,
    params_ref,
    hidden_ref,
    scale_ref,
    base_ref,
    weight_ref,
    adapter_ref,
):
    columns = weight_ref.shape[0]
    units = gate_ref.shape[1]
    task_rows = adapter_ref.shape[0] // HALVES
    groups = params_ref.shape[0]
    half = columns // groups
    for block in range(groups):
        target = pl.ds(block * half, half)
        for c in range(HALVES):
            source = pl.ds((block * HALVES + c) * half, half)
            weight_ref[target, pl.ds(c * 2 * units, units)] = gate_ref[source, :]
            weight_ref[target, pl.ds((c * 2 + 1) * units, units)] = up_ref[source, :]
            adapter_ref[pl.ds(c * task_rows, task_rows), target] = params_ref[
                block, pl.ds(0, task_rows), pl.ds(c * half, half)
            ]
    chips = 4
    step_rows = chips * HALVES * shard_rows
    shape = (chips, HALVES, shard_rows, units)
    flat = (chips * shard_rows, units)
    own_half = own_ref[0]
    own_column = pl.multiple_of(own_ref[1], LANES)
    own_group = own_ref[2]
    group_column = pl.multiple_of(own_ref[3], LANES)
    task = own_ref[4]
    adapter_up = params_ref[own_group, pl.ds(task_rows, task_rows), pl.ds(group_column, units)]
    task_of_lane = lax.broadcasted_iota(
        jnp.int32, (flat[0], task_rows), 1
    ) // (task_rows // TASK_COUNT)

    def step(i, carry):
        rows = pl.ds(pl.multiple_of(i * step_rows, step_rows), step_rows)
        out_rows = pl.ds(pl.multiple_of(i * flat[0], flat[0]), flat[0])
        x = x_ref[rows, pl.ds(0, columns)]
        acts = jnp.dot(x, weight_ref[...], preferred_element_type=F32)
        acts = acts.reshape(chips, HALVES, shard_rows, 4 * units)
        low = lax.dot_general(
            x, adapter_ref[...], (((1,), (1,)), ((), ())), preferred_element_type=F32
        ).reshape(chips, HALVES, shard_rows, HALVES * task_rows)
        exponents = x_ref[rows, pl.ds(columns, LANES)].astype(F32).reshape(shape)
        own = x_ref[rows, pl.ds(own_column, LANES)].astype(F32).reshape(shape)
        first, second = exponents[:, 0], exponents[:, 1]
        first_scale, second_scale = jnp.exp2(first - 15.0), jnp.exp2(second - 15.0)
        gate_act = (
            acts[:, 0, :, :units] * first_scale
            + acts[:, 1, :, 2 * units : 3 * units] * second_scale
        )
        up_act = (
            acts[:, 0, :, units : 2 * units] * first_scale
            + acts[:, 1, :, 3 * units :] * second_scale
        )
        hidden = (gate_act / (1.0 + jnp.exp(-gate_act)) * up_act).astype(BF16).astype(F32)
        row_exponent = jnp.maximum(first, second)
        hidden_ref[out_rows, :] = (hidden * jnp.exp2(-2.0 * row_exponent - 2.0)).reshape(flat)
        scale_ref[out_rows, :] = jnp.exp2(2.0 * row_exponent + 2.0).reshape(flat)
        low = (
            low[:, 0, :, :task_rows] * first_scale[..., :task_rows]
            + low[:, 1, :, task_rows:] * second_scale[..., :task_rows]
        ).reshape(flat[0], task_rows)
        low = jnp.where(task_of_lane == task, low, 0.0).astype(BF16)
        adapted = jnp.dot(low, adapter_up, preferred_element_type=F32)
        residual = jnp.where(
            own_half == 0, own[:, 0] * first_scale, own[:, 1] * second_scale
        ).reshape(flat)
        base_ref[out_rows, :] = residual + ADAPTER_SCALE * adapted
        return carry

    lax.fori_loop(0, x_ref.shape[0] // step_rows, step, 0)


def expert_layer(gathered, gate_weight, up_weight, params, own, shard_rows, task_rows):
    rows = gathered.shape[0]
    columns = gathered.shape[1] - LANES
    units = gate_weight.shape[1]
    out = jax.ShapeDtypeStruct((rows // HALVES, units), F32)
    vmem = pl.BlockSpec(memory_space=pltpu.VMEM)
    return pl.pallas_call(
        functools.partial(expert_kernel, shard_rows),
        out_shape=(out, out, out),
        in_specs=[pl.BlockSpec(memory_space=pltpu.SMEM), vmem, vmem, vmem, vmem],
        out_specs=(vmem, vmem, vmem),
        scratch_shapes=[
            pltpu.VMEM((columns, 4 * units), BF16),
            pltpu.VMEM((HALVES * task_rows, columns), BF16),
        ],
        compiler_params=pltpu.CompilerParams(vmem_limit_bytes=32 * 2**20),
        cost_estimate=pl.CostEstimate(
            flops=8 * rows * columns * units,
            bytes_accessed=2 * rows * columns + 8 * columns * units,
            transcendentals=2 * rows * units,
        ),
    )(own, gathered, gate_weight, up_weight, params)


def return_kernel(block, capacity, own_ref, h_ref, down_ref, scale_ref, base_ref, out_ref, note_ref):
    seq, rows, units = h_ref.shape
    slots = rows - NOTE_ROWS
    tensor = own_ref[0]
    expert = own_ref[1]
    group = own_ref[2]
    tensors = down_ref.shape[0] // (seq * units)
    cores = HALVES
    pair_rows = cores * capacity
    notes = h_ref[:, pl.ds(slots, NOTE_ROWS), :].astype(F32)
    notes = notes.reshape(seq // cores, cores, NOTE_ROWS, units).sum(axis=1)
    first, second = notes[:, 0, :].astype(jnp.int32), notes[:, 1, :].astype(jnp.int32)
    parts = notes[:, 2:8, :]
    weight = [
        parts[:, k, :] + (parts[:, k + 2, :] + parts[:, k + 4, :] / PART_STEP) / PART_STEP
        for k in range(2)
    ]
    place = positions((first == expert) | (second == expert), block, capacity)
    weight = jnp.where(first == expert, weight[0], weight[1])
    note_ref[...] = h_ref[group * cores, pl.ds(slots, NOTE_ROWS), :].astype(F32) + h_ref[
        group * cores + 1, pl.ds(slots, NOTE_ROWS), :
    ].astype(F32)

    width = 4
    out_ref[...] = jnp.zeros_like(out_ref)

    def step(i, carry):
        lhs = jnp.concatenate(
            [h_ref[i * width + k, pl.ds(0, slots), :] for k in range(width)], axis=1
        )
        rhs = jnp.concatenate(
            [
                down_ref[
                    pl.ds(
                        pl.multiple_of(((i * width + k) * tensors + tensor) * units, units), units
                    ),
                    :,
                ]
                for k in range(width)
            ],
            axis=0,
        )
        out_ref[...] += jnp.dot(lhs, rhs, preferred_element_type=F32)
        return carry

    lax.fori_loop(0, seq // width, step, 0)
    row = lax.broadcasted_iota(jnp.int32, (pair_rows, units), 0).astype(F32)
    for chip in range(seq // cores):
        at = pl.ds(chip * pair_rows, pair_rows)
        slot_weight = jnp.sum(
            jnp.where(place[chip : chip + 1, :] == row, weight[chip : chip + 1, :], 0.0),
            axis=1,
            keepdims=True,
        )
        out_ref[at, :] = slot_weight * (scale_ref[at, :] * out_ref[at, :]) + base_ref[at, :] / (
            2 * tensors
        )


def return_layer(hidden, down_weight, scale, base, own, block, capacity):
    seq, rows, units = hidden.shape
    slots = rows - NOTE_ROWS
    vmem = pl.BlockSpec(memory_space=pltpu.VMEM)
    return pl.pallas_call(
        functools.partial(return_kernel, block, capacity),
        out_shape=(
            jax.ShapeDtypeStruct((slots, units), F32),
            jax.ShapeDtypeStruct((NOTE_ROWS, units), F32),
        ),
        in_specs=[pl.BlockSpec(memory_space=pltpu.SMEM), vmem, vmem, vmem, vmem],
        out_specs=(vmem, vmem),
        compiler_params=pltpu.CompilerParams(vmem_limit_bytes=32 * 2**20),
        cost_estimate=pl.CostEstimate(
            flops=2 * seq * slots * units * units,
            bytes_accessed=2 * seq * slots * units + 2 * down_weight.size,
            transcendentals=0,
        ),
    )(own, hidden, down_weight, scale, base)


def local(
    tokens,
    routes,
    chosen_expert_weight,
    expert_gate_weight,
    expert_up_weight,
    expert_down_weight,
    adapter_down_weight,
    adapter_up_weight,
    document_task_index,
    counts,
    final_norm_scale,
):
    rows, feats = tokens.shape
    seq = lax.axis_size(SEQ)
    experts = lax.axis_size(EXPERT)
    cores = lax.axis_size("c")
    groups = lax.axis_size(GROUP)
    capacity = rows * 5 // 16
    shard_rows = cores * capacity
    width = feats * experts
    half = feats // cores
    columns = experts * half
    slice_width = width // seq
    slots = seq * capacity
    task_rows = adapter_down_weight.shape[0]
    s = lax.axis_index(SEQ)
    g = lax.axis_index(GROUP)
    per_feature_group = feats // slice_width
    own_group = s // per_feature_group
    group_column = (s % per_feature_group) * slice_width

    params = jnp.concatenate(
        [adapter_down_weight, adapter_up_weight]
        + [part[None].astype(BF16) for part in three_parts(final_norm_scale, 1.0)]
    )
    params = jnp.pad(params, ((0, PARAM_ROWS - params.shape[0]), (0, 0)))
    params = lax.all_gather(params, EXPERT, axis=0, tiled=False)

    ids = routes.T
    expert_ids = jnp.arange(experts, dtype=jnp.int32)[:, None]
    place = positions((ids[:1] == expert_ids) | (ids[1:] == expert_ids), rows, capacity)
    chooser = (
        place[:, None, :] == jnp.arange(capacity, dtype=jnp.int32).astype(F32)[None, :, None]
    ).astype(BF16)
    outgoing = jnp.dot(
        chooser.reshape(experts * capacity, rows), tokens, preferred_element_type=F32
    ).astype(BF16)
    outgoing = outgoing.reshape(experts, capacity, cores, half).transpose(0, 2, 1, 3)
    received = swap(outgoing.reshape(experts * cores, capacity, half), EXPERT + ("c",))
    shard = received.reshape(experts, cores, capacity, half).transpose(1, 2, 0, 3)
    shard = shard.reshape(shard_rows, columns).astype(F32)

    largest = jnp.max(jnp.abs(shard), axis=1, keepdims=True)
    exponent = jnp.maximum(
        jnp.floor(jnp.log2(jnp.maximum(largest, 1e-30)) + 1.01), LEAST_EXPONENT
    )
    scaled = (shard * jnp.exp2(15.0 - exponent)).astype(F16)
    sent = jnp.concatenate(
        [scaled, jnp.broadcast_to(exponent, (shard_rows, LANES)).astype(F16)], axis=1
    )
    gathered = lax.all_gather(sent, SEQ, axis=0, tiled=False)
    gathered = gathered.astype(BF16).reshape(seq * shard_rows, columns + LANES)
    per_half = half // slice_width
    own = jnp.stack(
        [
            (s // per_half) % cores,
            own_group * half + (s % per_half) * slice_width,
            own_group,
            group_column,
            document_task_index[0],
        ]
    )
    hidden, return_scale, base = expert_layer(
        gathered,
        expert_gate_weight[0],
        expert_up_weight[0],
        params,
        own,
        shard_rows,
        task_rows,
    )

    notes = jnp.concatenate(
        [ids.astype(F32)] + list(three_parts(chosen_expert_weight.T, PART_STEP))
    )
    core = lax.axis_index("c")
    notes = jnp.concatenate([jnp.where(core == k, notes, 0.0) for k in range(cores)], axis=1)
    notes = jnp.pad(notes, ((0, NOTE_ROWS - notes.shape[0]), (0, 0)))
    hidden = lax.all_gather(
        jnp.concatenate([hidden.astype(F16), notes.astype(F16)]), SEQ, axis=0, tiled=False
    )
    payload, group_notes = return_layer(
        hidden.astype(BF16),
        expert_down_weight[0],
        return_scale,
        base,
        jnp.stack([lax.axis_index("t"), lax.axis_index(EXPERT), g]),
        rows,
        capacity,
    )

    returned = swap(payload.reshape(groups, shard_rows, slice_width), GROUP)
    returned = jnp.sum(returned.reshape(experts, -1, shard_rows, slice_width), axis=1)
    returned = returned.reshape(experts * shard_rows, slice_width)

    group_ids = group_notes[:2].astype(jnp.int32)
    group_place = positions(
        (group_ids[:1] == expert_ids) | (group_ids[1:] == expert_ids), rows, capacity
    )
    group_rows = cores * rows
    combiner = (
        group_place[:, None, :]
        == jnp.arange(shard_rows, dtype=jnp.int32).astype(F32)[None, :, None]
    ).astype(F32)
    mixed = lax.dot_general(
        combiner.reshape(experts * shard_rows, group_rows),
        returned,
        (((0,), (0,)), ((), ())),
        precision=HIGH,
    )
    squares = jnp.sum(spread(jnp.sum(mixed * mixed, axis=1)[None], SEQ), axis=0)
    position = g * group_rows + jnp.arange(group_rows, dtype=jnp.int32)[None, :]
    factor = jnp.where(position < counts[0], lax.rsqrt(squares / width + 1e-05), 0.0)
    norm_scale = lax.dynamic_slice(
        params, (own_group, 2 * task_rows, group_column), (1, 3, slice_width)
    )
    norm_scale = jnp.sum(norm_scale.astype(F32), axis=1)
    pooled = jnp.dot(factor, mixed, precision=HIGH) * norm_scale
    pooled = jnp.sum(spread(pooled, GROUP), axis=0)
    pooled = spread(pooled, SEQ).reshape(1, width)
    return pooled * lax.rsqrt(jnp.mean(pooled * pooled, axis=1, keepdims=True) + 1e-06)


def solution(mesh):
    seq, experts, tensors = mesh.devices.shape
    parts = Mesh(
        mesh.devices.reshape(seq // 2, 2, experts // 2, 2, tensors), ("z", "c", "y", "h", "t")
    )
    return jax.shard_map(
        local,
        mesh=parts,
        in_specs=(
            P(SEQ, EXPERT),
            P(SEQ, None),
            P(SEQ, None),
            P(EXPERT, None, SEQ + ("t",)),
            P(EXPERT, None, SEQ + ("t",)),
            P(EXPERT, None, SEQ),
            P(None, EXPERT),
            P(None, EXPERT),
            P(),
            P(),
            P(EXPERT),
        ),
        out_specs=P(),
        check_vma=False,
    )
```

time: 210 us -> 222 us (1.057)
  between operations: 2.41 us -> 15.6 us
  matrix products: 7.9 us -> 1.25 us
  Pallas kernels: 4.39 us -> 11 us
  starting transfers between devices: 29 us -> 23.6 us
  other arithmetic: 5.65 us -> 8.66 us
  waiting for transfers between devices: 22.5 us -> 25.1 us
    dot_general x7 -> x4, matrix products: 7.73 us -> 1.07 us  [the longest x2 0.44 us: positions(): jnp.dot(named.astype(F32).astype(BF16), earlier_in_block(lanes, block), p...]
    all_to_all x4 -> x3, starting transfers between devices: 29 us -> 23.6 us  [swap(): return lax.all_to_all(x, axes, split_axis=0, concat_axis=0, tiled=True)]
    pallas_call x0 -> x1, Pallas kernels: none -> 4.31 us  [return_layer(): pl.pallas_call(functools.partial(return_kernel, block, capacity), out_sha...]
    all_to_all x4 -> x3, waiting for transfers between devices: 22.5 us -> 25.1 us  [swap(): return lax.all_to_all(x, axes, split_axis=0, concat_axis=0, tiled=True)]
    convert_element_type x1, other arithmetic: 0.96 us -> 3.35 us  [local(): gathered = gathered.astype(BF16).reshape(seq * shard_rows, columns + LANES)]
    pallas_call x1, Pallas kernels: 4.39 us -> 6.64 us  [expert_layer(): pl.pallas_call(functools.partial(expert_kernel, shard_rows), out_shape=(o...]
  transfers between devices with their start and end apart: 4 -> 4, of which waited for: 3 -> 3; matrix products, arithmetic and copies ran while one was open for 3% -> 4% of each run, Pallas kernels for 2% -> 0%
where the time goes in v5:
time: 222 us; the launch traced here: 221 us
  blocking collectives  126 us (57%)
  waiting for transfers between devices  25.1 us (11%)
  starting transfers between devices  23.6 us (11%)
  between operations  15.6 us (7%)
  Pallas kernels  11 us (5%)
  local copies, waits for them, and re-layouts  10 us (5%)
  other arithmetic  8.66 us (4%)
    all_gather x1, blocking collectives, local(): gathered = lax.all_gather(sent, SEQ, axis=0, tiled=False)  54.1 us
    all_gather x1, blocking collectives, local(): lax.all_gather(jnp.concatenate([hidden.astype(F16), notes.astype(F16)]),...  46.1 us
    all_to_all x2, blocking collectives, swap(): return lax.all_to_all(x, axes, split_axis=0, concat_axis=0, tiled=True)  25.8 us
    all_to_all x3, waiting for transfers between devices, swap(): return lax.all_to_all(x, axes, split_axis=0, concat_axis=0, tiled=True)  25.1 us
    all_to_all x3, starting transfers between devices, swap(): return lax.all_to_all(x, axes, split_axis=0, concat_axis=0, tiled=True)  23.6 us
    pallas_call x1, Pallas kernels, expert_layer(): pl.pallas_call(functools.partial(expert_kernel, shard_rows), out_shape=(o...  6.64 us
    unnamed x13, local copies, waits for them, and re-layouts  4.88 us
  transfers between devices with their start and end apart: 4, of which 3 were waited for; matrix products, arithmetic and copies ran while one was open for 4% of the time, Pallas kernels for 0%

profile of v5, /device:TPU:1, one launch (start us, length us, event | category | flops | bytes accessed | tf_op | source)
XLA Modules:
  0.0 221.2 jit_solution(7269713617798697158)
XLA Ops:
  6.5 0.0 copy-start
  6.5 0.0 all-gather.7.cloned.1.call-start
  6.5 0.7 fusion.27
  7.3 1.6 concatenate.17
  8.8 0.7 pad.9
  9.5 0.0 all-gather.7.cloned.1.call-update
  9.6 0.8 slice_bitcast_fusion.3
  10.3 0.2 fusion
  10.6 0.1 eq.121
  10.6 0.0 copy-done
  10.6 0.2 convolution_convert_fusion
  10.9 0.7 copy.46
  11.6 10.2 %all-to-all-start = ((bf16[16,20,256]{2,1,0:T(8,128)(2,1)}), bf16[16,20,256]{2,1,0:T(8,128)(2,1)S(1)}, u32[]{:S(2)}, u32[]{:S(2)}) async-start(bf16[16,20,256]{2,1,0:T(8,128)(2,1)} %bitcast.12), calls=%async_computation | async-start | bytes 393216 | tf_op jit(solution)/shard_map/all_to_all | solution.py:31
  21.8 0.7 bitcast_convert_fusion
  22.5 0.7 bitcast_reduce-precision_fusion
  23.2 0.1 pad_add_fusion.own_ref
  24.0 0.1 stack.35.own_ref
  24.1 0.1 fusion.24
  24.1 5.9 %all-to-all-done = bf16[16,20,256]{2,1,0:T(8,128)(2,1)S(1)} async-done(((bf16[16,20,256]{2,1,0:T(8,128)(2,1)}), bf16[16,20,256]{2,1,0:T(8,128)(2,1)S(1)}, u32[]{:S(2)}, u32[]{:S(2)}) %all-to-all-start) | async-done | bytes 163872 | tf_op jit(solution)/shard_map/all_to_all | solution.py:31
  30.0 0.1 abs_reduce_fusion
  30.2 0.1 copy.43
  30.3 0.1 reshape.146
  30.4 0.2 reshape.147
  30.7 0.1 copy.48
  30.8 0.1 reshape.153
  30.9 0.1 multiply_convert_fusion
  31.0 0.1 broadcast_in_dim.26
  31.1 54.1 %all-gather.8 = f16[1280,2176]{1,0:T(8,128)(2,1)S(1)} all-gather(f16[40,2176]{1,0:T(8,128)(2,1)S(1)} %pad_maximum_fusion), channel_id=2, replica_groups=mesh['z'=16,'c'=2,'y'=4,'h'=2,'t'=2] {'z','c'}, dimensions={0}, use_global_device_ids=true | all-gather | bytes 5744640 | tf_op jit(solution)/shard_map/all_gather | solution.py:308
  85.2 0.0 copy-start.4
  85.2 0.0 copy-start.5
  85.2 3.3 %convert_element_type.150.x_ref = bf16[1280,2176]{1,0:T(8,128)(2,1)} convert(f16[1280,2176]{1,0:T(8,128)(2,1)S(1)} %all-gather.8) | non-fusion elementwise | flops 2785280 | bytes 11141120 | tf_op jit(solution)/shard_map/convert_element_type | solution.py:309
  88.6 0.0 all-gather.7.cloned.1.call-done
  88.6 0.0 copy-done.4
  88.6 0.0 copy-done.5
  88.6 0.0 copy-start.1
  88.6 2.6 %copy-done.1 = bf16[1280,2176]{1,0:T(8,128)(2,1)S(1)} copy-done((bf16[1280,2176]{1,0:T(8,128)(2,1)S(1)}, bf16[1280,2176]{1,0:T(8,128)(2,1)}, u32[]{:S(2)}) %copy-start.1) | copy-done | bytes 5570584
  91.2 0.0 copy-start.3
  91.2 1.2 copy-done.3
  92.4 6.6 %shard_map.109 = (f32[640,128]{1,0:T(8,128)S(1)}, f32[640,128]{1,0:T(8,128)S(1)}, f32[640,128]{1,0:T(8,128)S(1)}) custom-call(s32[5]{0:T(128)S(1)} %stack.35.own_ref, bf16[1280,2176]{1,0:T(8,128)(2,1)S(1)} %copy-done.1, bf16[4096,128]{1,0:T(8,128)(2,1)S(1)} %bitcast.70, bf16[4096,128]{1,0:T(8,128)(2,1)S(1)} %bitcast.71, bf16[8,128,512]{2,1,0:T(8,128)(2,1)S(1)} %bitcast.69), custom_call_target="tpu_custom_call" | custom-call | flops 2684354560 | bytes 7340032 | tf_op jit(solution)/shard_map/pallas_call | solution.py:149
  99.1 0.1 pad_maximum_fusion.1
  99.1 46.1 %all-gather.9 = f16[20992,128]{1,0:T(8,128)(2,1)S(1)} all-gather(f16[656,128]{1,0:T(8,128)(2,1)S(1)} %pad_maximum_fusion.1), channel_id=4, replica_groups=mesh['z'=16,'c'=2,'y'=4,'h'=2,'t'=2] {'z','c'}, dimensions={0}, use_global_device_ids=true | all-gather | bytes 5541888 | tf_op jit(solution)/shard_map/all_gather | solution.py:336
  145.2 0.0 copy-start.2
  145.2 0.6 convert_element_type.151
  145.8 1.0 copy-done.2
  146.8 4.3 %shard_map.110 = (f32[640,128]{1,0:T(8,128)}, f32[16,128]{1,0:T(8,128)S(1)}) custom-call(s32[3]{0:T(128)S(1)} %pad_add_fusion.own_ref, bf16[32,656,128]{2,1,0:T(8,128)(2,1)S(1)} %bitcast.66, bf16[8192,128]{1,0:T(8,128)(2,1)S(1)} %bitcast.67, f32[640,128]{1,0:T(8,128)S(1)} %get-tuple-element.11.scale_ref, f32[640,128]{1,0:T(8,128)S(1)} %get-tuple-element.12.base_ref), custom_call_target="tpu_custom_call" | custom-call | flops 671088640 | bytes 7340032 | tf_op jit(solution)/shard_map/pallas_call | solution.py:230
  151.1 3.5 %all-to-all-start.1 = ((f32[16,40,128]{2,1,0:T(8,128)}), f32[16,40,128]{2,1,0:T(8,128)S(1)}, u32[]{:S(2)}, u32[]{:S(2)}) async-start(f32[16,40,128]{2,1,0:T(8,128)} %bitcast.23), calls=%async_computation.1 | async-start | bytes 655360 | tf_op jit(solution)/shard_map/all_to_all | solution.py:31
  154.7 0.2 fusion.1
  154.9 8.8 %all-to-all-done.1 = f32[16,40,128]{2,1,0:T(8,128)S(1)} async-done(((f32[16,40,128]{2,1,0:T(8,128)}), f32[16,40,128]{2,1,0:T(8,128)S(1)}, u32[]{:S(2)}, u32[]{:S(2)}) %all-to-all-start.1) | async-done | bytes 327712 | tf_op jit(solution)/shard_map/all_to_all | solution.py:31
  163.7 0.4 multiply_reduce_fusion
  164.1 0.6 broadcast_in_dim.29
  164.7 9.9 %all-to-all-start.2 = ((f32[32,1,128]{2,1,0:T(1,128)}), f32[32,1,128]{2,1,0:T(1,128)S(1)}, u32[]{:S(2)}, u32[]{:S(2)}) async-start(f32[32,1,128]{2,1,0:T(1,128)} %broadcast_in_dim.29), calls=%async_computation.2 | async-start | bytes 32768 | tf_op jit(solution)/shard_map/all_to_all | solution.py:31
  175.3 0.7 convert_reduce_fusion
  175.9 10.4 %all-to-all-done.2 = f32[32,1,128]{2,1,0:T(1,128)S(1)} async-done(((f32[32,1,128]{2,1,0:T(1,128)}), f32[32,1,128]{2,1,0:T(1,128)S(1)}, u32[]{:S(2)}, u32[]{:S(2)}) %all-to-all-start.2) | async-done | bytes 16416 | tf_op jit(solution)/shard_map/all_to_all | solution.py:31
  186.4 0.2 fusion.2
  186.5 0.1 broadcast_in_dim.31
  186.6 9.0 %all_to_all.25 = f32[16,1,128]{2,1,0:T(1,128)S(1)} all-to-all(f32[16,1,128]{2,1,0:T(1,128)S(1)} %broadcast_in_dim.31), channel_id=1, replica_groups=mesh['z'=16,'c'=2,'y'=4,'h'=2,'t'=2] {'y','h','t'}, dimensions={0} | all-to-all | bytes 16384 | tf_op jit(solution)/shard_map/all_to_all | solution.py:31
  195.6 16.8 %all_to_all.26 = f32[32,1,128]{2,1,0:T(1,128)S(1)} all-to-all(f32[32,1,128]{2,1,0:T(1,128)S(1)} %broadcast_in_dim.32), channel_id=1, replica_groups=mesh['z'=16,'c'=2,'y'=4,'h'=2,'t'=2] {'z','c'}, dimensions={0} | all-to-all | bytes 32768 | tf_op jit(solution)/shard_map/all_to_all | solution.py:31
  212.4 0.6 multiply_reduce_fusion.1
  213.8 0.6 multiply_bitcast_fusion
  (26 shorter events, 0.4 us)
Async XLA Ops:
  6.5 4.1 %copy-start = (bf16[64,512]{1,0:T(8,128)(2,1)S(1)}, bf16[64,512]{1,0:T(8,128)(2,1)}, u32[]{:S(2)}) copy-start(bf16[64,512]{1,0:T(8,128)(2,1)} %param.11) | copy-start | bytes 196612
  6.5 82.0 %all-gather.7.cloned.1.call-start = ((), (), s32[]{:S(2)}) async-start(), calls=%async_computation.5 | async-start | bytes 1179648 | tf_op jit(solution)/shard_map/all_gather | solution.py:284
  11.6 18.4 %all-to-all-start = ((bf16[16,20,256]{2,1,0:T(8,128)(2,1)}), bf16[16,20,256]{2,1,0:T(8,128)(2,1)S(1)}, u32[]{:S(2)}, u32[]{:S(2)}) async-start(bf16[16,20,256]{2,1,0:T(8,128)(2,1)} %bitcast.12), calls=%async_computation | async-start | bytes 393216 | tf_op jit(solution)/shard_map/all_to_all | solution.py:31
  85.2 3.4 %copy-start.4 = (bf16[1,4096,128]{2,1,0:T(8,128)(2,1)S(1)}, bf16[1,4096,128]{2,1,0:T(8,128)(2,1)}, u32[]{:S(2)}) copy-start(bf16[1,4096,128]{2,1,0:T(8,128)(2,1)} %param.14) | copy-start | bytes 3145732
  85.2 3.4 %copy-start.5 = (bf16[1,4096,128]{2,1,0:T(8,128)(2,1)S(1)}, bf16[1,4096,128]{2,1,0:T(8,128)(2,1)}, u32[]{:S(2)}) copy-start(bf16[1,4096,128]{2,1,0:T(8,128)(2,1)} %param.15) | copy-start | bytes 3145732
  88.6 2.6 %copy-start.1 = (bf16[1280,2176]{1,0:T(8,128)(2,1)S(1)}, bf16[1280,2176]{1,0:T(8,128)(2,1)}, u32[]{:S(2)}) copy-start(bf16[1280,2176]{1,0:T(8,128)(2,1)} %convert_element_type.150.x_ref) | copy-start | bytes 16711684
  91.2 1.2 copy-start.3
  145.2 1.6 copy-start.2
  151.1 12.6 %all-to-all-start.1 = ((f32[16,40,128]{2,1,0:T(8,128)}), f32[16,40,128]{2,1,0:T(8,128)S(1)}, u32[]{:S(2)}, u32[]{:S(2)}) async-start(f32[16,40,128]{2,1,0:T(8,128)} %bitcast.23), calls=%async_computation.1 | async-start | bytes 655360 | tf_op jit(solution)/shard_map/all_to_all | solution.py:31
  164.7 21.6 %all-to-all-start.2 = ((f32[32,1,128]{2,1,0:T(1,128)}), f32[32,1,128]{2,1,0:T(1,128)S(1)}, u32[]{:S(2)}, u32[]{:S(2)}) async-start(f32[32,1,128]{2,1,0:T(1,128)} %broadcast_in_dim.29), calls=%async_computation.2 | async-start | bytes 32768 | tf_op jit(solution)/shard_map/all_to_all | solution.py:31
Sparse Core Ops, SparseCore 0:
  10.6 65.7 all-gather.6

commit v6 on v5

--- a/solution.py
+++ b/solution.py
@@ -24,7 +24,7 @@
 LEAST_EXPONENT = -40.0
 NOTE_ROWS = 16
 PART_STEP = 256.0
-PARAM_ROWS = 128
+LOW_LANES = 32
 
 
 def swap(x, axes):
@@ -59,43 +59,105 @@
     return jnp.where(named, before + first, -1.0)
 
 
+def dispatch_kernel(
+    capacity, own_ref, routes_ref, tokens_ref, down_ref, up_ref, norm_ref, out_ref
+):
+    targets, _, out_lanes = out_ref.shape
+    experts = targets // HALVES
+    rows, feats = tokens_ref.shape
+    half = feats // HALVES
+    ranks = down_ref.shape[0] // HALVES
+    core = own_ref[0]
+    ids = routes_ref[...]
+    expert = lax.broadcasted_iota(jnp.int32, (experts, rows), 0)
+    place = positions((ids[:1] == expert) | (ids[1:] == expert), rows, capacity)
+    padded = -(-capacity // 16) * 16
+    slot = lax.broadcasted_iota(jnp.int32, (padded, rows), 0).astype(F32)
+    chooser = jnp.concatenate(
+        [(place[e : e + 1] == slot).astype(F32) for e in range(experts)], axis=0
+    ).astype(BF16)
+    for c in range(HALVES):
+        lanes = pl.ds(c * half, half)
+        x = tokens_ref[:, lanes]
+        low = lax.dot_general(
+            x, down_ref[:, lanes], (((1,), (1,)), ((), ())), preferred_element_type=F32
+        )
+        first = low.astype(BF16)
+        rest = low - first.astype(F32)
+        second = rest.astype(BF16)
+        third = (rest - second.astype(F32)).astype(BF16)
+        x = jnp.concatenate([x, jnp.zeros_like(first), first, second, third], axis=1)
+        chosen = jnp.dot(chooser, x, preferred_element_type=F32).astype(BF16).astype(F32)
+        column = pl.multiple_of(own_ref[1 + c], LANES)
+        norm = norm_ref[:, pl.ds(column, LANES)]
+        norm_first = norm.astype(BF16).astype(F32)
+        norm_rest = norm - norm_first
+        norm_second = norm_rest.astype(BF16).astype(F32)
+        up_rows = up_ref[pl.ds(pl.multiple_of(core * ranks, ranks), ranks), pl.ds(column, LANES)]
+        small = jnp.concatenate(
+            [
+                up_rows.astype(F32),
+                norm_first,
+                norm_second,
+                norm_rest - norm_second,
+                jnp.zeros((capacity - ranks - 3, LANES), F32),
+            ],
+            axis=0,
+        ).astype(BF16)
+        for e in range(experts):
+            out_ref[e * HALVES + c, :, pl.ds(0, out_lanes - LANES)] = chosen[
+                e * padded : e * padded + capacity
+            ].astype(BF16)
+            out_ref[e * HALVES + c, :, pl.ds(out_lanes - LANES, LANES)] = small
+
+
+def dispatch_layer(own, routes, tokens, adapter_down, adapter_up, norm_scale, experts, capacity):
+    rows, feats = tokens.shape
+    vmem = pl.BlockSpec(memory_space=pltpu.VMEM)
+    lanes = feats // HALVES + 2 * LANES
+    return pl.pallas_call(
+        functools.partial(dispatch_kernel, capacity),
+        out_shape=jax.ShapeDtypeStruct((experts * HALVES, capacity, lanes), BF16),
+        in_specs=[pl.BlockSpec(memory_space=pltpu.SMEM)] + [vmem] * 5,
+        out_specs=vmem,
+        compiler_params=pltpu.CompilerParams(vmem_limit_bytes=16 * 2**20),
+        cost_estimate=pl.CostEstimate(
+            flops=4 * rows * feats * experts * capacity,
+            bytes_accessed=2 * rows * feats + 2 * experts * HALVES * capacity * lanes,
+            transcendentals=0,
+        ),
+    )(own, routes, tokens, adapter_down, adapter_up, norm_scale)
+
+
 def expert_kernel(
     shard_rows,
     own_ref,
     x_ref,
     gate_ref,
     up_ref,
-    params_ref,
+    adapter_ref,
     hidden_ref,
     scale_ref,
     base_ref,
     weight_ref,
-    adapter_ref,
 ):
     columns = weight_ref.shape[0]
     units = gate_ref.shape[1]
-    task_rows = adapter_ref.shape[0] // HALVES
-    groups = params_ref.shape[0]
-    half = columns // groups
-    for block in range(groups):
+    task_rows = adapter_ref.shape[0]
+    half = 2 * LANES
+    for block in range(columns // half):
         target = pl.ds(block * half, half)
         for c in range(HALVES):
             source = pl.ds((block * HALVES + c) * half, half)
             weight_ref[target, pl.ds(c * 2 * units, units)] = gate_ref[source, :]
             weight_ref[target, pl.ds((c * 2 + 1) * units, units)] = up_ref[source, :]
-            adapter_ref[pl.ds(c * task_rows, task_rows), target] = params_ref[
-                block, pl.ds(0, task_rows), pl.ds(c * half, half)
-            ]
     chips = 4
     step_rows = chips * HALVES * shard_rows
     shape = (chips, HALVES, shard_rows, units)
     flat = (chips * shard_rows, units)
     own_half = own_ref[0]
     own_column = pl.multiple_of(own_ref[1], LANES)
-    own_group = own_ref[2]
-    group_column = pl.multiple_of(own_ref[3], LANES)
-    task = own_ref[4]
-    adapter_up = params_ref[own_group, pl.ds(task_rows, task_rows), pl.ds(group_column, units)]
+    task = own_ref[2]
     task_of_lane = lax.broadcasted_iota(
         jnp.int32, (flat[0], task_rows), 1
     ) // (task_rows // TASK_COUNT)
@@ -106,10 +168,14 @@
         x = x_ref[rows, pl.ds(0, columns)]
         acts = jnp.dot(x, weight_ref[...], preferred_element_type=F32)
         acts = acts.reshape(chips, HALVES, shard_rows, 4 * units)
-        low = lax.dot_general(
-            x, adapter_ref[...], (((1,), (1,)), ((), ())), preferred_element_type=F32
-        ).reshape(chips, HALVES, shard_rows, HALVES * task_rows)
-        exponents = x_ref[rows, pl.ds(columns, LANES)].astype(F32).reshape(shape)
+        beside = x_ref[rows, pl.ds(columns, LANES)].astype(F32)
+        exponent = beside[:, :LOW_LANES]
+        low = beside[:, LOW_LANES : 2 * LOW_LANES] + (
+            beside[:, 2 * LOW_LANES : 3 * LOW_LANES]
+            + beside[:, 3 * LOW_LANES :] / PART_STEP
+        ) / PART_STEP
+        low = (low * jnp.exp2(exponent - 7.0)).reshape(chips, HALVES, shard_rows, LOW_LANES)
+        exponents = jnp.concatenate([exponent] * (LANES // LOW_LANES), axis=1).reshape(shape)
         own = x_ref[rows, pl.ds(own_column, LANES)].astype(F32).reshape(shape)
         first, second = exponents[:, 0], exponents[:, 1]
         first_scale, second_scale = jnp.exp2(first - 15.0), jnp.exp2(second - 15.0)
@@ -125,12 +191,9 @@
         row_exponent = jnp.maximum(first, second)
         hidden_ref[out_rows, :] = (hidden * jnp.exp2(-2.0 * row_exponent - 2.0)).reshape(flat)
         scale_ref[out_rows, :] = jnp.exp2(2.0 * row_exponent + 2.0).reshape(flat)
-        low = (
-            low[:, 0, :, :task_rows] * first_scale[..., :task_rows]
-            + low[:, 1, :, task_rows:] * second_scale[..., :task_rows]
-        ).reshape(flat[0], task_rows)
+        low = (low[:, 0] + low[:, 1]).reshape(flat[0], LOW_LANES)
         low = jnp.where(task_of_lane == task, low, 0.0).astype(BF16)
-        adapted = jnp.dot(low, adapter_up, preferred_element_type=F32)
+        adapted = jnp.dot(low, adapter_ref[...], preferred_element_type=F32)
         residual = jnp.where(
             own_half == 0, own[:, 0] * first_scale, own[:, 1] * second_scale
         ).reshape(flat)
@@ -140,7 +203,7 @@
     lax.fori_loop(0, x_ref.shape[0] // step_rows, step, 0)
 
 
-def expert_layer(gathered, gate_weight, up_weight, params, own, shard_rows, task_rows):
+def expert_layer(gathered, gate_weight, up_weight, adapter_up, own, shard_rows):
     rows = gathered.shape[0]
     columns = gathered.shape[1] - LANES
     units = gate_weight.shape[1]
@@ -151,20 +214,28 @@
         out_shape=(out, out, out),
         in_specs=[pl.BlockSpec(memory_space=pltpu.SMEM), vmem, vmem, vmem, vmem],
         out_specs=(vmem, vmem, vmem),
-        scratch_shapes=[
-            pltpu.VMEM((columns, 4 * units), BF16),
-            pltpu.VMEM((HALVES * task_rows, columns), BF16),
-        ],
-        compiler_params=pltpu.CompilerParams(vmem_limit_bytes=32 * 2**20),
+        scratch_shapes=[pltpu.VMEM((columns, 4 * units), BF16)],
+        compiler_params=pltpu.CompilerParams(vmem_limit_bytes=24 * 2**20),
         cost_estimate=pl.CostEstimate(
             flops=8 * rows * columns * units,
             bytes_accessed=2 * rows * columns + 8 * columns * units,
             transcendentals=2 * rows * units,
         ),
-    )(own, gathered, gate_weight, up_weight, params)
-
-
-def return_kernel(block, capacity, own_ref, h_ref, down_ref, scale_ref, base_ref, out_ref, note_ref):
+    )(own, gathered, gate_weight, up_weight, adapter_up)
+
+
+def return_kernel(
+    block,
+    capacity,
+    own_ref,
+    h_ref,
+    down_ref,
+    scale_ref,
+    base_ref,
+    out_ref,
+    note_ref,
+    weight_ref,
+):
     seq, rows, units = h_ref.shape
     slots = rows - NOTE_ROWS
     tensor = own_ref[0]
@@ -187,29 +258,18 @@
         group * cores + 1, pl.ds(slots, NOTE_ROWS), :
     ].astype(F32)
 
-    width = 4
-    out_ref[...] = jnp.zeros_like(out_ref)
+    for k in range(seq):
+        source = pl.multiple_of((k * tensors + tensor) * units, units)
+        weight_ref[pl.ds(k * units, units), :] = down_ref[pl.ds(source, units), :]
+    step_rows = slots // 2
 
     def step(i, carry):
-        lhs = jnp.concatenate(
-            [h_ref[i * width + k, pl.ds(0, slots), :] for k in range(width)], axis=1
-        )
-        rhs = jnp.concatenate(
-            [
-                down_ref[
-                    pl.ds(
-                        pl.multiple_of(((i * width + k) * tensors + tensor) * units, units), units
-                    ),
-                    :,
-                ]
-                for k in range(width)
-            ],
-            axis=0,
-        )
-        out_ref[...] += jnp.dot(lhs, rhs, preferred_element_type=F32)
+        at = pl.ds(pl.multiple_of(i * step_rows, step_rows), step_rows)
+        lhs = jnp.concatenate([h_ref[k, at, :] for k in range(seq)], axis=1)
+        out_ref[at, :] = jnp.dot(lhs, weight_ref[...], preferred_element_type=F32)
         return carry
 
-    lax.fori_loop(0, seq // width, step, 0)
+    lax.fori_loop(0, slots // step_rows, step, 0)
     row = lax.broadcasted_iota(jnp.int32, (pair_rows, units), 0).astype(F32)
     for chip in range(seq // cores):
         at = pl.ds(chip * pair_rows, pair_rows)
@@ -235,7 +295,8 @@
         ),
         in_specs=[pl.BlockSpec(memory_space=pltpu.SMEM), vmem, vmem, vmem, vmem],
         out_specs=(vmem, vmem),
-        compiler_params=pltpu.CompilerParams(vmem_limit_bytes=32 * 2**20),
+        scratch_shapes=[pltpu.VMEM((seq * units, units), BF16)],
+        compiler_params=pltpu.CompilerParams(vmem_limit_bytes=24 * 2**20),
         cost_estimate=pl.CostEstimate(
             flops=2 * seq * slots * units * units,
             bytes_accessed=2 * seq * slots * units + 2 * down_weight.size,
@@ -274,28 +335,32 @@
     g = lax.axis_index(GROUP)
     per_feature_group = feats // slice_width
     own_group = s // per_feature_group
-    group_column = (s % per_feature_group) * slice_width
-
-    params = jnp.concatenate(
-        [adapter_down_weight, adapter_up_weight]
-        + [part[None].astype(BF16) for part in three_parts(final_norm_scale, 1.0)]
-    )
-    params = jnp.pad(params, ((0, PARAM_ROWS - params.shape[0]), (0, 0)))
-    params = lax.all_gather(params, EXPERT, axis=0, tiled=False)
-
+
+    core = lax.axis_index("c")
     ids = routes.T
-    expert_ids = jnp.arange(experts, dtype=jnp.int32)[:, None]
-    place = positions((ids[:1] == expert_ids) | (ids[1:] == expert_ids), rows, capacity)
-    chooser = (
-        place[:, None, :] == jnp.arange(capacity, dtype=jnp.int32).astype(F32)[None, :, None]
-    ).astype(BF16)
-    outgoing = jnp.dot(
-        chooser.reshape(experts * capacity, rows), tokens, preferred_element_type=F32
-    ).astype(BF16)
-    outgoing = outgoing.reshape(experts, capacity, cores, half).transpose(0, 2, 1, 3)
-    received = swap(outgoing.reshape(experts * cores, capacity, half), EXPERT + ("c",))
-    shard = received.reshape(experts, cores, capacity, half).transpose(1, 2, 0, 3)
+    outgoing = dispatch_layer(
+        jnp.stack(
+            [core] + [(s - core + k) % per_feature_group * slice_width for k in range(cores)]
+        ),
+        ids,
+        tokens,
+        adapter_down_weight,
+        adapter_up_weight,
+        final_norm_scale[None],
+        experts,
+        capacity,
+    )
+    received = swap(outgoing, EXPERT + ("c",)).reshape(experts, cores, capacity, -1)
+    shard = received[..., :half].transpose(1, 2, 0, 3)
     shard = shard.reshape(shard_rows, columns).astype(F32)
+    low = jnp.sum(received[..., half + LOW_LANES : half + LANES].astype(F32), axis=0)
+    low = low.reshape(shard_rows, 3, LOW_LANES).sum(axis=1)
+    small = lax.dynamic_index_in_dim(received, own_group, axis=0, keepdims=False)
+    small = small[..., half + LANES :]
+    adapter_up = small[:, : task_rows // cores].reshape(task_rows, slice_width)
+    norm_scale = jnp.sum(
+        small[:1, task_rows // cores : task_rows // cores + 3].astype(F32), axis=1
+    )
 
     largest = jnp.max(jnp.abs(shard), axis=1, keepdims=True)
     exponent = jnp.maximum(
@@ -303,7 +368,9 @@
     )
     scaled = (shard * jnp.exp2(15.0 - exponent)).astype(F16)
     sent = jnp.concatenate(
-        [scaled, jnp.broadcast_to(exponent, (shard_rows, LANES)).astype(F16)], axis=1
+        [scaled, jnp.broadcast_to(exponent, (shard_rows, LOW_LANES)).astype(F16)]
+        + [part.astype(F16) for part in three_parts(low * jnp.exp2(7.0 - exponent), PART_STEP)],
+        axis=1,
     )
     gathered = lax.all_gather(sent, SEQ, axis=0, tiled=False)
     gathered = gathered.astype(BF16).reshape(seq * shard_rows, columns + LANES)
@@ -312,8 +379,6 @@
         [
             (s // per_half) % cores,
             own_group * half + (s % per_half) * slice_width,
-            own_group,
-            group_column,
             document_task_index[0],
         ]
     )
@@ -321,16 +386,14 @@
         gathered,
         expert_gate_weight[0],
         expert_up_weight[0],
-        params,
+        adapter_up,
         own,
         shard_rows,
-        task_rows,
     )
 
     notes = jnp.concatenate(
         [ids.astype(F32)] + list(three_parts(chosen_expert_weight.T, PART_STEP))
     )
-    core = lax.axis_index("c")
     notes = jnp.concatenate([jnp.where(core == k, notes, 0.0) for k in range(cores)], axis=1)
     notes = jnp.pad(notes, ((0, NOTE_ROWS - notes.shape[0]), (0, 0)))
     hidden = lax.all_gather(
@@ -350,6 +413,7 @@
     returned = jnp.sum(returned.reshape(experts, -1, shard_rows, slice_width), axis=1)
     returned = returned.reshape(experts * shard_rows, slice_width)
 
+    expert_ids = jnp.arange(experts, dtype=jnp.int32)[:, None]
     group_ids = group_notes[:2].astype(jnp.int32)
     group_place = positions(
         (group_ids[:1] == expert_ids) | (group_ids[1:] == expert_ids), rows, capacity
@@ -368,10 +432,6 @@
     squares = jnp.sum(spread(jnp.sum(mixed * mixed, axis=1)[None], SEQ), axis=0)
     position = g * group_rows + jnp.arange(group_rows, dtype=jnp.int32)[None, :]
     factor = jnp.where(position < counts[0], lax.rsqrt(squares / width + 1e-05), 0.0)
-    norm_scale = lax.dynamic_slice(
-        params, (own_group, 2 * task_rows, group_column), (1, 3, slice_width)
-    )
-    norm_scale = jnp.sum(norm_scale.astype(F32), axis=1)
     pooled = jnp.dot(factor, mixed, precision=HIGH) * norm_scale
     pooled = jnp.sum(spread(pooled, GROUP), axis=0)
     pooled = spread(pooled, SEQ).reshape(1, width)

time: 222 us -> 202 us (0.910)
  between operations: 15.6 us -> 2.24 us
  local copies, waits for them, and re-layouts: 10 us -> 6.6 us
  other arithmetic: 8.66 us -> 5.34 us
  waiting for transfers between devices: 25.1 us -> 27.5 us
    convert_element_type x1, other arithmetic: 3.35 us -> 0.96 us  [local(): gathered = gathered.astype(BF16).reshape(seq * shard_rows, columns + LANES)]
    all_to_all x3, waiting for transfers between devices: 25.1 us -> 27.5 us  [swap(): return lax.all_to_all(x, axes, split_axis=0, concat_axis=0, tiled=True)]
    unnamed x13 -> x17, local copies, waits for them, and re-layouts: 4.88 us -> 5.34 us
  transfers between devices with their start and end apart: 4 -> 3, of which waited for: 3 -> 3; matrix products, arithmetic and copies ran while one was open for 4% -> 1% of each run, Pallas kernels for 0% -> 0%
where the time goes in v6:
time: 202 us; the launch traced here: 201 us
  blocking collectives  127 us (63%)
  waiting for transfers between devices  27.5 us (14%)
  starting transfers between devices  22.3 us (11%)
  Pallas kernels  9.56 us (5%)
  local copies, waits for them, and re-layouts  6.6 us (3%)
  other arithmetic  5.34 us (3%)
  between operations  2.24 us (1%)
    all_gather x1, blocking collectives, local(): gathered = lax.all_gather(sent, SEQ, axis=0, tiled=False)  53.7 us
    all_gather x1, blocking collectives, local(): lax.all_gather(jnp.concatenate([hidden.astype(F16), notes.astype(F16)]),...  47.5 us
    all_to_all x3, waiting for transfers between devices, swap(): return lax.all_to_all(x, axes, split_axis=0, concat_axis=0, tiled=True)  27.5 us
    all_to_all x2, blocking collectives, swap(): return lax.all_to_all(x, axes, split_axis=0, concat_axis=0, tiled=True)  25.8 us
    all_to_all x3, starting transfers between devices, swap(): return lax.all_to_all(x, axes, split_axis=0, concat_axis=0, tiled=True)  22.3 us
    unnamed x17, local copies, waits for them, and re-layouts  5.34 us
    pallas_call x1, Pallas kernels, expert_layer(): pl.pallas_call(functools.partial(expert_kernel, shard_rows), out_shape=(o...  4.44 us
  transfers between devices with their start and end apart: 3, of which 3 were waited for; matrix products, arithmetic and copies ran while one was open for 1% of the time, Pallas kernels for 0%

profile of v6, /device:TPU:1, one launch (start us, length us, event | category | flops | bytes accessed | tf_op | source)
XLA Modules:
  0.0 201.3 jit_solution(10430720697285159794)
XLA Ops:
  0.0 0.1 pad_add_fusion.2.own_ref
  0.1 0.0 copy-start.1
  0.1 0.8 copy-done.1
  0.9 0.0 copy-start.2
  0.9 0.8 copy-done.2
  1.7 0.0 copy-start.3
  1.7 0.8 copy-done.3
  2.4 0.0 copy-start.4
  2.4 0.7 copy-done.4
  3.1 0.0 copy-start.5
  3.1 0.7 copy-done.5
  3.8 1.9 shard_map.109
  5.7 10.2 %all-to-all-start = ((bf16[16,20,512]{2,1,0:T(8,128)(2,1)}), bf16[16,20,512]{2,1,0:T(8,128)(2,1)S(1)}, u32[]{:S(2)}, u32[]{:S(2)}) async-start(bf16[16,20,512]{2,1,0:T(8,128)(2,1)} %shard_map.109), calls=%async_computation | async-start | bytes 786432 | tf_op jit(solution)/shard_map/all_to_all | solution.py:31
  15.9 0.7 bitcast_convert_fusion
  16.6 0.7 bitcast_reduce-precision_fusion
  18.6 0.1 pad_add_fusion.own_ref
  18.7 0.1 pad_add_fusion.1.own_ref
  18.8 0.1 fusion.17
  18.9 7.0 %all-to-all-done = bf16[16,20,512]{2,1,0:T(8,128)(2,1)S(1)} async-done(((bf16[16,20,512]{2,1,0:T(8,128)(2,1)}), bf16[16,20,512]{2,1,0:T(8,128)(2,1)S(1)}, u32[]{:S(2)}, u32[]{:S(2)}) %all-to-all-start) | async-done | bytes 327712 | tf_op jit(solution)/shard_map/all_to_all | solution.py:31
  25.9 0.1 copy_convert_fusion
  25.9 0.2 abs_reduce_fusion
  26.2 0.1 convert_reduce_fusion
  26.3 0.1 copy.20
  26.4 0.1 reshape.152
  26.5 0.1 reshape.143
  26.6 0.1 reshape.132
  26.7 0.1 reshape.153
  26.8 0.1 multiply_convert_fusion
  26.9 0.1 reduce_sum.73
  27.0 0.1 fusion.14
  27.0 0.1 broadcast_in_dim.24
  27.1 0.1 concatenate.13
  27.2 53.7 %all-gather.4 = f16[1280,2176]{1,0:T(8,128)(2,1)S(1)} all-gather(f16[40,2176]{1,0:T(8,128)(2,1)S(1)} %concatenate.13), channel_id=2, replica_groups=mesh['z'=16,'c'=2,'y'=4,'h'=2,'t'=2] {'z','c'}, dimensions={0}, use_global_device_ids=true | all-gather | bytes 5744640 | tf_op jit(solution)/shard_map/all_gather | solution.py:375
  80.9 0.0 copy-start.6
  80.9 0.0 copy-start.7
  80.9 1.0 convert_element_type.101.x_ref
  81.9 0.2 copy-done.6
  82.1 0.3 copy-done.7
  82.5 4.4 %shard_map.110 = (f32[640,128]{1,0:T(8,128)S(1)}, f32[640,128]{1,0:T(8,128)S(1)}, f32[640,128]{1,0:T(8,128)S(1)}) custom-call(s32[3]{0:T(128)S(1)} %pad_add_fusion.1.own_ref, bf16[1280,2176]{1,0:T(8,128)(2,1)S(1)} %convert_element_type.101.x_ref, bf16[4096,128]{1,0:T(8,128)(2,1)S(1)} %bitcast.65, bf16[4096,128]{1,0:T(8,128)(2,1)S(1)} %bitcast.66, ...), custom_call_target="tpu_custom_call" | custom-call | flops 2684354560 | bytes 7340032 | tf_op jit(solution)/shard_map/pallas_call | solution.py:212
  86.9 0.1 pad_maximum_fusion
  87.0 47.5 %all-gather.5 = f16[20992,128]{1,0:T(8,128)(2,1)S(1)} all-gather(f16[656,128]{1,0:T(8,128)(2,1)S(1)} %pad_maximum_fusion), channel_id=3, replica_groups=mesh['z'=16,'c'=2,'y'=4,'h'=2,'t'=2] {'z','c'}, dimensions={0}, use_global_device_ids=true | all-gather | bytes 5541888 | tf_op jit(solution)/shard_map/all_gather | solution.py:399
  134.5 0.0 copy-start
  134.5 0.6 convert_element_type.102
  135.1 1.0 copy-done
  136.1 3.2 %shard_map.111 = (f32[640,128]{1,0:T(8,128)}, f32[16,128]{1,0:T(8,128)S(1)}) custom-call(s32[3]{0:T(128)S(1)} %pad_add_fusion.own_ref, bf16[32,656,128]{2,1,0:T(8,128)(2,1)S(1)} %bitcast.60, bf16[8192,128]{1,0:T(8,128)(2,1)S(1)} %bitcast.61, f32[640,128]{1,0:T(8,128)S(1)} %get-tuple-element.11.scale_ref, f32[640,128]{1,0:T(8,128)S(1)} %get-tuple-element.12.base_ref), custom_call_target="tpu_custom_call" | custom-call | flops 671088640 | bytes 7340032 | tf_op jit(solution)/shard_map/pallas_call | solution.py:290
  139.3 3.5 %all-to-all-start.1 = ((f32[16,40,128]{2,1,0:T(8,128)}), f32[16,40,128]{2,1,0:T(8,128)S(1)}, u32[]{:S(2)}, u32[]{:S(2)}) async-start(f32[16,40,128]{2,1,0:T(8,128)} %bitcast.22), calls=%async_computation.1 | async-start | bytes 655360 | tf_op jit(solution)/shard_map/all_to_all | solution.py:31
  142.9 0.2 fusion
  143.1 8.8 %all-to-all-done.1 = f32[16,40,128]{2,1,0:T(8,128)S(1)} async-done(((f32[16,40,128]{2,1,0:T(8,128)}), f32[16,40,128]{2,1,0:T(8,128)S(1)}, u32[]{:S(2)}, u32[]{:S(2)}) %all-to-all-start.1) | async-done | bytes 327712 | tf_op jit(solution)/shard_map/all_to_all | solution.py:31
  151.9 0.4 multiply_reduce_fusion
  152.3 0.6 broadcast_in_dim.48
  152.9 8.6 %all-to-all-start.2 = ((f32[32,1,128]{2,1,0:T(1,128)}), f32[32,1,128]{2,1,0:T(1,128)S(1)}, u32[]{:S(2)}, u32[]{:S(2)}) async-start(f32[32,1,128]{2,1,0:T(1,128)} %broadcast_in_dim.48), calls=%async_computation.2 | async-start | bytes 32768 | tf_op jit(solution)/shard_map/all_to_all | solution.py:31
  161.5 11.7 %all-to-all-done.2 = f32[32,1,128]{2,1,0:T(1,128)S(1)} async-done(((f32[32,1,128]{2,1,0:T(1,128)}), f32[32,1,128]{2,1,0:T(1,128)S(1)}, u32[]{:S(2)}, u32[]{:S(2)}) %all-to-all-start.2) | async-done | bytes 16416 | tf_op jit(solution)/shard_map/all_to_all | solution.py:31
  173.2 0.2 fusion.1
  173.4 0.1 broadcast_in_dim.50
  173.5 9.0 %all_to_all.25 = f32[16,1,128]{2,1,0:T(1,128)S(1)} all-to-all(f32[16,1,128]{2,1,0:T(1,128)S(1)} %broadcast_in_dim.50), channel_id=1, replica_groups=mesh['z'=16,'c'=2,'y'=4,'h'=2,'t'=2] {'y','h','t'}, dimensions={0} | all-to-all | bytes 16384 | tf_op jit(solution)/shard_map/all_to_all | solution.py:31
  182.5 16.8 %all_to_all.26 = f32[32,1,128]{2,1,0:T(1,128)S(1)} all-to-all(f32[32,1,128]{2,1,0:T(1,128)S(1)} %broadcast_in_dim.51), channel_id=1, replica_groups=mesh['z'=16,'c'=2,'y'=4,'h'=2,'t'=2] {'z','c'}, dimensions={0} | all-to-all | bytes 32768 | tf_op jit(solution)/shard_map/all_to_all | solution.py:31
  199.3 0.6 multiply_reduce_fusion.1
  200.7 0.6 multiply_bitcast_fusion
  (16 shorter events, 0.2 us)
Async XLA Ops:
  0.1 0.8 copy-start.1
  0.9 0.8 copy-start.2
  1.7 0.8 copy-start.3
  2.4 0.7 copy-start.4
  3.1 0.7 copy-start.5
  5.7 20.2 %all-to-all-start = ((bf16[16,20,512]{2,1,0:T(8,128)(2,1)}), bf16[16,20,512]{2,1,0:T(8,128)(2,1)S(1)}, u32[]{:S(2)}, u32[]{:S(2)}) async-start(bf16[16,20,512]{2,1,0:T(8,128)(2,1)} %shard_map.109), calls=%async_computation | async-start | bytes 786432 | tf_op jit(solution)/shard_map/all_to_all | solution.py:31
  80.9 1.2 copy-start.6
  80.9 1.5 copy-start.7
  134.5 1.6 copy-start
  139.3 12.6 %all-to-all-start.1 = ((f32[16,40,128]{2,1,0:T(8,128)}), f32[16,40,128]{2,1,0:T(8,128)S(1)}, u32[]{:S(2)}, u32[]{:S(2)}) async-start(f32[16,40,128]{2,1,0:T(8,128)} %bitcast.22), calls=%async_computation.1 | async-start | bytes 655360 | tf_op jit(solution)/shard_map/all_to_all | solution.py:31
  152.9 20.3 %all-to-all-start.2 = ((f32[32,1,128]{2,1,0:T(1,128)}), f32[32,1,128]{2,1,0:T(1,128)S(1)}, u32[]{:S(2)}, u32[]{:S(2)}) async-start(f32[32,1,128]{2,1,0:T(1,128)} %broadcast_in_dim.48), calls=%async_computation.2 | async-start | bytes 32768 | tf_op jit(solution)/shard_map/all_to_all | solution.py:31

commit v7 on v6

v7 whole, which is shorter than its diff:
```python
import functools

import jax
import jax.numpy as jnp
from jax import lax
from jax.experimental import pallas as pl
from jax.experimental.pallas import tpu as pltpu
from jax.sharding import Mesh
from jax.sharding import PartitionSpec as P

TASK_COUNT = 2
ADAPTER_SCALE = 0.5

SEQ = ("z", "c")
EXPERT = ("y", "h")
GROUP = ("y", "h", "t")
HALVES = 2

BF16 = jnp.bfloat16
F16 = jnp.float16
F32 = jnp.float32
HIGH = lax.Precision.HIGHEST
LANES = 128
LEAST_EXPONENT = -40.0
NOTE_ROWS = 16
PART_STEP = 256.0
LOW_LANES = 32


def swap(x, axes):
    return lax.all_to_all(x, axes, split_axis=0, concat_axis=0, tiled=True)


def spread(x, axes):
    return swap(jnp.broadcast_to(x[None], (lax.axis_size(axes),) + x.shape), axes)


def three_parts(x, step):
    first = lax.reduce_precision(x, 8, 7)
    rest = (x - first) * step
    second = lax.reduce_precision(rest, 8, 7)
    return first, second, (rest - second) * step


def earlier_in_block(lanes, block):
    i = lax.broadcasted_iota(jnp.int32, (lanes, lanes), 0)
    j = lax.broadcasted_iota(jnp.int32, (lanes, lanes), 1)
    return ((i < j) & (i // block == j // block)).astype(F32).astype(BF16)


def slots_of(named, block):
    before = jnp.dot(
        named.astype(F32).astype(BF16),
        earlier_in_block(named.shape[1], block),
        preferred_element_type=F32,
    )
    return jnp.where(named, before, -1.0)


def block_of(shape, block):
    return (lax.broadcasted_iota(jnp.int32, shape, 1) // block).astype(F32)


def dispatch_kernel(own_ref, *refs):
    out_ref, held, sem = refs[5], refs[6:11], refs[11]
    copies = [pltpu.make_async_copy(refs[k], held[k], sem.at[k]) for k in range(5)]
    for copy in copies:
        copy.start()
    for copy in copies:
        copy.wait()
    routes_ref, tokens_ref, down_ref, up_ref, norm_ref = held
    targets, set_slots, _ = out_ref.shape
    experts = targets // HALVES
    rows, feats = tokens_ref.shape
    half = feats // HALVES
    ranks = down_ref.shape[0] // HALVES
    core = own_ref[0]
    first_slot = (own_ref[3] * set_slots).astype(F32)
    ids = routes_ref[...]
    expert = lax.broadcasted_iota(jnp.int32, (experts, rows), 0)
    place = slots_of((ids[:1] == expert) | (ids[1:] == expert), rows)
    padded = 16
    row = lax.broadcasted_iota(jnp.int32, (padded, rows), 0)
    slot = jnp.where(row < set_slots, row.astype(F32) + first_slot, -2.0)
    chooser = jnp.concatenate(
        [(place[e : e + 1] == slot).astype(F32) for e in range(experts)], axis=0
    ).astype(BF16)
    for c in range(HALVES):
        lanes = pl.ds(c * half, half)
        x = tokens_ref[:, lanes]
        low = lax.dot_general(
            x, down_ref[:, lanes], (((1,), (1,)), ((), ())), preferred_element_type=F32
        )
        first = low.astype(BF16)
        rest = low - first.astype(F32)
        second = rest.astype(BF16)
        third = (rest - second.astype(F32)).astype(BF16)
        x = jnp.concatenate([x, jnp.zeros_like(first), first, second, third], axis=1)
        chosen = jnp.dot(chooser, x, preferred_element_type=F32)
        column = pl.multiple_of(own_ref[1 + c], LANES)
        norm = norm_ref[:, pl.ds(column, LANES)]
        norm_first = norm.astype(BF16).astype(F32)
        norm_rest = norm - norm_first
        norm_second = norm_rest.astype(BF16).astype(F32)
        up_rows = up_ref[pl.ds(pl.multiple_of(core * ranks, ranks), ranks), pl.ds(column, LANES)]
        up_rows = up_rows.astype(F32)
        small = [
            up_rows[:set_slots],
            jnp.concatenate(
                [
                    up_rows[set_slots:],
                    norm_first,
                    norm_second,
                    norm_rest - norm_second,
                    jnp.zeros((2 * set_slots - ranks - 3, LANES), F32),
                ],
                axis=0,
            ),
        ]
        small = jnp.concatenate(small, axis=1).astype(BF16)
        for e in range(experts):
            out_ref[e * HALVES + c, :, pl.ds(0, half + LANES)] = chosen[
                e * padded : e * padded + set_slots
            ].astype(BF16)
            out_ref[e * HALVES + c, :, pl.ds(half + LANES, 2 * LANES)] = small


def dispatch_layer(own, routes, tokens, adapter_down, adapter_up, norm_scale, experts, set_slots):
    rows, feats = tokens.shape
    lanes = feats // HALVES + 3 * LANES
    operands = (routes, tokens, adapter_down, adapter_up, norm_scale)
    return pl.pallas_call(
        dispatch_kernel,
        out_shape=jax.ShapeDtypeStruct((experts * HALVES, set_slots, lanes), BF16),
        in_specs=[pl.BlockSpec(memory_space=pltpu.SMEM)]
        + [pl.BlockSpec(memory_space=pl.ANY)] * len(operands),
        out_specs=pl.BlockSpec(memory_space=pltpu.VMEM),
        scratch_shapes=[pltpu.VMEM(x.shape, x.dtype) for x in operands]
        + [pltpu.SemaphoreType.DMA((len(operands),))],
        compiler_params=pltpu.CompilerParams(vmem_limit_bytes=16 * 2**20),
        cost_estimate=pl.CostEstimate(
            flops=4 * rows * feats * experts * set_slots,
            bytes_accessed=2 * rows * feats + 2 * experts * HALVES * set_slots * lanes,
            transcendentals=0,
        ),
    )(own, *operands)


def expert_kernel(
    shard_rows,
    own_ref,
    x_ref,
    gate_ref,
    up_ref,
    far_gate_ref,
    far_up_ref,
    adapter_ref,
    hidden_ref,
    scale_ref,
    base_ref,
    weight_ref,
):
    quarters, columns, _ = weight_ref.shape
    units = gate_ref.shape[1]
    task_rows = adapter_ref.shape[0]
    half = 2 * LANES
    blocks = columns // half
    for c in range(HALVES):
        for q in range(HALVES):
            for block in range(blocks):
                source = pl.ds(((q * blocks + block) * HALVES + c) * half, half)
                target = pl.ds(block * half, half)
                for k, ref in enumerate((gate_ref, up_ref, far_gate_ref, far_up_ref)):
                    weight_ref[c * HALVES + q, target, pl.ds(k * units, units)] = ref[source, :]
    rows = shard_rows // HALVES
    group = -(-rows // 8) * 8
    chips = x_ref.shape[0] // (HALVES * shard_rows)
    flat = chips * group
    own_core, own_quarter = own_ref[0], own_ref[1]
    own_column = pl.multiple_of(own_ref[2], LANES)
    task = own_ref[3]
    tensor = own_ref[4]

    def part(value, c, q):
        value = value.reshape(chips, HALVES, shard_rows, value.shape[-1])[:, c]
        value = value[:, :group] if q == 0 else value[:, shard_rows - group :]
        return value.reshape(flat, value.shape[-1])

    def aligned(value, q):
        return value if q == 0 else pltpu.roll(value, flat - (group - rows), 0)

    x = x_ref[:, pl.ds(0, columns)].astype(F32)
    own = x_ref[:, pl.ds(own_column, LANES)].astype(F32)
    beside = x_ref[:, pl.ds(columns, LANES)].astype(F32)
    acts = jnp.zeros((flat, 4 * units), F32)
    low = jnp.zeros((flat, LOW_LANES), F32)
    residual = jnp.zeros((flat, units), F32)
    row_exponent = None
    for c in range(HALVES):
        tile = part(beside, c, 0)
        exponent = tile[:, :LOW_LANES]
        low_part = tile[:, LOW_LANES : 2 * LOW_LANES] + (
            tile[:, 2 * LOW_LANES : 3 * LOW_LANES] + tile[:, 3 * LOW_LANES :] / PART_STEP
        ) / PART_STEP
        low += low_part * jnp.exp2(exponent - 7.0)
        exponent = jnp.concatenate([exponent] * (LANES // LOW_LANES), axis=1)
        scale = jnp.exp2(exponent - 15.0)
        row_exponent = exponent if c == 0 else jnp.maximum(row_exponent, exponent)
        half_acts = jnp.zeros((flat, 4 * units), F32)
        for q in range(HALVES):
            product = jnp.dot(
                part(x, c, q).astype(BF16),
                weight_ref[c * HALVES + q],
                preferred_element_type=F32,
            )
            half_acts += aligned(product, q)
            mine = (own_core == c) & (own_quarter == q)
            residual += jnp.where(mine, aligned(part(own, c, q), q) * scale, 0.0)
        acts += half_acts * jnp.concatenate([scale] * 4, axis=1)
    low_lane = lax.broadcasted_iota(jnp.int32, low.shape, 1) // (task_rows // TASK_COUNT)
    low = jnp.where(low_lane == task, low, 0.0).astype(BF16)
    base = residual + ADAPTER_SCALE * jnp.dot(
        low, adapter_ref[...], preferred_element_type=F32
    )
    down_scale = jnp.exp2(-2.0 * row_exponent - 2.0)
    up_scale = jnp.exp2(2.0 * row_exponent + 2.0)

    def hidden(gate_act, up_act):
        value = (gate_act / (1.0 + jnp.exp(-gate_act)) * up_act).astype(BF16).astype(F32)
        return value * down_scale

    near = hidden(acts[:, :units], acts[:, units : 2 * units])
    far = hidden(acts[:, 2 * units : 3 * units], acts[:, 3 * units :])
    pair = (jnp.where(tensor == 0, near, far), jnp.where(tensor == 0, far, near))
    for chip in range(chips):
        source = slice(chip * group, chip * group + rows)
        for k in range(2):
            hidden_ref[pl.ds((k * chips + chip) * rows, rows), :] = pair[k][source]
        scale_ref[pl.ds(chip * rows, rows), :] = up_scale[source]
        base_ref[pl.ds(chip * rows, rows), :] = base[source]


def expert_layer(gathered, weights, adapter_up, own, shard_rows):
    rows = gathered.shape[0]
    columns = gathered.shape[1] - LANES
    units = weights[0].shape[1]
    out = jax.ShapeDtypeStruct((rows // 4, units), F32)
    vmem = pl.BlockSpec(memory_space=pltpu.VMEM)
    return pl.pallas_call(
        functools.partial(expert_kernel, shard_rows),
        out_shape=(jax.ShapeDtypeStruct((rows // 2, units), F32), out, out),
        in_specs=[pl.BlockSpec(memory_space=pltpu.SMEM)] + [vmem] * 6,
        out_specs=(vmem, vmem, vmem),
        scratch_shapes=[pltpu.VMEM((2 * HALVES, columns, 4 * units), BF16)],
        compiler_params=pltpu.CompilerParams(vmem_limit_bytes=32 * 2**20),
        cost_estimate=pl.CostEstimate(
            flops=8 * rows * columns * units,
            bytes_accessed=2 * rows * columns + 8 * columns * units,
            transcendentals=2 * rows * units,
        ),
    )(own, gathered, *weights, adapter_up)


def return_kernel(
    block, set_slots, own_ref, h_ref, down_ref, scale_ref, base_ref, out_ref, note_ref
):
    seq, rows, units = h_ref.shape
    slots = (rows - NOTE_ROWS) // 2
    tensor = own_ref[0]
    expert = own_ref[1]
    group = own_ref[2]
    cores = HALVES
    at_notes = pl.ds(2 * slots, NOTE_ROWS)
    notes = h_ref[:, at_notes, :].astype(F32)
    notes = notes.reshape(seq // cores, cores, NOTE_ROWS, units).sum(axis=1)
    first, second = notes[:, 0, :].astype(jnp.int32), notes[:, 1, :].astype(jnp.int32)
    parts = notes[:, 2:8, :]
    weight = [
        parts[:, k, :] + (parts[:, k + 2, :] + parts[:, k + 4, :] / PART_STEP) / PART_STEP
        for k in range(2)
    ]
    slot = slots_of((first == expert) | (second == expert), block)
    slot = slot - (tensor * set_slots).astype(F32)
    in_set = (slot >= 0.0) & (slot < set_slots)
    place = jnp.where(in_set, slot + set_slots * block_of(slot.shape, block), -1000.0)
    weight = jnp.where(first == expert, weight[0], weight[1])
    note_ref[...] = (
        h_ref[group * cores, at_notes, :].astype(F32)
        + h_ref[group * cores + 1, at_notes, :].astype(F32)
    )

    lhs = jnp.concatenate(
        [h_ref[k, pl.ds(i * slots, slots), :] for k in range(seq) for i in range(2)], axis=1
    )
    out_ref[...] = jnp.dot(lhs, down_ref[...], preferred_element_type=F32)
    chip_rows = cores * set_slots
    pair_rows = 2 * chip_rows
    row = lax.broadcasted_iota(jnp.int32, (pair_rows, units), 0).astype(F32)
    for pair in range(seq // cores // 2):
        at = pl.ds(pair * pair_rows, pair_rows)
        one, two = slice(2 * pair, 2 * pair + 1), slice(2 * pair + 1, 2 * pair + 2)
        slot_weight = jnp.sum(
            jnp.where(place[one] == row, weight[one], 0.0)
            + jnp.where(place[two] + chip_rows == row, weight[two], 0.0),
            axis=1,
            keepdims=True,
        )
        out_ref[at, :] = slot_weight * (scale_ref[at, :] * out_ref[at, :]) + 0.5 * base_ref[at, :]


def return_layer(hidden, down_weight, scale, base, own, block, set_slots):
    seq, rows, units = hidden.shape
    slots = (rows - NOTE_ROWS) // 2
    vmem = pl.BlockSpec(memory_space=pltpu.VMEM)
    return pl.pallas_call(
        functools.partial(return_kernel, block, set_slots),
        out_shape=(
            jax.ShapeDtypeStruct((slots, units), F32),
            jax.ShapeDtypeStruct((NOTE_ROWS, units), F32),
        ),
        in_specs=[pl.BlockSpec(memory_space=pltpu.SMEM), vmem, vmem, vmem, vmem],
        out_specs=(vmem, vmem),
        compiler_params=pltpu.CompilerParams(vmem_limit_bytes=24 * 2**20),
        cost_estimate=pl.CostEstimate(
            flops=4 * seq * slots * units * units,
            bytes_accessed=4 * seq * slots * units + 2 * down_weight.size,
            transcendentals=0,
        ),
    )(own, hidden, down_weight, scale, base)


def norm_kernel(x_ref, out_ref):
    x = x_ref[:, 0, :]
    mean = jnp.sum(jnp.sum(x * x, axis=1, keepdims=True), axis=0, keepdims=True) / x.size
    x = x * lax.rsqrt(mean + 1e-06)
    for k in range(x.shape[0]):
        out_ref[:, pl.ds(k * LANES, LANES)] = x[k : k + 1, :]


def norm_layer(pooled):
    return pl.pallas_call(
        norm_kernel,
        out_shape=jax.ShapeDtypeStruct((1, pooled.size), F32),
        in_specs=[pl.BlockSpec(memory_space=pltpu.VMEM)],
        out_specs=pl.BlockSpec(memory_space=pltpu.VMEM),
    )(pooled)


def local(
    tokens,
    routes,
    chosen_expert_weight,
    expert_gate_weight,
    expert_up_weight,
    expert_down_weight,
    adapter_down_weight,
    adapter_up_weight,
    document_task_index,
    counts,
    final_norm_scale,
):
    rows, feats = tokens.shape
    seq = lax.axis_size(SEQ)
    experts = lax.axis_size(EXPERT)
    cores = lax.axis_size("c")
    groups = lax.axis_size(GROUP)
    tensors = lax.axis_size("t")
    capacity = rows * 5 // 16
    set_slots = capacity // tensors
    chip_rows = cores * set_slots
    shard_rows = HALVES * chip_rows
    width = feats * experts
    half = feats // cores
    columns = experts * half // HALVES
    slice_width = width // seq
    task_rows = adapter_down_weight.shape[0]
    s = lax.axis_index(SEQ)
    t = lax.axis_index("t")
    g = lax.axis_index(GROUP)
    per_feature_group = feats // slice_width
    own_group = s // per_feature_group

    core = lax.axis_index("c")
    ids = routes.T
    outgoing = dispatch_layer(
        jnp.stack(
            [core] + [(s - core + k) % per_feature_group * slice_width for k in range(cores)] + [t]
        ),
        ids,
        tokens,
        adapter_down_weight,
        adapter_up_weight,
        final_norm_scale[None],
        experts,
        set_slots,
    )
    far_weights, _ = lax.optimization_barrier(
        ((expert_gate_weight[0], expert_up_weight[0]), outgoing)
    )
    other = [(k, tensors - 1 - k) for k in range(tensors)]
    far_weights = [lax.ppermute(w, "t", other) for w in far_weights]
    received = swap(outgoing, EXPERT + ("c",)).reshape(experts, cores, set_slots, -1)
    shard = received[..., :half].transpose(1, 2, 0, 3).reshape(chip_rows, experts * half)
    low = jnp.sum(received[..., half + LOW_LANES : half + LANES].astype(F32), axis=0)
    low = low.reshape(chip_rows, 3, LOW_LANES).sum(axis=1)
    small = lax.dynamic_index_in_dim(received, own_group, axis=0, keepdims=False)
    small = jnp.concatenate(
        [small[..., half + LANES : half + 2 * LANES], small[..., half + 2 * LANES :]], axis=1
    )
    adapter_up = small[:, : task_rows // cores].reshape(task_rows, slice_width)
    norm_scale = jnp.sum(
        small[:1, task_rows // cores : task_rows // cores + 3].astype(F32), axis=1
    )

    shard = shard.astype(F32)
    largest = jnp.max(jnp.abs(shard), axis=1, keepdims=True)
    exponent = jnp.maximum(
        jnp.floor(jnp.log2(jnp.maximum(largest, 1e-30)) + 1.01), LEAST_EXPONENT
    )
    scaled = (shard * jnp.exp2(15.0 - exponent)).astype(F16)
    beside = jnp.concatenate(
        [jnp.broadcast_to(exponent, (chip_rows, LOW_LANES))]
        + list(three_parts(low * jnp.exp2(7.0 - exponent), PART_STEP)),
        axis=1,
    ).astype(F16)
    sent = jnp.concatenate(
        [
            jnp.concatenate([scaled[:, q * columns : (q + 1) * columns], beside], axis=1)
            for q in range(HALVES)
        ]
    )
    gathered = lax.all_gather(sent, SEQ, axis=0, tiled=False)
    gathered = gathered.astype(BF16).reshape(seq * shard_rows, columns + LANES)
    per_half = half // slice_width
    own_column = own_group * half + (s % per_half) * slice_width
    hidden, return_scale, base = expert_layer(
        gathered,
        [expert_gate_weight[0], expert_up_weight[0]] + far_weights,
        adapter_up,
        jnp.stack(
            [
                (s // per_half) % cores,
                own_column // columns,
                own_column % columns,
                document_task_index[0],
                t,
            ]
        ),
        shard_rows,
    )

    notes = jnp.concatenate(
        [ids.astype(F32)] + list(three_parts(chosen_expert_weight.T, PART_STEP))
    )
    notes = jnp.concatenate([jnp.where(core == k, notes, 0.0) for k in range(cores)], axis=1)
    notes = jnp.pad(notes, ((0, NOTE_ROWS - notes.shape[0]), (0, 0)))
    hidden = lax.all_gather(
        jnp.concatenate([hidden.astype(F16), notes.astype(F16)]), SEQ, axis=0, tiled=False
    )
    payload, group_notes = return_layer(
        hidden.astype(BF16),
        expert_down_weight[0],
        return_scale,
        base,
        jnp.stack([t, lax.axis_index(EXPERT), g]),
        rows,
        set_slots,
    )

    returned = swap(payload.reshape(groups, chip_rows, slice_width), GROUP)

    expert_ids = jnp.arange(experts, dtype=jnp.int32)[:, None]
    group_ids = group_notes[:2].astype(jnp.int32)
    slot = slots_of((group_ids[:1] == expert_ids) | (group_ids[1:] == expert_ids), rows)
    slot_set = jnp.floor(slot / set_slots)
    place = jnp.where(
        slot >= 0.0,
        slot + slot_set * (chip_rows - set_slots) + set_slots * block_of(slot.shape, rows),
        -1.0,
    )
    group_rows = cores * rows
    combiner = (
        place[:, None, :]
        == jnp.arange(tensors * chip_rows, dtype=jnp.int32).astype(F32)[None, :, None]
    ).astype(F32)
    mixed = lax.dot_general(
        combiner.reshape(groups * chip_rows, group_rows),
        returned.reshape(groups * chip_rows, slice_width),
        (((0,), (0,)), ((), ())),
        precision=HIGH,
    )
    squares = jnp.sum(spread(jnp.sum(mixed * mixed, axis=1)[None], SEQ), axis=0)
    position = g * group_rows + jnp.arange(group_rows, dtype=jnp.int32)[None, :]
    factor = jnp.where(position < counts[0], lax.rsqrt(squares / width + 1e-05), 0.0)
    pooled = jnp.dot(factor, mixed, precision=HIGH) * norm_scale
    pooled = jnp.sum(spread(pooled, GROUP), axis=0)
    return norm_layer(spread(pooled, SEQ))


def solution(mesh):
    seq, experts, tensors = mesh.devices.shape
    parts = Mesh(
        mesh.devices.reshape(seq // 2, 2, experts // 2, 2, tensors), ("z", "c", "y", "h", "t")
    )
    return jax.shard_map(
        local,
        mesh=parts,
        in_specs=(
            P(SEQ, EXPERT),
            P(SEQ, None),
            P(SEQ, None),
            P(EXPERT, None, SEQ + ("t",)),
            P(EXPERT, None, SEQ + ("t",)),
            P(EXPERT, None, SEQ),
            P(None, EXPERT),
            P(None, EXPERT),
            P(),
            P(),
            P(EXPERT),
        ),
        out_specs=P(),
        check_vma=False,
    )
```

time: 202 us -> 192 us (0.950)
  blocking collectives: 127 us -> 119 us
  starting transfers between devices: 22.3 us -> 30.2 us
  waiting for transfers between devices: 27.5 us -> 20 us
    all_gather x1, blocking collectives: 53.7 us -> 45.4 us  [local(): gathered = lax.all_gather(sent, SEQ, axis=0, tiled=False)]
    all_to_all x3, waiting for transfers between devices: 27.5 us -> 20 us  [swap(): return lax.all_to_all(x, axes, split_axis=0, concat_axis=0, tiled=True)]
    ppermute x0 -> x2, starting transfers between devices: none -> 5.27 us  [local(): far_weights = [lax.ppermute(w, 't', other) for w in far_weights]]
    all_to_all x3, starting transfers between devices: 22.3 us -> 24.9 us  [swap(): return lax.all_to_all(x, axes, split_axis=0, concat_axis=0, tiled=True)]
    pallas_call x3 -> x4, Pallas kernels: 9.56 us -> 8.43 us  [the longest x1 2.85 us: expert_layer(): pl.pallas_call(functools.partial(expert_kernel, shard_rows), out_shape=(j...]
    unnamed x17 -> x18, local copies, waits for them, and re-layouts: 5.34 us -> 5.78 us
  transfers between devices with their start and end apart: 3 -> 5, of which waited for: 3 -> 3; matrix products, arithmetic and copies ran while one was open for 1% -> 2% of each run, Pallas kernels for 0% -> 0%
where the time goes in v7:
time: 192 us; the launch traced here: 191 us
  blocking collectives  119 us (62%)
  starting transfers between devices  30.2 us (16%)
  waiting for transfers between devices  20 us (10%)
  Pallas kernels  8.43 us (4%)
  local copies, waits for them, and re-layouts  7.9 us (4%)
  other arithmetic  3.52 us (2%)
    all_gather x1, blocking collectives, local(): lax.all_gather(jnp.concatenate([hidden.astype(F16), notes.astype(F16)]),...  46.9 us
    all_gather x1, blocking collectives, local(): gathered = lax.all_gather(sent, SEQ, axis=0, tiled=False)  45.4 us
    all_to_all x2, blocking collectives, swap(): return lax.all_to_all(x, axes, split_axis=0, concat_axis=0, tiled=True)  26.5 us
    all_to_all x3, starting transfers between devices, swap(): return lax.all_to_all(x, axes, split_axis=0, concat_axis=0, tiled=True)  24.9 us
    all_to_all x3, waiting for transfers between devices, swap(): return lax.all_to_all(x, axes, split_axis=0, concat_axis=0, tiled=True)  20 us
    unnamed x18, local copies, waits for them, and re-layouts  5.78 us
    ppermute x2, starting transfers between devices, local(): far_weights = [lax.ppermute(w, 't', other) for w in far_weights]  5.27 us
  transfers between devices with their start and end apart: 5, of which 3 were waited for; matrix products, arithmetic and copies ran while one was open for 2% of the time, Pallas kernels for 0%

profile of v7, /device:TPU:1, one launch (start us, length us, event | category | flops | bytes accessed | tf_op | source)
XLA Modules:
  0.0 191.2 jit_solution(9710533453493822384)
XLA Ops:
  0.0 0.1 pad_add_fusion.1.own_ref
  0.1 0.0 copy-start.3
  0.1 0.8 copy-done.3
  0.9 0.0 copy-start.4
  0.9 0.8 copy-done.4
  1.7 0.0 copy-start.5
  1.7 0.8 copy-done.5
  2.4 0.0 copy-start.6
  2.4 0.7 copy-done.6
  3.1 0.0 copy-start.7
  3.1 0.7 copy-done.7
  3.8 2.1 %shard_map.109 = bf16[16,10,640]{2,1,0:T(8,128)(2,1)} custom-call(s32[4]{0:T(128)S(1)} %pad_add_fusion.1.own_ref, s32[2,64]{1,0:T(2,128)S(1)} %bitcast.64, bf16[64,512]{1,0:T(8,128)(2,1)S(1)} %copy-done.3, bf16[32,512]{1,0:T(8,128)(2,1)S(1)} %copy-done.4, bf16[32,512]{1,0:T(8,128)(2,1)S(1)} %copy-done.5, f32[1,512]{1,0:T(1,128)S(1)} %bitcast.65), custom_call_target="tpu_custom_call" | custom-call | flops 10485760 | bytes 270336 | tf_op jit(solution)/shard_map/pallas_call | solution.py:132
  5.9 10.2 %all-to-all-start = ((bf16[16,10,640]{2,1,0:T(8,128)(2,1)}), bf16[16,10,640]{2,1,0:T(8,128)(2,1)S(1)}, u32[]{:S(2)}, u32[]{:S(2)}) async-start(bf16[16,10,640]{2,1,0:T(8,128)(2,1)} %shard_map.109), calls=%async_computation | async-start | bytes 655360 | tf_op jit(solution)/shard_map/all_to_all | solution.py:31
  16.1 1.9 collective-permute-start
  18.0 3.4 %collective-permute-start.1 = (bf16[4096,128]{1,0:T(8,128)(2,1)}, bf16[4096,128]{1,0:T(8,128)(2,1)S(1)}, u32[]{:S(2)}, u32[]{:S(2)}) collective-permute-start(bf16[4096,128]{1,0:T(8,128)(2,1)} %bitcast.61), channel_id=1, source_target_pairs={{0,1},{1,0},{2,3},{3,2},{4,5},{5,4},{6,7},{7,6},{8,9},{9,8},{10,11... | collective-permute-start | bytes 3145736 | tf_op jit(solution)/shard_map/ppermute | solution.py:401
  21.4 0.7 bitcast_convert_fusion
  22.1 0.7 bitcast_reduce-precision_fusion
  24.1 0.1 stack.45.own_ref
  24.2 0.1 pad_add_fusion.own_ref
  24.3 0.1 fusion.13
  24.4 1.0 all-to-all-done
  25.4 0.1 copy_convert_fusion
  25.4 0.2 abs_reduce_fusion
  25.6 0.1 convert_reduce_fusion
  25.7 0.1 copy.19
  25.8 0.1 reshape.155
  25.9 0.1 multiply_convert_fusion
  26.0 0.1 reshape.146
  26.1 0.1 reshape.135
  26.2 0.1 reshape.156
  26.3 0.1 fusion.10
  26.4 0.1 broadcast_in_dim.25
  26.5 0.1 concatenate.27
  26.6 0.1 concatenate.26
  26.7 45.4 %all-gather.4 = f16[1280,1152]{1,0:T(8,128)(2,1)S(1)} all-gather(f16[40,1152]{1,0:T(8,128)(2,1)S(1)} %pad_maximum_fusion.1), channel_id=2, replica_groups=mesh['z'=16,'c'=2,'y'=4,'h'=2,'t'=2] {'z','c'}, dimensions={0}, use_global_device_ids=true | all-gather | bytes 3041280 | tf_op jit(solution)/shard_map/all_gather | solution.py:432
  72.1 0.0 copy-start.1
  72.1 0.0 copy-start.2
  72.1 0.4 convert_element_type.84.x_ref
  72.6 0.0 collective-permute-done.far_gate_ref
  72.6 0.0 collective-permute-done.1.far_up_ref
  72.6 0.7 copy-done.1
  73.3 0.3 copy-done.2
  73.6 2.8 %shard_map.110 = (f32[640,128]{1,0:T(8,128)S(1)}, f32[320,128]{1,0:T(8,128)S(1)}, f32[320,128]{1,0:T(8,128)S(1)}) custom-call(s32[5]{0:T(128)S(1)} %stack.45.own_ref, bf16[1280,1152]{1,0:T(8,128)(2,1)S(1)} %convert_element_type.84.x_ref, bf16[4096,128]{1,0:T(8,128)(2,1)S(1)} %bitcast.60, bf16[4096,128]{1,0:T(8,128)(2,1)S(1)} %bitcast.62, ...), custom_call_target="tpu_custom_call" | custom-call | flops 1342177280 | bytes 3670016 | tf_op jit(solution)/shard_map/pallas_call | solution.py:249
  76.5 0.1 pad_maximum_fusion
  76.6 46.9 %all-gather.5 = f16[20992,128]{1,0:T(8,128)(2,1)S(1)} all-gather(f16[656,128]{1,0:T(8,128)(2,1)S(1)} %pad_maximum_fusion), channel_id=3, replica_groups=mesh['z'=16,'c'=2,'y'=4,'h'=2,'t'=2] {'z','c'}, dimensions={0}, use_global_device_ids=true | all-gather | bytes 5541888 | tf_op jit(solution)/shard_map/all_gather | solution.py:457
  123.5 0.0 copy-start
  123.5 0.6 convert_element_type.85
  124.2 1.0 copy-done
  125.1 2.1 %shard_map.111 = (f32[320,128]{1,0:T(8,128)S(1)}, f32[16,128]{1,0:T(8,128)S(1)}) custom-call(s32[3]{0:T(128)S(1)} %pad_add_fusion.own_ref, bf16[32,656,128]{2,1,0:T(8,128)(2,1)S(1)} %bitcast.57, bf16[8192,128]{1,0:T(8,128)(2,1)S(1)} %bitcast.58, f32[320,128]{1,0:T(8,128)S(1)} %get-tuple-element.15.scale_ref, f32[320,128]{1,0:T(8,128)S(1)} %get-tuple-element.16.base_ref), custom_call_target="tpu_custom_call" | custom-call | flops 671088640 | bytes 7340032 | tf_op jit(solution)/shard_map/pallas_call | solution.py:315
  127.2 0.7 reshape.138
  127.9 6.2 %all-to-all-start.1 = ((f32[16,20,128]{2,1,0:T(8,128)}), f32[16,20,128]{2,1,0:T(8,128)S(1)}, u32[]{:S(2)}, u32[]{:S(2)}) async-start(f32[16,20,128]{2,1,0:T(8,128)} %reshape.138), calls=%async_computation.1 | async-start | bytes 393216 | tf_op jit(solution)/shard_map/all_to_all | solution.py:31
  134.2 0.2 add_select_fusion
  134.4 0.1 broadcast_compare_fusion
  134.5 7.3 %all-to-all-done.1 = f32[16,20,128]{2,1,0:T(8,128)S(1)} async-done(((f32[16,20,128]{2,1,0:T(8,128)}), f32[16,20,128]{2,1,0:T(8,128)S(1)}, u32[]{:S(2)}, u32[]{:S(2)}) %all-to-all-start.1) | async-done | bytes 163872 | tf_op jit(solution)/shard_map/all_to_all | solution.py:31
  141.8 0.4 multiply_reduce_fusion
  142.2 0.6 broadcast_in_dim.48
  142.8 8.5 %all-to-all-start.2 = ((f32[32,1,128]{2,1,0:T(1,128)}), f32[32,1,128]{2,1,0:T(1,128)S(1)}, u32[]{:S(2)}, u32[]{:S(2)}) async-start(f32[32,1,128]{2,1,0:T(1,128)} %broadcast_in_dim.48), calls=%async_computation.2 | async-start | bytes 32768 | tf_op jit(solution)/shard_map/all_to_all | solution.py:31
  151.3 11.7 %all-to-all-done.2 = f32[32,1,128]{2,1,0:T(1,128)S(1)} async-done(((f32[32,1,128]{2,1,0:T(1,128)}), f32[32,1,128]{2,1,0:T(1,128)S(1)}, u32[]{:S(2)}, u32[]{:S(2)}) %all-to-all-start.2) | async-done | bytes 16416 | tf_op jit(solution)/shard_map/all_to_all | solution.py:31
  163.0 0.2 fusion
  163.2 0.1 broadcast_in_dim.50
  163.3 9.1 %all_to_all.25 = f32[16,1,128]{2,1,0:T(1,128)S(1)} all-to-all(f32[16,1,128]{2,1,0:T(1,128)S(1)} %broadcast_in_dim.50), channel_id=1, replica_groups=mesh['z'=16,'c'=2,'y'=4,'h'=2,'t'=2] {'y','h','t'}, dimensions={0} | all-to-all | bytes 16384 | tf_op jit(solution)/shard_map/all_to_all | solution.py:31
  172.4 17.4 %all_to_all.26.x_ref = f32[32,1,128]{2,1,0:T(1,128)} all-to-all(f32[32,1,128]{2,1,0:T(1,128)S(1)} %broadcast_in_dim.51), channel_id=1, replica_groups=mesh['z'=16,'c'=2,'y'=4,'h'=2,'t'=2] {'z','c'}, dimensions={0} | all-to-all | bytes 32768 | tf_op jit(solution)/shard_map/all_to_all | solution.py:31
  189.8 1.4 shard_map.112
  (21 shorter events, 0.3 us)
Async XLA Ops:
  0.1 0.8 copy-start.3
  0.9 0.8 copy-start.4
  1.7 0.8 copy-start.5
  2.4 0.7 copy-start.6
  3.1 0.7 copy-start.7
  5.9 19.5 %all-to-all-start = ((bf16[16,10,640]{2,1,0:T(8,128)(2,1)}), bf16[16,10,640]{2,1,0:T(8,128)(2,1)S(1)}, u32[]{:S(2)}, u32[]{:S(2)}) async-start(bf16[16,10,640]{2,1,0:T(8,128)(2,1)} %shard_map.109), calls=%async_computation | async-start | bytes 655360 | tf_op jit(solution)/shard_map/all_to_all | solution.py:31
  16.1 56.5 %collective-permute-start = (bf16[4096,128]{1,0:T(8,128)(2,1)}, bf16[4096,128]{1,0:T(8,128)(2,1)S(1)}, u32[]{:S(2)}, u32[]{:S(2)}) collective-permute-start(bf16[4096,128]{1,0:T(8,128)(2,1)} %bitcast.59), channel_id=1, source_target_pairs={{0,1},{1,0},{2,3},{3,2},{4,5},{5,4},{6,7},{7,6},{8,9},{9,8},{10,11... | collective-permute-start | bytes 3145736 | tf_op jit(solution)/shard_map/ppermute | solution.py:401
  18.0 54.6 %collective-permute-start.1 = (bf16[4096,128]{1,0:T(8,128)(2,1)}, bf16[4096,128]{1,0:T(8,128)(2,1)S(1)}, u32[]{:S(2)}, u32[]{:S(2)}) collective-permute-start(bf16[4096,128]{1,0:T(8,128)(2,1)} %bitcast.61), channel_id=1, source_target_pairs={{0,1},{1,0},{2,3},{3,2},{4,5},{5,4},{6,7},{7,6},{8,9},{9,8},{10,11... | collective-permute-start | bytes 3145736 | tf_op jit(solution)/shard_map/ppermute | solution.py:401
  72.1 1.2 copy-start.1
  72.1 1.5 copy-start.2
  123.5 1.6 copy-start
  127.9 13.9 %all-to-all-start.1 = ((f32[16,20,128]{2,1,0:T(8,128)}), f32[16,20,128]{2,1,0:T(8,128)S(1)}, u32[]{:S(2)}, u32[]{:S(2)}) async-start(f32[16,20,128]{2,1,0:T(8,128)} %reshape.138), calls=%async_computation.1 | async-start | bytes 393216 | tf_op jit(solution)/shard_map/all_to_all | solution.py:31
  142.8 20.2 %all-to-all-start.2 = ((f32[32,1,128]{2,1,0:T(1,128)}), f32[32,1,128]{2,1,0:T(1,128)S(1)}, u32[]{:S(2)}, u32[]{:S(2)}) async-start(f32[32,1,128]{2,1,0:T(1,128)} %broadcast_in_dim.48), calls=%async_computation.2 | async-start | bytes 32768 | tf_op jit(solution)/shard_map/all_to_all | solution.py:31

commit v8 on v7

--- a/solution.py
+++ b/solution.py
@@ -133,11 +133,11 @@
         dispatch_kernel,
         out_shape=jax.ShapeDtypeStruct((experts * HALVES, set_slots, lanes), BF16),
         in_specs=[pl.BlockSpec(memory_space=pltpu.SMEM)]
-        + [pl.BlockSpec(memory_space=pl.ANY)] * len(operands),
+        + [pl.BlockSpec(memory_space=pltpu.HBM)] * len(operands),
         out_specs=pl.BlockSpec(memory_space=pltpu.VMEM),
         scratch_shapes=[pltpu.VMEM(x.shape, x.dtype) for x in operands]
         + [pltpu.SemaphoreType.DMA((len(operands),))],
-        compiler_params=pltpu.CompilerParams(vmem_limit_bytes=16 * 2**20),
+        compiler_params=pltpu.CompilerParams(vmem_limit_bytes=60 * 2**20),
         cost_estimate=pl.CostEstimate(
             flops=4 * rows * feats * experts * set_slots,
             bytes_accessed=2 * rows * feats + 2 * experts * HALVES * set_slots * lanes,
@@ -262,7 +262,15 @@
 
 
 def return_kernel(
-    block, set_slots, own_ref, h_ref, down_ref, scale_ref, base_ref, out_ref, note_ref
+    block,
+    set_slots,
+    own_ref,
+    h_ref,
+    down_ref,
+    scale_ref,
+    base_ref,
+    out_ref,
+    note_ref,
 ):
     seq, rows, units = h_ref.shape
     slots = (rows - NOTE_ROWS) // 2
@@ -292,12 +300,12 @@
     lhs = jnp.concatenate(
         [h_ref[k, pl.ds(i * slots, slots), :] for k in range(seq) for i in range(2)], axis=1
     )
-    out_ref[...] = jnp.dot(lhs, down_ref[...], preferred_element_type=F32)
+    out = jnp.dot(lhs, down_ref[...], preferred_element_type=F32)
     chip_rows = cores * set_slots
     pair_rows = 2 * chip_rows
     row = lax.broadcasted_iota(jnp.int32, (pair_rows, units), 0).astype(F32)
     for pair in range(seq // cores // 2):
-        at = pl.ds(pair * pair_rows, pair_rows)
+        at = slice(pair * pair_rows, (pair + 1) * pair_rows)
         one, two = slice(2 * pair, 2 * pair + 1), slice(2 * pair + 1, 2 * pair + 2)
         slot_weight = jnp.sum(
             jnp.where(place[one] == row, weight[one], 0.0)
@@ -305,7 +313,9 @@
             axis=1,
             keepdims=True,
         )
-        out_ref[at, :] = slot_weight * (scale_ref[at, :] * out_ref[at, :]) + 0.5 * base_ref[at, :]
+        value = slot_weight * (scale_ref[at, :] * out[at]) + 0.5 * base_ref[at, :]
+        out_ref[2 * pair] = value[:chip_rows]
+        out_ref[2 * pair + 1] = value[chip_rows:]
 
 
 def return_layer(hidden, down_weight, scale, base, own, block, set_slots):
@@ -315,7 +325,7 @@
     return pl.pallas_call(
         functools.partial(return_kernel, block, set_slots),
         out_shape=(
-            jax.ShapeDtypeStruct((slots, units), F32),
+            jax.ShapeDtypeStruct((seq // HALVES, HALVES * set_slots, units), F32),
             jax.ShapeDtypeStruct((NOTE_ROWS, units), F32),
         ),
         in_specs=[pl.BlockSpec(memory_space=pltpu.SMEM), vmem, vmem, vmem, vmem],
@@ -327,23 +337,6 @@
             transcendentals=0,
         ),
     )(own, hidden, down_weight, scale, base)
-
-
-def norm_kernel(x_ref, out_ref):
-    x = x_ref[:, 0, :]
-    mean = jnp.sum(jnp.sum(x * x, axis=1, keepdims=True), axis=0, keepdims=True) / x.size
-    x = x * lax.rsqrt(mean + 1e-06)
-    for k in range(x.shape[0]):
-        out_ref[:, pl.ds(k * LANES, LANES)] = x[k : k + 1, :]
-
-
-def norm_layer(pooled):
-    return pl.pallas_call(
-        norm_kernel,
-        out_shape=jax.ShapeDtypeStruct((1, pooled.size), F32),
-        in_specs=[pl.BlockSpec(memory_space=pltpu.VMEM)],
-        out_specs=pl.BlockSpec(memory_space=pltpu.VMEM),
-    )(pooled)
 
 
 def local(
@@ -394,11 +387,9 @@
         experts,
         set_slots,
     )
-    far_weights, _ = lax.optimization_barrier(
-        ((expert_gate_weight[0], expert_up_weight[0]), outgoing)
-    )
+    later_up, _ = lax.optimization_barrier((expert_up_weight[0], outgoing))
     other = [(k, tensors - 1 - k) for k in range(tensors)]
-    far_weights = [lax.ppermute(w, "t", other) for w in far_weights]
+    far_weights = [lax.ppermute(w, "t", other) for w in (expert_gate_weight[0], later_up)]
     received = swap(outgoing, EXPERT + ("c",)).reshape(experts, cores, set_slots, -1)
     shard = received[..., :half].transpose(1, 2, 0, 3).reshape(chip_rows, experts * half)
     low = jnp.sum(received[..., half + LOW_LANES : half + LANES].astype(F32), axis=0)
@@ -467,7 +458,7 @@
         set_slots,
     )
 
-    returned = swap(payload.reshape(groups, chip_rows, slice_width), GROUP)
+    returned = swap(payload, GROUP)
 
     expert_ids = jnp.arange(experts, dtype=jnp.int32)[:, None]
     group_ids = group_notes[:2].astype(jnp.int32)
@@ -494,7 +485,12 @@
     factor = jnp.where(position < counts[0], lax.rsqrt(squares / width + 1e-05), 0.0)
     pooled = jnp.dot(factor, mixed, precision=HIGH) * norm_scale
     pooled = jnp.sum(spread(pooled, GROUP), axis=0)
-    return norm_layer(spread(pooled, SEQ))
+    own_squares = jnp.sum(pooled * pooled, axis=1, keepdims=True)
+    pooled = spread(
+        jnp.concatenate([pooled, jnp.broadcast_to(own_squares, pooled.shape)]), SEQ
+    )
+    inverse = lax.rsqrt(jnp.sum(pooled[:, 1:], axis=0, keepdims=True) / width + 1e-06)
+    return (pooled[:, :1] * inverse).reshape(1, width)
 
 
 def solution(mesh):

time: 192 us -> 190 us (0.990)
  local copies, waits for them, and re-layouts: 7.9 us -> 4.15 us
    unnamed x18 -> x8, local copies, waits for them, and re-layouts: 5.78 us -> 2.06 us
where the time goes in v8:
time: 190 us; the launch traced here: 189 us
  blocking collectives  119 us (63%)
  starting transfers between devices  30.2 us (16%)
  waiting for transfers between devices  20 us (11%)
  Pallas kernels  8.44 us (4%)
  other arithmetic  5.32 us (3%)
  local copies, waits for them, and re-layouts  4.15 us (2%)
    all_gather x1, blocking collectives, local(): lax.all_gather(jnp.concatenate([hidden.astype(F16), notes.astype(F16)]),...  46.9 us
    all_gather x1, blocking collectives, local(): gathered = lax.all_gather(sent, SEQ, axis=0, tiled=False)  45.4 us
    all_to_all x2, blocking collectives, swap(): return lax.all_to_all(x, axes, split_axis=0, concat_axis=0, tiled=True)  26.3 us
    all_to_all x3, starting transfers between devices, swap(): return lax.all_to_all(x, axes, split_axis=0, concat_axis=0, tiled=True)  24.9 us
    all_to_all x3, waiting for transfers between devices, swap(): return lax.all_to_all(x, axes, split_axis=0, concat_axis=0, tiled=True)  20 us
    ppermute x2, starting transfers between devices, local(): lax.ppermute(w, 't', other)  5.27 us
  transfers between devices with their start and end apart: 5, of which 3 were waited for; matrix products, arithmetic and copies ran while one was open for 2% of the time, Pallas kernels for 0%

profile of v8, /device:TPU:1, one launch (start us, length us, event | category | flops | bytes accessed | tf_op | source)
XLA Modules:
  0.0 189.1 jit_solution(16800379959849257995)
XLA Ops:
  0.0 0.6 pad_add_fusion.1.own_ref
  0.6 2.8 %shard_map.109 = bf16[16,10,640]{2,1,0:T(8,128)(2,1)} custom-call(s32[4]{0:T(128)} %pad_add_fusion.1.own_ref, s32[2,64]{1,0:T(2,128)} %bitcast.76, bf16[64,512]{1,0:T(8,128)(2,1)} %refs_1_.1, bf16[32,512]{1,0:T(8,128)(2,1)} %refs_2_.1, bf16[32,512]{1,0:T(8,128)(2,1)} %refs_3_.1, f32[1,512]{1,0:T(1,128)} %bitcast.77), custom_call_target="tpu_custom_call" | custom-call | flops 10485760 | bytes 270336 | tf_op jit(solution)/shard_map/pallas_call | solution.py:132
  3.4 10.2 %all-to-all-start = ((bf16[16,10,640]{2,1,0:T(8,128)(2,1)}), bf16[16,10,640]{2,1,0:T(8,128)(2,1)S(1)}, u32[]{:S(2)}, u32[]{:S(2)}) async-start(bf16[16,10,640]{2,1,0:T(8,128)(2,1)} %shard_map.109), calls=%async_computation | async-start | bytes 655360 | tf_op jit(solution)/shard_map/all_to_all | solution.py:31
  13.7 1.9 %collective-permute-start = (bf16[4096,128]{1,0:T(8,128)(2,1)}, bf16[4096,128]{1,0:T(8,128)(2,1)S(1)}, u32[]{:S(2)}, u32[]{:S(2)}) collective-permute-start(bf16[4096,128]{1,0:T(8,128)(2,1)} %bitcast.62), channel_id=1, source_target_pairs={{0,1},{1,0},{2,3},{3,2},{4,5},{5,4},{6,7},{7,6},{8,9},{9,8},{10,11... | collective-permute-start | bytes 3145736 | tf_op jit(solution)/shard_map/ppermute | solution.py:392
  15.6 3.4 %collective-permute-start.1 = (bf16[4096,128]{1,0:T(8,128)(2,1)}, bf16[4096,128]{1,0:T(8,128)(2,1)S(1)}, u32[]{:S(2)}, u32[]{:S(2)}) collective-permute-start(bf16[4096,128]{1,0:T(8,128)(2,1)} %bitcast.64), channel_id=1, source_target_pairs={{0,1},{1,0},{2,3},{3,2},{4,5},{5,4},{6,7},{7,6},{8,9},{9,8},{10,11... | collective-permute-start | bytes 3145736 | tf_op jit(solution)/shard_map/ppermute | solution.py:392
  19.0 0.7 bitcast_convert_fusion
  19.7 0.7 bitcast_reduce-precision_fusion
  21.7 0.1 stack.45.own_ref
  21.8 0.1 pad_add_fusion.own_ref
  21.9 0.1 fusion.14
  21.9 1.0 all-to-all-done
  22.9 0.1 copy_convert_fusion
  23.0 0.2 abs_reduce_fusion
  23.2 0.1 convert_reduce_fusion
  23.3 0.1 copy.20
  23.4 0.1 reshape.174
  23.5 0.1 multiply_convert_fusion
  23.6 0.1 reshape.165
  23.7 0.1 reshape.154
  23.8 0.1 reshape.175
  23.9 0.1 fusion.11
  24.0 0.1 broadcast_in_dim.25
  24.1 0.1 concatenate.30
  24.2 0.1 concatenate.29
  24.3 45.4 %all-gather.4 = f16[1280,1152]{1,0:T(8,128)(2,1)S(1)} all-gather(f16[40,1152]{1,0:T(8,128)(2,1)S(1)} %pad_maximum_fusion.1), channel_id=2, replica_groups=mesh['z'=16,'c'=2,'y'=4,'h'=2,'t'=2] {'z','c'}, dimensions={0}, use_global_device_ids=true | all-gather | bytes 3041280 | tf_op jit(solution)/shard_map/all_gather | solution.py:423
  69.7 0.0 copy-start.1
  69.7 0.0 copy-start.2
  69.7 0.4 convert_element_type.84.x_ref
  70.2 0.0 collective-permute-done.far_gate_ref
  70.2 0.0 collective-permute-done.1.far_up_ref
  70.2 0.7 copy-done.1
  70.9 0.3 copy-done.2
  71.2 2.8 %shard_map.110 = (f32[640,128]{1,0:T(8,128)S(1)}, f32[320,128]{1,0:T(8,128)S(1)}, f32[320,128]{1,0:T(8,128)S(1)}) custom-call(s32[5]{0:T(128)S(1)} %stack.45.own_ref, bf16[1280,1152]{1,0:T(8,128)(2,1)S(1)} %convert_element_type.84.x_ref, bf16[4096,128]{1,0:T(8,128)(2,1)S(1)} %bitcast.63, bf16[4096,128]{1,0:T(8,128)(2,1)S(1)} %bitcast.65, ...), custom_call_target="tpu_custom_call" | custom-call | flops 1342177280 | bytes 3670016 | tf_op jit(solution)/shard_map/pallas_call | solution.py:249
  74.1 0.1 pad_maximum_fusion
  74.1 46.9 %all-gather.5 = f16[20992,128]{1,0:T(8,128)(2,1)S(1)} all-gather(f16[656,128]{1,0:T(8,128)(2,1)S(1)} %pad_maximum_fusion), channel_id=3, replica_groups=mesh['z'=16,'c'=2,'y'=4,'h'=2,'t'=2] {'z','c'}, dimensions={0}, use_global_device_ids=true | all-gather | bytes 5541888 | tf_op jit(solution)/shard_map/all_gather | solution.py:448
  121.1 0.0 copy-start
  121.1 0.6 convert_element_type.85
  121.7 1.0 copy-done
  122.7 2.8 %shard_map.111 = (f32[16,20,128]{2,1,0:T(8,128)}, f32[16,128]{1,0:T(8,128)S(1)}) custom-call(s32[3]{0:T(128)S(1)} %pad_add_fusion.own_ref, bf16[32,656,128]{2,1,0:T(8,128)(2,1)S(1)} %bitcast.60, bf16[8192,128]{1,0:T(8,128)(2,1)S(1)} %bitcast.61, f32[320,128]{1,0:T(8,128)S(1)} %get-tuple-element.13.scale_ref, f32[320,128]{1,0:T(8,128)S(1)} %get-tuple-element.14.base_ref), custom_call_target="tpu_custom_call" | custom-call | flops 671088640 | bytes 7340032 | tf_op jit(solution)/shard_map/pallas_call | solution.py:325
  125.4 6.2 %all-to-all-start.1 = ((f32[16,20,128]{2,1,0:T(8,128)}), f32[16,20,128]{2,1,0:T(8,128)S(1)}, u32[]{:S(2)}, u32[]{:S(2)}) async-start(f32[16,20,128]{2,1,0:T(8,128)} %get-tuple-element.16), calls=%async_computation.1 | async-start | bytes 393216 | tf_op jit(solution)/shard_map/all_to_all | solution.py:31
  131.6 0.2 add_select_fusion
  131.9 0.1 broadcast_compare_fusion
  132.0 7.3 %all-to-all-done.1 = f32[16,20,128]{2,1,0:T(8,128)S(1)} async-done(((f32[16,20,128]{2,1,0:T(8,128)}), f32[16,20,128]{2,1,0:T(8,128)S(1)}, u32[]{:S(2)}, u32[]{:S(2)}) %all-to-all-start.1) | async-done | bytes 163872 | tf_op jit(solution)/shard_map/all_to_all | solution.py:31
  139.3 0.4 multiply_reduce_fusion
  139.7 0.6 broadcast_in_dim.28
  140.3 8.5 %all-to-all-start.2 = ((f32[32,1,128]{2,1,0:T(1,128)}), f32[32,1,128]{2,1,0:T(1,128)S(1)}, u32[]{:S(2)}, u32[]{:S(2)}) async-start(f32[32,1,128]{2,1,0:T(1,128)} %broadcast_in_dim.28), calls=%async_computation.2 | async-start | bytes 32768 | tf_op jit(solution)/shard_map/all_to_all | solution.py:31
  148.8 11.7 %all-to-all-done.2 = f32[32,1,128]{2,1,0:T(1,128)S(1)} async-done(((f32[32,1,128]{2,1,0:T(1,128)}), f32[32,1,128]{2,1,0:T(1,128)S(1)}, u32[]{:S(2)}, u32[]{:S(2)}) %all-to-all-start.2) | async-done | bytes 16416 | tf_op jit(solution)/shard_map/all_to_all | solution.py:31
  160.6 0.2 fusion
  160.7 0.1 broadcast_in_dim.30
  160.8 9.1 %all_to_all.25 = f32[16,1,128]{2,1,0:T(1,128)S(1)} all-to-all(f32[16,1,128]{2,1,0:T(1,128)S(1)} %broadcast_in_dim.30), channel_id=1, replica_groups=mesh['z'=16,'c'=2,'y'=4,'h'=2,'t'=2] {'y','h','t'}, dimensions={0} | all-to-all | bytes 16384 | tf_op jit(solution)/shard_map/all_to_all | solution.py:31
  169.9 0.6 multiply_reduce_fusion.1
  170.5 0.6 concatenate.36
  171.2 17.2 %all_to_all.26 = f32[32,2,128]{2,1,0:T(2,128)S(1)} all-to-all(f32[32,2,128]{2,1,0:T(2,128)S(1)} %broadcast_in_dim.56), channel_id=1, replica_groups=mesh['z'=16,'c'=2,'y'=4,'h'=2,'t'=2] {'z','c'}, dimensions={0} | all-to-all | bytes 65536 | tf_op jit(solution)/shard_map/all_to_all | solution.py:31
  188.4 0.1 slice_reduce_fusion
  188.5 0.6 fusion.8
  (22 shorter events, 0.3 us)
Async XLA Ops:
  3.4 19.5 %all-to-all-start = ((bf16[16,10,640]{2,1,0:T(8,128)(2,1)}), bf16[16,10,640]{2,1,0:T(8,128)(2,1)S(1)}, u32[]{:S(2)}, u32[]{:S(2)}) async-start(bf16[16,10,640]{2,1,0:T(8,128)(2,1)} %shard_map.109), calls=%async_computation | async-start | bytes 655360 | tf_op jit(solution)/shard_map/all_to_all | solution.py:31
  13.7 56.5 %collective-permute-start = (bf16[4096,128]{1,0:T(8,128)(2,1)}, bf16[4096,128]{1,0:T(8,128)(2,1)S(1)}, u32[]{:S(2)}, u32[]{:S(2)}) collective-permute-start(bf16[4096,128]{1,0:T(8,128)(2,1)} %bitcast.62), channel_id=1, source_target_pairs={{0,1},{1,0},{2,3},{3,2},{4,5},{5,4},{6,7},{7,6},{8,9},{9,8},{10,11... | collective-permute-start | bytes 3145736 | tf_op jit(solution)/shard_map/ppermute | solution.py:392
  15.6 54.6 %collective-permute-start.1 = (bf16[4096,128]{1,0:T(8,128)(2,1)}, bf16[4096,128]{1,0:T(8,128)(2,1)S(1)}, u32[]{:S(2)}, u32[]{:S(2)}) collective-permute-start(bf16[4096,128]{1,0:T(8,128)(2,1)} %bitcast.64), channel_id=1, source_target_pairs={{0,1},{1,0},{2,3},{3,2},{4,5},{5,4},{6,7},{7,6},{8,9},{9,8},{10,11... | collective-permute-start | bytes 3145736 | tf_op jit(solution)/shard_map/ppermute | solution.py:392
  69.7 1.2 copy-start.1
  69.7 1.5 copy-start.2
  121.1 1.6 copy-start
  125.4 13.9 %all-to-all-start.1 = ((f32[16,20,128]{2,1,0:T(8,128)}), f32[16,20,128]{2,1,0:T(8,128)S(1)}, u32[]{:S(2)}, u32[]{:S(2)}) async-start(f32[16,20,128]{2,1,0:T(8,128)} %get-tuple-element.16), calls=%async_computation.1 | async-start | bytes 393216 | tf_op jit(solution)/shard_map/all_to_all | solution.py:31
  140.3 20.2 %all-to-all-start.2 = ((f32[32,1,128]{2,1,0:T(1,128)}), f32[32,1,128]{2,1,0:T(1,128)S(1)}, u32[]{:S(2)}, u32[]{:S(2)}) async-start(f32[32,1,128]{2,1,0:T(1,128)} %broadcast_in_dim.28), calls=%async_computation.2 | async-start | bytes 32768 | tf_op jit(solution)/shard_map/all_to_all | solution.py:31

commit v9 on v8

--- a/solution.py
+++ b/solution.py
@@ -22,7 +22,7 @@
 HIGH = lax.Precision.HIGHEST
 LANES = 128
 LEAST_EXPONENT = -40.0
-NOTE_ROWS = 16
+NOTE_ROWS = 8
 PART_STEP = 256.0
 LOW_LANES = 32
 
@@ -148,6 +148,7 @@
 
 def expert_kernel(
     shard_rows,
+    block,
     own_ref,
     x_ref,
     gate_ref,
@@ -156,8 +157,9 @@
     far_up_ref,
     adapter_ref,
     hidden_ref,
-    scale_ref,
+    factor_ref,
     base_ref,
+    note_ref,
     weight_ref,
 ):
     quarters, columns, _ = weight_ref.shape
@@ -167,9 +169,9 @@
     blocks = columns // half
     for c in range(HALVES):
         for q in range(HALVES):
-            for block in range(blocks):
-                source = pl.ds(((q * blocks + block) * HALVES + c) * half, half)
-                target = pl.ds(block * half, half)
+            for n in range(blocks):
+                source = pl.ds(((q * blocks + n) * HALVES + c) * half, half)
+                target = pl.ds(n * half, half)
                 for k, ref in enumerate((gate_ref, up_ref, far_gate_ref, far_up_ref)):
                     weight_ref[c * HALVES + q, target, pl.ds(k * units, units)] = ref[source, :]
     rows = shard_rows // HALVES
@@ -225,6 +227,23 @@
     down_scale = jnp.exp2(-2.0 * row_exponent - 2.0)
     up_scale = jnp.exp2(2.0 * row_exponent + 2.0)
 
+    notes = sum(aligned(part(beside, c, 1), 1) for c in range(HALVES))
+    notes = notes.reshape(chips, group, LANES)[:, :NOTE_ROWS]
+    note_ref[...] = notes
+    first, second = notes[:, 0, :].astype(jnp.int32), notes[:, 1, :].astype(jnp.int32)
+    weight = [
+        notes[:, k + 2, :] + (notes[:, k + 4, :] + notes[:, k + 6, :] / PART_STEP) / PART_STEP
+        for k in range(2)
+    ]
+    expert = own_ref[5]
+    set_slots = rows // HALVES
+    slot = slots_of((first == expert) | (second == expert), block)
+    slot = slot - (tensor * set_slots).astype(F32)
+    in_set = (slot >= 0.0) & (slot < set_slots)
+    place = jnp.where(in_set, slot + set_slots * block_of(slot.shape, block), -1.0)
+    weight = jnp.where(first == expert, weight[0], weight[1])
+    row = lax.broadcasted_iota(jnp.int32, (group, LANES), 0).astype(F32)
+
     def hidden(gate_act, up_act):
         value = (gate_act / (1.0 + jnp.exp(-gate_act)) * up_act).astype(BF16).astype(F32)
         return value * down_scale
@@ -236,21 +255,31 @@
         source = slice(chip * group, chip * group + rows)
         for k in range(2):
             hidden_ref[pl.ds((k * chips + chip) * rows, rows), :] = pair[k][source]
-        scale_ref[pl.ds(chip * rows, rows), :] = up_scale[source]
-        base_ref[pl.ds(chip * rows, rows), :] = base[source]
-
-
-def expert_layer(gathered, weights, adapter_up, own, shard_rows):
+        slot_weight = jnp.sum(
+            jnp.where(place[chip : chip + 1] == row, weight[chip : chip + 1], 0.0),
+            axis=1,
+            keepdims=True,
+        )[:rows]
+        factor_ref[pl.ds(chip * rows, rows), :] = slot_weight * up_scale[source]
+        base_ref[pl.ds(chip * rows, rows), :] = 0.5 * base[source]
+
+
+def expert_layer(gathered, weights, adapter_up, own, shard_rows, block):
     rows = gathered.shape[0]
     columns = gathered.shape[1] - LANES
     units = weights[0].shape[1]
     out = jax.ShapeDtypeStruct((rows // 4, units), F32)
     vmem = pl.BlockSpec(memory_space=pltpu.VMEM)
     return pl.pallas_call(
-        functools.partial(expert_kernel, shard_rows),
-        out_shape=(jax.ShapeDtypeStruct((rows // 2, units), F32), out, out),
+        functools.partial(expert_kernel, shard_rows, block),
+        out_shape=(
+            jax.ShapeDtypeStruct((rows // 2, units), F32),
+            out,
+            out,
+            jax.ShapeDtypeStruct((rows // (2 * shard_rows), NOTE_ROWS, LANES), F32),
+        ),
         in_specs=[pl.BlockSpec(memory_space=pltpu.SMEM)] + [vmem] * 6,
-        out_specs=(vmem, vmem, vmem),
+        out_specs=(vmem, vmem, vmem, vmem),
         scratch_shapes=[pltpu.VMEM((2 * HALVES, columns, 4 * units), BF16)],
         compiler_params=pltpu.CompilerParams(vmem_limit_bytes=32 * 2**20),
         cost_estimate=pl.CostEstimate(
@@ -259,84 +288,6 @@
             transcendentals=2 * rows * units,
         ),
     )(own, gathered, *weights, adapter_up)
-
-
-def return_kernel(
-    block,
-    set_slots,
-    own_ref,
-    h_ref,
-    down_ref,
-    scale_ref,
-    base_ref,
-    out_ref,
-    note_ref,
-):
-    seq, rows, units = h_ref.shape
-    slots = (rows - NOTE_ROWS) // 2
-    tensor = own_ref[0]
-    expert = own_ref[1]
-    group = own_ref[2]
-    cores = HALVES
-    at_notes = pl.ds(2 * slots, NOTE_ROWS)
-    notes = h_ref[:, at_notes, :].astype(F32)
-    notes = notes.reshape(seq // cores, cores, NOTE_ROWS, units).sum(axis=1)
-    first, second = notes[:, 0, :].astype(jnp.int32), notes[:, 1, :].astype(jnp.int32)
-    parts = notes[:, 2:8, :]
-    weight = [
-        parts[:, k, :] + (parts[:, k + 2, :] + parts[:, k + 4, :] / PART_STEP) / PART_STEP
-        for k in range(2)
-    ]
-    slot = slots_of((first == expert) | (second == expert), block)
-    slot = slot - (tensor * set_slots).astype(F32)
-    in_set = (slot >= 0.0) & (slot < set_slots)
-    place = jnp.where(in_set, slot + set_slots * block_of(slot.shape, block), -1000.0)
-    weight = jnp.where(first == expert, weight[0], weight[1])
-    note_ref[...] = (
-        h_ref[group * cores, at_notes, :].astype(F32)
-        + h_ref[group * cores + 1, at_notes, :].astype(F32)
-    )
-
-    lhs = jnp.concatenate(
-        [h_ref[k, pl.ds(i * slots, slots), :] for k in range(seq) for i in range(2)], axis=1
-    )
-    out = jnp.dot(lhs, down_ref[...], preferred_element_type=F32)
-    chip_rows = cores * set_slots
-    pair_rows = 2 * chip_rows
-    row = lax.broadcasted_iota(jnp.int32, (pair_rows, units), 0).astype(F32)
-    for pair in range(seq // cores // 2):
-        at = slice(pair * pair_rows, (pair + 1) * pair_rows)
-        one, two = slice(2 * pair, 2 * pair + 1), slice(2 * pair + 1, 2 * pair + 2)
-        slot_weight = jnp.sum(
-            jnp.where(place[one] == row, weight[one], 0.0)
-            + jnp.where(place[two] + chip_rows == row, weight[two], 0.0),
-            axis=1,
-            keepdims=True,
-        )
-        value = slot_weight * (scale_ref[at, :] * out[at]) + 0.5 * base_ref[at, :]
-        out_ref[2 * pair] = value[:chip_rows]
-        out_ref[2 * pair + 1] = value[chip_rows:]
-
-
-def return_layer(hidden, down_weight, scale, base, own, block, set_slots):
-    seq, rows, units = hidden.shape
-    slots = (rows - NOTE_ROWS) // 2
-    vmem = pl.BlockSpec(memory_space=pltpu.VMEM)
-    return pl.pallas_call(
-        functools.partial(return_kernel, block, set_slots),
-        out_shape=(
-            jax.ShapeDtypeStruct((seq // HALVES, HALVES * set_slots, units), F32),
-            jax.ShapeDtypeStruct((NOTE_ROWS, units), F32),
-        ),
-        in_specs=[pl.BlockSpec(memory_space=pltpu.SMEM), vmem, vmem, vmem, vmem],
-        out_specs=(vmem, vmem),
-        compiler_params=pltpu.CompilerParams(vmem_limit_bytes=24 * 2**20),
-        cost_estimate=pl.CostEstimate(
-            flops=4 * seq * slots * units * units,
-            bytes_accessed=4 * seq * slots * units + 2 * down_weight.size,
-            transcendentals=0,
-        ),
-    )(own, hidden, down_weight, scale, base)
 
 
 def local(
@@ -414,17 +365,22 @@
         + list(three_parts(low * jnp.exp2(7.0 - exponent), PART_STEP)),
         axis=1,
     ).astype(F16)
+    notes = jnp.concatenate(
+        [ids.astype(F32)] + list(three_parts(chosen_expert_weight.T, PART_STEP))
+    )
+    notes = jnp.concatenate([jnp.where(core == k, notes, 0.0) for k in range(cores)], axis=1)
+    notes = jnp.pad(notes, ((0, chip_rows - NOTE_ROWS), (0, 0))).astype(F16)
     sent = jnp.concatenate(
         [
-            jnp.concatenate([scaled[:, q * columns : (q + 1) * columns], beside], axis=1)
-            for q in range(HALVES)
+            jnp.concatenate([scaled[:, q * columns : (q + 1) * columns], tile], axis=1)
+            for q, tile in enumerate((beside, notes))
         ]
     )
     gathered = lax.all_gather(sent, SEQ, axis=0, tiled=False)
     gathered = gathered.astype(BF16).reshape(seq * shard_rows, columns + LANES)
     per_half = half // slice_width
     own_column = own_group * half + (s % per_half) * slice_width
-    hidden, return_scale, base = expert_layer(
+    hidden, factor, base, notes = expert_layer(
         gathered,
         [expert_gate_weight[0], expert_up_weight[0]] + far_weights,
         adapter_up,
@@ -435,33 +391,28 @@
                 own_column % columns,
                 document_task_index[0],
                 t,
+                lax.axis_index(EXPERT),
             ]
         ),
         shard_rows,
-    )
-
-    notes = jnp.concatenate(
-        [ids.astype(F32)] + list(three_parts(chosen_expert_weight.T, PART_STEP))
-    )
-    notes = jnp.concatenate([jnp.where(core == k, notes, 0.0) for k in range(cores)], axis=1)
-    notes = jnp.pad(notes, ((0, NOTE_ROWS - notes.shape[0]), (0, 0)))
-    hidden = lax.all_gather(
-        jnp.concatenate([hidden.astype(F16), notes.astype(F16)]), SEQ, axis=0, tiled=False
-    )
-    payload, group_notes = return_layer(
-        hidden.astype(BF16),
-        expert_down_weight[0],
-        return_scale,
-        base,
-        jnp.stack([t, lax.axis_index(EXPERT), g]),
         rows,
-        set_slots,
-    )
+    )
+
+    units = hidden.shape[-1]
+    hidden = lax.all_gather(hidden.astype(F16), SEQ, axis=0, tiled=False)
+    part = lax.dot_general(
+        hidden.reshape(seq * tensors, -1, units).astype(BF16),
+        expert_down_weight[0].reshape(seq * tensors, units, slice_width),
+        (((0, 2), (0, 1)), ((), ())),
+        preferred_element_type=F32,
+    )
+    payload = (part * factor + base).reshape(groups, chip_rows, slice_width)
 
     returned = swap(payload, GROUP)
 
     expert_ids = jnp.arange(experts, dtype=jnp.int32)[:, None]
-    group_ids = group_notes[:2].astype(jnp.int32)
+    group_ids = lax.dynamic_index_in_dim(notes, g, axis=0, keepdims=False)
+    group_ids = group_ids[:2].astype(jnp.int32)
     slot = slots_of((group_ids[:1] == expert_ids) | (group_ids[1:] == expert_ids), rows)
     slot_set = jnp.floor(slot / set_slots)
     place = jnp.where(
@@ -485,12 +436,8 @@
     factor = jnp.where(position < counts[0], lax.rsqrt(squares / width + 1e-05), 0.0)
     pooled = jnp.dot(factor, mixed, precision=HIGH) * norm_scale
     pooled = jnp.sum(spread(pooled, GROUP), axis=0)
-    own_squares = jnp.sum(pooled * pooled, axis=1, keepdims=True)
-    pooled = spread(
-        jnp.concatenate([pooled, jnp.broadcast_to(own_squares, pooled.shape)]), SEQ
-    )
-    inverse = lax.rsqrt(jnp.sum(pooled[:, 1:], axis=0, keepdims=True) / width + 1e-06)
-    return (pooled[:, :1] * inverse).reshape(1, width)
+    pooled = spread(pooled, SEQ).reshape(1, width)
+    return pooled * lax.rsqrt(jnp.mean(pooled * pooled, axis=1, keepdims=True) + 1e-06)
 
 
 def solution(mesh):

time: 190 us -> 193 us (1.016)
  other arithmetic: 5.32 us -> 8.72 us
  local copies, waits for them, and re-layouts: 4.15 us -> 6.44 us
  blocking collectives: 119 us -> 117 us
    pallas_call x2 -> x1, Pallas kernels: 5.6 us -> 3.79 us  [expert_layer(): pl.pallas_call(functools.partial(expert_kernel, shard_rows, block), out_s...]
  transfers between devices with their start and end apart: 5 -> 5, of which waited for: 3 -> 2; matrix products, arithmetic and copies ran while one was open for 2% -> 5% of each run, Pallas kernels for 0% -> 0%
where the time goes in v9:
time: 193 us; the launch traced here: 192 us
  blocking collectives  117 us (61%)
  starting transfers between devices  30.2 us (16%)
  waiting for transfers between devices  19 us (10%)
  other arithmetic  8.72 us (5%)
  Pallas kernels  6.64 us (3%)
  local copies, waits for them, and re-layouts  6.44 us (3%)
  between operations  2.32 us (1%)
  matrix products  2.3 us (1%)
    all_gather x1, blocking collectives, local(): hidden = lax.all_gather(hidden.astype(F16), SEQ, axis=0, tiled=False)  45.5 us
    all_gather x1, blocking collectives, local(): gathered = lax.all_gather(sent, SEQ, axis=0, tiled=False)  45.3 us
    all_to_all x2, blocking collectives, swap(): return lax.all_to_all(x, axes, split_axis=0, concat_axis=0, tiled=True)  26 us
    all_to_all x3, starting transfers between devices, swap(): return lax.all_to_all(x, axes, split_axis=0, concat_axis=0, tiled=True)  24.9 us
    all_to_all x3, waiting for transfers between devices, swap(): return lax.all_to_all(x, axes, split_axis=0, concat_axis=0, tiled=True)  19 us
    ppermute x2, starting transfers between devices, local(): lax.ppermute(w, 't', other)  5.28 us
  transfers between devices with their start and end apart: 5, of which 2 were waited for; matrix products, arithmetic and copies ran while one was open for 5% of the time, Pallas kernels for 0%

profile of v9, /device:TPU:1, one launch (start us, length us, event | category | flops | bytes accessed | tf_op | source)
XLA Modules:
  0.0 192.3 jit_solution(14344161000732017465)
XLA Ops:
  0.0 0.0 copy-start
  0.0 0.7 pad_add_fusion.own_ref
  0.7 2.9 %shard_map.109 = bf16[16,10,640]{2,1,0:T(8,128)(2,1)} custom-call(s32[4]{0:T(128)} %pad_add_fusion.own_ref, s32[2,64]{1,0:T(2,128)} %bitcast.78, bf16[64,512]{1,0:T(8,128)(2,1)} %refs_1_.1, bf16[32,512]{1,0:T(8,128)(2,1)} %refs_2_.1, bf16[32,512]{1,0:T(8,128)(2,1)} %refs_3_.1, f32[1,512]{1,0:T(1,128)} %bitcast.79), custom_call_target="tpu_custom_call" | custom-call | flops 10485760 | bytes 270336 | tf_op jit(solution)/shard_map/pallas_call | solution.py:132
  3.5 10.2 %all-to-all-start = ((bf16[16,10,640]{2,1,0:T(8,128)(2,1)}), bf16[16,10,640]{2,1,0:T(8,128)(2,1)S(1)}, u32[]{:S(2)}, u32[]{:S(2)}) async-start(bf16[16,10,640]{2,1,0:T(8,128)(2,1)} %shard_map.109), calls=%async_computation | async-start | bytes 655360 | tf_op jit(solution)/shard_map/all_to_all | solution.py:31
  13.7 1.9 collective-permute-start
  15.7 3.4 %collective-permute-start.1 = (bf16[4096,128]{1,0:T(8,128)(2,1)}, bf16[4096,128]{1,0:T(8,128)(2,1)}, u32[]{:S(2)}, u32[]{:S(2)}) collective-permute-start(bf16[4096,128]{1,0:T(8,128)(2,1)} %bitcast.65), channel_id=1, source_target_pairs={{0,1},{1,0},{2,3},{3,2},{4,5},{5,4},{6,7},{7,6},{8,9},{9,8},{10,11... | collective-permute-start | bytes 3145736 | tf_op jit(solution)/shard_map/ppermute | solution.py:343
  19.0 0.6 iota_shift-right-logical_fusion
  19.6 0.6 compare_and_fusion
  20.2 0.7 bitcast_convert_fusion
  21.5 0.7 bitcast_reduce-precision_fusion
  22.9 0.1 stack.36.own_ref
  23.0 0.1 fusion.13
  23.1 0.0 all-to-all-done
  23.1 0.1 copy_convert_fusion
  23.2 0.2 abs_reduce_fusion
  23.3 0.1 convert_reduce_fusion
  23.5 0.7 copy.20
  24.2 0.1 reshape.191
  24.3 1.0 multiply_convert_fusion
  25.3 0.7 fusion.35
  26.0 0.6 reshape.182
  26.6 0.1 reshape.171
  26.7 0.1 reshape.192
  26.8 0.7 fusion.10
  27.5 0.7 broadcast_in_dim.25
  28.2 0.9 concatenate.22
  29.1 0.8 maximum_maximum_fusion
  29.9 45.3 %all-gather.4 = f16[1280,1152]{1,0:T(8,128)(2,1)S(1)} all-gather(f16[40,1152]{1,0:T(8,128)(2,1)S(1)} %maximum_maximum_fusion), channel_id=2, replica_groups=mesh['z'=16,'c'=2,'y'=4,'h'=2,'t'=2] {'z','c'}, dimensions={0}, use_global_device_ids=true | all-gather | bytes 3041280 | tf_op jit(solution)/shard_map/all_gather | solution.py:379
  75.2 0.0 copy-start.1
  75.2 0.0 copy-start.2
  75.2 0.4 convert_element_type.89.x_ref
  75.7 0.0 collective-permute-done.far_gate_ref
  75.7 0.0 collective-permute-done.1.far_up_ref
  75.7 0.7 copy-done.1
  76.4 0.3 copy-done.2
  76.8 3.8 %shard_map.110 = (f32[640,128]{1,0:T(8,128)S(1)}, f32[320,128]{1,0:T(8,128)S(1)}, f32[320,128]{1,0:T(8,128)S(1)}, f32[16,8,128]{2,1,0:T(8,128)S(1)}) custom-call(s32[6]{0:T(128)S(1)} %stack.36.own_ref, bf16[1280,1152]{1,0:T(8,128)(2,1)S(1)} %convert_element_type.89.x_ref, bf16[4096,128]{1,0:T(8,128)(2,1)S(1)} %bitcast.64, bf16[4096,128]{1,0:T(8,128)(2,1)S(1)} %bitcast.66, ...), custom_call_target="tpu_custom_call" | custom-call | flops 1342177280 | bytes 3670016 | tf_op jit(solution)/shard_map/pallas_call | solution.py:273
  80.6 45.5 %all-gather.5 = f16[20480,128]{1,0:T(8,128)(2,1)S(1)} all-gather(f16[640,128]{1,0:T(8,128)(2,1)S(1)} %convert_element_type.83), channel_id=3, replica_groups=mesh['z'=16,'c'=2,'y'=4,'h'=2,'t'=2] {'z','c'}, dimensions={0}, use_global_device_ids=true | all-gather | bytes 5406720 | tf_op jit(solution)/shard_map/all_gather | solution.py:402
  126.1 0.6 convert_element_type.90
  126.7 0.0 copy-done
  126.7 0.0 copy-start.3
  126.7 0.0 copy-start.4
  126.8 0.0 copy-start.5
  126.8 1.5 convolution_bitcast_fusion
  128.3 0.7 reshape.174
  129.0 6.2 %all-to-all-start.1 = ((f32[16,20,128]{2,1,0:T(8,128)}), f32[16,20,128]{2,1,0:T(8,128)S(1)}, u32[]{:S(2)}, u32[]{:S(2)}) async-start(f32[16,20,128]{2,1,0:T(8,128)} %reshape.174), calls=%async_computation.1 | async-start | bytes 393216 | tf_op jit(solution)/shard_map/all_to_all | solution.py:31
  135.2 0.0 copy-done.3
  135.2 0.0 copy-done.4
  135.2 0.0 copy-done.5
  135.2 0.2 add_select_fusion
  135.5 0.1 broadcast_compare_fusion
  135.6 7.3 %all-to-all-done.1 = f32[16,20,128]{2,1,0:T(8,128)S(1)} async-done(((f32[16,20,128]{2,1,0:T(8,128)}), f32[16,20,128]{2,1,0:T(8,128)S(1)}, u32[]{:S(2)}, u32[]{:S(2)}) %all-to-all-start.1) | async-done | bytes 163872 | tf_op jit(solution)/shard_map/all_to_all | solution.py:31
  142.9 0.4 multiply_reduce_fusion
  143.2 0.6 broadcast_in_dim.49
  143.9 8.5 %all-to-all-start.2 = ((f32[32,1,128]{2,1,0:T(1,128)}), f32[32,1,128]{2,1,0:T(1,128)S(1)}, u32[]{:S(2)}, u32[]{:S(2)}) async-start(f32[32,1,128]{2,1,0:T(1,128)} %broadcast_in_dim.49), calls=%async_computation.2 | async-start | bytes 32768 | tf_op jit(solution)/shard_map/all_to_all | solution.py:31
  152.4 11.7 %all-to-all-done.2 = f32[32,1,128]{2,1,0:T(1,128)S(1)} async-done(((f32[32,1,128]{2,1,0:T(1,128)}), f32[32,1,128]{2,1,0:T(1,128)S(1)}, u32[]{:S(2)}, u32[]{:S(2)}) %all-to-all-start.2) | async-done | bytes 16416 | tf_op jit(solution)/shard_map/all_to_all | solution.py:31
  164.1 0.2 fusion
  164.3 0.1 broadcast_in_dim.51
  164.4 9.1 %all_to_all.25 = f32[16,1,128]{2,1,0:T(1,128)S(1)} all-to-all(f32[16,1,128]{2,1,0:T(1,128)S(1)} %broadcast_in_dim.51), channel_id=1, replica_groups=mesh['z'=16,'c'=2,'y'=4,'h'=2,'t'=2] {'y','h','t'}, dimensions={0} | all-to-all | bytes 16384 | tf_op jit(solution)/shard_map/all_to_all | solution.py:31
  173.5 16.8 %all_to_all.26 = f32[32,1,128]{2,1,0:T(1,128)S(1)} all-to-all(f32[32,1,128]{2,1,0:T(1,128)S(1)} %broadcast_in_dim.52), channel_id=1, replica_groups=mesh['z'=16,'c'=2,'y'=4,'h'=2,'t'=2] {'z','c'}, dimensions={0} | all-to-all | bytes 32768 | tf_op jit(solution)/shard_map/all_to_all | solution.py:31
  190.4 0.6 multiply_reduce_fusion.1
  191.7 0.6 multiply_bitcast_fusion
  (19 shorter events, 0.3 us)
Async XLA Ops:
  0.0 126.7 %copy-start = (bf16[1,8192,128]{2,1,0:T(8,128)(2,1)S(1)}, bf16[1,8192,128]{2,1,0:T(8,128)(2,1)}, u32[]{:S(2)}) copy-start(bf16[1,8192,128]{2,1,0:T(8,128)(2,1)} %param.16) | copy-start | bytes 6291460
  3.5 19.6 %all-to-all-start = ((bf16[16,10,640]{2,1,0:T(8,128)(2,1)}), bf16[16,10,640]{2,1,0:T(8,128)(2,1)S(1)}, u32[]{:S(2)}, u32[]{:S(2)}) async-start(bf16[16,10,640]{2,1,0:T(8,128)(2,1)} %shard_map.109), calls=%async_computation | async-start | bytes 655360 | tf_op jit(solution)/shard_map/all_to_all | solution.py:31
  13.7 62.0 %collective-permute-start = (bf16[4096,128]{1,0:T(8,128)(2,1)}, bf16[4096,128]{1,0:T(8,128)(2,1)S(1)}, u32[]{:S(2)}, u32[]{:S(2)}) collective-permute-start(bf16[4096,128]{1,0:T(8,128)(2,1)} %bitcast.63), channel_id=1, source_target_pairs={{0,1},{1,0},{2,3},{3,2},{4,5},{5,4},{6,7},{7,6},{8,9},{9,8},{10,11... | collective-permute-start | bytes 3145736 | tf_op jit(solution)/shard_map/ppermute | solution.py:343
  15.7 60.1 %collective-permute-start.1 = (bf16[4096,128]{1,0:T(8,128)(2,1)}, bf16[4096,128]{1,0:T(8,128)(2,1)}, u32[]{:S(2)}, u32[]{:S(2)}) collective-permute-start(bf16[4096,128]{1,0:T(8,128)(2,1)} %bitcast.65), channel_id=1, source_target_pairs={{0,1},{1,0},{2,3},{3,2},{4,5},{5,4},{6,7},{7,6},{8,9},{9,8},{10,11... | collective-permute-start | bytes 3145736 | tf_op jit(solution)/shard_map/ppermute | solution.py:343
  75.2 1.2 copy-start.1
  75.2 1.5 copy-start.2
  126.7 8.5 %copy-start.3 = (s32[128]{0:T(128)S(1)}, s32[128]{0:T(128)}, u32[]{:S(2)}) copy-start(s32[128]{0:T(128)} %get-tuple-element.34) | copy-start | bytes 1540
  126.7 8.5 %copy-start.4 = (s32[128]{0:T(128)S(1)}, s32[128]{0:T(128)}, u32[]{:S(2)}) copy-start(s32[128]{0:T(128)} %get-tuple-element.35) | copy-start | bytes 1540
  126.8 8.5 %copy-start.5 = (pred[128]{0:T(512)(128)(4,1)S(1)}, pred[128]{0:T(512)(128)(4,1)}, u32[]{:S(2)}) copy-start(pred[128]{0:T(512)(128)(4,1)} %compare_and_fusion) | copy-start | bytes 388
  129.0 13.8 %all-to-all-start.1 = ((f32[16,20,128]{2,1,0:T(8,128)}), f32[16,20,128]{2,1,0:T(8,128)S(1)}, u32[]{:S(2)}, u32[]{:S(2)}) async-start(f32[16,20,128]{2,1,0:T(8,128)} %reshape.174), calls=%async_computation.1 | async-start | bytes 393216 | tf_op jit(solution)/shard_map/all_to_all | solution.py:31
  143.9 20.2 %all-to-all-start.2 = ((f32[32,1,128]{2,1,0:T(1,128)}), f32[32,1,128]{2,1,0:T(1,128)S(1)}, u32[]{:S(2)}, u32[]{:S(2)}) async-start(f32[32,1,128]{2,1,0:T(1,128)} %broadcast_in_dim.49), calls=%async_computation.2 | async-start | bytes 32768 | tf_op jit(solution)/shard_map/all_to_all | solution.py:31

commit v10 on v9

--- a/solution.py
+++ b/solution.py
@@ -35,11 +35,11 @@
     return swap(jnp.broadcast_to(x[None], (lax.axis_size(axes),) + x.shape), axes)
 
 
-def three_parts(x, step):
-    first = lax.reduce_precision(x, 8, 7)
-    rest = (x - first) * step
-    second = lax.reduce_precision(rest, 8, 7)
-    return first, second, (rest - second) * step
+def rounded_parts(x):
+    first = x.astype(BF16).astype(F32)
+    rest = (x - first) * PART_STEP
+    second = rest.astype(BF16).astype(F32)
+    return first, second, (rest - second) * PART_STEP
 
 
 def earlier_in_block(lanes, block):
@@ -62,13 +62,13 @@
 
 
 def dispatch_kernel(own_ref, *refs):
-    out_ref, held, sem = refs[5], refs[6:11], refs[11]
-    copies = [pltpu.make_async_copy(refs[k], held[k], sem.at[k]) for k in range(5)]
+    out_ref, note_ref, held, sem = refs[6], refs[7], refs[8:14], refs[14]
+    copies = [pltpu.make_async_copy(refs[k], held[k], sem.at[k]) for k in range(6)]
     for copy in copies:
         copy.start()
     for copy in copies:
         copy.wait()
-    routes_ref, tokens_ref, down_ref, up_ref, norm_ref = held
+    routes_ref, chosen_ref, tokens_ref, down_ref, up_ref, norm_ref = held
     targets, set_slots, _ = out_ref.shape
     experts = targets // HALVES
     rows, feats = tokens_ref.shape
@@ -77,6 +77,10 @@
     core = own_ref[0]
     first_slot = (own_ref[3] * set_slots).astype(F32)
     ids = routes_ref[...]
+    notes = jnp.concatenate([ids.astype(F32)] + list(rounded_parts(chosen_ref[...])), axis=0)
+    notes = jnp.concatenate([jnp.where(core == k, notes, 0.0) for k in range(HALVES)], axis=1)
+    note_ref[...] = jnp.zeros_like(note_ref)
+    note_ref[pl.ds(0, NOTE_ROWS), :] = notes
     expert = lax.broadcasted_iota(jnp.int32, (experts, rows), 0)
     place = slots_of((ids[:1] == expert) | (ids[1:] == expert), rows)
     padded = 16
@@ -125,16 +129,21 @@
             out_ref[e * HALVES + c, :, pl.ds(half + LANES, 2 * LANES)] = small
 
 
-def dispatch_layer(own, routes, tokens, adapter_down, adapter_up, norm_scale, experts, set_slots):
+def dispatch_layer(
+    own, routes, chosen, tokens, adapter_down, adapter_up, norm_scale, experts, set_slots
+):
     rows, feats = tokens.shape
     lanes = feats // HALVES + 3 * LANES
-    operands = (routes, tokens, adapter_down, adapter_up, norm_scale)
+    operands = (routes, chosen, tokens, adapter_down, adapter_up, norm_scale)
     return pl.pallas_call(
         dispatch_kernel,
-        out_shape=jax.ShapeDtypeStruct((experts * HALVES, set_slots, lanes), BF16),
+        out_shape=(
+            jax.ShapeDtypeStruct((experts * HALVES, set_slots, lanes), BF16),
+            jax.ShapeDtypeStruct((HALVES * set_slots, LANES), F32),
+        ),
         in_specs=[pl.BlockSpec(memory_space=pltpu.SMEM)]
         + [pl.BlockSpec(memory_space=pltpu.HBM)] * len(operands),
-        out_specs=pl.BlockSpec(memory_space=pltpu.VMEM),
+        out_specs=(pl.BlockSpec(memory_space=pltpu.VMEM),) * 2,
         scratch_shapes=[pltpu.VMEM(x.shape, x.dtype) for x in operands]
         + [pltpu.SemaphoreType.DMA((len(operands),))],
         compiler_params=pltpu.CompilerParams(vmem_limit_bytes=60 * 2**20),
@@ -144,6 +153,73 @@
             transcendentals=0,
         ),
     )(own, *operands)
+
+
+def rows_kernel(own_ref, received_ref, note_ref, sent_ref, adapter_ref, norm_ref):
+    messages, set_slots, _ = received_ref.shape
+    groups = messages // HALVES
+    half = 2 * LANES
+    rows = HALVES * set_slots
+    columns = sent_ref.shape[1] - LANES
+    ranks = adapter_ref.shape[0] // HALVES
+
+    def both(e, first, lanes):
+        return jnp.concatenate(
+            [
+                received_ref[e * HALVES + c, :, pl.ds(first, lanes)].astype(F32)
+                for c in range(HALVES)
+            ],
+            axis=0,
+        )
+
+    x = jnp.concatenate([both(e, 0, half) for e in range(groups)], axis=1)
+    largest = jnp.max(jnp.abs(x), axis=1, keepdims=True)
+    exponent = jnp.maximum(
+        jnp.floor(jnp.log2(jnp.maximum(largest, 1e-30)) + 1.01), LEAST_EXPONENT
+    )
+    x = x * jnp.exp2(15.0 - exponent)
+    low = sum(both(e, half, LANES) for e in range(groups))
+    low = sum(low[:, k * LOW_LANES : (k + 1) * LOW_LANES] for k in range(1, 4))
+    low = low * jnp.exp2(7.0 - exponent)
+    sent_ref[pl.ds(0, rows), pl.ds(0, columns)] = x[:, :columns]
+    sent_ref[pl.ds(rows, rows), pl.ds(0, columns)] = x[:, columns:]
+    sent_ref[pl.ds(0, rows), pl.ds(columns, LANES)] = jnp.concatenate(
+        [jnp.broadcast_to(exponent, low.shape)] + list(rounded_parts(low)), axis=1
+    )
+    sent_ref[pl.ds(rows, rows), pl.ds(columns, LANES)] = note_ref[...]
+
+    adapter = []
+    for c in range(HALVES):
+        small = received_ref[own_ref[0] * HALVES + c, :, pl.ds(half + LANES, 2 * LANES)]
+        small = small.astype(F32)
+        small = jnp.concatenate([small[:, :LANES], small[:, LANES:]], axis=0)
+        adapter.append(small[:ranks])
+        if c == 0:
+            norm_ref[...] = (
+                small[ranks : ranks + 1] + small[ranks + 1 : ranks + 2]
+            ) + small[ranks + 2 : ranks + 3]
+    adapter_ref[...] = jnp.concatenate(adapter, axis=0).astype(BF16)
+
+
+def rows_layer(own_group, received, notes, task_rows):
+    messages, set_slots, _ = received.shape
+    rows = HALVES * set_slots
+    vmem = pl.BlockSpec(memory_space=pltpu.VMEM)
+    columns = messages // HALVES * 2 * LANES // HALVES
+    return pl.pallas_call(
+        rows_kernel,
+        out_shape=(
+            jax.ShapeDtypeStruct((HALVES * rows, columns + LANES), F32),
+            jax.ShapeDtypeStruct((task_rows, LANES), BF16),
+            jax.ShapeDtypeStruct((1, LANES), F32),
+        ),
+        in_specs=[pl.BlockSpec(memory_space=pltpu.SMEM), vmem, vmem],
+        out_specs=(vmem, vmem, vmem),
+        compiler_params=pltpu.CompilerParams(vmem_limit_bytes=16 * 2**20),
+        cost_estimate=pl.CostEstimate(
+            flops=8 * rows * columns, bytes_accessed=8 * rows * columns, transcendentals=4 * rows
+        ),
+    )(own_group[None], received, notes)
 
 
 def expert_kernel(
@@ -326,11 +402,12 @@
 
     core = lax.axis_index("c")
     ids = routes.T
-    outgoing = dispatch_layer(
+    outgoing, notes = dispatch_layer(
         jnp.stack(
             [core] + [(s - core + k) % per_feature_group * slice_width for k in range(cores)] + [t]
         ),
         ids,
+        chosen_expert_weight.T,
         tokens,
         adapter_down_weight,
         adapter_up_weight,
@@ -341,41 +418,10 @@
     later_up, _ = lax.optimization_barrier((expert_up_weight[0], outgoing))
     other = [(k, tensors - 1 - k) for k in range(tensors)]
     far_weights = [lax.ppermute(w, "t", other) for w in (expert_gate_weight[0], later_up)]
-    received = swap(outgoing, EXPERT + ("c",)).reshape(experts, cores, set_slots, -1)
-    shard = received[..., :half].transpose(1, 2, 0, 3).reshape(chip_rows, experts * half)
-    low = jnp.sum(received[..., half + LOW_LANES : half + LANES].astype(F32), axis=0)
-    low = low.reshape(chip_rows, 3, LOW_LANES).sum(axis=1)
-    small = lax.dynamic_index_in_dim(received, own_group, axis=0, keepdims=False)
-    small = jnp.concatenate(
-        [small[..., half + LANES : half + 2 * LANES], small[..., half + 2 * LANES :]], axis=1
-    )
-    adapter_up = small[:, : task_rows // cores].reshape(task_rows, slice_width)
-    norm_scale = jnp.sum(
-        small[:1, task_rows // cores : task_rows // cores + 3].astype(F32), axis=1
-    )
-
-    shard = shard.astype(F32)
-    largest = jnp.max(jnp.abs(shard), axis=1, keepdims=True)
-    exponent = jnp.maximum(
-        jnp.floor(jnp.log2(jnp.maximum(largest, 1e-30)) + 1.01), LEAST_EXPONENT
-    )
-    scaled = (shard * jnp.exp2(15.0 - exponent)).astype(F16)
-    beside = jnp.concatenate(
-        [jnp.broadcast_to(exponent, (chip_rows, LOW_LANES))]
-        + list(three_parts(low * jnp.exp2(7.0 - exponent), PART_STEP)),
-        axis=1,
-    ).astype(F16)
-    notes = jnp.concatenate(
-        [ids.astype(F32)] + list(three_parts(chosen_expert_weight.T, PART_STEP))
-    )
-    notes = jnp.concatenate([jnp.where(core == k, notes, 0.0) for k in range(cores)], axis=1)
-    notes = jnp.pad(notes, ((0, chip_rows - NOTE_ROWS), (0, 0))).astype(F16)
-    sent = jnp.concatenate(
-        [
-            jnp.concatenate([scaled[:, q * columns : (q + 1) * columns], tile], axis=1)
-            for q, tile in enumerate((beside, notes))
-        ]
-    )
+    received = swap(outgoing, EXPERT + ("c",))
+
+    sent, adapter_up, norm_scale = rows_layer(own_group, received, notes, task_rows)
+    sent = sent.astype(F16)
     gathered = lax.all_gather(sent, SEQ, axis=0, tiled=False)
     gathered = gathered.astype(BF16).reshape(seq * shard_rows, columns + LANES)
     per_half = half // slice_width

time: 193 us -> 189 us (0.979)
  other arithmetic: 8.72 us -> 3.2 us
  local copies, waits for them, and re-layouts: 6.44 us -> 3.26 us
  waiting for transfers between devices: 19 us -> 21.5 us
    all_to_all x3, waiting for transfers between devices: 19 us -> 21.5 us  [swap(): return lax.all_to_all(x, axes, split_axis=0, concat_axis=0, tiled=True)]
  transfers between devices with their start and end apart: 5 -> 5, of which waited for: 2 -> 3; matrix products, arithmetic and copies ran while one was open for 5% -> 0% of each run, Pallas kernels for 0% -> 0%
where the time goes in v10:
time: 189 us; the launch traced here: 188 us
  blocking collectives  118 us (62%)
  starting transfers between devices  30.6 us (16%)
  waiting for transfers between devices  21.5 us (11%)
  Pallas kernels  6.98 us (4%)
  local copies, waits for them, and re-layouts  3.26 us (2%)
  other arithmetic  3.2 us (2%)
  matrix products  2.3 us (1%)
  between operations  2.25 us (1%)
    all_gather x1, blocking collectives, local(): hidden = lax.all_gather(hidden.astype(F16), SEQ, axis=0, tiled=False)  46.5 us
    all_gather x1, blocking collectives, local(): gathered = lax.all_gather(sent, SEQ, axis=0, tiled=False)  45.4 us
    all_to_all x2, blocking collectives, swap(): return lax.all_to_all(x, axes, split_axis=0, concat_axis=0, tiled=True)  26 us
    all_to_all x3, starting transfers between devices, swap(): return lax.all_to_all(x, axes, split_axis=0, concat_axis=0, tiled=True)  25.4 us
    all_to_all x3, waiting for transfers between devices, swap(): return lax.all_to_all(x, axes, split_axis=0, concat_axis=0, tiled=True)  21.5 us
    ppermute x2, starting transfers between devices, local(): lax.ppermute(w, 't', other)  5.28 us
    pallas_call x1, Pallas kernels, expert_layer(): pl.pallas_call(functools.partial(expert_kernel, shard_rows, block), out_s...  3.88 us
  transfers between devices with their start and end apart: 5, of which 3 were waited for; matrix products, arithmetic and copies ran while one was open for 0% of the time, Pallas kernels for 0%

profile of v10, /device:TPU:1, one launch (start us, length us, event | category | flops | bytes accessed | tf_op | source)
XLA Modules:
  0.0 187.9 jit_solution(2963861413957740884)
XLA Ops:
  0.0 0.0 copy-start
  0.0 0.7 pad_add_fusion.own_ref
  0.7 2.9 %shard_map.109 = (bf16[16,10,640]{2,1,0:T(8,128)(2,1)}, f32[20,128]{1,0:T(8,128)}) custom-call(s32[4]{0:T(128)} %pad_add_fusion.own_ref, s32[2,64]{1,0:T(2,128)} %bitcast.50, f32[2,64]{1,0:T(2,128)} %bitcast.51, bf16[64,512]{1,0:T(8,128)(2,1)} %refs_2_.1, bf16[32,512]{1,0:T(8,128)(2,1)} %refs_3_.1, bf16[32,512]{1,0:T(8,128)(2,1)} %refs_4_.1, f32[1,512]{1,0:T(1,128)} %bitcast.49), custom_call_target="tpu_custom_call" | custom-call | flops 10485760 | bytes 270336 | tf_op jit(solution)/shard_map/pallas_call | solution.py:138
  3.6 10.2 %all-to-all-start = ((bf16[16,10,640]{2,1,0:T(8,128)(2,1)}), bf16[16,10,640]{2,1,0:T(8,128)(2,1)S(1)}, u32[]{:S(2)}, u32[]{:S(2)}) async-start(bf16[16,10,640]{2,1,0:T(8,128)(2,1)} %get-tuple-element.15), calls=%async_computation | async-start | bytes 655360 | tf_op jit(solution)/shard_map/all_to_all | solution.py:31
  13.8 1.9 %collective-permute-start = (bf16[4096,128]{1,0:T(8,128)(2,1)}, bf16[4096,128]{1,0:T(8,128)(2,1)S(1)}, u32[]{:S(2)}, u32[]{:S(2)}) collective-permute-start(bf16[4096,128]{1,0:T(8,128)(2,1)} %bitcast.41), channel_id=1, source_target_pairs={{0,1},{1,0},{2,3},{3,2},{4,5},{5,4},{6,7},{7,6},{8,9},{9,8},{10,11... | collective-permute-start | bytes 3145736 | tf_op jit(solution)/shard_map/ppermute | solution.py:420
  15.7 3.4 %collective-permute-start.1 = (bf16[4096,128]{1,0:T(8,128)(2,1)}, bf16[4096,128]{1,0:T(8,128)(2,1)}, u32[]{:S(2)}, u32[]{:S(2)}) collective-permute-start(bf16[4096,128]{1,0:T(8,128)(2,1)} %bitcast.43), channel_id=1, source_target_pairs={{0,1},{1,0},{2,3},{3,2},{4,5},{5,4},{6,7},{7,6},{8,9},{9,8},{10,11... | collective-permute-start | bytes 3145736 | tf_op jit(solution)/shard_map/ppermute | solution.py:420
  19.8 0.1 stack.36.own_ref
  19.9 3.1 %all-to-all-done.received_ref = bf16[16,10,640]{2,1,0:T(8,128)(2,1)S(1)} async-done(((bf16[16,10,640]{2,1,0:T(8,128)(2,1)}), bf16[16,10,640]{2,1,0:T(8,128)(2,1)S(1)}, u32[]{:S(2)}, u32[]{:S(2)}) %all-to-all-start) | async-done | bytes 204832 | tf_op jit(solution)/shard_map/all_to_all | solution.py:31
  23.1 0.0 copy-start.3
  23.1 0.7 copy-done.3
  23.8 0.2 shard_map.110
  24.0 45.4 %all-gather.4 = f16[1280,1152]{1,0:T(8,128)(2,1)S(1)} all-gather(f16[40,1152]{1,0:T(8,128)(2,1)S(1)} %convert_element_type.42), channel_id=2, replica_groups=mesh['z'=16,'c'=2,'y'=4,'h'=2,'t'=2] {'z','c'}, dimensions={0}, use_global_device_ids=true | all-gather | bytes 3041280 | tf_op jit(solution)/shard_map/all_gather | solution.py:425
  69.4 0.0 copy-start.1
  69.4 0.0 copy-start.2
  69.4 0.4 convert_element_type.54.x_ref
  69.8 0.0 collective-permute-done.far_gate_ref
  69.8 0.0 collective-permute-done.1.far_up_ref
  69.8 0.8 copy-done.1
  70.6 0.3 copy-done.2
  70.9 3.9 %shard_map.111 = (f32[640,128]{1,0:T(8,128)S(1)}, f32[320,128]{1,0:T(8,128)S(1)}, f32[320,128]{1,0:T(8,128)S(1)}, f32[16,8,128]{2,1,0:T(8,128)S(1)}) custom-call(s32[6]{0:T(128)S(1)} %stack.36.own_ref, bf16[1280,1152]{1,0:T(8,128)(2,1)S(1)} %convert_element_type.54.x_ref, bf16[4096,128]{1,0:T(8,128)(2,1)S(1)} %bitcast.42, bf16[4096,128]{1,0:T(8,128)(2,1)S(1)} %bitcast.44, ...), custom_call_target="tpu_custom_call" | custom-call | flops 1342177280 | bytes 3670016 | tf_op jit(solution)/shard_map/pallas_call | solution.py:349
  74.9 46.5 %all-gather.5 = f16[20480,128]{1,0:T(8,128)(2,1)S(1)} all-gather(f16[640,128]{1,0:T(8,128)(2,1)S(1)} %convert_element_type.51), channel_id=3, replica_groups=mesh['z'=16,'c'=2,'y'=4,'h'=2,'t'=2] {'z','c'}, dimensions={0}, use_global_device_ids=true | all-gather | bytes 5406720 | tf_op jit(solution)/shard_map/all_gather | solution.py:448
  121.3 0.6 convert_element_type.55
  122.0 0.0 copy-done
  122.0 1.5 convolution_bitcast_fusion
  123.5 0.7 reshape.109
  124.2 6.7 %all-to-all-start.1 = ((f32[16,20,128]{2,1,0:T(8,128)}), f32[16,20,128]{2,1,0:T(8,128)S(1)}, u32[]{:S(2)}, u32[]{:S(2)}) async-start(f32[16,20,128]{2,1,0:T(8,128)} %reshape.109), calls=%async_computation.1 | async-start | bytes 393216 | tf_op jit(solution)/shard_map/all_to_all | solution.py:31
  130.9 0.2 add_select_fusion
  131.2 0.1 broadcast_compare_fusion
  131.3 7.3 %all-to-all-done.1 = f32[16,20,128]{2,1,0:T(8,128)S(1)} async-done(((f32[16,20,128]{2,1,0:T(8,128)}), f32[16,20,128]{2,1,0:T(8,128)S(1)}, u32[]{:S(2)}, u32[]{:S(2)}) %all-to-all-start.1) | async-done | bytes 163872 | tf_op jit(solution)/shard_map/all_to_all | solution.py:31
  138.6 0.4 multiply_reduce_fusion
  139.0 0.6 broadcast_in_dim.42
  139.6 8.4 %all-to-all-start.2 = ((f32[32,1,128]{2,1,0:T(1,128)}), f32[32,1,128]{2,1,0:T(1,128)S(1)}, u32[]{:S(2)}, u32[]{:S(2)}) async-start(f32[32,1,128]{2,1,0:T(1,128)} %broadcast_in_dim.42), calls=%async_computation.2 | async-start | bytes 32768 | tf_op jit(solution)/shard_map/all_to_all | solution.py:31
  148.7 11.1 %all-to-all-done.2 = f32[32,1,128]{2,1,0:T(1,128)S(1)} async-done(((f32[32,1,128]{2,1,0:T(1,128)}), f32[32,1,128]{2,1,0:T(1,128)S(1)}, u32[]{:S(2)}, u32[]{:S(2)}) %all-to-all-start.2) | async-done | bytes 16416 | tf_op jit(solution)/shard_map/all_to_all | solution.py:31
  159.8 0.2 fusion
  159.9 0.1 broadcast_in_dim.45
  160.0 9.1 %all_to_all.25 = f32[16,1,128]{2,1,0:T(1,128)S(1)} all-to-all(f32[16,1,128]{2,1,0:T(1,128)S(1)} %broadcast_in_dim.45), channel_id=1, replica_groups=mesh['z'=16,'c'=2,'y'=4,'h'=2,'t'=2] {'y','h','t'}, dimensions={0} | all-to-all | bytes 16384 | tf_op jit(solution)/shard_map/all_to_all | solution.py:31
  169.1 16.8 %all_to_all.26 = f32[32,1,128]{2,1,0:T(1,128)S(1)} all-to-all(f32[32,1,128]{2,1,0:T(1,128)S(1)} %broadcast_in_dim.46), channel_id=1, replica_groups=mesh['z'=16,'c'=2,'y'=4,'h'=2,'t'=2] {'z','c'}, dimensions={0} | all-to-all | bytes 32768 | tf_op jit(solution)/shard_map/all_to_all | solution.py:31
  186.0 0.6 multiply_reduce_fusion.1
  187.3 0.6 multiply_bitcast_fusion
  (13 shorter events, 0.2 us)
Async XLA Ops:
  0.0 122.0 %copy-start = (bf16[1,8192,128]{2,1,0:T(8,128)(2,1)S(1)}, bf16[1,8192,128]{2,1,0:T(8,128)(2,1)}, u32[]{:S(2)}) copy-start(bf16[1,8192,128]{2,1,0:T(8,128)(2,1)} %param.16) | copy-start | bytes 6291460
  3.6 19.5 %all-to-all-start = ((bf16[16,10,640]{2,1,0:T(8,128)(2,1)}), bf16[16,10,640]{2,1,0:T(8,128)(2,1)S(1)}, u32[]{:S(2)}, u32[]{:S(2)}) async-start(bf16[16,10,640]{2,1,0:T(8,128)(2,1)} %get-tuple-element.15), calls=%async_computation | async-start | bytes 655360 | tf_op jit(solution)/shard_map/all_to_all | solution.py:31
  13.8 56.0 %collective-permute-start = (bf16[4096,128]{1,0:T(8,128)(2,1)}, bf16[4096,128]{1,0:T(8,128)(2,1)S(1)}, u32[]{:S(2)}, u32[]{:S(2)}) collective-permute-start(bf16[4096,128]{1,0:T(8,128)(2,1)} %bitcast.41), channel_id=1, source_target_pairs={{0,1},{1,0},{2,3},{3,2},{4,5},{5,4},{6,7},{7,6},{8,9},{9,8},{10,11... | collective-permute-start | bytes 3145736 | tf_op jit(solution)/shard_map/ppermute | solution.py:420
  15.7 54.1 %collective-permute-start.1 = (bf16[4096,128]{1,0:T(8,128)(2,1)}, bf16[4096,128]{1,0:T(8,128)(2,1)}, u32[]{:S(2)}, u32[]{:S(2)}) collective-permute-start(bf16[4096,128]{1,0:T(8,128)(2,1)} %bitcast.43), channel_id=1, source_target_pairs={{0,1},{1,0},{2,3},{3,2},{4,5},{5,4},{6,7},{7,6},{8,9},{9,8},{10,11... | collective-permute-start | bytes 3145736 | tf_op jit(solution)/shard_map/ppermute | solution.py:420
  23.1 0.7 copy-start.3
  69.4 1.2 copy-start.1
  69.4 1.5 copy-start.2
  124.2 14.4 %all-to-all-start.1 = ((f32[16,20,128]{2,1,0:T(8,128)}), f32[16,20,128]{2,1,0:T(8,128)S(1)}, u32[]{:S(2)}, u32[]{:S(2)}) async-start(f32[16,20,128]{2,1,0:T(8,128)} %reshape.109), calls=%async_computation.1 | async-start | bytes 393216 | tf_op jit(solution)/shard_map/all_to_all | solution.py:31
  139.6 20.1 %all-to-all-start.2 = ((f32[32,1,128]{2,1,0:T(1,128)}), f32[32,1,128]{2,1,0:T(1,128)S(1)}, u32[]{:S(2)}, u32[]{:S(2)}) async-start(f32[32,1,128]{2,1,0:T(1,128)} %broadcast_in_dim.42), calls=%async_computation.2 | async-start | bytes 32768 | tf_op jit(solution)/shard_map/all_to_all | solution.py:31

commit v11 on v10

--- a/solution.py
+++ b/solution.py
@@ -61,8 +61,9 @@
     return (lax.broadcasted_iota(jnp.int32, shape, 1) // block).astype(F32)
 
 
-def dispatch_kernel(own_ref, *refs):
+def dispatch_kernel(*refs):
     out_ref, note_ref, held, sem = refs[6], refs[7], refs[8:14], refs[14]
+    core, chip = lax.axis_index("c"), lax.axis_index("z")
     copies = [pltpu.make_async_copy(refs[k], held[k], sem.at[k]) for k in range(6)]
     for copy in copies:
         copy.start()
@@ -74,8 +75,7 @@
     rows, feats = tokens_ref.shape
     half = feats // HALVES
     ranks = down_ref.shape[0] // HALVES
-    core = own_ref[0]
-    first_slot = (own_ref[3] * set_slots).astype(F32)
+    first_slot = (lax.axis_index("t") * set_slots).astype(F32)
     ids = routes_ref[...]
     notes = jnp.concatenate([ids.astype(F32)] + list(rounded_parts(chosen_ref[...])), axis=0)
     notes = jnp.concatenate([jnp.where(core == k, notes, 0.0) for k in range(HALVES)], axis=1)
@@ -101,7 +101,7 @@
         third = (rest - second.astype(F32)).astype(BF16)
         x = jnp.concatenate([x, jnp.zeros_like(first), first, second, third], axis=1)
         chosen = jnp.dot(chooser, x, preferred_element_type=F32)
-        column = pl.multiple_of(own_ref[1 + c], LANES)
+        column = pl.multiple_of((chip * HALVES + c) % (feats // LANES) * LANES, LANES)
         norm = norm_ref[:, pl.ds(column, LANES)]
         norm_first = norm.astype(BF16).astype(F32)
         norm_rest = norm - norm_first
@@ -130,7 +130,7 @@
 
 
 def dispatch_layer(
-    own, routes, chosen, tokens, adapter_down, adapter_up, norm_scale, experts, set_slots
+    routes, chosen, tokens, adapter_down, adapter_up, norm_scale, experts, set_slots
 ):
     rows, feats = tokens.shape
     lanes = feats // HALVES + 3 * LANES
@@ -141,8 +141,7 @@
             jax.ShapeDtypeStruct((experts * HALVES, set_slots, lanes), BF16),
             jax.ShapeDtypeStruct((HALVES * set_slots, LANES), F32),
         ),
-        in_specs=[pl.BlockSpec(memory_space=pltpu.SMEM)]
-        + [pl.BlockSpec(memory_space=pltpu.HBM)] * len(operands),
+        in_specs=[pl.BlockSpec(memory_space=pltpu.HBM)] * len(operands),
         out_specs=(pl.BlockSpec(memory_space=pltpu.VMEM),) * 2,
         scratch_shapes=[pltpu.VMEM(x.shape, x.dtype) for x in operands]
         + [pltpu.SemaphoreType.DMA((len(operands),))],
@@ -152,10 +151,10 @@
             bytes_accessed=2 * rows * feats + 2 * experts * HALVES * set_slots * lanes,
             transcendentals=0,
         ),
-    )(own, *operands)
-
-
-def rows_kernel(own_ref, received_ref, note_ref, sent_ref, adapter_ref, norm_ref):
+    )(*operands)
+
+
+def rows_kernel(own_ref, received_ref, sent_ref, adapter_ref, norm_ref):
     messages, set_slots, _ = received_ref.shape
     groups = messages // HALVES
     half = 2 * LANES
@@ -186,7 +185,7 @@
     sent_ref[pl.ds(0, rows), pl.ds(columns, LANES)] = jnp.concatenate(
         [jnp.broadcast_to(exponent, low.shape)] + list(rounded_parts(low)), axis=1
     )
-    sent_ref[pl.ds(rows, rows), pl.ds(columns, LANES)] = note_ref[...]
+    sent_ref[pl.ds(rows, rows), pl.ds(columns, LANES)] = jnp.zeros((rows, LANES), F32)
 
     adapter = []
     for c in range(HALVES):
@@ -201,7 +200,7 @@
     adapter_ref[...] = jnp.concatenate(adapter, axis=0).astype(BF16)
 
 
-def rows_layer(own_group, received, notes, task_rows):
+def rows_layer(own_group, received, task_rows):
     messages, set_slots, _ = received.shape
     rows = HALVES * set_slots
     vmem = pl.BlockSpec(memory_space=pltpu.VMEM)
@@ -213,24 +212,75 @@
             jax.ShapeDtypeStruct((task_rows, LANES), BF16),
             jax.ShapeDtypeStruct((1, LANES), F32),
         ),
-        in_specs=[pl.BlockSpec(memory_space=pltpu.SMEM), vmem, vmem],
+        in_specs=[pl.BlockSpec(memory_space=pltpu.SMEM), vmem],
         out_specs=(vmem, vmem, vmem),
-        compiler_params=pltpu.CompilerParams(vmem_limit_bytes=16 * 2**20),
+        compiler_params=pltpu.CompilerParams(vmem_limit_bytes=8 * 2**20),
         cost_estimate=pl.CostEstimate(
             flops=8 * rows * columns, bytes_accessed=8 * rows * columns, transcendentals=4 * rows
         ),
-    )(own_group[None], received, notes)
-
-
-def expert_kernel(
+    )(own_group[None], received)
+
+
+class Rows:
+    def __init__(self, x_ref, shard_rows):
+        self.x_ref = x_ref
+        self.shard_rows = shard_rows
+        self.rows = shard_rows // HALVES
+        self.group = -(-self.rows // 8) * 8
+        self.chips = x_ref.shape[0] // (HALVES * shard_rows)
+        self.flat = self.chips * self.group
+        self.columns = x_ref.shape[1] - LANES
+        self.x = x_ref[:, pl.ds(0, self.columns)].astype(F32)
+        self.beside = x_ref[:, pl.ds(self.columns, LANES)].astype(F32)
+        exponents = [self.part(self.beside, c, 0)[:, :LOW_LANES] for c in range(HALVES)]
+        exponents = [jnp.concatenate([e] * (LANES // LOW_LANES), axis=1) for e in exponents]
+        self.scales = [jnp.exp2(e - 15.0) for e in exponents]
+        self.row_exponent = jnp.maximum(*exponents)
+
+    def part(self, value, c, q):
+        value = value.reshape(self.chips, HALVES, self.shard_rows, value.shape[-1])[:, c]
+        value = value[:, : self.group] if q == 0 else value[:, self.shard_rows - self.group :]
+        return value.reshape(self.flat, value.shape[-1])
+
+    def aligned(self, value, q):
+        return value if q == 0 else pltpu.roll(value, self.flat - (self.group - self.rows), 0)
+
+    def hidden(self, weight_ref, gate_ref, up_ref):
+        units = gate_ref.shape[1]
+        half = 2 * LANES
+        blocks = self.columns // half
+        acts = jnp.zeros((self.flat, 2 * units), F32)
+        for c in range(HALVES):
+            half_acts = jnp.zeros((self.flat, 2 * units), F32)
+            for q in range(HALVES):
+                for n in range(blocks):
+                    source = pl.ds(((q * blocks + n) * HALVES + c) * half, half)
+                    target = pl.ds(n * half, half)
+                    for k, ref in enumerate((gate_ref, up_ref)):
+                        weight_ref[c * HALVES + q, target, pl.ds(k * units, units)] = ref[source, :]
+                product = jnp.dot(
+                    self.part(self.x, c, q).astype(BF16),
+                    weight_ref[c * HALVES + q],
+                    preferred_element_type=F32,
+                )
+                half_acts += self.aligned(product, q)
+            acts += half_acts * jnp.concatenate([self.scales[c]] * 2, axis=1)
+        gate_act, up_act = acts[:, :units], acts[:, units:]
+        value = (gate_act / (1.0 + jnp.exp(-gate_act)) * up_act).astype(BF16).astype(F32)
+        return value * jnp.exp2(-2.0 * self.row_exponent - 2.0)
+
+    def of_chip(self, chip):
+        source = slice(chip * self.group, chip * self.group + self.rows)
+        return source, pl.ds(chip * self.rows, self.rows)
+
+
+def near_kernel(
     shard_rows,
     block,
     own_ref,
     x_ref,
     gate_ref,
     up_ref,
-    far_gate_ref,
-    far_up_ref,
     adapter_ref,
     hidden_ref,
     factor_ref,
@@ -238,132 +288,118 @@
     note_ref,
     weight_ref,
 ):
-    quarters, columns, _ = weight_ref.shape
-    units = gate_ref.shape[1]
+    r = Rows(x_ref, shard_rows)
     task_rows = adapter_ref.shape[0]
-    half = 2 * LANES
-    blocks = columns // half
-    for c in range(HALVES):
-        for q in range(HALVES):
-            for n in range(blocks):
-                source = pl.ds(((q * blocks + n) * HALVES + c) * half, half)
-                target = pl.ds(n * half, half)
-                for k, ref in enumerate((gate_ref, up_ref, far_gate_ref, far_up_ref)):
-                    weight_ref[c * HALVES + q, target, pl.ds(k * units, units)] = ref[source, :]
-    rows = shard_rows // HALVES
-    group = -(-rows // 8) * 8
-    chips = x_ref.shape[0] // (HALVES * shard_rows)
-    flat = chips * group
     own_core, own_quarter = own_ref[0], own_ref[1]
     own_column = pl.multiple_of(own_ref[2], LANES)
-    task = own_ref[3]
-    tensor = own_ref[4]
-
-    def part(value, c, q):
-        value = value.reshape(chips, HALVES, shard_rows, value.shape[-1])[:, c]
-        value = value[:, :group] if q == 0 else value[:, shard_rows - group :]
-        return value.reshape(flat, value.shape[-1])
-
-    def aligned(value, q):
-        return value if q == 0 else pltpu.roll(value, flat - (group - rows), 0)
-
-    x = x_ref[:, pl.ds(0, columns)].astype(F32)
+    task, tensor, expert = own_ref[3], own_ref[4], own_ref[5]
+    hidden = r.hidden(weight_ref, gate_ref, up_ref)
+
     own = x_ref[:, pl.ds(own_column, LANES)].astype(F32)
-    beside = x_ref[:, pl.ds(columns, LANES)].astype(F32)
-    acts = jnp.zeros((flat, 4 * units), F32)
-    low = jnp.zeros((flat, LOW_LANES), F32)
-    residual = jnp.zeros((flat, units), F32)
-    row_exponent = None
+    low = jnp.zeros((r.flat, LOW_LANES), F32)
+    residual = jnp.zeros((r.flat, LANES), F32)
     for c in range(HALVES):
-        tile = part(beside, c, 0)
-        exponent = tile[:, :LOW_LANES]
+        tile = r.part(r.beside, c, 0)
         low_part = tile[:, LOW_LANES : 2 * LOW_LANES] + (
             tile[:, 2 * LOW_LANES : 3 * LOW_LANES] + tile[:, 3 * LOW_LANES :] / PART_STEP
         ) / PART_STEP
-        low += low_part * jnp.exp2(exponent - 7.0)
-        exponent = jnp.concatenate([exponent] * (LANES // LOW_LANES), axis=1)
-        scale = jnp.exp2(exponent - 15.0)
-        row_exponent = exponent if c == 0 else jnp.maximum(row_exponent, exponent)
-        half_acts = jnp.zeros((flat, 4 * units), F32)
+        low += low_part * jnp.exp2(tile[:, :LOW_LANES] - 7.0)
         for q in range(HALVES):
-            product = jnp.dot(
-                part(x, c, q).astype(BF16),
-                weight_ref[c * HALVES + q],
-                preferred_element_type=F32,
-            )
-            half_acts += aligned(product, q)
             mine = (own_core == c) & (own_quarter == q)
-            residual += jnp.where(mine, aligned(part(own, c, q), q) * scale, 0.0)
-        acts += half_acts * jnp.concatenate([scale] * 4, axis=1)
+            residual += jnp.where(mine, r.aligned(r.part(own, c, q), q) * r.scales[c], 0.0)
     low_lane = lax.broadcasted_iota(jnp.int32, low.shape, 1) // (task_rows // TASK_COUNT)
     low = jnp.where(low_lane == task, low, 0.0).astype(BF16)
     base = residual + ADAPTER_SCALE * jnp.dot(
         low, adapter_ref[...], preferred_element_type=F32
     )
-    down_scale = jnp.exp2(-2.0 * row_exponent - 2.0)
-    up_scale = jnp.exp2(2.0 * row_exponent + 2.0)
-
-    notes = sum(aligned(part(beside, c, 1), 1) for c in range(HALVES))
-    notes = notes.reshape(chips, group, LANES)[:, :NOTE_ROWS]
+    up_scale = jnp.exp2(2.0 * r.row_exponent + 2.0)
+
+    notes = sum(r.aligned(r.part(r.beside, c, 1), 1) for c in range(HALVES))
+    notes = notes.reshape(r.chips, r.group, LANES)[:, :NOTE_ROWS]
     note_ref[...] = notes
     first, second = notes[:, 0, :].astype(jnp.int32), notes[:, 1, :].astype(jnp.int32)
     weight = [
         notes[:, k + 2, :] + (notes[:, k + 4, :] + notes[:, k + 6, :] / PART_STEP) / PART_STEP
         for k in range(2)
     ]
-    expert = own_ref[5]
-    set_slots = rows // HALVES
+    set_slots = r.rows // HALVES
     slot = slots_of((first == expert) | (second == expert), block)
     slot = slot - (tensor * set_slots).astype(F32)
     in_set = (slot >= 0.0) & (slot < set_slots)
     place = jnp.where(in_set, slot + set_slots * block_of(slot.shape, block), -1.0)
     weight = jnp.where(first == expert, weight[0], weight[1])
-    row = lax.broadcasted_iota(jnp.int32, (group, LANES), 0).astype(F32)
-
-    def hidden(gate_act, up_act):
-        value = (gate_act / (1.0 + jnp.exp(-gate_act)) * up_act).astype(BF16).astype(F32)
-        return value * down_scale
-
-    near = hidden(acts[:, :units], acts[:, units : 2 * units])
-    far = hidden(acts[:, 2 * units : 3 * units], acts[:, 3 * units :])
-    pair = (jnp.where(tensor == 0, near, far), jnp.where(tensor == 0, far, near))
-    for chip in range(chips):
-        source = slice(chip * group, chip * group + rows)
-        for k in range(2):
-            hidden_ref[pl.ds((k * chips + chip) * rows, rows), :] = pair[k][source]
+    row = lax.broadcasted_iota(jnp.int32, (r.group, LANES), 0).astype(F32)
+    for chip in range(r.chips):
+        source, target = r.of_chip(chip)
         slot_weight = jnp.sum(
             jnp.where(place[chip : chip + 1] == row, weight[chip : chip + 1], 0.0),
             axis=1,
             keepdims=True,
-        )[:rows]
-        factor_ref[pl.ds(chip * rows, rows), :] = slot_weight * up_scale[source]
-        base_ref[pl.ds(chip * rows, rows), :] = 0.5 * base[source]
-
-
-def expert_layer(gathered, weights, adapter_up, own, shard_rows, block):
+        )[: r.rows]
+        hidden_ref[target, :] = hidden[source]
+        factor_ref[target, :] = slot_weight * up_scale[source]
+        base_ref[target, :] = 0.5 * base[source]
+
+
+def far_kernel(
+    shard_rows, own_ref, x_ref, gate_ref, up_ref, near_ref, hidden_ref, weight_ref
+):
+    r = Rows(x_ref, shard_rows)
+    far = r.hidden(weight_ref, gate_ref, up_ref)
+    slots = r.chips * r.rows
+    near_at = own_ref[0] * slots
+    far_at = slots - near_at
+    hidden_ref[pl.ds(pl.multiple_of(near_at, 8), slots), :] = near_ref[...]
+    for chip in range(0, r.chips, 2):
+        one, two = r.of_chip(chip)[0], r.of_chip(chip + 1)[0]
+        start = pl.multiple_of(far_at + chip * r.rows, 8)
+        hidden_ref[pl.ds(start, 2 * r.rows), :] = jnp.concatenate([far[one], far[two]], axis=0)
+
+
+def near_layer(gathered, weights, adapter_up, own, shard_rows, block):
     rows = gathered.shape[0]
     columns = gathered.shape[1] - LANES
     units = weights[0].shape[1]
     out = jax.ShapeDtypeStruct((rows // 4, units), F32)
     vmem = pl.BlockSpec(memory_space=pltpu.VMEM)
     return pl.pallas_call(
-        functools.partial(expert_kernel, shard_rows, block),
+        functools.partial(near_kernel, shard_rows, block),
         out_shape=(
-            jax.ShapeDtypeStruct((rows // 2, units), F32),
+            out,
             out,
             out,
             jax.ShapeDtypeStruct((rows // (2 * shard_rows), NOTE_ROWS, LANES), F32),
         ),
-        in_specs=[pl.BlockSpec(memory_space=pltpu.SMEM)] + [vmem] * 6,
+        in_specs=[pl.BlockSpec(memory_space=pltpu.SMEM)] + [vmem] * 4,
         out_specs=(vmem, vmem, vmem, vmem),
-        scratch_shapes=[pltpu.VMEM((2 * HALVES, columns, 4 * units), BF16)],
-        compiler_params=pltpu.CompilerParams(vmem_limit_bytes=32 * 2**20),
+        scratch_shapes=[pltpu.VMEM((2 * HALVES, columns, 2 * units), BF16)],
+        compiler_params=pltpu.CompilerParams(vmem_limit_bytes=24 * 2**20),
         cost_estimate=pl.CostEstimate(
-            flops=8 * rows * columns * units,
-            bytes_accessed=2 * rows * columns + 8 * columns * units,
+            flops=4 * rows * columns * units,
+            bytes_accessed=2 * rows * columns + 4 * columns * units,
             transcendentals=2 * rows * units,
         ),
     )(own, gathered, *weights, adapter_up)
+
+
+def far_layer(gathered, weights, near, tensor, shard_rows):
+    rows = gathered.shape[0]
+    columns = gathered.shape[1] - LANES
+    units = weights[0].shape[1]
+    vmem = pl.BlockSpec(memory_space=pltpu.VMEM)
+    return pl.pallas_call(
+        functools.partial(far_kernel, shard_rows),
+        out_shape=jax.ShapeDtypeStruct((rows // 2, units), F32),
+        in_specs=[pl.BlockSpec(memory_space=pltpu.SMEM)] + [vmem] * 4,
+        out_specs=vmem,
+        scratch_shapes=[pltpu.VMEM((2 * HALVES, columns, 2 * units), BF16)],
+        compiler_params=pltpu.CompilerParams(vmem_limit_bytes=24 * 2**20),
+        cost_estimate=pl.CostEstimate(
+            flops=4 * rows * columns * units,
+            bytes_accessed=2 * rows * columns + 4 * columns * units,
+            transcendentals=2 * rows * units,
+        ),
+    )(tensor[None], gathered, *weights, near)
 
 
 def local(
@@ -400,12 +436,8 @@
     per_feature_group = feats // slice_width
     own_group = s // per_feature_group
 
-    core = lax.axis_index("c")
     ids = routes.T
     outgoing, notes = dispatch_layer(
-        jnp.stack(
-            [core] + [(s - core + k) % per_feature_group * slice_width for k in range(cores)] + [t]
-        ),
         ids,
         chosen_expert_weight.T,
         tokens,
@@ -420,15 +452,15 @@
     far_weights = [lax.ppermute(w, "t", other) for w in (expert_gate_weight[0], later_up)]
     received = swap(outgoing, EXPERT + ("c",))
 
-    sent, adapter_up, norm_scale = rows_layer(own_group, received, notes, task_rows)
-    sent = sent.astype(F16)
+    sent, adapter_up, norm_scale = rows_layer(own_group, received, task_rows)
+    sent = (sent + jnp.pad(notes, ((chip_rows, 0), (columns, 0)))).astype(F16)
     gathered = lax.all_gather(sent, SEQ, axis=0, tiled=False)
     gathered = gathered.astype(BF16).reshape(seq * shard_rows, columns + LANES)
     per_half = half // slice_width
     own_column = own_group * half + (s % per_half) * slice_width
-    hidden, factor, base, notes = expert_layer(
+    near, factor, base, notes = near_layer(
         gathered,
-        [expert_gate_weight[0], expert_up_weight[0]] + far_weights,
+        (expert_gate_weight[0], expert_up_weight[0]),
         adapter_up,
         jnp.stack(
             [
@@ -443,6 +475,7 @@
         shard_rows,
         rows,
     )
+    hidden = far_layer(gathered, far_weights, near, t, shard_rows)
 
     units = hidden.shape[-1]
     hidden = lax.all_gather(hidden.astype(F16), SEQ, axis=0, tiled=False)

time: 189 us -> 186 us (0.984)
    pallas_call x1 -> x2, Pallas kernels: 3.88 us -> 4.41 us  [the longest x1 2.37 us: far_layer(): pl.pallas_call(functools.partial(far_kernel, shard_rows), out_shape=jax.S...]
  transfers between devices with their start and end apart: 5 -> 5, of which waited for: 3 -> 3; matrix products, arithmetic and copies ran while one was open for 0% -> 1% of each run, Pallas kernels for 0% -> 1%
where the time goes in v11:
time: 186 us; the launch traced here: 185 us
  blocking collectives  117 us (63%)
  starting transfers between devices  29.2 us (16%)
  waiting for transfers between devices  21.8 us (12%)
  Pallas kernels  6.99 us (4%)
  other arithmetic  3.27 us (2%)
  local copies, waits for them, and re-layouts  2.52 us (1%)
  matrix products  2.3 us (1%)
  between operations  2.24 us (1%)
    all_gather x1, blocking collectives, local(): hidden = lax.all_gather(hidden.astype(F16), SEQ, axis=0, tiled=False)  45.6 us
    all_gather x1, blocking collectives, local(): gathered = lax.all_gather(sent, SEQ, axis=0, tiled=False)  45.4 us
    all_to_all x2, blocking collectives, swap(): return lax.all_to_all(x, axes, split_axis=0, concat_axis=0, tiled=True)  26 us
    all_to_all x3, starting transfers between devices, swap(): return lax.all_to_all(x, axes, split_axis=0, concat_axis=0, tiled=True)  23.9 us
    all_to_all x3, waiting for transfers between devices, swap(): return lax.all_to_all(x, axes, split_axis=0, concat_axis=0, tiled=True)  21.8 us
    ppermute x2, starting transfers between devices, local(): lax.ppermute(w, 't', other)  5.28 us
  transfers between devices with their start and end apart: 5, of which 3 were waited for; matrix products, arithmetic and copies ran while one was open for 1% of the time, Pallas kernels for 1%

profile of v11, /device:TPU:1, one launch (start us, length us, event | category | flops | bytes accessed | tf_op | source)
XLA Modules:
  0.0 185.2 jit_solution(2119026113861927313)
XLA Ops:
  0.0 0.0 copy-start
  0.0 2.4 %shard_map.109 = (bf16[16,10,640]{2,1,0:T(8,128)(2,1)}, f32[20,128]{1,0:T(8,128)}) custom-call(s32[2,64]{1,0:T(2,128)} %bitcast.51, f32[2,64]{1,0:T(2,128)} %bitcast.52, bf16[64,512]{1,0:T(8,128)(2,1)} %refs_2_.1, bf16[32,512]{1,0:T(8,128)(2,1)} %refs_3_.1, bf16[32,512]{1,0:T(8,128)(2,1)} %refs_4_.1, f32[1,512]{1,0:T(1,128)} %bitcast.50), custom_call_target="tpu_custom_call" | custom-call | flops 10485760 | bytes 270336 | tf_op jit(solution)/shard_map/pallas_call | solution.py:138
  2.4 10.2 %all-to-all-start = ((bf16[16,10,640]{2,1,0:T(8,128)(2,1)}), bf16[16,10,640]{2,1,0:T(8,128)(2,1)S(1)}, u32[]{:S(2)}, u32[]{:S(2)}) async-start(bf16[16,10,640]{2,1,0:T(8,128)(2,1)} %get-tuple-element.15), calls=%async_computation | async-start | bytes 655360 | tf_op jit(solution)/shard_map/all_to_all | solution.py:31
  12.6 1.9 %collective-permute-start = (bf16[4096,128]{1,0:T(8,128)(2,1)}, bf16[4096,128]{1,0:T(8,128)(2,1)S(1)}, u32[]{:S(2)}, u32[]{:S(2)}) collective-permute-start(bf16[4096,128]{1,0:T(8,128)(2,1)} %bitcast.42), channel_id=1, source_target_pairs={{0,1},{1,0},{2,3},{3,2},{4,5},{5,4},{6,7},{7,6},{8,9},{9,8},{10,11... | collective-permute-start | bytes 3145736 | tf_op jit(solution)/shard_map/ppermute | solution.py:452
  14.5 3.4 %collective-permute-start.1 = (bf16[4096,128]{1,0:T(8,128)(2,1)}, bf16[4096,128]{1,0:T(8,128)(2,1)}, u32[]{:S(2)}, u32[]{:S(2)}) collective-permute-start(bf16[4096,128]{1,0:T(8,128)(2,1)} %bitcast.44), channel_id=1, source_target_pairs={{0,1},{1,0},{2,3},{3,2},{4,5},{5,4},{6,7},{7,6},{8,9},{9,8},{10,11... | collective-permute-start | bytes 3145736 | tf_op jit(solution)/shard_map/ppermute | solution.py:452
  18.6 0.1 stack.23.own_ref
  18.7 3.1 %all-to-all-done.received_ref = bf16[16,10,640]{2,1,0:T(8,128)(2,1)S(1)} async-done(((bf16[16,10,640]{2,1,0:T(8,128)(2,1)}), bf16[16,10,640]{2,1,0:T(8,128)(2,1)S(1)}, u32[]{:S(2)}, u32[]{:S(2)}) %all-to-all-start) | async-done | bytes 204832 | tf_op jit(solution)/shard_map/all_to_all | solution.py:31
  21.9 0.2 shard_map.110
  22.1 0.7 add_convert_fusion
  22.8 45.4 %all-gather.4 = f16[1280,1152]{1,0:T(8,128)(2,1)S(1)} all-gather(f16[40,1152]{1,0:T(8,128)(2,1)S(1)} %add_convert_fusion), channel_id=2, replica_groups=mesh['z'=16,'c'=2,'y'=4,'h'=2,'t'=2] {'z','c'}, dimensions={0}, use_global_device_ids=true | all-gather | bytes 3041280 | tf_op jit(solution)/shard_map/all_gather | solution.py:457
  68.2 0.0 copy-start.1
  68.2 0.0 copy-start.2
  68.2 0.5 convert_element_type.56.x_ref
  68.7 0.7 copy-done.1
  69.4 0.3 copy-done.2
  69.7 2.0 %shard_map.111 = (f32[320,128]{1,0:T(8,128)S(1)}, f32[320,128]{1,0:T(8,128)S(1)}, f32[320,128]{1,0:T(8,128)S(1)}, f32[16,8,128]{2,1,0:T(8,128)S(1)}) custom-call(s32[6]{0:T(128)S(1)} %stack.23.own_ref, bf16[1280,1152]{1,0:T(8,128)(2,1)S(1)} %convert_element_type.56.x_ref, bf16[4096,128]{1,0:T(8,128)(2,1)S(1)} %bitcast.43, bf16[4096,128]{1,0:T(8,128)(2,1)S(1)} %bitcast.45, ...), custom_call_target="tpu_custom_call" | custom-call | flops 671088640 | bytes 3145728 | tf_op jit(solution)/shard_map/pallas_call | solution.py:365
  71.8 0.2 add_select_fusion
  72.0 0.0 collective-permute-done.gate_ref
  72.0 0.0 collective-permute-done.1.up_ref
  72.1 2.4 %shard_map.112 = f32[640,128]{1,0:T(8,128)S(1)} custom-call(s32[1]{0:T(128)} %bitcast.4.own_ref, bf16[1280,1152]{1,0:T(8,128)(2,1)S(1)} %convert_element_type.56.x_ref, bf16[4096,128]{1,0:T(8,128)(2,1)S(1)} %collective-permute-done.gate_ref, bf16[4096,128]{1,0:T(8,128)(2,1)} %collective-permute-done.1.up_ref, f32[320,128]{1,0:T(8,128)S(1)} %get-tuple-element.21.near_ref), custom_call_target="tpu_custom_call" | custom-call | flops 671088640 | bytes 3145728 | tf_op jit(solution)/shard_map/pallas_call | solution.py:390
  74.5 45.6 %all-gather.5 = f16[20480,128]{1,0:T(8,128)(2,1)S(1)} all-gather(f16[640,128]{1,0:T(8,128)(2,1)S(1)} %convert_element_type.53), channel_id=3, replica_groups=mesh['z'=16,'c'=2,'y'=4,'h'=2,'t'=2] {'z','c'}, dimensions={0}, use_global_device_ids=true | all-gather | bytes 5406720 | tf_op jit(solution)/shard_map/all_gather | solution.py:481
  120.0 0.6 convert_element_type.57
  120.6 0.0 copy-done
  120.6 1.5 fusion.1
  122.2 0.7 reshape.109
  122.9 5.3 %all-to-all-start.1 = ((f32[16,20,128]{2,1,0:T(8,128)}), f32[16,20,128]{2,1,0:T(8,128)S(1)}, u32[]{:S(2)}, u32[]{:S(2)}) async-start(f32[16,20,128]{2,1,0:T(8,128)} %reshape.109), calls=%async_computation.1 | async-start | bytes 393216 | tf_op jit(solution)/shard_map/all_to_all | solution.py:31
  128.2 0.1 broadcast_compare_fusion
  128.3 7.6 %all-to-all-done.1 = f32[16,20,128]{2,1,0:T(8,128)S(1)} async-done(((f32[16,20,128]{2,1,0:T(8,128)}), f32[16,20,128]{2,1,0:T(8,128)S(1)}, u32[]{:S(2)}, u32[]{:S(2)}) %all-to-all-start.1) | async-done | bytes 163872 | tf_op jit(solution)/shard_map/all_to_all | solution.py:31
  135.8 0.4 multiply_reduce_fusion
  136.2 0.6 broadcast_in_dim.43
  136.8 8.4 %all-to-all-start.2 = ((f32[32,1,128]{2,1,0:T(1,128)}), f32[32,1,128]{2,1,0:T(1,128)S(1)}, u32[]{:S(2)}, u32[]{:S(2)}) async-start(f32[32,1,128]{2,1,0:T(1,128)} %broadcast_in_dim.43), calls=%async_computation.2 | async-start | bytes 32768 | tf_op jit(solution)/shard_map/all_to_all | solution.py:31
  145.9 11.1 %all-to-all-done.2 = f32[32,1,128]{2,1,0:T(1,128)S(1)} async-done(((f32[32,1,128]{2,1,0:T(1,128)}), f32[32,1,128]{2,1,0:T(1,128)S(1)}, u32[]{:S(2)}, u32[]{:S(2)}) %all-to-all-start.2) | async-done | bytes 16416 | tf_op jit(solution)/shard_map/all_to_all | solution.py:31
  157.0 0.2 fusion.2
  157.2 0.1 broadcast_in_dim.46
  157.2 9.1 %all_to_all.25 = f32[16,1,128]{2,1,0:T(1,128)S(1)} all-to-all(f32[16,1,128]{2,1,0:T(1,128)S(1)} %broadcast_in_dim.46), channel_id=1, replica_groups=mesh['z'=16,'c'=2,'y'=4,'h'=2,'t'=2] {'y','h','t'}, dimensions={0} | all-to-all | bytes 16384 | tf_op jit(solution)/shard_map/all_to_all | solution.py:31
  166.4 16.8 %all_to_all.26 = f32[32,1,128]{2,1,0:T(1,128)S(1)} all-to-all(f32[32,1,128]{2,1,0:T(1,128)S(1)} %broadcast_in_dim.47), channel_id=1, replica_groups=mesh['z'=16,'c'=2,'y'=4,'h'=2,'t'=2] {'z','c'}, dimensions={0} | all-to-all | bytes 32768 | tf_op jit(solution)/shard_map/all_to_all | solution.py:31
  183.2 0.6 multiply_reduce_fusion.1
  184.5 0.6 multiply_bitcast_fusion
  (11 shorter events, 0.1 us)
Async XLA Ops:
  0.0 120.6 %copy-start = (bf16[1,8192,128]{2,1,0:T(8,128)(2,1)S(1)}, bf16[1,8192,128]{2,1,0:T(8,128)(2,1)}, u32[]{:S(2)}) copy-start(bf16[1,8192,128]{2,1,0:T(8,128)(2,1)} %param.16) | copy-start | bytes 6291460
  2.4 19.5 %all-to-all-start = ((bf16[16,10,640]{2,1,0:T(8,128)(2,1)}), bf16[16,10,640]{2,1,0:T(8,128)(2,1)S(1)}, u32[]{:S(2)}, u32[]{:S(2)}) async-start(bf16[16,10,640]{2,1,0:T(8,128)(2,1)} %get-tuple-element.15), calls=%async_computation | async-start | bytes 655360 | tf_op jit(solution)/shard_map/all_to_all | solution.py:31
  12.6 59.4 %collective-permute-start = (bf16[4096,128]{1,0:T(8,128)(2,1)}, bf16[4096,128]{1,0:T(8,128)(2,1)S(1)}, u32[]{:S(2)}, u32[]{:S(2)}) collective-permute-start(bf16[4096,128]{1,0:T(8,128)(2,1)} %bitcast.42), channel_id=1, source_target_pairs={{0,1},{1,0},{2,3},{3,2},{4,5},{5,4},{6,7},{7,6},{8,9},{9,8},{10,11... | collective-permute-start | bytes 3145736 | tf_op jit(solution)/shard_map/ppermute | solution.py:452
  14.5 57.5 %collective-permute-start.1 = (bf16[4096,128]{1,0:T(8,128)(2,1)}, bf16[4096,128]{1,0:T(8,128)(2,1)}, u32[]{:S(2)}, u32[]{:S(2)}) collective-permute-start(bf16[4096,128]{1,0:T(8,128)(2,1)} %bitcast.44), channel_id=1, source_target_pairs={{0,1},{1,0},{2,3},{3,2},{4,5},{5,4},{6,7},{7,6},{8,9},{9,8},{10,11... | collective-permute-start | bytes 3145736 | tf_op jit(solution)/shard_map/ppermute | solution.py:452
  68.2 1.2 copy-start.1
  68.2 1.5 copy-start.2
  122.9 13.0 %all-to-all-start.1 = ((f32[16,20,128]{2,1,0:T(8,128)}), f32[16,20,128]{2,1,0:T(8,128)S(1)}, u32[]{:S(2)}, u32[]{:S(2)}) async-start(f32[16,20,128]{2,1,0:T(8,128)} %reshape.109), calls=%async_computation.1 | async-start | bytes 393216 | tf_op jit(solution)/shard_map/all_to_all | solution.py:31
  136.8 20.1 %all-to-all-start.2 = ((f32[32,1,128]{2,1,0:T(1,128)}), f32[32,1,128]{2,1,0:T(1,128)S(1)}, u32[]{:S(2)}, u32[]{:S(2)}) async-start(f32[32,1,128]{2,1,0:T(1,128)} %broadcast_in_dim.43), calls=%async_computation.2 | async-start | bytes 32768 | tf_op jit(solution)/shard_map/all_to_all | solution.py:31

commit v12 on v11

--- a/solution.py
+++ b/solution.py
@@ -402,6 +402,25 @@
     )(tensor[None], gathered, *weights, near)
 
 
+def norm_kernel(x_ref, out_ref):
+    x = x_ref[...]
+    mean = jnp.sum(jnp.sum(x * x, axis=0, keepdims=True), axis=1, keepdims=True) / x.size
+    x = x * lax.rsqrt(mean + 1e-06)
+    for k in range(x.shape[0]):
+        out_ref[:, pl.ds(k * LANES, LANES)] = x[k : k + 1, :]
+
+
+def norm_layer(pooled):
+    vmem = pl.BlockSpec(memory_space=pltpu.VMEM)
+    return pl.pallas_call(
+        norm_kernel,
+        out_shape=jax.ShapeDtypeStruct((1, pooled.size), F32),
+        in_specs=[vmem],
+        out_specs=vmem,
+        compiler_params=pltpu.CompilerParams(vmem_limit_bytes=4 * 2**20),
+    )(pooled)
+
+
 def local(
     tokens,
     routes,
@@ -448,12 +467,14 @@
         set_slots,
     )
     later_up, _ = lax.optimization_barrier((expert_up_weight[0], outgoing))
+    notes = jnp.pad(notes, ((chip_rows, 0), (columns, 0))).astype(F16)
+    notes, later_up = lax.optimization_barrier((notes, later_up))
     other = [(k, tensors - 1 - k) for k in range(tensors)]
     far_weights = [lax.ppermute(w, "t", other) for w in (expert_gate_weight[0], later_up)]
     received = swap(outgoing, EXPERT + ("c",))
 
     sent, adapter_up, norm_scale = rows_layer(own_group, received, task_rows)
-    sent = (sent + jnp.pad(notes, ((chip_rows, 0), (columns, 0)))).astype(F16)
+    sent = sent.astype(F16) + notes
     gathered = lax.all_gather(sent, SEQ, axis=0, tiled=False)
     gathered = gathered.astype(BF16).reshape(seq * shard_rows, columns + LANES)
     per_half = half // slice_width
@@ -487,8 +508,6 @@
     )
     payload = (part * factor + base).reshape(groups, chip_rows, slice_width)
 
-    returned = swap(payload, GROUP)
-
     expert_ids = jnp.arange(experts, dtype=jnp.int32)[:, None]
     group_ids = lax.dynamic_index_in_dim(notes, g, axis=0, keepdims=False)
     group_ids = group_ids[:2].astype(jnp.int32)
@@ -504,19 +523,25 @@
         place[:, None, :]
         == jnp.arange(tensors * chip_rows, dtype=jnp.int32).astype(F32)[None, :, None]
     ).astype(F32)
+    combiner = combiner.reshape(groups * chip_rows, group_rows)
+    position = g * group_rows + jnp.arange(group_rows, dtype=jnp.int32)[None, :]
+    counted = (position < counts[0]).astype(F32)
+    payload, combiner, counted, norm_scale = lax.optimization_barrier(
+        (payload, combiner, counted, norm_scale)
+    )
+
+    returned = swap(payload, GROUP)
     mixed = lax.dot_general(
-        combiner.reshape(groups * chip_rows, group_rows),
+        combiner,
         returned.reshape(groups * chip_rows, slice_width),
         (((0,), (0,)), ((), ())),
         precision=HIGH,
     )
     squares = jnp.sum(spread(jnp.sum(mixed * mixed, axis=1)[None], SEQ), axis=0)
-    position = g * group_rows + jnp.arange(group_rows, dtype=jnp.int32)[None, :]
-    factor = jnp.where(position < counts[0], lax.rsqrt(squares / width + 1e-05), 0.0)
+    factor = counted * lax.rsqrt(squares / width + 1e-05)
     pooled = jnp.dot(factor, mixed, precision=HIGH) * norm_scale
     pooled = jnp.sum(spread(pooled, GROUP), axis=0)
-    pooled = spread(pooled, SEQ).reshape(1, width)
-    return pooled * lax.rsqrt(jnp.mean(pooled * pooled, axis=1, keepdims=True) + 1e-06)
+    return norm_layer(spread(pooled, SEQ).reshape(seq, slice_width))
 
 
 def solution(mesh):

time: 186 us -> 184 us (0.989)
  blocking collectives: 117 us -> 150 us
  waiting for transfers between devices: 21.8 us -> 0.99 us
  starting transfers between devices: 29.2 us -> 15.5 us
    all_to_all x2 -> x4, blocking collectives: 26 us -> 59.1 us  [swap(): return lax.all_to_all(x, axes, split_axis=0, concat_axis=0, tiled=True)]
    all_to_all x3 -> x1, waiting for transfers between devices: 21.8 us -> 0.98 us  [swap(): return lax.all_to_all(x, axes, split_axis=0, concat_axis=0, tiled=True)]
    all_to_all x3 -> x1, starting transfers between devices: 23.9 us -> 10.2 us  [swap(): return lax.all_to_all(x, axes, split_axis=0, concat_axis=0, tiled=True)]
  transfers between devices with their start and end apart: 5 -> 3, of which waited for: 3 -> 1; matrix products, arithmetic and copies ran while one was open for 1% -> 2% of each run, Pallas kernels for 1% -> 1%
where the time goes in v12:
time: 184 us; the launch traced here: 183 us
  blocking collectives  150 us (82%)
  starting transfers between devices  15.5 us (8%)
  Pallas kernels  7.7 us (4%)
  other arithmetic  3.62 us (2%)
  matrix products  2.45 us (1%)
  local copies, waits for them, and re-layouts  1.98 us (1%)
    all_to_all x4, blocking collectives, swap(): return lax.all_to_all(x, axes, split_axis=0, concat_axis=0, tiled=True)  59.1 us
    all_gather x1, blocking collectives, local(): hidden = lax.all_gather(hidden.astype(F16), SEQ, axis=0, tiled=False)  45.6 us
    all_gather x1, blocking collectives, local(): gathered = lax.all_gather(sent, SEQ, axis=0, tiled=False)  44.9 us
    all_to_all x1, starting transfers between devices, swap(): return lax.all_to_all(x, axes, split_axis=0, concat_axis=0, tiled=True)  10.2 us
    ppermute x2, starting transfers between devices, local(): lax.ppermute(w, 't', other)  5.28 us
  transfers between devices with their start and end apart: 3, of which 1 were waited for; matrix products, arithmetic and copies ran while one was open for 2% of the time, Pallas kernels for 1%

profile of v12, /device:TPU:1, one launch (start us, length us, event | category | flops | bytes accessed | tf_op | source)
XLA Modules:
  0.0 183.3 jit_solution(10626339077730542011)
XLA Ops:
  0.0 0.0 copy-start
  0.0 2.4 %shard_map.109 = (bf16[16,10,640]{2,1,0:T(8,128)(2,1)}, f32[20,128]{1,0:T(8,128)}) custom-call(s32[2,64]{1,0:T(2,128)} %bitcast.59, f32[2,64]{1,0:T(2,128)} %bitcast.60, bf16[64,512]{1,0:T(8,128)(2,1)} %refs_2_.1, bf16[32,512]{1,0:T(8,128)(2,1)} %refs_3_.1, bf16[32,512]{1,0:T(8,128)(2,1)} %refs_4_.1, f32[1,512]{1,0:T(1,128)} %bitcast.58), custom_call_target="tpu_custom_call" | custom-call | flops 10485760 | bytes 270336 | tf_op jit(solution)/shard_map/pallas_call | solution.py:138
  2.4 10.2 %all-to-all-start = ((bf16[16,10,640]{2,1,0:T(8,128)(2,1)}), bf16[16,10,640]{2,1,0:T(8,128)(2,1)S(1)}, u32[]{:S(2)}, u32[]{:S(2)}) async-start(bf16[16,10,640]{2,1,0:T(8,128)(2,1)} %get-tuple-element.21), calls=%async_computation | async-start | bytes 655360 | tf_op jit(solution)/shard_map/all_to_all | solution.py:31
  12.6 0.7 convert.4
  13.3 0.6 pad.5
  14.0 1.9 %collective-permute-start.1 = (bf16[4096,128]{1,0:T(8,128)(2,1)}, bf16[4096,128]{1,0:T(8,128)(2,1)S(1)}, u32[]{:S(2)}, u32[]{:S(2)}) collective-permute-start(bf16[4096,128]{1,0:T(8,128)(2,1)} %bitcast.50), channel_id=1, source_target_pairs={{0,1},{1,0},{2,3},{3,2},{4,5},{5,4},{6,7},{7,6},{8,9},{9,8},{10,11... | collective-permute-start | bytes 3145736 | tf_op jit(solution)/shard_map/ppermute | solution.py:473
  15.9 3.4 %collective-permute-start = (bf16[4096,128]{1,0:T(8,128)(2,1)}, bf16[4096,128]{1,0:T(8,128)(2,1)}, u32[]{:S(2)}, u32[]{:S(2)}) collective-permute-start(bf16[4096,128]{1,0:T(8,128)(2,1)} %bitcast.52), channel_id=1, source_target_pairs={{0,1},{1,0},{2,3},{3,2},{4,5},{5,4},{6,7},{7,6},{8,9},{9,8},{10,11... | collective-permute-start | bytes 3145736 | tf_op jit(solution)/shard_map/ppermute | solution.py:473
  20.0 0.1 eq.69
  20.8 0.1 stack.20.own_ref
  20.9 1.0 all-to-all-done.received_ref
  21.9 0.2 shard_map.110
  22.1 0.9 convert_add_fusion
  23.0 44.9 %all-gather.4 = f16[1280,1152]{1,0:T(8,128)(2,1)S(1)} all-gather(f16[40,1152]{1,0:T(8,128)(2,1)S(1)} %convert_add_fusion), channel_id=2, replica_groups=mesh['z'=16,'c'=2,'y'=4,'h'=2,'t'=2] {'z','c'}, dimensions={0}, use_global_device_ids=true | all-gather | bytes 3041280 | tf_op jit(solution)/shard_map/all_gather | solution.py:478
  67.9 0.0 copy-start.1
  67.9 0.0 copy-start.2
  67.9 0.5 convert_element_type.73.x_ref
  68.4 0.7 copy-done.1
  69.1 0.3 copy-done.2
  69.4 2.0 %shard_map.111 = (f32[320,128]{1,0:T(8,128)S(1)}, f32[320,128]{1,0:T(8,128)S(1)}, f32[320,128]{1,0:T(8,128)S(1)}, f32[16,8,128]{2,1,0:T(8,128)S(1)}) custom-call(s32[6]{0:T(128)S(1)} %stack.20.own_ref, bf16[1280,1152]{1,0:T(8,128)(2,1)S(1)} %convert_element_type.73.x_ref, bf16[4096,128]{1,0:T(8,128)(2,1)S(1)} %bitcast.53, bf16[4096,128]{1,0:T(8,128)(2,1)S(1)} %bitcast.51, ...), custom_call_target="tpu_custom_call" | custom-call | flops 671088640 | bytes 3145728 | tf_op jit(solution)/shard_map/pallas_call | solution.py:365
  71.5 0.2 add_select_fusion
  71.8 0.8 fusion.3
  72.5 0.0 collective-permute-done.1.up_ref
  72.6 0.0 collective-permute-done.gate_ref
  72.6 2.4 %shard_map.112 = f32[640,128]{1,0:T(8,128)S(1)} custom-call(s32[1]{0:T(128)} %bitcast.own_ref, bf16[1280,1152]{1,0:T(8,128)(2,1)S(1)} %convert_element_type.73.x_ref, bf16[4096,128]{1,0:T(8,128)(2,1)} %collective-permute-done.gate_ref, bf16[4096,128]{1,0:T(8,128)(2,1)S(1)} %collective-permute-done.1.up_ref, f32[320,128]{1,0:T(8,128)S(1)} %get-tuple-element.28.near_ref), custom_call_target="tpu_custom_call" | custom-call | flops 671088640 | bytes 3145728 | tf_op jit(solution)/shard_map/pallas_call | solution.py:390
  75.0 45.6 %all-gather.5 = f16[20480,128]{1,0:T(8,128)(2,1)S(1)} all-gather(f16[640,128]{1,0:T(8,128)(2,1)S(1)} %convert_element_type.61), channel_id=3, replica_groups=mesh['z'=16,'c'=2,'y'=4,'h'=2,'t'=2] {'z','c'}, dimensions={0}, use_global_device_ids=true | all-gather | bytes 5406720 | tf_op jit(solution)/shard_map/all_gather | solution.py:502
  120.5 0.6 convert_element_type.74
  121.1 0.0 copy-done
  121.1 0.0 copy-start.3
  121.2 1.5 fusion.1
  122.7 13.0 %all_to_all.25 = f32[16,20,128]{2,1,0:T(8,128)S(1)} all-to-all(f32[16,20,128]{2,1,0:T(8,128)S(1)} %reshape.82), channel_id=1, replica_groups=mesh['z'=16,'c'=2,'y'=4,'h'=2,'t'=2] {'y','h','t'}, dimensions={0} | all-to-all | bytes 327680 | tf_op jit(solution)/shard_map/all_to_all | solution.py:31
  135.7 0.0 copy-done.3
  135.8 0.5 multiply_reduce_fusion
  136.3 20.1 %all_to_all.26 = f32[32,1,128]{2,1,0:T(1,128)S(1)} all-to-all(f32[32,1,128]{2,1,0:T(1,128)S(1)} %broadcast_in_dim.41), channel_id=1, replica_groups=mesh['z'=16,'c'=2,'y'=4,'h'=2,'t'=2] {'z','c'}, dimensions={0} | all-to-all | bytes 32768 | tf_op jit(solution)/shard_map/all_to_all | solution.py:31
  156.4 0.2 fusion.2
  156.6 0.1 broadcast_in_dim.43
  156.6 9.1 %all_to_all.27 = f32[16,1,128]{2,1,0:T(1,128)S(1)} all-to-all(f32[16,1,128]{2,1,0:T(1,128)S(1)} %broadcast_in_dim.43), channel_id=1, replica_groups=mesh['z'=16,'c'=2,'y'=4,'h'=2,'t'=2] {'y','h','t'}, dimensions={0} | all-to-all | bytes 16384 | tf_op jit(solution)/shard_map/all_to_all | solution.py:31
  165.8 16.8 %all_to_all.28 = f32[32,1,128]{2,1,0:T(1,128)S(1)} all-to-all(f32[32,1,128]{2,1,0:T(1,128)S(1)} %broadcast_in_dim.44), channel_id=1, replica_groups=mesh['z'=16,'c'=2,'y'=4,'h'=2,'t'=2] {'z','c'}, dimensions={0} | all-to-all | bytes 32768 | tf_op jit(solution)/shard_map/all_to_all | solution.py:31
  182.6 0.7 shard_map.113
  (15 shorter events, 0.2 us)
Async XLA Ops:
  0.0 121.1 %copy-start = (bf16[1,8192,128]{2,1,0:T(8,128)(2,1)S(1)}, bf16[1,8192,128]{2,1,0:T(8,128)(2,1)}, u32[]{:S(2)}) copy-start(bf16[1,8192,128]{2,1,0:T(8,128)(2,1)} %param.16) | copy-start | bytes 6291460
  2.4 19.5 %all-to-all-start = ((bf16[16,10,640]{2,1,0:T(8,128)(2,1)}), bf16[16,10,640]{2,1,0:T(8,128)(2,1)S(1)}, u32[]{:S(2)}, u32[]{:S(2)}) async-start(bf16[16,10,640]{2,1,0:T(8,128)(2,1)} %get-tuple-element.21), calls=%async_computation | async-start | bytes 655360 | tf_op jit(solution)/shard_map/all_to_all | solution.py:31
  14.0 58.6 %collective-permute-start.1 = (bf16[4096,128]{1,0:T(8,128)(2,1)}, bf16[4096,128]{1,0:T(8,128)(2,1)S(1)}, u32[]{:S(2)}, u32[]{:S(2)}) collective-permute-start(bf16[4096,128]{1,0:T(8,128)(2,1)} %bitcast.50), channel_id=1, source_target_pairs={{0,1},{1,0},{2,3},{3,2},{4,5},{5,4},{6,7},{7,6},{8,9},{9,8},{10,11... | collective-permute-start | bytes 3145736 | tf_op jit(solution)/shard_map/ppermute | solution.py:473
  15.9 56.7 %collective-permute-start = (bf16[4096,128]{1,0:T(8,128)(2,1)}, bf16[4096,128]{1,0:T(8,128)(2,1)}, u32[]{:S(2)}, u32[]{:S(2)}) collective-permute-start(bf16[4096,128]{1,0:T(8,128)(2,1)} %bitcast.52), channel_id=1, source_target_pairs={{0,1},{1,0},{2,3},{3,2},{4,5},{5,4},{6,7},{7,6},{8,9},{9,8},{10,11... | collective-permute-start | bytes 3145736 | tf_op jit(solution)/shard_map/ppermute | solution.py:473
  67.9 1.2 copy-start.1
  67.9 1.5 copy-start.2
  121.1 14.6 %copy-start.3 = (f32[320,128]{1,0:T(8,128)S(1)}, f32[320,128]{1,0:T(8,128)}, u32[]{:S(2)}) copy-start(f32[320,128]{1,0:T(8,128)} %fusion.3) | copy-start | bytes 491524

commit v13 on v12

--- a/solution.py
+++ b/solution.py
@@ -221,6 +221,32 @@
     )(own_group[None], received)
 
 
+def hidden_rows(parts, scales, shrink, shift, weight_ref, gate_ref, up_ref):
+    units = gate_ref.shape[1]
+    half = 2 * LANES
+    flat, columns = parts[0].shape
+    blocks = columns // half
+    acts = jnp.zeros((flat, 2 * units), F32)
+    for c in range(HALVES):
+        half_acts = jnp.zeros((flat, 2 * units), F32)
+        for q in range(HALVES):
+            for n in range(blocks):
+                source = pl.ds(((q * blocks + n) * HALVES + c) * half, half)
+                target = pl.ds(n * half, half)
+                for k, ref in enumerate((gate_ref, up_ref)):
+                    weight_ref[c * HALVES + q, target, pl.ds(k * units, units)] = ref[source, :]
+            product = jnp.dot(
+                parts[c * HALVES + q],
+                weight_ref[c * HALVES + q],
+                preferred_element_type=F32,
+            )
+            half_acts += product if q == 0 else pltpu.roll(product, flat - shift, 0)
+        acts += half_acts * jnp.concatenate([scales[c]] * 2, axis=1)
+    gate_act, up_act = acts[:, :units], acts[:, units:]
+    value = (gate_act / (1.0 + jnp.exp(-gate_act)) * up_act).astype(BF16).astype(F32)
+    return value * shrink
+
+
 class Rows:
     def __init__(self, x_ref, shard_rows):
         self.x_ref = x_ref
@@ -230,7 +256,10 @@
         self.chips = x_ref.shape[0] // (HALVES * shard_rows)
         self.flat = self.chips * self.group
         self.columns = x_ref.shape[1] - LANES
-        self.x = x_ref[:, pl.ds(0, self.columns)].astype(F32)
+        x = x_ref[:, pl.ds(0, self.columns)].astype(F32)
+        self.parts = [
+            self.part(x, c, q).astype(BF16) for c in range(HALVES) for q in range(HALVES)
+        ]
         self.beside = x_ref[:, pl.ds(self.columns, LANES)].astype(F32)
         exponents = [self.part(self.beside, c, 0)[:, :LOW_LANES] for c in range(HALVES)]
         exponents = [jnp.concatenate([e] * (LANES // LOW_LANES), axis=1) for e in exponents]
@@ -244,30 +273,6 @@
 
     def aligned(self, value, q):
         return value if q == 0 else pltpu.roll(value, self.flat - (self.group - self.rows), 0)
-
-    def hidden(self, weight_ref, gate_ref, up_ref):
-        units = gate_ref.shape[1]
-        half = 2 * LANES
-        blocks = self.columns // half
-        acts = jnp.zeros((self.flat, 2 * units), F32)
-        for c in range(HALVES):
-            half_acts = jnp.zeros((self.flat, 2 * units), F32)
-            for q in range(HALVES):
-                for n in range(blocks):
-                    source = pl.ds(((q * blocks + n) * HALVES + c) * half, half)
-                    target = pl.ds(n * half, half)
-                    for k, ref in enumerate((gate_ref, up_ref)):
-                        weight_ref[c * HALVES + q, target, pl.ds(k * units, units)] = ref[source, :]
-                product = jnp.dot(
-                    self.part(self.x, c, q).astype(BF16),
-                    weight_ref[c * HALVES + q],
-                    preferred_element_type=F32,
-                )
-                half_acts += self.aligned(product, q)
-            acts += half_acts * jnp.concatenate([self.scales[c]] * 2, axis=1)
-        gate_act, up_act = acts[:, :units], acts[:, units:]
-        value = (gate_act / (1.0 + jnp.exp(-gate_act)) * up_act).astype(BF16).astype(F32)
-        return value * jnp.exp2(-2.0 * self.row_exponent - 2.0)
 
     def of_chip(self, chip):
         source = slice(chip * self.group, chip * self.group + self.rows)
@@ -286,6 +291,8 @@
     factor_ref,
     base_ref,
     note_ref,
+    part_ref,
+    row_ref,
     weight_ref,
 ):
     r = Rows(x_ref, shard_rows)
@@ -293,7 +300,14 @@
     own_core, own_quarter = own_ref[0], own_ref[1]
     own_column = pl.multiple_of(own_ref[2], LANES)
     task, tensor, expert = own_ref[3], own_ref[4], own_ref[5]
-    hidden = r.hidden(weight_ref, gate_ref, up_ref)
+    shrink = jnp.exp2(-2.0 * r.row_exponent - 2.0)
+    for k in range(len(r.parts)):
+        part_ref[k] = r.parts[k]
+    for k, value in enumerate(r.scales + [shrink]):
+        row_ref[k] = value
+    hidden = hidden_rows(
+        r.parts, r.scales, shrink, r.group - r.rows, weight_ref, gate_ref, up_ref
+    )
 
     own = x_ref[:, pl.ds(own_column, LANES)].astype(F32)
     low = jnp.zeros((r.flat, LOW_LANES), F32)
@@ -342,24 +356,30 @@
 
 
 def far_kernel(
-    shard_rows, own_ref, x_ref, gate_ref, up_ref, near_ref, hidden_ref, weight_ref
+    rows, group, own_ref, part_ref, row_ref, gate_ref, up_ref, near_ref, hidden_ref, weight_ref
 ):
-    r = Rows(x_ref, shard_rows)
-    far = r.hidden(weight_ref, gate_ref, up_ref)
-    slots = r.chips * r.rows
+    parts = [part_ref[k] for k in range(part_ref.shape[0])]
+    scales = [row_ref[k] for k in range(HALVES)]
+    far = hidden_rows(
+        parts, scales, row_ref[HALVES], group - rows, weight_ref, gate_ref, up_ref
+    )
+    chips = far.shape[0] // group
+    slots = chips * rows
     near_at = own_ref[0] * slots
     far_at = slots - near_at
     hidden_ref[pl.ds(pl.multiple_of(near_at, 8), slots), :] = near_ref[...]
-    for chip in range(0, r.chips, 2):
-        one, two = r.of_chip(chip)[0], r.of_chip(chip + 1)[0]
-        start = pl.multiple_of(far_at + chip * r.rows, 8)
-        hidden_ref[pl.ds(start, 2 * r.rows), :] = jnp.concatenate([far[one], far[two]], axis=0)
+    for chip in range(0, chips, 2):
+        pair = [far[k * group : k * group + rows] for k in (chip, chip + 1)]
+        start = pl.multiple_of(far_at + chip * rows, 8)
+        hidden_ref[pl.ds(start, 2 * rows), :] = jnp.concatenate(pair, axis=0)
 
 
 def near_layer(gathered, weights, adapter_up, own, shard_rows, block):
     rows = gathered.shape[0]
     columns = gathered.shape[1] - LANES
     units = weights[0].shape[1]
+    chips = rows // (HALVES * shard_rows)
+    flat = chips * (-(-shard_rows // HALVES // 8) * 8)
     out = jax.ShapeDtypeStruct((rows // 4, units), F32)
     vmem = pl.BlockSpec(memory_space=pltpu.VMEM)
     return pl.pallas_call(
@@ -368,38 +388,40 @@
             out,
             out,
             out,
-            jax.ShapeDtypeStruct((rows // (2 * shard_rows), NOTE_ROWS, LANES), F32),
+            jax.ShapeDtypeStruct((chips, NOTE_ROWS, LANES), F32),
+            jax.ShapeDtypeStruct((2 * HALVES, flat, columns), BF16),
+            jax.ShapeDtypeStruct((HALVES + 1, flat, LANES), F32),
         ),
         in_specs=[pl.BlockSpec(memory_space=pltpu.SMEM)] + [vmem] * 4,
-        out_specs=(vmem, vmem, vmem, vmem),
+        out_specs=(vmem,) * 6,
         scratch_shapes=[pltpu.VMEM((2 * HALVES, columns, 2 * units), BF16)],
         compiler_params=pltpu.CompilerParams(vmem_limit_bytes=24 * 2**20),
         cost_estimate=pl.CostEstimate(
             flops=4 * rows * columns * units,
-            bytes_accessed=2 * rows * columns + 4 * columns * units,
+            bytes_accessed=4 * rows * columns + 4 * columns * units,
             transcendentals=2 * rows * units,
         ),
     )(own, gathered, *weights, adapter_up)
 
 
-def far_layer(gathered, weights, near, tensor, shard_rows):
-    rows = gathered.shape[0]
-    columns = gathered.shape[1] - LANES
-    units = weights[0].shape[1]
+def far_layer(parts, row_scales, weights, near, tensor, shard_rows):
+    _, flat, columns = parts.shape
+    slots, units = near.shape
+    rows = shard_rows // HALVES
     vmem = pl.BlockSpec(memory_space=pltpu.VMEM)
     return pl.pallas_call(
-        functools.partial(far_kernel, shard_rows),
-        out_shape=jax.ShapeDtypeStruct((rows // 2, units), F32),
-        in_specs=[pl.BlockSpec(memory_space=pltpu.SMEM)] + [vmem] * 4,
+        functools.partial(far_kernel, rows, flat * rows // slots),
+        out_shape=jax.ShapeDtypeStruct((2 * slots, units), F32),
+        in_specs=[pl.BlockSpec(memory_space=pltpu.SMEM)] + [vmem] * 5,
         out_specs=vmem,
         scratch_shapes=[pltpu.VMEM((2 * HALVES, columns, 2 * units), BF16)],
         compiler_params=pltpu.CompilerParams(vmem_limit_bytes=24 * 2**20),
         cost_estimate=pl.CostEstimate(
-            flops=4 * rows * columns * units,
-            bytes_accessed=2 * rows * columns + 4 * columns * units,
-            transcendentals=2 * rows * units,
-        ),
-    )(tensor[None], gathered, *weights, near)
+            flops=16 * flat * columns * units,
+            bytes_accessed=8 * flat * columns + 16 * columns * units,
+            transcendentals=2 * flat * units,
+        ),
+    )(tensor[None], parts, row_scales, *weights, near)
 
 
 def norm_kernel(x_ref, out_ref):
@@ -467,19 +489,17 @@
         set_slots,
     )
     later_up, _ = lax.optimization_barrier((expert_up_weight[0], outgoing))
-    notes = jnp.pad(notes, ((chip_rows, 0), (columns, 0))).astype(F16)
-    notes, later_up = lax.optimization_barrier((notes, later_up))
     other = [(k, tensors - 1 - k) for k in range(tensors)]
     far_weights = [lax.ppermute(w, "t", other) for w in (expert_gate_weight[0], later_up)]
     received = swap(outgoing, EXPERT + ("c",))
 
     sent, adapter_up, norm_scale = rows_layer(own_group, received, task_rows)
-    sent = sent.astype(F16) + notes
+    sent = (sent + jnp.pad(notes, ((chip_rows, 0), (columns, 0)))).astype(F16)
     gathered = lax.all_gather(sent, SEQ, axis=0, tiled=False)
     gathered = gathered.astype(BF16).reshape(seq * shard_rows, columns + LANES)
     per_half = half // slice_width
     own_column = own_group * half + (s % per_half) * slice_width
-    near, factor, base, notes = near_layer(
+    near, factor, base, notes, parts, row_scales = near_layer(
         gathered,
         (expert_gate_weight[0], expert_up_weight[0]),
         adapter_up,
@@ -496,12 +516,13 @@
         shard_rows,
         rows,
     )
-    hidden = far_layer(gathered, far_weights, near, t, shard_rows)
+    hidden = far_layer(parts, row_scales, far_weights, near, t, shard_rows)
 
     units = hidden.shape[-1]
-    hidden = lax.all_gather(hidden.astype(F16), SEQ, axis=0, tiled=False)
+    hidden = hidden.astype(F16).reshape(tensors, -1, units)
+    hidden = lax.all_gather(hidden, SEQ, axis=0, tiled=True)
     part = lax.dot_general(
-        hidden.reshape(seq * tensors, -1, units).astype(BF16),
+        hidden.astype(BF16),
         expert_down_weight[0].reshape(seq * tensors, units, slice_width),
         (((0, 2), (0, 1)), ((), ())),
         preferred_element_type=F32,

time: 184 us -> 182 us (0.989)
  transfers between devices with their start and end apart: 3 -> 3, of which waited for: 1 -> 1; matrix products, arithmetic and copies ran while one was open for 2% -> 1% of each run, Pallas kernels for 1% -> 1%
where the time goes in v13:
time: 182 us
  blocking collectives  149 us (82%)
  starting transfers between devices  15.5 us (9%)
  Pallas kernels  7.88 us (4%)
  matrix products  2.47 us (1%)
  waiting for transfers between devices  2.35 us (1%)
  other arithmetic  2.09 us (1%)
    all_to_all x4, blocking collectives, swap(): return lax.all_to_all(x, axes, split_axis=0, concat_axis=0, tiled=True)  57.9 us
    all_gather x1, blocking collectives, local(): hidden = lax.all_gather(hidden, SEQ, axis=0, tiled=True)  45.5 us
    all_gather x1, blocking collectives, local(): gathered = lax.all_gather(sent, SEQ, axis=0, tiled=False)  45.4 us
    all_to_all x1, starting transfers between devices, swap(): return lax.all_to_all(x, axes, split_axis=0, concat_axis=0, tiled=True)  10.2 us
    ppermute x2, starting transfers between devices, local(): lax.ppermute(w, 't', other)  5.28 us
  transfers between devices with their start and end apart: 3, of which 1 were waited for; matrix products, arithmetic and copies ran while one was open for 1% of the time, Pallas kernels for 1%

profile of v13, /device:TPU:1, one launch (start us, length us, event | category | flops | bytes accessed | tf_op | source)
XLA Modules:
  0.0 181.9 jit_solution(11775891587439303872)
XLA Ops:
  0.0 0.0 copy-start
  0.0 2.4 %shard_map.109 = (bf16[16,10,640]{2,1,0:T(8,128)(2,1)}, f32[20,128]{1,0:T(8,128)}) custom-call(s32[2,64]{1,0:T(2,128)} %bitcast.58, f32[2,64]{1,0:T(2,128)} %bitcast.59, bf16[64,512]{1,0:T(8,128)(2,1)} %refs_2_.1, bf16[32,512]{1,0:T(8,128)(2,1)} %refs_3_.1, bf16[32,512]{1,0:T(8,128)(2,1)} %refs_4_.1, f32[1,512]{1,0:T(1,128)} %bitcast.57), custom_call_target="tpu_custom_call" | custom-call | flops 10485760 | bytes 270336 | tf_op jit(solution)/shard_map/pallas_call | solution.py:138
  2.4 10.2 %all-to-all-start = ((bf16[16,10,640]{2,1,0:T(8,128)(2,1)}), bf16[16,10,640]{2,1,0:T(8,128)(2,1)S(1)}, u32[]{:S(2)}, u32[]{:S(2)}) async-start(bf16[16,10,640]{2,1,0:T(8,128)(2,1)} %get-tuple-element.21), calls=%async_computation | async-start | bytes 655360 | tf_op jit(solution)/shard_map/all_to_all | solution.py:31
  12.6 1.9 %collective-permute-start.1 = (bf16[4096,128]{1,0:T(8,128)(2,1)}, bf16[4096,128]{1,0:T(8,128)(2,1)S(1)}, u32[]{:S(2)}, u32[]{:S(2)}) collective-permute-start(bf16[4096,128]{1,0:T(8,128)(2,1)} %bitcast.49), channel_id=1, source_target_pairs={{0,1},{1,0},{2,3},{3,2},{4,5},{5,4},{6,7},{7,6},{8,9},{9,8},{10,11... | collective-permute-start | bytes 3145736 | tf_op jit(solution)/shard_map/ppermute | solution.py:493
  14.5 3.4 %collective-permute-start = (bf16[4096,128]{1,0:T(8,128)(2,1)}, bf16[4096,128]{1,0:T(8,128)(2,1)}, u32[]{:S(2)}, u32[]{:S(2)}) collective-permute-start(bf16[4096,128]{1,0:T(8,128)(2,1)} %bitcast.51), channel_id=1, source_target_pairs={{0,1},{1,0},{2,3},{3,2},{4,5},{5,4},{6,7},{7,6},{8,9},{9,8},{10,11... | collective-permute-start | bytes 3145736 | tf_op jit(solution)/shard_map/ppermute | solution.py:493
  18.7 0.1 eq.69
  19.4 0.1 stack.20.own_ref
  19.5 2.3 %all-to-all-done.received_ref = bf16[16,10,640]{2,1,0:T(8,128)(2,1)S(1)} async-done(((bf16[16,10,640]{2,1,0:T(8,128)(2,1)}), bf16[16,10,640]{2,1,0:T(8,128)(2,1)S(1)}, u32[]{:S(2)}, u32[]{:S(2)}) %all-to-all-start) | async-done | bytes 204832 | tf_op jit(solution)/shard_map/all_to_all | solution.py:31
  21.9 0.2 shard_map.110
  22.1 0.7 add_convert_fusion
  22.8 45.4 %all-gather.3 = f16[1280,1152]{1,0:T(8,128)(2,1)S(1)} all-gather(f16[40,1152]{1,0:T(8,128)(2,1)S(1)} %add_convert_fusion), channel_id=2, replica_groups=mesh['z'=16,'c'=2,'y'=4,'h'=2,'t'=2] {'z','c'}, dimensions={0}, use_global_device_ids=true | all-gather | bytes 3041280 | tf_op jit(solution)/shard_map/all_gather | solution.py:498
  68.2 0.0 copy-start.1
  68.2 0.0 copy-start.2
  68.2 0.5 convert_element_type.68.x_ref
  68.7 0.7 copy-done.1
  69.4 0.3 copy-done.2
  69.7 2.3 %shard_map.111 = (f32[320,128]{1,0:T(8,128)S(1)}, f32[320,128]{1,0:T(8,128)S(1)}, f32[320,128]{1,0:T(8,128)S(1)}, f32[16,8,128]{2,1,0:T(8,128)S(1)}, bf16[4,384,...) custom-call(s32[6]{0:T(128)S(1)} %stack.20.own_ref, bf16[1280,1152]{1,0:T(8,128)(2,1)S(1)} %convert_element_type.68.x_ref, ...), custom_call_target="tpu_custom_call" | custom-call | flops 671088640 | bytes 5767168 | tf_op jit(solution)/shard_map/pallas_call | solution.py:385
  72.0 0.2 add_select_fusion
  72.2 0.8 fusion.12
  73.0 0.0 collective-permute-done.1.up_ref
  73.0 0.0 collective-permute-done.gate_ref
  73.0 2.3 %shard_map.112 = f32[640,128]{1,0:T(8,128)S(1)} custom-call(s32[1]{0:T(128)} %bitcast.own_ref, bf16[4,384,1024]{2,1,0:T(8,128)(2,1)S(1)} %get-tuple-element.25.part_ref, f32[3,384,128]{2,1,0:T(8,128)S(1)} %get-tuple-element.26.row_ref, bf16[4096,128]{1,0:T(8,128)(2,1)} %collective-permute-done.gate_ref, bf16[4096,128]{1,0:T(8,128)(2,1)S(1)} %collective-permute-done.1.up_ref, ...), custom_call_target="tpu_custom_call" | custom-call | flops 805306368 | bytes 5242880 | tf_op jit(solution)/shard_map/pallas_call | solution.py:412
  75.4 45.5 %all-gather.4 = f16[64,320,128]{2,1,0:T(8,128)(2,1)S(1)} all-gather(f16[2,320,128]{2,1,0:T(8,128)(2,1)S(1)} %bitcast.54), channel_id=1, replica_groups=mesh['z'=16,'c'=2,'y'=4,'h'=2,'t'=2] {'z','c'}, dimensions={0}, use_global_device_ids=true | all-gather | bytes 5406720 | tf_op jit(solution)/shard_map/all_gather | solution.py:523
  120.9 0.0 copy-done
  120.9 0.0 copy-start.3
  120.9 1.5 fusion.8
  122.5 12.4 %all_to_all.25 = f32[16,20,128]{2,1,0:T(8,128)S(1)} all-to-all(f32[16,20,128]{2,1,0:T(8,128)S(1)} %reshape.84), channel_id=1, replica_groups=mesh['z'=16,'c'=2,'y'=4,'h'=2,'t'=2] {'y','h','t'}, dimensions={0} | all-to-all | bytes 327680 | tf_op jit(solution)/shard_map/all_to_all | solution.py:31
  134.9 0.0 copy-done.3
  134.9 0.5 multiply_reduce_fusion
  135.5 19.5 %all_to_all.26 = f32[32,1,128]{2,1,0:T(1,128)S(1)} all-to-all(f32[32,1,128]{2,1,0:T(1,128)S(1)} %broadcast_in_dim.41), channel_id=1, replica_groups=mesh['z'=16,'c'=2,'y'=4,'h'=2,'t'=2] {'z','c'}, dimensions={0} | all-to-all | bytes 32768 | tf_op jit(solution)/shard_map/all_to_all | solution.py:31
  155.0 0.2 fusion.11
  155.2 0.1 broadcast_in_dim.43
  155.2 9.1 %all_to_all.27 = f32[16,1,128]{2,1,0:T(1,128)S(1)} all-to-all(f32[16,1,128]{2,1,0:T(1,128)S(1)} %broadcast_in_dim.43), channel_id=1, replica_groups=mesh['z'=16,'c'=2,'y'=4,'h'=2,'t'=2] {'y','h','t'}, dimensions={0} | all-to-all | bytes 16384 | tf_op jit(solution)/shard_map/all_to_all | solution.py:31
  164.4 16.8 %all_to_all.28 = f32[32,1,128]{2,1,0:T(1,128)S(1)} all-to-all(f32[32,1,128]{2,1,0:T(1,128)S(1)} %broadcast_in_dim.44), channel_id=1, replica_groups=mesh['z'=16,'c'=2,'y'=4,'h'=2,'t'=2] {'z','c'}, dimensions={0} | all-to-all | bytes 32768 | tf_op jit(solution)/shard_map/all_to_all | solution.py:31
  181.2 0.7 shard_map.113
  (15 shorter events, 0.2 us)
Async XLA Ops:
  0.0 120.9 %copy-start = (bf16[1,8192,128]{2,1,0:T(8,128)(2,1)S(1)}, bf16[1,8192,128]{2,1,0:T(8,128)(2,1)}, u32[]{:S(2)}) copy-start(bf16[1,8192,128]{2,1,0:T(8,128)(2,1)} %param.16) | copy-start | bytes 6291460
  2.4 19.5 %all-to-all-start = ((bf16[16,10,640]{2,1,0:T(8,128)(2,1)}), bf16[16,10,640]{2,1,0:T(8,128)(2,1)S(1)}, u32[]{:S(2)}, u32[]{:S(2)}) async-start(bf16[16,10,640]{2,1,0:T(8,128)(2,1)} %get-tuple-element.21), calls=%async_computation | async-start | bytes 655360 | tf_op jit(solution)/shard_map/all_to_all | solution.py:31
  12.6 60.4 %collective-permute-start.1 = (bf16[4096,128]{1,0:T(8,128)(2,1)}, bf16[4096,128]{1,0:T(8,128)(2,1)S(1)}, u32[]{:S(2)}, u32[]{:S(2)}) collective-permute-start(bf16[4096,128]{1,0:T(8,128)(2,1)} %bitcast.49), channel_id=1, source_target_pairs={{0,1},{1,0},{2,3},{3,2},{4,5},{5,4},{6,7},{7,6},{8,9},{9,8},{10,11... | collective-permute-start | bytes 3145736 | tf_op jit(solution)/shard_map/ppermute | solution.py:493
  14.5 58.5 %collective-permute-start = (bf16[4096,128]{1,0:T(8,128)(2,1)}, bf16[4096,128]{1,0:T(8,128)(2,1)}, u32[]{:S(2)}, u32[]{:S(2)}) collective-permute-start(bf16[4096,128]{1,0:T(8,128)(2,1)} %bitcast.51), channel_id=1, source_target_pairs={{0,1},{1,0},{2,3},{3,2},{4,5},{5,4},{6,7},{7,6},{8,9},{9,8},{10,11... | collective-permute-start | bytes 3145736 | tf_op jit(solution)/shard_map/ppermute | solution.py:493
  68.2 1.2 copy-start.1
  68.2 1.5 copy-start.2
  120.9 14.0 %copy-start.3 = (f32[320,128]{1,0:T(8,128)S(1)}, f32[320,128]{1,0:T(8,128)}, u32[]{:S(2)}) copy-start(f32[320,128]{1,0:T(8,128)} %fusion.12) | copy-start | bytes 491524

commit v14 on v13

--- a/solution.py
+++ b/solution.py
@@ -145,7 +145,7 @@
         out_specs=(pl.BlockSpec(memory_space=pltpu.VMEM),) * 2,
         scratch_shapes=[pltpu.VMEM(x.shape, x.dtype) for x in operands]
         + [pltpu.SemaphoreType.DMA((len(operands),))],
-        compiler_params=pltpu.CompilerParams(vmem_limit_bytes=60 * 2**20),
+        compiler_params=pltpu.CompilerParams(vmem_limit_bytes=57 * 2**20),
         cost_estimate=pl.CostEstimate(
             flops=4 * rows * feats * experts * set_slots,
             bytes_accessed=2 * rows * feats + 2 * experts * HALVES * set_slots * lanes,
@@ -290,10 +290,11 @@
     hidden_ref,
     factor_ref,
     base_ref,
-    note_ref,
+    combiner_ref,
     part_ref,
     row_ref,
     weight_ref,
+    note_ref,
 ):
     r = Rows(x_ref, shard_rows)
     task_rows = adapter_ref.shape[0]
@@ -354,6 +355,20 @@
         factor_ref[target, :] = slot_weight * up_scale[source]
         base_ref[target, :] = 0.5 * base[source]
 
+    ids = note_ref[own_ref[6]][:2].astype(jnp.int32)
+    experts = combiner_ref.shape[0] // (2 * r.rows)
+    named = lax.broadcasted_iota(jnp.int32, (experts, LANES), 0)
+    slot = slots_of((ids[:1] == named) | (ids[1:] == named), block)
+    slot_set = jnp.floor(slot / set_slots)
+    place = jnp.where(
+        slot >= 0.0,
+        slot + slot_set * (r.rows - set_slots) + set_slots * block_of(slot.shape, block),
+        -1.0,
+    )
+    row = lax.broadcasted_iota(jnp.int32, (2 * r.rows, LANES), 0).astype(F32)
+    for e in range(experts):
+        combiner_ref[pl.ds(e * 2 * r.rows, 2 * r.rows), :] = (place[e : e + 1] == row).astype(F32)
+
 
 def far_kernel(
     rows, group, own_ref, part_ref, row_ref, gate_ref, up_ref, near_ref, hidden_ref, weight_ref
@@ -374,7 +389,7 @@
         hidden_ref[pl.ds(start, 2 * rows), :] = jnp.concatenate(pair, axis=0)
 
 
-def near_layer(gathered, weights, adapter_up, own, shard_rows, block):
+def near_layer(gathered, weights, adapter_up, own, shard_rows, block, experts):
     rows = gathered.shape[0]
     columns = gathered.shape[1] - LANES
     units = weights[0].shape[1]
@@ -388,13 +403,16 @@
             out,
             out,
             out,
-            jax.ShapeDtypeStruct((chips, NOTE_ROWS, LANES), F32),
+            jax.ShapeDtypeStruct((experts * shard_rows, LANES), F32),
             jax.ShapeDtypeStruct((2 * HALVES, flat, columns), BF16),
             jax.ShapeDtypeStruct((HALVES + 1, flat, LANES), F32),
         ),
         in_specs=[pl.BlockSpec(memory_space=pltpu.SMEM)] + [vmem] * 4,
         out_specs=(vmem,) * 6,
-        scratch_shapes=[pltpu.VMEM((2 * HALVES, columns, 2 * units), BF16)],
+        scratch_shapes=[
+            pltpu.VMEM((2 * HALVES, columns, 2 * units), BF16),
+            pltpu.VMEM((chips, NOTE_ROWS, LANES), F32),
+        ],
         compiler_params=pltpu.CompilerParams(vmem_limit_bytes=24 * 2**20),
         cost_estimate=pl.CostEstimate(
             flops=4 * rows * columns * units,
@@ -499,7 +517,7 @@
     gathered = gathered.astype(BF16).reshape(seq * shard_rows, columns + LANES)
     per_half = half // slice_width
     own_column = own_group * half + (s % per_half) * slice_width
-    near, factor, base, notes, parts, row_scales = near_layer(
+    near, factor, base, combiner, parts, row_scales = near_layer(
         gathered,
         (expert_gate_weight[0], expert_up_weight[0]),
         adapter_up,
@@ -511,10 +529,12 @@
                 document_task_index[0],
                 t,
                 lax.axis_index(EXPERT),
+                g,
             ]
         ),
         shard_rows,
         rows,
+        experts,
     )
     hidden = far_layer(parts, row_scales, far_weights, near, t, shard_rows)
 
@@ -529,22 +549,7 @@
     )
     payload = (part * factor + base).reshape(groups, chip_rows, slice_width)
 
-    expert_ids = jnp.arange(experts, dtype=jnp.int32)[:, None]
-    group_ids = lax.dynamic_index_in_dim(notes, g, axis=0, keepdims=False)
-    group_ids = group_ids[:2].astype(jnp.int32)
-    slot = slots_of((group_ids[:1] == expert_ids) | (group_ids[1:] == expert_ids), rows)
-    slot_set = jnp.floor(slot / set_slots)
-    place = jnp.where(
-        slot >= 0.0,
-        slot + slot_set * (chip_rows - set_slots) + set_slots * block_of(slot.shape, rows),
-        -1.0,
-    )
     group_rows = cores * rows
-    combiner = (
-        place[:, None, :]
-        == jnp.arange(tensors * chip_rows, dtype=jnp.int32).astype(F32)[None, :, None]
-    ).astype(F32)
-    combiner = combiner.reshape(groups * chip_rows, group_rows)
     position = g * group_rows + jnp.arange(group_rows, dtype=jnp.int32)[None, :]
     counted = (position < counts[0]).astype(F32)
     payload, combiner, counted, norm_scale = lax.optimization_barrier(

time: 182 us -> 182 us (level)
  no operation moved by 1% of the time
where the time goes in v14:
time: 182 us
  blocking collectives  149 us (82%)
  starting transfers between devices  15.5 us (9%)
  Pallas kernels  7.89 us (4%)
  waiting for transfers between devices  2.52 us (1%)
  matrix products  2.23 us (1%)
  local copies, waits for them, and re-layouts  1.89 us (1%)
    all_to_all x4, blocking collectives, swap(): return lax.all_to_all(x, axes, split_axis=0, concat_axis=0, tiled=True)  58.2 us
    all_gather x1, blocking collectives, local(): hidden = lax.all_gather(hidden, SEQ, axis=0, tiled=True)  45.5 us
    all_gather x1, blocking collectives, local(): gathered = lax.all_gather(sent, SEQ, axis=0, tiled=False)  45.4 us
    all_to_all x1, starting transfers between devices, swap(): return lax.all_to_all(x, axes, split_axis=0, concat_axis=0, tiled=True)  10.2 us
    ppermute x2, starting transfers between devices, local(): lax.ppermute(w, 't', other)  5.28 us
  transfers between devices with their start and end apart: 3, of which 1 were waited for; matrix products, arithmetic and copies ran while one was open for 1% of the time, Pallas kernels for 1%

profile of v14, /device:TPU:1, one launch (start us, length us, event | category | flops | bytes accessed | tf_op | source)
XLA Modules:
  0.0 181.8 jit_solution(10195033446430103879)
XLA Ops:
  0.0 0.0 copy-start
  0.0 2.4 %shard_map.109 = (bf16[16,10,640]{2,1,0:T(8,128)(2,1)}, f32[20,128]{1,0:T(8,128)}) custom-call(s32[2,64]{1,0:T(2,128)} %bitcast.51, f32[2,64]{1,0:T(2,128)} %bitcast.52, bf16[64,512]{1,0:T(8,128)(2,1)} %refs_2_.1, bf16[32,512]{1,0:T(8,128)(2,1)} %refs_3_.1, bf16[32,512]{1,0:T(8,128)(2,1)} %refs_4_.1, f32[1,512]{1,0:T(1,128)} %bitcast.50), custom_call_target="tpu_custom_call" | custom-call | flops 10485760 | bytes 270336 | tf_op jit(solution)/shard_map/pallas_call | solution.py:138
  2.4 10.2 %all-to-all-start = ((bf16[16,10,640]{2,1,0:T(8,128)(2,1)}), bf16[16,10,640]{2,1,0:T(8,128)(2,1)S(1)}, u32[]{:S(2)}, u32[]{:S(2)}) async-start(bf16[16,10,640]{2,1,0:T(8,128)(2,1)} %get-tuple-element.21), calls=%async_computation | async-start | bytes 655360 | tf_op jit(solution)/shard_map/all_to_all | solution.py:31
  12.6 1.9 %collective-permute-start.1 = (bf16[4096,128]{1,0:T(8,128)(2,1)}, bf16[4096,128]{1,0:T(8,128)(2,1)S(1)}, u32[]{:S(2)}, u32[]{:S(2)}) collective-permute-start(bf16[4096,128]{1,0:T(8,128)(2,1)} %bitcast.42), channel_id=1, source_target_pairs={{0,1},{1,0},{2,3},{3,2},{4,5},{5,4},{6,7},{7,6},{8,9},{9,8},{10,11... | collective-permute-start | bytes 3145736 | tf_op jit(solution)/shard_map/ppermute | solution.py:511
  14.5 3.4 %collective-permute-start = (bf16[4096,128]{1,0:T(8,128)(2,1)}, bf16[4096,128]{1,0:T(8,128)(2,1)}, u32[]{:S(2)}, u32[]{:S(2)}) collective-permute-start(bf16[4096,128]{1,0:T(8,128)(2,1)} %bitcast.44), channel_id=1, source_target_pairs={{0,1},{1,0},{2,3},{3,2},{4,5},{5,4},{6,7},{7,6},{8,9},{9,8},{10,11... | collective-permute-start | bytes 3145736 | tf_op jit(solution)/shard_map/ppermute | solution.py:511
  19.3 0.1 stack.24.own_ref
  19.4 2.5 %all-to-all-done.received_ref = bf16[16,10,640]{2,1,0:T(8,128)(2,1)S(1)} async-done(((bf16[16,10,640]{2,1,0:T(8,128)(2,1)}), bf16[16,10,640]{2,1,0:T(8,128)(2,1)S(1)}, u32[]{:S(2)}, u32[]{:S(2)}) %all-to-all-start) | async-done | bytes 204832 | tf_op jit(solution)/shard_map/all_to_all | solution.py:31
  21.9 0.2 shard_map.110
  22.1 0.7 add_convert_fusion
  22.8 45.4 %all-gather.3 = f16[1280,1152]{1,0:T(8,128)(2,1)S(1)} all-gather(f16[40,1152]{1,0:T(8,128)(2,1)S(1)} %add_convert_fusion), channel_id=2, replica_groups=mesh['z'=16,'c'=2,'y'=4,'h'=2,'t'=2] {'z','c'}, dimensions={0}, use_global_device_ids=true | all-gather | bytes 3041280 | tf_op jit(solution)/shard_map/all_gather | solution.py:516
  68.2 0.0 copy-start.1
  68.2 0.0 copy-start.2
  68.2 0.5 convert_element_type.30.x_ref
  68.7 0.7 copy-done.1
  69.4 0.3 copy-done.2
  69.7 2.3 %shard_map.111 = (f32[320,128]{1,0:T(8,128)S(1)}, f32[320,128]{1,0:T(8,128)S(1)}, f32[320,128]{1,0:T(8,128)S(1)}, f32[320,128]{1,0:T(8,128)S(1)}, bf16[4,384,102...) custom-call(s32[7]{0:T(128)S(1)} %stack.24.own_ref, bf16[1280,1152]{1,0:T(8,128)(2,1)S(1)} %convert_element_type.30.x_ref, ...), custom_call_target="tpu_custom_call" | custom-call | flops 671088640 | bytes 5767168 | tf_op jit(solution)/shard_map/pallas_call | solution.py:400
  72.0 0.0 copy-start.3
  72.0 0.7 copy-done.3
  72.6 0.0 collective-permute-done.1.up_ref
  72.6 0.0 collective-permute-done.gate_ref
  72.6 2.3 %shard_map.112 = f32[640,128]{1,0:T(8,128)S(1)} custom-call(s32[1]{0:T(128)} %bitcast.own_ref, bf16[4,384,1024]{2,1,0:T(8,128)(2,1)S(1)} %get-tuple-element.25.part_ref, f32[3,384,128]{2,1,0:T(8,128)S(1)} %get-tuple-element.26.row_ref, bf16[4096,128]{1,0:T(8,128)(2,1)} %collective-permute-done.gate_ref, bf16[4096,128]{1,0:T(8,128)(2,1)S(1)} %collective-permute-done.1.up_ref, ...), custom_call_target="tpu_custom_call" | custom-call | flops 805306368 | bytes 5242880 | tf_op jit(solution)/shard_map/pallas_call | solution.py:430
  75.0 45.5 %all-gather.4 = f16[64,320,128]{2,1,0:T(8,128)(2,1)S(1)} all-gather(f16[2,320,128]{2,1,0:T(8,128)(2,1)S(1)} %bitcast.47), channel_id=1, replica_groups=mesh['z'=16,'c'=2,'y'=4,'h'=2,'t'=2] {'z','c'}, dimensions={0}, use_global_device_ids=true | all-gather | bytes 5406720 | tf_op jit(solution)/shard_map/all_gather | solution.py:543
  120.6 0.0 copy-done
  120.6 0.0 copy-start.4
  120.6 1.5 fusion.8
  122.1 12.1 %all_to_all.25 = f32[16,20,128]{2,1,0:T(8,128)S(1)} all-to-all(f32[16,20,128]{2,1,0:T(8,128)S(1)} %reshape.70), channel_id=1, replica_groups=mesh['z'=16,'c'=2,'y'=4,'h'=2,'t'=2] {'y','h','t'}, dimensions={0} | all-to-all | bytes 327680 | tf_op jit(solution)/shard_map/all_to_all | solution.py:31
  134.2 0.0 copy-done.4
  134.2 0.5 multiply_reduce_fusion
  134.8 20.1 %all_to_all.26 = f32[32,1,128]{2,1,0:T(1,128)S(1)} all-to-all(f32[32,1,128]{2,1,0:T(1,128)S(1)} %broadcast_in_dim.32), channel_id=1, replica_groups=mesh['z'=16,'c'=2,'y'=4,'h'=2,'t'=2] {'z','c'}, dimensions={0} | all-to-all | bytes 32768 | tf_op jit(solution)/shard_map/all_to_all | solution.py:31
  154.9 0.2 fusion.11
  155.1 0.1 broadcast_in_dim.34
  155.2 9.1 %all_to_all.27 = f32[16,1,128]{2,1,0:T(1,128)S(1)} all-to-all(f32[16,1,128]{2,1,0:T(1,128)S(1)} %broadcast_in_dim.34), channel_id=1, replica_groups=mesh['z'=16,'c'=2,'y'=4,'h'=2,'t'=2] {'y','h','t'}, dimensions={0} | all-to-all | bytes 16384 | tf_op jit(solution)/shard_map/all_to_all | solution.py:31
  164.3 16.8 %all_to_all.28 = f32[32,1,128]{2,1,0:T(1,128)S(1)} all-to-all(f32[32,1,128]{2,1,0:T(1,128)S(1)} %broadcast_in_dim.35), channel_id=1, replica_groups=mesh['z'=16,'c'=2,'y'=4,'h'=2,'t'=2] {'z','c'}, dimensions={0} | all-to-all | bytes 32768 | tf_op jit(solution)/shard_map/all_to_all | solution.py:31
  181.1 0.7 shard_map.113
  (8 shorter events, 0.1 us)
Async XLA Ops:
  0.0 120.6 %copy-start = (bf16[1,8192,128]{2,1,0:T(8,128)(2,1)S(1)}, bf16[1,8192,128]{2,1,0:T(8,128)(2,1)}, u32[]{:S(2)}) copy-start(bf16[1,8192,128]{2,1,0:T(8,128)(2,1)} %param.16) | copy-start | bytes 6291460
  2.4 19.5 %all-to-all-start = ((bf16[16,10,640]{2,1,0:T(8,128)(2,1)}), bf16[16,10,640]{2,1,0:T(8,128)(2,1)S(1)}, u32[]{:S(2)}, u32[]{:S(2)}) async-start(bf16[16,10,640]{2,1,0:T(8,128)(2,1)} %get-tuple-element.21), calls=%async_computation | async-start | bytes 655360 | tf_op jit(solution)/shard_map/all_to_all | solution.py:31
  12.6 60.0 %collective-permute-start.1 = (bf16[4096,128]{1,0:T(8,128)(2,1)}, bf16[4096,128]{1,0:T(8,128)(2,1)S(1)}, u32[]{:S(2)}, u32[]{:S(2)}) collective-permute-start(bf16[4096,128]{1,0:T(8,128)(2,1)} %bitcast.42), channel_id=1, source_target_pairs={{0,1},{1,0},{2,3},{3,2},{4,5},{5,4},{6,7},{7,6},{8,9},{9,8},{10,11... | collective-permute-start | bytes 3145736 | tf_op jit(solution)/shard_map/ppermute | solution.py:511
  14.5 58.1 %collective-permute-start = (bf16[4096,128]{1,0:T(8,128)(2,1)}, bf16[4096,128]{1,0:T(8,128)(2,1)}, u32[]{:S(2)}, u32[]{:S(2)}) collective-permute-start(bf16[4096,128]{1,0:T(8,128)(2,1)} %bitcast.44), channel_id=1, source_target_pairs={{0,1},{1,0},{2,3},{3,2},{4,5},{5,4},{6,7},{7,6},{8,9},{9,8},{10,11... | collective-permute-start | bytes 3145736 | tf_op jit(solution)/shard_map/ppermute | solution.py:511
  68.2 1.2 copy-start.1
  68.2 1.5 copy-start.2
  72.0 0.7 copy-start.3
  120.6 13.7 %copy-start.4 = (f32[320,128]{1,0:T(8,128)S(1)}, f32[320,128]{1,0:T(8,128)}, u32[]{:S(2)}) copy-start(f32[320,128]{1,0:T(8,128)} %copy-done.3) | copy-start | bytes 491524

commit v15 on v14

--- a/solution.py
+++ b/solution.py
@@ -413,7 +413,7 @@
             pltpu.VMEM((2 * HALVES, columns, 2 * units), BF16),
             pltpu.VMEM((chips, NOTE_ROWS, LANES), F32),
         ],
-        compiler_params=pltpu.CompilerParams(vmem_limit_bytes=24 * 2**20),
+        compiler_params=pltpu.CompilerParams(vmem_limit_bytes=16 * 2**20),
         cost_estimate=pl.CostEstimate(
             flops=4 * rows * columns * units,
             bytes_accessed=4 * rows * columns + 4 * columns * units,
@@ -433,7 +433,7 @@
         in_specs=[pl.BlockSpec(memory_space=pltpu.SMEM)] + [vmem] * 5,
         out_specs=vmem,
         scratch_shapes=[pltpu.VMEM((2 * HALVES, columns, 2 * units), BF16)],
-        compiler_params=pltpu.CompilerParams(vmem_limit_bytes=24 * 2**20),
+        compiler_params=pltpu.CompilerParams(vmem_limit_bytes=10 * 2**20),
         cost_estimate=pl.CostEstimate(
             flops=16 * flat * columns * units,
             bytes_accessed=8 * flat * columns + 16 * columns * units,
@@ -506,9 +506,11 @@
         experts,
         set_slots,
     )
-    later_up, _ = lax.optimization_barrier((expert_up_weight[0], outgoing))
+    later_weights, _ = lax.optimization_barrier(
+        ((expert_gate_weight[0], expert_up_weight[0]), outgoing)
+    )
     other = [(k, tensors - 1 - k) for k in range(tensors)]
-    far_weights = [lax.ppermute(w, "t", other) for w in (expert_gate_weight[0], later_up)]
+    far_weights = [lax.ppermute(w, "t", other) for w in later_weights]
     received = swap(outgoing, EXPERT + ("c",))
 
     sent, adapter_up, norm_scale = rows_layer(own_group, received, task_rows)
@@ -541,9 +543,10 @@
     units = hidden.shape[-1]
     hidden = hidden.astype(F16).reshape(tensors, -1, units)
     hidden = lax.all_gather(hidden, SEQ, axis=0, tiled=True)
+    hidden, down = lax.optimization_barrier((hidden, expert_down_weight[0]))
     part = lax.dot_general(
         hidden.astype(BF16),
-        expert_down_weight[0].reshape(seq * tensors, units, slice_width),
+        down.reshape(seq * tensors, units, slice_width),
         (((0, 2), (0, 1)), ((), ())),
         preferred_element_type=F32,
     )

time: 182 us -> 181 us (level)
  no operation moved by 1% of the time
where the time goes in v15:
time: 181 us
  blocking collectives  150 us (83%)
  starting transfers between devices  15.5 us (9%)
  Pallas kernels  6.58 us (4%)
  waiting for transfers between devices  2.52 us (1%)
  matrix products  2.23 us (1%)
    all_to_all x4, blocking collectives, swap(): return lax.all_to_all(x, axes, split_axis=0, concat_axis=0, tiled=True)  58.7 us
    all_gather x1, blocking collectives, local(): hidden = lax.all_gather(hidden, SEQ, axis=0, tiled=True)  45.6 us
    all_gather x1, blocking collectives, local(): gathered = lax.all_gather(sent, SEQ, axis=0, tiled=False)  45.4 us
    all_to_all x1, starting transfers between devices, swap(): return lax.all_to_all(x, axes, split_axis=0, concat_axis=0, tiled=True)  10.2 us
    ppermute x2, starting transfers between devices, local(): far_weights = [lax.ppermute(w, 't', other) for w in later_weights]  5.27 us
  transfers between devices with their start and end apart: 3, of which 1 were waited for; matrix products, arithmetic and copies ran while one was open for 1% of the time, Pallas kernels for 1%

profile of v15, /device:TPU:1, one launch (start us, length us, event | category | flops | bytes accessed | tf_op | source)
XLA Modules:
  0.0 180.5 jit_solution(3963234573198094312)
XLA Ops:
  0.0 2.2 %shard_map.109 = (bf16[16,10,640]{2,1,0:T(8,128)(2,1)}, f32[20,128]{1,0:T(8,128)}) custom-call(s32[2,64]{1,0:T(2,128)} %bitcast.52, f32[2,64]{1,0:T(2,128)} %bitcast.53, bf16[64,512]{1,0:T(8,128)(2,1)} %refs_2_.1, bf16[32,512]{1,0:T(8,128)(2,1)} %refs_3_.1, bf16[32,512]{1,0:T(8,128)(2,1)} %refs_4_.1, f32[1,512]{1,0:T(1,128)} %bitcast.51), custom_call_target="tpu_custom_call" | custom-call | flops 10485760 | bytes 270336 | tf_op jit(solution)/shard_map/pallas_call | solution.py:138
  2.2 10.2 %all-to-all-start = ((bf16[16,10,640]{2,1,0:T(8,128)(2,1)}), bf16[16,10,640]{2,1,0:T(8,128)(2,1)S(1)}, u32[]{:S(2)}, u32[]{:S(2)}) async-start(bf16[16,10,640]{2,1,0:T(8,128)(2,1)} %get-tuple-element.24), calls=%async_computation | async-start | bytes 655360 | tf_op jit(solution)/shard_map/all_to_all | solution.py:31
  12.4 1.9 %collective-permute-start = (bf16[4096,128]{1,0:T(8,128)(2,1)}, bf16[4096,128]{1,0:T(8,128)(2,1)S(1)}, u32[]{:S(2)}, u32[]{:S(2)}) collective-permute-start(bf16[4096,128]{1,0:T(8,128)(2,1)} %bitcast.42), channel_id=1, source_target_pairs={{0,1},{1,0},{2,3},{3,2},{4,5},{5,4},{6,7},{7,6},{8,9},{9,8},{10,11... | collective-permute-start | bytes 3145736 | tf_op jit(solution)/shard_map/ppermute | solution.py:513
  14.4 3.4 %collective-permute-start.1 = (bf16[4096,128]{1,0:T(8,128)(2,1)}, bf16[4096,128]{1,0:T(8,128)(2,1)S(1)}, u32[]{:S(2)}, u32[]{:S(2)}) collective-permute-start(bf16[4096,128]{1,0:T(8,128)(2,1)} %bitcast.44), channel_id=1, source_target_pairs={{0,1},{1,0},{2,3},{3,2},{4,5},{5,4},{6,7},{7,6},{8,9},{9,8},{10,11... | collective-permute-start | bytes 3145736 | tf_op jit(solution)/shard_map/ppermute | solution.py:513
  19.1 0.1 stack.24.own_ref
  19.2 2.5 %all-to-all-done.received_ref = bf16[16,10,640]{2,1,0:T(8,128)(2,1)S(1)} async-done(((bf16[16,10,640]{2,1,0:T(8,128)(2,1)}), bf16[16,10,640]{2,1,0:T(8,128)(2,1)S(1)}, u32[]{:S(2)}, u32[]{:S(2)}) %all-to-all-start) | async-done | bytes 204832 | tf_op jit(solution)/shard_map/all_to_all | solution.py:31
  21.7 0.2 shard_map.110
  21.9 0.7 add_convert_fusion
  22.7 45.4 %all-gather.3 = f16[1280,1152]{1,0:T(8,128)(2,1)S(1)} all-gather(f16[40,1152]{1,0:T(8,128)(2,1)S(1)} %add_convert_fusion), channel_id=2, replica_groups=mesh['z'=16,'c'=2,'y'=4,'h'=2,'t'=2] {'z','c'}, dimensions={0}, use_global_device_ids=true | all-gather | bytes 3041280 | tf_op jit(solution)/shard_map/all_gather | solution.py:518
  68.0 0.0 copy-start
  68.0 0.0 copy-start.1
  68.0 0.5 convert_element_type.30.x_ref
  68.5 0.7 copy-done
  69.2 0.3 copy-done.1
  69.6 2.3 %shard_map.111 = (f32[320,128]{1,0:T(8,128)S(1)}, f32[320,128]{1,0:T(8,128)S(1)}, f32[320,128]{1,0:T(8,128)S(1)}, f32[320,128]{1,0:T(8,128)S(1)}, bf16[4,384,102...) custom-call(s32[7]{0:T(128)S(1)} %stack.24.own_ref, bf16[1280,1152]{1,0:T(8,128)(2,1)S(1)} %convert_element_type.30.x_ref, ...), custom_call_target="tpu_custom_call" | custom-call | flops 671088640 | bytes 5767168 | tf_op jit(solution)/shard_map/pallas_call | solution.py:400
  71.8 0.0 collective-permute-done.gate_ref
  71.8 0.0 collective-permute-done.1.up_ref
  71.8 1.2 shard_map.112
  73.0 0.0 copy-start.2
  73.1 45.6 %all-gather.4 = f16[64,320,128]{2,1,0:T(8,128)(2,1)S(1)} all-gather(f16[2,320,128]{2,1,0:T(8,128)(2,1)S(1)} %bitcast.48), channel_id=1, replica_groups=mesh['z'=16,'c'=2,'y'=4,'h'=2,'t'=2] {'z','c'}, dimensions={0}, use_global_device_ids=true | all-gather | bytes 5406720 | tf_op jit(solution)/shard_map/all_gather | solution.py:545
  118.7 0.0 copy-done.2
  118.7 1.5 fusion.8
  120.3 11.9 %all_to_all.25 = f32[16,20,128]{2,1,0:T(8,128)S(1)} all-to-all(f32[16,20,128]{2,1,0:T(8,128)S(1)} %reshape.74), channel_id=1, replica_groups=mesh['z'=16,'c'=2,'y'=4,'h'=2,'t'=2] {'y','h','t'}, dimensions={0} | all-to-all | bytes 327680 | tf_op jit(solution)/shard_map/all_to_all | solution.py:31
  132.2 0.5 multiply_reduce_fusion
  132.7 20.9 %all_to_all.26 = f32[32,1,128]{2,1,0:T(1,128)S(1)} all-to-all(f32[32,1,128]{2,1,0:T(1,128)S(1)} %broadcast_in_dim.32), channel_id=1, replica_groups=mesh['z'=16,'c'=2,'y'=4,'h'=2,'t'=2] {'z','c'}, dimensions={0} | all-to-all | bytes 32768 | tf_op jit(solution)/shard_map/all_to_all | solution.py:31
  153.6 0.2 fusion.11
  153.8 0.1 broadcast_in_dim.34
  153.8 9.1 %all_to_all.27 = f32[16,1,128]{2,1,0:T(1,128)S(1)} all-to-all(f32[16,1,128]{2,1,0:T(1,128)S(1)} %broadcast_in_dim.34), channel_id=1, replica_groups=mesh['z'=16,'c'=2,'y'=4,'h'=2,'t'=2] {'y','h','t'}, dimensions={0} | all-to-all | bytes 16384 | tf_op jit(solution)/shard_map/all_to_all | solution.py:31
  163.0 16.8 %all_to_all.28 = f32[32,1,128]{2,1,0:T(1,128)S(1)} all-to-all(f32[32,1,128]{2,1,0:T(1,128)S(1)} %broadcast_in_dim.35), channel_id=1, replica_groups=mesh['z'=16,'c'=2,'y'=4,'h'=2,'t'=2] {'z','c'}, dimensions={0} | all-to-all | bytes 32768 | tf_op jit(solution)/shard_map/all_to_all | solution.py:31
  179.8 0.7 shard_map.113
  (8 shorter events, 0.1 us)
Async XLA Ops:
  2.2 19.5 %all-to-all-start = ((bf16[16,10,640]{2,1,0:T(8,128)(2,1)}), bf16[16,10,640]{2,1,0:T(8,128)(2,1)S(1)}, u32[]{:S(2)}, u32[]{:S(2)}) async-start(bf16[16,10,640]{2,1,0:T(8,128)(2,1)} %get-tuple-element.24), calls=%async_computation | async-start | bytes 655360 | tf_op jit(solution)/shard_map/all_to_all | solution.py:31
  12.4 59.4 %collective-permute-start = (bf16[4096,128]{1,0:T(8,128)(2,1)}, bf16[4096,128]{1,0:T(8,128)(2,1)S(1)}, u32[]{:S(2)}, u32[]{:S(2)}) collective-permute-start(bf16[4096,128]{1,0:T(8,128)(2,1)} %bitcast.42), channel_id=1, source_target_pairs={{0,1},{1,0},{2,3},{3,2},{4,5},{5,4},{6,7},{7,6},{8,9},{9,8},{10,11... | collective-permute-start | bytes 3145736 | tf_op jit(solution)/shard_map/ppermute | solution.py:513
  14.4 57.5 %collective-permute-start.1 = (bf16[4096,128]{1,0:T(8,128)(2,1)}, bf16[4096,128]{1,0:T(8,128)(2,1)S(1)}, u32[]{:S(2)}, u32[]{:S(2)}) collective-permute-start(bf16[4096,128]{1,0:T(8,128)(2,1)} %bitcast.44), channel_id=1, source_target_pairs={{0,1},{1,0},{2,3},{3,2},{4,5},{5,4},{6,7},{7,6},{8,9},{9,8},{10,11... | collective-permute-start | bytes 3145736 | tf_op jit(solution)/shard_map/ppermute | solution.py:513
  68.0 1.2 copy-start
  68.0 1.5 copy-start.1
  73.0 45.7 %copy-start.2 = (bf16[1,8192,128]{2,1,0:T(8,128)(2,1)S(1)}, bf16[1,8192,128]{2,1,0:T(8,128)(2,1)}, u32[]{:S(2)}) copy-start(bf16[1,8192,128]{2,1,0:T(8,128)(2,1)} %param.16) | copy-start | bytes 6291460

commit v16 on v15

--- a/solution.py
+++ b/solution.py
@@ -180,12 +180,13 @@
     low = sum(both(e, half, LANES) for e in range(groups))
     low = sum(low[:, k * LOW_LANES : (k + 1) * LOW_LANES] for k in range(1, 4))
     low = low * jnp.exp2(7.0 - exponent)
-    sent_ref[pl.ds(0, rows), pl.ds(0, columns)] = x[:, :columns]
-    sent_ref[pl.ds(rows, rows), pl.ds(0, columns)] = x[:, columns:]
-    sent_ref[pl.ds(0, rows), pl.ds(columns, LANES)] = jnp.concatenate(
+    beside = jnp.concatenate(
         [jnp.broadcast_to(exponent, low.shape)] + list(rounded_parts(low)), axis=1
     )
-    sent_ref[pl.ds(rows, rows), pl.ds(columns, LANES)] = jnp.zeros((rows, LANES), F32)
+    sent_ref[:, pl.ds(0, columns)] = jnp.concatenate([x[:, :columns], x[:, columns:]], axis=0)
+    sent_ref[:, pl.ds(columns, LANES)] = jnp.concatenate(
+        [beside, jnp.zeros_like(beside)], axis=0
+    )
 
     adapter = []
     for c in range(HALVES):
@@ -274,9 +275,10 @@
     def aligned(self, value, q):
         return value if q == 0 else pltpu.roll(value, self.flat - (self.group - self.rows), 0)
 
-    def of_chip(self, chip):
-        source = slice(chip * self.group, chip * self.group + self.rows)
-        return source, pl.ds(chip * self.rows, self.rows)
+    def of_chips(self, value, chips):
+        return jnp.concatenate(
+            [value[k * self.group : k * self.group + self.rows] for k in chips], axis=0
+        )
 
 
 def near_kernel(
@@ -344,16 +346,20 @@
     place = jnp.where(in_set, slot + set_slots * block_of(slot.shape, block), -1.0)
     weight = jnp.where(first == expert, weight[0], weight[1])
     row = lax.broadcasted_iota(jnp.int32, (r.group, LANES), 0).astype(F32)
-    for chip in range(r.chips):
-        source, target = r.of_chip(chip)
-        slot_weight = jnp.sum(
-            jnp.where(place[chip : chip + 1] == row, weight[chip : chip + 1], 0.0),
-            axis=1,
-            keepdims=True,
-        )[: r.rows]
-        hidden_ref[target, :] = hidden[source]
-        factor_ref[target, :] = slot_weight * up_scale[source]
-        base_ref[target, :] = 0.5 * base[source]
+    for chip in range(0, r.chips, 2):
+        pair = (chip, chip + 1)
+        slot_weight = [
+            jnp.sum(
+                jnp.where(place[k : k + 1] == row, weight[k : k + 1], 0.0), axis=1, keepdims=True
+            )
+            for k in pair
+        ]
+        target = pl.ds(chip * r.rows, 2 * r.rows)
+        hidden_ref[target, :] = r.of_chips(hidden, pair)
+        factor_ref[target, :] = jnp.concatenate(
+            [w[: r.rows] for w in slot_weight], axis=0
+        ) * r.of_chips(up_scale, pair)
+        base_ref[target, :] = 0.5 * r.of_chips(base, pair)
 
     ids = note_ref[own_ref[6]][:2].astype(jnp.int32)
     experts = combiner_ref.shape[0] // (2 * r.rows)

time: 181 us -> 181 us (level)
  no operation moved by 1% of the time
where the time goes in v16:
time: 181 us
  blocking collectives  150 us (83%)
  starting transfers between devices  15.5 us (9%)
  Pallas kernels  6.72 us (4%)
  waiting for transfers between devices  2.52 us (1%)
  matrix products  2.23 us (1%)
    all_to_all x4, blocking collectives, swap(): return lax.all_to_all(x, axes, split_axis=0, concat_axis=0, tiled=True)  58.5 us
    all_gather x1, blocking collectives, local(): hidden = lax.all_gather(hidden, SEQ, axis=0, tiled=True)  45.7 us
    all_gather x1, blocking collectives, local(): gathered = lax.all_gather(sent, SEQ, axis=0, tiled=False)  45.4 us
    all_to_all x1, starting transfers between devices, swap(): return lax.all_to_all(x, axes, split_axis=0, concat_axis=0, tiled=True)  10.2 us
    ppermute x2, starting transfers between devices, local(): far_weights = [lax.ppermute(w, 't', other) for w in later_weights]  5.27 us
  transfers between devices with their start and end apart: 3, of which 1 were waited for; matrix products, arithmetic and copies ran while one was open for 1% of the time, Pallas kernels for 1%

profile of v16, /device:TPU:1, one launch (start us, length us, event | category | flops | bytes accessed | tf_op | source)
XLA Modules:
  0.0 180.5 jit_solution(7929823508897621682)
XLA Ops:
  0.0 2.2 %shard_map.109 = (bf16[16,10,640]{2,1,0:T(8,128)(2,1)}, f32[20,128]{1,0:T(8,128)}) custom-call(s32[2,64]{1,0:T(2,128)} %bitcast.52, f32[2,64]{1,0:T(2,128)} %bitcast.53, bf16[64,512]{1,0:T(8,128)(2,1)} %refs_2_.1, bf16[32,512]{1,0:T(8,128)(2,1)} %refs_3_.1, bf16[32,512]{1,0:T(8,128)(2,1)} %refs_4_.1, f32[1,512]{1,0:T(1,128)} %bitcast.51), custom_call_target="tpu_custom_call" | custom-call | flops 10485760 | bytes 270336 | tf_op jit(solution)/shard_map/pallas_call | solution.py:138
  2.2 10.2 %all-to-all-start = ((bf16[16,10,640]{2,1,0:T(8,128)(2,1)}), bf16[16,10,640]{2,1,0:T(8,128)(2,1)S(1)}, u32[]{:S(2)}, u32[]{:S(2)}) async-start(bf16[16,10,640]{2,1,0:T(8,128)(2,1)} %get-tuple-element.24), calls=%async_computation | async-start | bytes 655360 | tf_op jit(solution)/shard_map/all_to_all | solution.py:31
  12.4 1.9 %collective-permute-start = (bf16[4096,128]{1,0:T(8,128)(2,1)}, bf16[4096,128]{1,0:T(8,128)(2,1)S(1)}, u32[]{:S(2)}, u32[]{:S(2)}) collective-permute-start(bf16[4096,128]{1,0:T(8,128)(2,1)} %bitcast.42), channel_id=1, source_target_pairs={{0,1},{1,0},{2,3},{3,2},{4,5},{5,4},{6,7},{7,6},{8,9},{9,8},{10,11... | collective-permute-start | bytes 3145736 | tf_op jit(solution)/shard_map/ppermute | solution.py:519
  14.4 3.4 %collective-permute-start.1 = (bf16[4096,128]{1,0:T(8,128)(2,1)}, bf16[4096,128]{1,0:T(8,128)(2,1)S(1)}, u32[]{:S(2)}, u32[]{:S(2)}) collective-permute-start(bf16[4096,128]{1,0:T(8,128)(2,1)} %bitcast.44), channel_id=1, source_target_pairs={{0,1},{1,0},{2,3},{3,2},{4,5},{5,4},{6,7},{7,6},{8,9},{9,8},{10,11... | collective-permute-start | bytes 3145736 | tf_op jit(solution)/shard_map/ppermute | solution.py:519
  19.1 0.1 stack.24.own_ref
  19.2 2.5 %all-to-all-done.received_ref = bf16[16,10,640]{2,1,0:T(8,128)(2,1)S(1)} async-done(((bf16[16,10,640]{2,1,0:T(8,128)(2,1)}), bf16[16,10,640]{2,1,0:T(8,128)(2,1)S(1)}, u32[]{:S(2)}, u32[]{:S(2)}) %all-to-all-start) | async-done | bytes 204832 | tf_op jit(solution)/shard_map/all_to_all | solution.py:31
  21.7 0.2 shard_map.110
  21.9 0.7 add_convert_fusion
  22.7 45.4 %all-gather.3 = f16[1280,1152]{1,0:T(8,128)(2,1)S(1)} all-gather(f16[40,1152]{1,0:T(8,128)(2,1)S(1)} %add_convert_fusion), channel_id=2, replica_groups=mesh['z'=16,'c'=2,'y'=4,'h'=2,'t'=2] {'z','c'}, dimensions={0}, use_global_device_ids=true | all-gather | bytes 3041280 | tf_op jit(solution)/shard_map/all_gather | solution.py:524
  68.0 0.0 copy-start
  68.0 0.0 copy-start.1
  68.0 0.5 convert_element_type.30.x_ref
  68.5 0.7 copy-done
  69.2 0.3 copy-done.1
  69.6 2.4 %shard_map.111 = (f32[320,128]{1,0:T(8,128)S(1)}, f32[320,128]{1,0:T(8,128)S(1)}, f32[320,128]{1,0:T(8,128)S(1)}, f32[320,128]{1,0:T(8,128)S(1)}, bf16[4,384,102...) custom-call(s32[7]{0:T(128)S(1)} %stack.24.own_ref, bf16[1280,1152]{1,0:T(8,128)(2,1)S(1)} %convert_element_type.30.x_ref, ...), custom_call_target="tpu_custom_call" | custom-call | flops 671088640 | bytes 5767168 | tf_op jit(solution)/shard_map/pallas_call | solution.py:406
  72.0 0.0 collective-permute-done.gate_ref
  72.0 0.0 collective-permute-done.1.up_ref
  72.0 1.2 shard_map.112
  73.2 0.0 copy-start.2
  73.2 45.7 %all-gather.4 = f16[64,320,128]{2,1,0:T(8,128)(2,1)S(1)} all-gather(f16[2,320,128]{2,1,0:T(8,128)(2,1)S(1)} %bitcast.48), channel_id=1, replica_groups=mesh['z'=16,'c'=2,'y'=4,'h'=2,'t'=2] {'z','c'}, dimensions={0}, use_global_device_ids=true | all-gather | bytes 5406720 | tf_op jit(solution)/shard_map/all_gather | solution.py:551
  118.9 0.0 copy-done.2
  118.9 1.5 fusion.8
  120.5 11.8 %all_to_all.25 = f32[16,20,128]{2,1,0:T(8,128)S(1)} all-to-all(f32[16,20,128]{2,1,0:T(8,128)S(1)} %reshape.74), channel_id=1, replica_groups=mesh['z'=16,'c'=2,'y'=4,'h'=2,'t'=2] {'y','h','t'}, dimensions={0} | all-to-all | bytes 327680 | tf_op jit(solution)/shard_map/all_to_all | solution.py:31
  132.3 0.5 multiply_reduce_fusion
  132.8 20.8 %all_to_all.26 = f32[32,1,128]{2,1,0:T(1,128)S(1)} all-to-all(f32[32,1,128]{2,1,0:T(1,128)S(1)} %broadcast_in_dim.32), channel_id=1, replica_groups=mesh['z'=16,'c'=2,'y'=4,'h'=2,'t'=2] {'z','c'}, dimensions={0} | all-to-all | bytes 32768 | tf_op jit(solution)/shard_map/all_to_all | solution.py:31
  153.6 0.2 fusion.11
  153.8 0.1 broadcast_in_dim.34
  153.8 9.1 %all_to_all.27 = f32[16,1,128]{2,1,0:T(1,128)S(1)} all-to-all(f32[16,1,128]{2,1,0:T(1,128)S(1)} %broadcast_in_dim.34), channel_id=1, replica_groups=mesh['z'=16,'c'=2,'y'=4,'h'=2,'t'=2] {'y','h','t'}, dimensions={0} | all-to-all | bytes 16384 | tf_op jit(solution)/shard_map/all_to_all | solution.py:31
  163.0 16.8 %all_to_all.28 = f32[32,1,128]{2,1,0:T(1,128)S(1)} all-to-all(f32[32,1,128]{2,1,0:T(1,128)S(1)} %broadcast_in_dim.35), channel_id=1, replica_groups=mesh['z'=16,'c'=2,'y'=4,'h'=2,'t'=2] {'z','c'}, dimensions={0} | all-to-all | bytes 32768 | tf_op jit(solution)/shard_map/all_to_all | solution.py:31
  179.8 0.7 shard_map.113
  (8 shorter events, 0.1 us)
Async XLA Ops:
  2.2 19.5 %all-to-all-start = ((bf16[16,10,640]{2,1,0:T(8,128)(2,1)}), bf16[16,10,640]{2,1,0:T(8,128)(2,1)S(1)}, u32[]{:S(2)}, u32[]{:S(2)}) async-start(bf16[16,10,640]{2,1,0:T(8,128)(2,1)} %get-tuple-element.24), calls=%async_computation | async-start | bytes 655360 | tf_op jit(solution)/shard_map/all_to_all | solution.py:31
  12.4 59.5 %collective-permute-start = (bf16[4096,128]{1,0:T(8,128)(2,1)}, bf16[4096,128]{1,0:T(8,128)(2,1)S(1)}, u32[]{:S(2)}, u32[]{:S(2)}) collective-permute-start(bf16[4096,128]{1,0:T(8,128)(2,1)} %bitcast.42), channel_id=1, source_target_pairs={{0,1},{1,0},{2,3},{3,2},{4,5},{5,4},{6,7},{7,6},{8,9},{9,8},{10,11... | collective-permute-start | bytes 3145736 | tf_op jit(solution)/shard_map/ppermute | solution.py:519
  14.4 57.6 %collective-permute-start.1 = (bf16[4096,128]{1,0:T(8,128)(2,1)}, bf16[4096,128]{1,0:T(8,128)(2,1)S(1)}, u32[]{:S(2)}, u32[]{:S(2)}) collective-permute-start(bf16[4096,128]{1,0:T(8,128)(2,1)} %bitcast.44), channel_id=1, source_target_pairs={{0,1},{1,0},{2,3},{3,2},{4,5},{5,4},{6,7},{7,6},{8,9},{9,8},{10,11... | collective-permute-start | bytes 3145736 | tf_op jit(solution)/shard_map/ppermute | solution.py:519
  68.0 1.2 copy-start
  68.0 1.5 copy-start.1
  73.2 45.7 %copy-start.2 = (bf16[1,8192,128]{2,1,0:T(8,128)(2,1)S(1)}, bf16[1,8192,128]{2,1,0:T(8,128)(2,1)}, u32[]{:S(2)}) copy-start(bf16[1,8192,128]{2,1,0:T(8,128)(2,1)} %param.16) | copy-start | bytes 6291460

commit v17 on v16

--- a/solution.py
+++ b/solution.py
@@ -257,10 +257,6 @@
         self.chips = x_ref.shape[0] // (HALVES * shard_rows)
         self.flat = self.chips * self.group
         self.columns = x_ref.shape[1] - LANES
-        x = x_ref[:, pl.ds(0, self.columns)].astype(F32)
-        self.parts = [
-            self.part(x, c, q).astype(BF16) for c in range(HALVES) for q in range(HALVES)
-        ]
         self.beside = x_ref[:, pl.ds(self.columns, LANES)].astype(F32)
         exponents = [self.part(self.beside, c, 0)[:, :LOW_LANES] for c in range(HALVES)]
         exponents = [jnp.concatenate([e] * (LANES // LOW_LANES), axis=1) for e in exponents]
@@ -272,6 +268,10 @@
         value = value[:, : self.group] if q == 0 else value[:, self.shard_rows - self.group :]
         return value.reshape(self.flat, value.shape[-1])
 
+    def parts(self):
+        x = self.x_ref[:, pl.ds(0, self.columns)].astype(F32)
+        return [self.part(x, c, q).astype(BF16) for c in range(HALVES) for q in range(HALVES)]
+
     def aligned(self, value, q):
         return value if q == 0 else pltpu.roll(value, self.flat - (self.group - self.rows), 0)
 
@@ -281,21 +281,15 @@
         )
 
 
-def near_kernel(
+def slots_kernel(
     shard_rows,
     block,
     own_ref,
     x_ref,
-    gate_ref,
-    up_ref,
     adapter_ref,
-    hidden_ref,
     factor_ref,
     base_ref,
     combiner_ref,
-    part_ref,
-    row_ref,
-    weight_ref,
     note_ref,
 ):
     r = Rows(x_ref, shard_rows)
@@ -303,15 +297,6 @@
     own_core, own_quarter = own_ref[0], own_ref[1]
     own_column = pl.multiple_of(own_ref[2], LANES)
     task, tensor, expert = own_ref[3], own_ref[4], own_ref[5]
-    shrink = jnp.exp2(-2.0 * r.row_exponent - 2.0)
-    for k in range(len(r.parts)):
-        part_ref[k] = r.parts[k]
-    for k, value in enumerate(r.scales + [shrink]):
-        row_ref[k] = value
-    hidden = hidden_rows(
-        r.parts, r.scales, shrink, r.group - r.rows, weight_ref, gate_ref, up_ref
-    )
-
     own = x_ref[:, pl.ds(own_column, LANES)].astype(F32)
     low = jnp.zeros((r.flat, LOW_LANES), F32)
     residual = jnp.zeros((r.flat, LANES), F32)
@@ -355,7 +340,6 @@
             for k in pair
         ]
         target = pl.ds(chip * r.rows, 2 * r.rows)
-        hidden_ref[target, :] = r.of_chips(hidden, pair)
         factor_ref[target, :] = jnp.concatenate(
             [w[: r.rows] for w in slot_weight], axis=0
         ) * r.of_chips(up_scale, pair)
@@ -376,6 +360,24 @@
         combiner_ref[pl.ds(e * 2 * r.rows, 2 * r.rows), :] = (place[e : e + 1] == row).astype(F32)
 
 
+def near_kernel(
+    shard_rows, x_ref, gate_ref, up_ref, hidden_ref, part_ref, row_ref, weight_ref
+):
+    r = Rows(x_ref, shard_rows)
+    parts = r.parts()
+    shrink = jnp.exp2(-2.0 * r.row_exponent - 2.0)
+    for k, value in enumerate(parts):
+        part_ref[k] = value
+    for k, value in enumerate(r.scales + [shrink]):
+        row_ref[k] = value
+    hidden = hidden_rows(
+        parts, r.scales, shrink, r.group - r.rows, weight_ref, gate_ref, up_ref
+    )
+    for chip in range(0, r.chips, 2):
+        target = pl.ds(chip * r.rows, 2 * r.rows)
+        hidden_ref[target, :] = r.of_chips(hidden, (chip, chip + 1))
+
+
 def far_kernel(
     rows, group, own_ref, part_ref, row_ref, gate_ref, up_ref, near_ref, hidden_ref, weight_ref
 ):
@@ -395,37 +397,48 @@
         hidden_ref[pl.ds(start, 2 * rows), :] = jnp.concatenate(pair, axis=0)
 
 
-def near_layer(gathered, weights, adapter_up, own, shard_rows, block, experts):
+def slots_layer(gathered, adapter_up, own, shard_rows, block, experts):
+    rows = gathered.shape[0]
+    chips = rows // (HALVES * shard_rows)
+    out = jax.ShapeDtypeStruct((rows // 4, LANES), F32)
+    vmem = pl.BlockSpec(memory_space=pltpu.VMEM)
+    return pl.pallas_call(
+        functools.partial(slots_kernel, shard_rows, block),
+        out_shape=(out, out, jax.ShapeDtypeStruct((experts * shard_rows, LANES), F32)),
+        in_specs=[pl.BlockSpec(memory_space=pltpu.SMEM), vmem, vmem],
+        out_specs=(vmem,) * 3,
+        scratch_shapes=[pltpu.VMEM((chips, NOTE_ROWS, LANES), F32)],
+        compiler_params=pltpu.CompilerParams(vmem_limit_bytes=12 * 2**20),
+        cost_estimate=pl.CostEstimate(
+            flops=64 * rows * LANES, bytes_accessed=16 * rows * LANES, transcendentals=rows * LANES
+        ),
+    )(own, gathered, adapter_up)
+
+
+def near_layer(gathered, weights, shard_rows):
     rows = gathered.shape[0]
     columns = gathered.shape[1] - LANES
     units = weights[0].shape[1]
     chips = rows // (HALVES * shard_rows)
     flat = chips * (-(-shard_rows // HALVES // 8) * 8)
-    out = jax.ShapeDtypeStruct((rows // 4, units), F32)
     vmem = pl.BlockSpec(memory_space=pltpu.VMEM)
     return pl.pallas_call(
-        functools.partial(near_kernel, shard_rows, block),
+        functools.partial(near_kernel, shard_rows),
         out_shape=(
-            out,
-            out,
-            out,
-            jax.ShapeDtypeStruct((experts * shard_rows, LANES), F32),
+            jax.ShapeDtypeStruct((rows // 4, units), F32),
             jax.ShapeDtypeStruct((2 * HALVES, flat, columns), BF16),
             jax.ShapeDtypeStruct((HALVES + 1, flat, LANES), F32),
         ),
-        in_specs=[pl.BlockSpec(memory_space=pltpu.SMEM)] + [vmem] * 4,
-        out_specs=(vmem,) * 6,
-        scratch_shapes=[
-            pltpu.VMEM((2 * HALVES, columns, 2 * units), BF16),
-            pltpu.VMEM((chips, NOTE_ROWS, LANES), F32),
-        ],
+        in_specs=[vmem] * 3,
+        out_specs=(vmem,) * 3,
+        scratch_shapes=[pltpu.VMEM((2 * HALVES, columns, 2 * units), BF16)],
         compiler_params=pltpu.CompilerParams(vmem_limit_bytes=16 * 2**20),
         cost_estimate=pl.CostEstimate(
             flops=4 * rows * columns * units,
             bytes_accessed=4 * rows * columns + 4 * columns * units,
             transcendentals=2 * rows * units,
         ),
-    )(own, gathered, *weights, adapter_up)
+    )(gathered, *weights)
 
 
 def far_layer(parts, row_scales, weights, near, tensor, shard_rows):
@@ -525,9 +538,8 @@
     gathered = gathered.astype(BF16).reshape(seq * shard_rows, columns + LANES)
     per_half = half // slice_width
     own_column = own_group * half + (s % per_half) * slice_width
-    near, factor, base, combiner, parts, row_scales = near_layer(
+    factor, base, combiner = slots_layer(
         gathered,
-        (expert_gate_weight[0], expert_up_weight[0]),
         adapter_up,
         jnp.stack(
             [
@@ -543,6 +555,9 @@
         shard_rows,
         rows,
         experts,
+    )
+    near, parts, row_scales = near_layer(
+        gathered, (expert_gate_weight[0], expert_up_weight[0]), shard_rows
     )
     hidden = far_layer(parts, row_scales, far_weights, near, t, shard_rows)
 

time: 181 us -> 181 us (level)
  transfers between devices with their start and end apart: 3 -> 3, of which waited for: 1 -> 1; matrix products, arithmetic and copies ran while one was open for 1% -> 1% of each run, Pallas kernels for 1% -> 2%
where the time goes in v17:
time: 181 us; the launch traced here: 180 us
  blocking collectives  150 us (83%)
  starting transfers between devices  15.5 us (9%)
  Pallas kernels  6.89 us (4%)
  waiting for transfers between devices  2.52 us (1%)
  matrix products  2.23 us (1%)
    all_to_all x4, blocking collectives, swap(): return lax.all_to_all(x, axes, split_axis=0, concat_axis=0, tiled=True)  59.4 us
    all_gather x1, blocking collectives, local(): hidden = lax.all_gather(hidden, SEQ, axis=0, tiled=True)  45.6 us
    all_gather x1, blocking collectives, local(): gathered = lax.all_gather(sent, SEQ, axis=0, tiled=False)  45.4 us
    all_to_all x1, starting transfers between devices, swap(): return lax.all_to_all(x, axes, split_axis=0, concat_axis=0, tiled=True)  10.2 us
    ppermute x2, starting transfers between devices, local(): far_weights = [lax.ppermute(w, 't', other) for w in later_weights]  5.27 us
  transfers between devices with their start and end apart: 3, of which 1 were waited for; matrix products, arithmetic and copies ran while one was open for 1% of the time, Pallas kernels for 2%

profile of v17, /device:TPU:1, one launch (start us, length us, event | category | flops | bytes accessed | tf_op | source)
XLA Modules:
  0.0 180.5 jit_solution(9803453831214272396)
XLA Ops:
  0.0 2.2 %shard_map.109 = (bf16[16,10,640]{2,1,0:T(8,128)(2,1)}, f32[20,128]{1,0:T(8,128)}) custom-call(s32[2,64]{1,0:T(2,128)} %bitcast.52, f32[2,64]{1,0:T(2,128)} %bitcast.53, bf16[64,512]{1,0:T(8,128)(2,1)} %refs_2_.1, bf16[32,512]{1,0:T(8,128)(2,1)} %refs_3_.1, bf16[32,512]{1,0:T(8,128)(2,1)} %refs_4_.1, f32[1,512]{1,0:T(1,128)} %bitcast.51), custom_call_target="tpu_custom_call" | custom-call | flops 10485760 | bytes 270336 | tf_op jit(solution)/shard_map/pallas_call | solution.py:138
  2.2 10.2 %all-to-all-start = ((bf16[16,10,640]{2,1,0:T(8,128)(2,1)}), bf16[16,10,640]{2,1,0:T(8,128)(2,1)S(1)}, u32[]{:S(2)}, u32[]{:S(2)}) async-start(bf16[16,10,640]{2,1,0:T(8,128)(2,1)} %get-tuple-element.24), calls=%async_computation | async-start | bytes 655360 | tf_op jit(solution)/shard_map/all_to_all | solution.py:31
  12.4 1.9 %collective-permute-start = (bf16[4096,128]{1,0:T(8,128)(2,1)}, bf16[4096,128]{1,0:T(8,128)(2,1)S(1)}, u32[]{:S(2)}, u32[]{:S(2)}) collective-permute-start(bf16[4096,128]{1,0:T(8,128)(2,1)} %bitcast.42), channel_id=1, source_target_pairs={{0,1},{1,0},{2,3},{3,2},{4,5},{5,4},{6,7},{7,6},{8,9},{9,8},{10,11... | collective-permute-start | bytes 3145736 | tf_op jit(solution)/shard_map/ppermute | solution.py:532
  14.4 3.4 %collective-permute-start.1 = (bf16[4096,128]{1,0:T(8,128)(2,1)}, bf16[4096,128]{1,0:T(8,128)(2,1)S(1)}, u32[]{:S(2)}, u32[]{:S(2)}) collective-permute-start(bf16[4096,128]{1,0:T(8,128)(2,1)} %bitcast.44), channel_id=1, source_target_pairs={{0,1},{1,0},{2,3},{3,2},{4,5},{5,4},{6,7},{7,6},{8,9},{9,8},{10,11... | collective-permute-start | bytes 3145736 | tf_op jit(solution)/shard_map/ppermute | solution.py:532
  19.1 0.1 stack.24.own_ref
  19.2 2.5 %all-to-all-done.received_ref = bf16[16,10,640]{2,1,0:T(8,128)(2,1)S(1)} async-done(((bf16[16,10,640]{2,1,0:T(8,128)(2,1)}), bf16[16,10,640]{2,1,0:T(8,128)(2,1)S(1)}, u32[]{:S(2)}, u32[]{:S(2)}) %all-to-all-start) | async-done | bytes 204832 | tf_op jit(solution)/shard_map/all_to_all | solution.py:31
  21.7 0.2 shard_map.110
  21.9 0.7 add_convert_fusion
  22.7 45.4 %all-gather.3 = f16[1280,1152]{1,0:T(8,128)(2,1)S(1)} all-gather(f16[40,1152]{1,0:T(8,128)(2,1)S(1)} %add_convert_fusion), channel_id=2, replica_groups=mesh['z'=16,'c'=2,'y'=4,'h'=2,'t'=2] {'z','c'}, dimensions={0}, use_global_device_ids=true | all-gather | bytes 3041280 | tf_op jit(solution)/shard_map/all_gather | solution.py:537
  68.0 0.0 copy-start
  68.0 0.0 copy-start.1
  68.0 0.5 convert_element_type.30.x_ref
  68.5 1.4 shard_map.113
  69.9 0.0 copy-done
  69.9 0.0 copy-done.1
  69.9 1.3 shard_map.111
  71.2 0.0 collective-permute-done.gate_ref
  71.2 0.0 collective-permute-done.1.up_ref
  71.2 1.1 shard_map.112
  72.3 0.0 copy-start.2
  72.4 45.6 %all-gather.4 = f16[64,320,128]{2,1,0:T(8,128)(2,1)S(1)} all-gather(f16[2,320,128]{2,1,0:T(8,128)(2,1)S(1)} %bitcast.48), channel_id=1, replica_groups=mesh['z'=16,'c'=2,'y'=4,'h'=2,'t'=2] {'z','c'}, dimensions={0}, use_global_device_ids=true | all-gather | bytes 5406720 | tf_op jit(solution)/shard_map/all_gather | solution.py:566
  118.0 0.0 copy-done.2
  118.0 1.5 fusion.8
  119.6 13.4 %all_to_all.25 = f32[16,20,128]{2,1,0:T(8,128)S(1)} all-to-all(f32[16,20,128]{2,1,0:T(8,128)S(1)} %reshape.74), channel_id=1, replica_groups=mesh['z'=16,'c'=2,'y'=4,'h'=2,'t'=2] {'y','h','t'}, dimensions={0} | all-to-all | bytes 327680 | tf_op jit(solution)/shard_map/all_to_all | solution.py:31
  133.0 0.5 multiply_reduce_fusion
  133.5 20.0 %all_to_all.26 = f32[32,1,128]{2,1,0:T(1,128)S(1)} all-to-all(f32[32,1,128]{2,1,0:T(1,128)S(1)} %broadcast_in_dim.32), channel_id=1, replica_groups=mesh['z'=16,'c'=2,'y'=4,'h'=2,'t'=2] {'z','c'}, dimensions={0} | all-to-all | bytes 32768 | tf_op jit(solution)/shard_map/all_to_all | solution.py:31
  153.5 0.2 fusion.11
  153.7 0.1 broadcast_in_dim.34
  153.8 9.1 %all_to_all.27 = f32[16,1,128]{2,1,0:T(1,128)S(1)} all-to-all(f32[16,1,128]{2,1,0:T(1,128)S(1)} %broadcast_in_dim.34), channel_id=1, replica_groups=mesh['z'=16,'c'=2,'y'=4,'h'=2,'t'=2] {'y','h','t'}, dimensions={0} | all-to-all | bytes 16384 | tf_op jit(solution)/shard_map/all_to_all | solution.py:31
  162.9 16.8 %all_to_all.28 = f32[32,1,128]{2,1,0:T(1,128)S(1)} all-to-all(f32[32,1,128]{2,1,0:T(1,128)S(1)} %broadcast_in_dim.35), channel_id=1, replica_groups=mesh['z'=16,'c'=2,'y'=4,'h'=2,'t'=2] {'z','c'}, dimensions={0} | all-to-all | bytes 32768 | tf_op jit(solution)/shard_map/all_to_all | solution.py:31
  179.8 0.7 shard_map.114
  (8 shorter events, 0.1 us)
Async XLA Ops:
  2.2 19.5 %all-to-all-start = ((bf16[16,10,640]{2,1,0:T(8,128)(2,1)}), bf16[16,10,640]{2,1,0:T(8,128)(2,1)S(1)}, u32[]{:S(2)}, u32[]{:S(2)}) async-start(bf16[16,10,640]{2,1,0:T(8,128)(2,1)} %get-tuple-element.24), calls=%async_computation | async-start | bytes 655360 | tf_op jit(solution)/shard_map/all_to_all | solution.py:31
  12.4 58.8 %collective-permute-start = (bf16[4096,128]{1,0:T(8,128)(2,1)}, bf16[4096,128]{1,0:T(8,128)(2,1)S(1)}, u32[]{:S(2)}, u32[]{:S(2)}) collective-permute-start(bf16[4096,128]{1,0:T(8,128)(2,1)} %bitcast.42), channel_id=1, source_target_pairs={{0,1},{1,0},{2,3},{3,2},{4,5},{5,4},{6,7},{7,6},{8,9},{9,8},{10,11... | collective-permute-start | bytes 3145736 | tf_op jit(solution)/shard_map/ppermute | solution.py:532
  14.4 56.9 %collective-permute-start.1 = (bf16[4096,128]{1,0:T(8,128)(2,1)}, bf16[4096,128]{1,0:T(8,128)(2,1)S(1)}, u32[]{:S(2)}, u32[]{:S(2)}) collective-permute-start(bf16[4096,128]{1,0:T(8,128)(2,1)} %bitcast.44), channel_id=1, source_target_pairs={{0,1},{1,0},{2,3},{3,2},{4,5},{5,4},{6,7},{7,6},{8,9},{9,8},{10,11... | collective-permute-start | bytes 3145736 | tf_op jit(solution)/shard_map/ppermute | solution.py:532
  68.0 1.9 %copy-start = (bf16[1,4096,128]{2,1,0:T(8,128)(2,1)S(1)}, bf16[1,4096,128]{2,1,0:T(8,128)(2,1)}, u32[]{:S(2)}) copy-start(bf16[1,4096,128]{2,1,0:T(8,128)(2,1)} %param.14) | copy-start | bytes 3145732
  68.0 1.9 %copy-start.1 = (bf16[1,4096,128]{2,1,0:T(8,128)(2,1)S(1)}, bf16[1,4096,128]{2,1,0:T(8,128)(2,1)}, u32[]{:S(2)}) copy-start(bf16[1,4096,128]{2,1,0:T(8,128)(2,1)} %param.15) | copy-start | bytes 3145732
  72.3 45.7 %copy-start.2 = (bf16[1,8192,128]{2,1,0:T(8,128)(2,1)S(1)}, bf16[1,8192,128]{2,1,0:T(8,128)(2,1)}, u32[]{:S(2)}) copy-start(bf16[1,8192,128]{2,1,0:T(8,128)(2,1)} %param.16) | copy-start | bytes 6291460

commit v18 on v17

--- a/solution.py
+++ b/solution.py
@@ -62,7 +62,7 @@
 
 
 def dispatch_kernel(*refs):
-    out_ref, note_ref, held, sem = refs[6], refs[7], refs[8:14], refs[14]
+    out_ref, held, sem = refs[6], refs[7:13], refs[13]
     core, chip = lax.axis_index("c"), lax.axis_index("z")
     copies = [pltpu.make_async_copy(refs[k], held[k], sem.at[k]) for k in range(6)]
     for copy in copies:
@@ -78,9 +78,21 @@
     first_slot = (lax.axis_index("t") * set_slots).astype(F32)
     ids = routes_ref[...]
     notes = jnp.concatenate([ids.astype(F32)] + list(rounded_parts(chosen_ref[...])), axis=0)
-    notes = jnp.concatenate([jnp.where(core == k, notes, 0.0) for k in range(HALVES)], axis=1)
-    note_ref[...] = jnp.zeros_like(note_ref)
-    note_ref[pl.ds(0, NOTE_ROWS), :] = notes
+    group = lax.axis_index("y") * lax.axis_size("h") + lax.axis_index("h")
+    mine = lax.broadcasted_iota(jnp.int32, notes.shape, 0) == group
+    note = jnp.sum(jnp.where(mine, notes, 0.0), axis=0, keepdims=True)
+    note = jnp.concatenate(
+        [note[:, :LOW_LANES], note[:, LOW_LANES:], jnp.zeros((set_slots - 2, LOW_LANES), F32)],
+        axis=0,
+    )
+    note = jnp.concatenate(
+        [
+            jnp.zeros((set_slots, half), F32),
+            note,
+            jnp.zeros((set_slots, LANES - LOW_LANES), F32),
+        ],
+        axis=1,
+    )
     expert = lax.broadcasted_iota(jnp.int32, (experts, rows), 0)
     place = slots_of((ids[:1] == expert) | (ids[1:] == expert), rows)
     padded = 16
@@ -123,9 +135,8 @@
         ]
         small = jnp.concatenate(small, axis=1).astype(BF16)
         for e in range(experts):
-            out_ref[e * HALVES + c, :, pl.ds(0, half + LANES)] = chosen[
-                e * padded : e * padded + set_slots
-            ].astype(BF16)
+            message = chosen[e * padded : e * padded + set_slots] + note
+            out_ref[e * HALVES + c, :, pl.ds(0, half + LANES)] = message.astype(BF16)
             out_ref[e * HALVES + c, :, pl.ds(half + LANES, 2 * LANES)] = small
 
 
@@ -137,12 +148,9 @@
     operands = (routes, chosen, tokens, adapter_down, adapter_up, norm_scale)
     return pl.pallas_call(
         dispatch_kernel,
-        out_shape=(
-            jax.ShapeDtypeStruct((experts * HALVES, set_slots, lanes), BF16),
-            jax.ShapeDtypeStruct((HALVES * set_slots, LANES), F32),
-        ),
+        out_shape=jax.ShapeDtypeStruct((experts * HALVES, set_slots, lanes), BF16),
         in_specs=[pl.BlockSpec(memory_space=pltpu.HBM)] * len(operands),
-        out_specs=(pl.BlockSpec(memory_space=pltpu.VMEM),) * 2,
+        out_specs=pl.BlockSpec(memory_space=pltpu.VMEM),
         scratch_shapes=[pltpu.VMEM(x.shape, x.dtype) for x in operands]
         + [pltpu.SemaphoreType.DMA((len(operands),))],
         compiler_params=pltpu.CompilerParams(vmem_limit_bytes=57 * 2**20),
@@ -177,7 +185,18 @@
         jnp.floor(jnp.log2(jnp.maximum(largest, 1e-30)) + 1.01), LEAST_EXPONENT
     )
     x = x * jnp.exp2(15.0 - exponent)
-    low = sum(both(e, half, LANES) for e in range(groups))
+    sides = [both(e, half, LANES) for e in range(groups)]
+    low = sum(sides)
+    notes = jnp.concatenate(
+        [
+            jnp.concatenate(
+                [side[r : r + 1, :LOW_LANES] for r in (0, 1, set_slots, set_slots + 1)], axis=1
+            )
+            for side in sides
+        ]
+        + [jnp.zeros((rows - groups, LANES), F32)],
+        axis=0,
+    )
     low = sum(low[:, k * LOW_LANES : (k + 1) * LOW_LANES] for k in range(1, 4))
     low = low * jnp.exp2(7.0 - exponent)
     beside = jnp.concatenate(
@@ -185,7 +204,7 @@
     )
     sent_ref[:, pl.ds(0, columns)] = jnp.concatenate([x[:, :columns], x[:, columns:]], axis=0)
     sent_ref[:, pl.ds(columns, LANES)] = jnp.concatenate(
-        [beside, jnp.zeros_like(beside)], axis=0
+        [beside, notes], axis=0
     )
 
     adapter = []
@@ -316,7 +335,7 @@
     )
     up_scale = jnp.exp2(2.0 * r.row_exponent + 2.0)
 
-    notes = sum(r.aligned(r.part(r.beside, c, 1), 1) for c in range(HALVES))
+    notes = r.aligned(r.part(r.beside, 0, 1), 1)
     notes = notes.reshape(r.chips, r.group, LANES)[:, :NOTE_ROWS]
     note_ref[...] = notes
     first, second = notes[:, 0, :].astype(jnp.int32), notes[:, 1, :].astype(jnp.int32)
@@ -515,7 +534,7 @@
     own_group = s // per_feature_group
 
     ids = routes.T
-    outgoing, notes = dispatch_layer(
+    outgoing = dispatch_layer(
         ids,
         chosen_expert_weight.T,
         tokens,
@@ -533,7 +552,7 @@
     received = swap(outgoing, EXPERT + ("c",))
 
     sent, adapter_up, norm_scale = rows_layer(own_group, received, task_rows)
-    sent = (sent + jnp.pad(notes, ((chip_rows, 0), (columns, 0)))).astype(F16)
+    sent = sent.astype(F16)
     gathered = lax.all_gather(sent, SEQ, axis=0, tiled=False)
     gathered = gathered.astype(BF16).reshape(seq * shard_rows, columns + LANES)
     per_half = half // slice_width

time: 181 us -> 181 us (level)
  transfers between devices with their start and end apart: 3 -> 3, of which waited for: 1 -> 1; matrix products, arithmetic and copies ran while one was open for 1% -> 0% of each run, Pallas kernels for 2% -> 2%
where the time goes in v18:
time: 181 us; the launch traced here: 180 us
  blocking collectives  151 us (83%)
  starting transfers between devices  15.5 us (9%)
  Pallas kernels  6.9 us (4%)
  waiting for transfers between devices  2.52 us (1%)
  matrix products  2.23 us (1%)
    all_to_all x4, blocking collectives, swap(): return lax.all_to_all(x, axes, split_axis=0, concat_axis=0, tiled=True)  60 us
    all_gather x1, blocking collectives, local(): hidden = lax.all_gather(hidden, SEQ, axis=0, tiled=True)  45.7 us
    all_gather x1, blocking collectives, local(): gathered = lax.all_gather(sent, SEQ, axis=0, tiled=False)  45.4 us
    all_to_all x1, starting transfers between devices, swap(): return lax.all_to_all(x, axes, split_axis=0, concat_axis=0, tiled=True)  10.2 us
    ppermute x2, starting transfers between devices, local(): far_weights = [lax.ppermute(w, 't', other) for w in later_weights]  5.27 us
  transfers between devices with their start and end apart: 3, of which 1 were waited for; matrix products, arithmetic and copies ran while one was open for 0% of the time, Pallas kernels for 2%

profile of v18, /device:TPU:1, one launch (start us, length us, event | category | flops | bytes accessed | tf_op | source)
XLA Modules:
  0.0 180.5 jit_solution(9766168351066762980)
XLA Ops:
  0.0 2.2 %shard_map.109 = bf16[16,10,640]{2,1,0:T(8,128)(2,1)} custom-call(s32[2,64]{1,0:T(2,128)} %bitcast.52, f32[2,64]{1,0:T(2,128)} %bitcast.53, bf16[64,512]{1,0:T(8,128)(2,1)} %refs_2_.1, bf16[32,512]{1,0:T(8,128)(2,1)} %refs_3_.1, bf16[32,512]{1,0:T(8,128)(2,1)} %refs_4_.1, f32[1,512]{1,0:T(1,128)} %bitcast.51), custom_call_target="tpu_custom_call" | custom-call | flops 10485760 | bytes 270336 | tf_op jit(solution)/shard_map/pallas_call | solution.py:149
  2.2 10.2 %all-to-all-start = ((bf16[16,10,640]{2,1,0:T(8,128)(2,1)}), bf16[16,10,640]{2,1,0:T(8,128)(2,1)S(1)}, u32[]{:S(2)}, u32[]{:S(2)}) async-start(bf16[16,10,640]{2,1,0:T(8,128)(2,1)} %shard_map.109), calls=%async_computation | async-start | bytes 655360 | tf_op jit(solution)/shard_map/all_to_all | solution.py:31
  12.4 1.9 %collective-permute-start = (bf16[4096,128]{1,0:T(8,128)(2,1)}, bf16[4096,128]{1,0:T(8,128)(2,1)S(1)}, u32[]{:S(2)}, u32[]{:S(2)}) collective-permute-start(bf16[4096,128]{1,0:T(8,128)(2,1)} %bitcast.42), channel_id=1, source_target_pairs={{0,1},{1,0},{2,3},{3,2},{4,5},{5,4},{6,7},{7,6},{8,9},{9,8},{10,11... | collective-permute-start | bytes 3145736 | tf_op jit(solution)/shard_map/ppermute | solution.py:551
  14.4 3.4 %collective-permute-start.1 = (bf16[4096,128]{1,0:T(8,128)(2,1)}, bf16[4096,128]{1,0:T(8,128)(2,1)S(1)}, u32[]{:S(2)}, u32[]{:S(2)}) collective-permute-start(bf16[4096,128]{1,0:T(8,128)(2,1)} %bitcast.44), channel_id=1, source_target_pairs={{0,1},{1,0},{2,3},{3,2},{4,5},{5,4},{6,7},{7,6},{8,9},{9,8},{10,11... | collective-permute-start | bytes 3145736 | tf_op jit(solution)/shard_map/ppermute | solution.py:551
  19.1 0.1 stack.24.own_ref
  19.2 2.5 %all-to-all-done.received_ref = bf16[16,10,640]{2,1,0:T(8,128)(2,1)S(1)} async-done(((bf16[16,10,640]{2,1,0:T(8,128)(2,1)}), bf16[16,10,640]{2,1,0:T(8,128)(2,1)S(1)}, u32[]{:S(2)}, u32[]{:S(2)}) %all-to-all-start) | async-done | bytes 204832 | tf_op jit(solution)/shard_map/all_to_all | solution.py:31
  21.7 0.2 shard_map.110
  21.9 45.4 %all-gather.3 = f16[1280,1152]{1,0:T(8,128)(2,1)S(1)} all-gather(f16[40,1152]{1,0:T(8,128)(2,1)S(1)} %convert_element_type.23), channel_id=2, replica_groups=mesh['z'=16,'c'=2,'y'=4,'h'=2,'t'=2] {'z','c'}, dimensions={0}, use_global_device_ids=true | all-gather | bytes 3041280 | tf_op jit(solution)/shard_map/all_gather | solution.py:556
  67.3 0.0 copy-start
  67.3 0.0 copy-start.1
  67.3 0.5 convert_element_type.28.x_ref
  67.8 1.4 shard_map.113
  69.2 0.0 copy-done
  69.2 0.0 copy-done.1
  69.2 1.3 shard_map.111
  70.5 0.0 collective-permute-done.gate_ref
  70.5 0.0 collective-permute-done.1.up_ref
  70.5 1.1 shard_map.112
  71.6 0.0 copy-start.2
  71.7 45.7 %all-gather.4 = f16[64,320,128]{2,1,0:T(8,128)(2,1)S(1)} all-gather(f16[2,320,128]{2,1,0:T(8,128)(2,1)S(1)} %bitcast.48), channel_id=1, replica_groups=mesh['z'=16,'c'=2,'y'=4,'h'=2,'t'=2] {'z','c'}, dimensions={0}, use_global_device_ids=true | all-gather | bytes 5406720 | tf_op jit(solution)/shard_map/all_gather | solution.py:585
  117.4 0.0 copy-done.2
  117.4 1.5 fusion.8
  118.9 14.0 %all_to_all.25 = f32[16,20,128]{2,1,0:T(8,128)S(1)} all-to-all(f32[16,20,128]{2,1,0:T(8,128)S(1)} %reshape.74), channel_id=1, replica_groups=mesh['z'=16,'c'=2,'y'=4,'h'=2,'t'=2] {'y','h','t'}, dimensions={0} | all-to-all | bytes 327680 | tf_op jit(solution)/shard_map/all_to_all | solution.py:31
  133.0 0.5 multiply_reduce_fusion
  133.5 20.0 %all_to_all.26 = f32[32,1,128]{2,1,0:T(1,128)S(1)} all-to-all(f32[32,1,128]{2,1,0:T(1,128)S(1)} %broadcast_in_dim.32), channel_id=1, replica_groups=mesh['z'=16,'c'=2,'y'=4,'h'=2,'t'=2] {'z','c'}, dimensions={0} | all-to-all | bytes 32768 | tf_op jit(solution)/shard_map/all_to_all | solution.py:31
  153.5 0.2 fusion.11
  153.7 0.1 broadcast_in_dim.34
  153.8 9.1 %all_to_all.27 = f32[16,1,128]{2,1,0:T(1,128)S(1)} all-to-all(f32[16,1,128]{2,1,0:T(1,128)S(1)} %broadcast_in_dim.34), channel_id=1, replica_groups=mesh['z'=16,'c'=2,'y'=4,'h'=2,'t'=2] {'y','h','t'}, dimensions={0} | all-to-all | bytes 16384 | tf_op jit(solution)/shard_map/all_to_all | solution.py:31
  162.9 16.8 %all_to_all.28 = f32[32,1,128]{2,1,0:T(1,128)S(1)} all-to-all(f32[32,1,128]{2,1,0:T(1,128)S(1)} %broadcast_in_dim.35), channel_id=1, replica_groups=mesh['z'=16,'c'=2,'y'=4,'h'=2,'t'=2] {'z','c'}, dimensions={0} | all-to-all | bytes 32768 | tf_op jit(solution)/shard_map/all_to_all | solution.py:31
  179.8 0.7 shard_map.114
  (9 shorter events, 0.1 us)
Async XLA Ops:
  2.2 19.5 %all-to-all-start = ((bf16[16,10,640]{2,1,0:T(8,128)(2,1)}), bf16[16,10,640]{2,1,0:T(8,128)(2,1)S(1)}, u32[]{:S(2)}, u32[]{:S(2)}) async-start(bf16[16,10,640]{2,1,0:T(8,128)(2,1)} %shard_map.109), calls=%async_computation | async-start | bytes 655360 | tf_op jit(solution)/shard_map/all_to_all | solution.py:31
  12.4 58.1 %collective-permute-start = (bf16[4096,128]{1,0:T(8,128)(2,1)}, bf16[4096,128]{1,0:T(8,128)(2,1)S(1)}, u32[]{:S(2)}, u32[]{:S(2)}) collective-permute-start(bf16[4096,128]{1,0:T(8,128)(2,1)} %bitcast.42), channel_id=1, source_target_pairs={{0,1},{1,0},{2,3},{3,2},{4,5},{5,4},{6,7},{7,6},{8,9},{9,8},{10,11... | collective-permute-start | bytes 3145736 | tf_op jit(solution)/shard_map/ppermute | solution.py:551
  14.4 56.2 %collective-permute-start.1 = (bf16[4096,128]{1,0:T(8,128)(2,1)}, bf16[4096,128]{1,0:T(8,128)(2,1)S(1)}, u32[]{:S(2)}, u32[]{:S(2)}) collective-permute-start(bf16[4096,128]{1,0:T(8,128)(2,1)} %bitcast.44), channel_id=1, source_target_pairs={{0,1},{1,0},{2,3},{3,2},{4,5},{5,4},{6,7},{7,6},{8,9},{9,8},{10,11... | collective-permute-start | bytes 3145736 | tf_op jit(solution)/shard_map/ppermute | solution.py:551
  67.3 1.9 %copy-start = (bf16[1,4096,128]{2,1,0:T(8,128)(2,1)S(1)}, bf16[1,4096,128]{2,1,0:T(8,128)(2,1)}, u32[]{:S(2)}) copy-start(bf16[1,4096,128]{2,1,0:T(8,128)(2,1)} %param.14) | copy-start | bytes 3145732
  67.3 1.9 %copy-start.1 = (bf16[1,4096,128]{2,1,0:T(8,128)(2,1)S(1)}, bf16[1,4096,128]{2,1,0:T(8,128)(2,1)}, u32[]{:S(2)}) copy-start(bf16[1,4096,128]{2,1,0:T(8,128)(2,1)} %param.15) | copy-start | bytes 3145732
  71.6 45.7 %copy-start.2 = (bf16[1,8192,128]{2,1,0:T(8,128)(2,1)S(1)}, bf16[1,8192,128]{2,1,0:T(8,128)(2,1)}, u32[]{:S(2)}) copy-start(bf16[1,8192,128]{2,1,0:T(8,128)(2,1)} %param.16) | copy-start | bytes 6291460

commit v19 on v18

--- a/solution.py
+++ b/solution.py
@@ -406,14 +406,15 @@
         parts, scales, row_ref[HALVES], group - rows, weight_ref, gate_ref, up_ref
     )
     chips = far.shape[0] // group
-    slots = chips * rows
-    near_at = own_ref[0] * slots
-    far_at = slots - near_at
-    hidden_ref[pl.ds(pl.multiple_of(near_at, 8), slots), :] = near_ref[...]
+    units = near_ref.shape[1]
+    near_at = pl.multiple_of(own_ref[0] * units, LANES)
+    far_at = pl.multiple_of((1 - own_ref[0]) * units, LANES)
+    hidden_ref[:, pl.ds(near_at, units)] = near_ref[...]
     for chip in range(0, chips, 2):
         pair = [far[k * group : k * group + rows] for k in (chip, chip + 1)]
-        start = pl.multiple_of(far_at + chip * rows, 8)
-        hidden_ref[pl.ds(start, 2 * rows), :] = jnp.concatenate(pair, axis=0)
+        hidden_ref[pl.ds(chip * rows, 2 * rows), pl.ds(far_at, units)] = jnp.concatenate(
+            pair, axis=0
+        )
 
 
 def slots_layer(gathered, adapter_up, own, shard_rows, block, experts):
@@ -467,7 +468,7 @@
     vmem = pl.BlockSpec(memory_space=pltpu.VMEM)
     return pl.pallas_call(
         functools.partial(far_kernel, rows, flat * rows // slots),
-        out_shape=jax.ShapeDtypeStruct((2 * slots, units), F32),
+        out_shape=jax.ShapeDtypeStruct((slots, 2 * units), F32),
         in_specs=[pl.BlockSpec(memory_space=pltpu.SMEM)] + [vmem] * 5,
         out_specs=vmem,
         scratch_shapes=[pltpu.VMEM((2 * HALVES, columns, 2 * units), BF16)],
@@ -581,12 +582,11 @@
     hidden = far_layer(parts, row_scales, far_weights, near, t, shard_rows)
 
     units = hidden.shape[-1]
-    hidden = hidden.astype(F16).reshape(tensors, -1, units)
-    hidden = lax.all_gather(hidden, SEQ, axis=0, tiled=True)
+    hidden = lax.all_gather(hidden.astype(F16), SEQ, axis=0, tiled=False)
     hidden, down = lax.optimization_barrier((hidden, expert_down_weight[0]))
     part = lax.dot_general(
         hidden.astype(BF16),
-        down.reshape(seq * tensors, units, slice_width),
+        down.reshape(seq, units, slice_width),
         (((0, 2), (0, 1)), ((), ())),
         preferred_element_type=F32,
     )

time: 181 us -> 181 us (level)
  no operation moved by 1% of the time
where the time goes in v19:
time: 181 us; the launch traced here: 180 us
  blocking collectives  151 us (83%)
  starting transfers between devices  15.5 us (9%)
  Pallas kernels  6.9 us (4%)
  waiting for transfers between devices  2.52 us (1%)
  matrix products  2.22 us (1%)
    all_to_all x4, blocking collectives, swap(): return lax.all_to_all(x, axes, split_axis=0, concat_axis=0, tiled=True)  60 us
    all_gather x1, blocking collectives, local(): hidden = lax.all_gather(hidden.astype(F16), SEQ, axis=0, tiled=False)  45.7 us
    all_gather x1, blocking collectives, local(): gathered = lax.all_gather(sent, SEQ, axis=0, tiled=False)  45.4 us
    all_to_all x1, starting transfers between devices, swap(): return lax.all_to_all(x, axes, split_axis=0, concat_axis=0, tiled=True)  10.2 us
    ppermute x2, starting transfers between devices, local(): far_weights = [lax.ppermute(w, 't', other) for w in later_weights]  5.27 us
  transfers between devices with their start and end apart: 3, of which 1 were waited for; matrix products, arithmetic and copies ran while one was open for 0% of the time, Pallas kernels for 2%

profile of v19, /device:TPU:1, one launch (start us, length us, event | category | flops | bytes accessed | tf_op | source)
XLA Modules:
  0.0 180.5 jit_solution(9139817253549459705)
XLA Ops:
  0.0 2.2 %shard_map.109 = bf16[16,10,640]{2,1,0:T(8,128)(2,1)} custom-call(s32[2,64]{1,0:T(2,128)} %bitcast.52, f32[2,64]{1,0:T(2,128)} %bitcast.53, bf16[64,512]{1,0:T(8,128)(2,1)} %refs_2_.1, bf16[32,512]{1,0:T(8,128)(2,1)} %refs_3_.1, bf16[32,512]{1,0:T(8,128)(2,1)} %refs_4_.1, f32[1,512]{1,0:T(1,128)} %bitcast.51), custom_call_target="tpu_custom_call" | custom-call | flops 10485760 | bytes 270336 | tf_op jit(solution)/shard_map/pallas_call | solution.py:149
  2.2 10.2 %all-to-all-start = ((bf16[16,10,640]{2,1,0:T(8,128)(2,1)}), bf16[16,10,640]{2,1,0:T(8,128)(2,1)S(1)}, u32[]{:S(2)}, u32[]{:S(2)}) async-start(bf16[16,10,640]{2,1,0:T(8,128)(2,1)} %shard_map.109), calls=%async_computation | async-start | bytes 655360 | tf_op jit(solution)/shard_map/all_to_all | solution.py:31
  12.4 1.9 %collective-permute-start = (bf16[4096,128]{1,0:T(8,128)(2,1)}, bf16[4096,128]{1,0:T(8,128)(2,1)S(1)}, u32[]{:S(2)}, u32[]{:S(2)}) collective-permute-start(bf16[4096,128]{1,0:T(8,128)(2,1)} %bitcast.42), channel_id=1, source_target_pairs={{0,1},{1,0},{2,3},{3,2},{4,5},{5,4},{6,7},{7,6},{8,9},{9,8},{10,11... | collective-permute-start | bytes 3145736 | tf_op jit(solution)/shard_map/ppermute | solution.py:552
  14.4 3.4 %collective-permute-start.1 = (bf16[4096,128]{1,0:T(8,128)(2,1)}, bf16[4096,128]{1,0:T(8,128)(2,1)S(1)}, u32[]{:S(2)}, u32[]{:S(2)}) collective-permute-start(bf16[4096,128]{1,0:T(8,128)(2,1)} %bitcast.44), channel_id=1, source_target_pairs={{0,1},{1,0},{2,3},{3,2},{4,5},{5,4},{6,7},{7,6},{8,9},{9,8},{10,11... | collective-permute-start | bytes 3145736 | tf_op jit(solution)/shard_map/ppermute | solution.py:552
  19.1 0.1 stack.24.own_ref
  19.2 2.5 %all-to-all-done.received_ref = bf16[16,10,640]{2,1,0:T(8,128)(2,1)S(1)} async-done(((bf16[16,10,640]{2,1,0:T(8,128)(2,1)}), bf16[16,10,640]{2,1,0:T(8,128)(2,1)S(1)}, u32[]{:S(2)}, u32[]{:S(2)}) %all-to-all-start) | async-done | bytes 204832 | tf_op jit(solution)/shard_map/all_to_all | solution.py:31
  21.7 0.2 shard_map.110
  21.9 45.4 %all-gather.4 = f16[1280,1152]{1,0:T(8,128)(2,1)S(1)} all-gather(f16[40,1152]{1,0:T(8,128)(2,1)S(1)} %convert_element_type.23), channel_id=2, replica_groups=mesh['z'=16,'c'=2,'y'=4,'h'=2,'t'=2] {'z','c'}, dimensions={0}, use_global_device_ids=true | all-gather | bytes 3041280 | tf_op jit(solution)/shard_map/all_gather | solution.py:557
  67.3 0.0 copy-start
  67.3 0.0 copy-start.1
  67.3 0.5 convert_element_type.28.x_ref
  67.8 1.4 shard_map.113
  69.2 0.0 copy-done
  69.2 0.0 copy-done.1
  69.2 1.3 shard_map.111
  70.5 0.0 collective-permute-done.gate_ref
  70.5 0.0 collective-permute-done.1.up_ref
  70.5 1.1 shard_map.112
  71.6 0.0 copy-start.2
  71.7 45.7 %all-gather.5 = f16[10240,256]{1,0:T(8,128)(2,1)S(1)} all-gather(f16[320,256]{1,0:T(8,128)(2,1)S(1)} %convert_element_type.25), channel_id=3, replica_groups=mesh['z'=16,'c'=2,'y'=4,'h'=2,'t'=2] {'z','c'}, dimensions={0}, use_global_device_ids=true | all-gather | bytes 5406720 | tf_op jit(solution)/shard_map/all_gather | solution.py:585
  117.4 0.0 copy-done.2
  117.4 1.5 fusion.8
  118.9 14.0 %all_to_all.25 = f32[16,20,128]{2,1,0:T(8,128)S(1)} all-to-all(f32[16,20,128]{2,1,0:T(8,128)S(1)} %reshape.70), channel_id=1, replica_groups=mesh['z'=16,'c'=2,'y'=4,'h'=2,'t'=2] {'y','h','t'}, dimensions={0} | all-to-all | bytes 327680 | tf_op jit(solution)/shard_map/all_to_all | solution.py:31
  133.0 0.5 multiply_reduce_fusion
  133.5 20.0 %all_to_all.26 = f32[32,1,128]{2,1,0:T(1,128)S(1)} all-to-all(f32[32,1,128]{2,1,0:T(1,128)S(1)} %broadcast_in_dim.32), channel_id=1, replica_groups=mesh['z'=16,'c'=2,'y'=4,'h'=2,'t'=2] {'z','c'}, dimensions={0} | all-to-all | bytes 32768 | tf_op jit(solution)/shard_map/all_to_all | solution.py:31
  153.5 0.2 fusion.11
  153.7 0.1 broadcast_in_dim.34
  153.8 9.1 %all_to_all.27 = f32[16,1,128]{2,1,0:T(1,128)S(1)} all-to-all(f32[16,1,128]{2,1,0:T(1,128)S(1)} %broadcast_in_dim.34), channel_id=1, replica_groups=mesh['z'=16,'c'=2,'y'=4,'h'=2,'t'=2] {'y','h','t'}, dimensions={0} | all-to-all | bytes 16384 | tf_op jit(solution)/shard_map/all_to_all | solution.py:31
  162.9 16.8 %all_to_all.28 = f32[32,1,128]{2,1,0:T(1,128)S(1)} all-to-all(f32[32,1,128]{2,1,0:T(1,128)S(1)} %broadcast_in_dim.35), channel_id=1, replica_groups=mesh['z'=16,'c'=2,'y'=4,'h'=2,'t'=2] {'z','c'}, dimensions={0} | all-to-all | bytes 32768 | tf_op jit(solution)/shard_map/all_to_all | solution.py:31
  179.8 0.7 shard_map.114
  (9 shorter events, 0.1 us)
Async XLA Ops:
  2.2 19.5 %all-to-all-start = ((bf16[16,10,640]{2,1,0:T(8,128)(2,1)}), bf16[16,10,640]{2,1,0:T(8,128)(2,1)S(1)}, u32[]{:S(2)}, u32[]{:S(2)}) async-start(bf16[16,10,640]{2,1,0:T(8,128)(2,1)} %shard_map.109), calls=%async_computation | async-start | bytes 655360 | tf_op jit(solution)/shard_map/all_to_all | solution.py:31
  12.4 58.1 %collective-permute-start = (bf16[4096,128]{1,0:T(8,128)(2,1)}, bf16[4096,128]{1,0:T(8,128)(2,1)S(1)}, u32[]{:S(2)}, u32[]{:S(2)}) collective-permute-start(bf16[4096,128]{1,0:T(8,128)(2,1)} %bitcast.42), channel_id=1, source_target_pairs={{0,1},{1,0},{2,3},{3,2},{4,5},{5,4},{6,7},{7,6},{8,9},{9,8},{10,11... | collective-permute-start | bytes 3145736 | tf_op jit(solution)/shard_map/ppermute | solution.py:552
  14.4 56.2 %collective-permute-start.1 = (bf16[4096,128]{1,0:T(8,128)(2,1)}, bf16[4096,128]{1,0:T(8,128)(2,1)S(1)}, u32[]{:S(2)}, u32[]{:S(2)}) collective-permute-start(bf16[4096,128]{1,0:T(8,128)(2,1)} %bitcast.44), channel_id=1, source_target_pairs={{0,1},{1,0},{2,3},{3,2},{4,5},{5,4},{6,7},{7,6},{8,9},{9,8},{10,11... | collective-permute-start | bytes 3145736 | tf_op jit(solution)/shard_map/ppermute | solution.py:552
  67.3 1.9 %copy-start = (bf16[1,4096,128]{2,1,0:T(8,128)(2,1)S(1)}, bf16[1,4096,128]{2,1,0:T(8,128)(2,1)}, u32[]{:S(2)}) copy-start(bf16[1,4096,128]{2,1,0:T(8,128)(2,1)} %param.14) | copy-start | bytes 3145732
  67.3 1.9 %copy-start.1 = (bf16[1,4096,128]{2,1,0:T(8,128)(2,1)S(1)}, bf16[1,4096,128]{2,1,0:T(8,128)(2,1)}, u32[]{:S(2)}) copy-start(bf16[1,4096,128]{2,1,0:T(8,128)(2,1)} %param.15) | copy-start | bytes 3145732
  71.6 45.7 %copy-start.2 = (bf16[1,8192,128]{2,1,0:T(8,128)(2,1)S(1)}, bf16[1,8192,128]{2,1,0:T(8,128)(2,1)}, u32[]{:S(2)}) copy-start(bf16[1,8192,128]{2,1,0:T(8,128)(2,1)} %param.16) | copy-start | bytes 6291460
